TPU v7x, 32 devices: a whole 2x2x4 slice. The times are simulated.
32 devices in a mesh: dp: 2 (over x), ctx: 16 (over z, y, core).
Axes of the slice: x: 2, y: 2, z: 4, core: 2. Of those that a mesh axis runs over, the one named last changes fastest.
Arguments:
- queries: bfloat16 [4, 1024, 2048], P('dp', 'ctx'), may hold values from -52 to 52
- key_rows: bfloat16 [4, 1024, 2048], P('dp', 'ctx'), may hold values from -4 to 4
- value_rows: bfloat16 [4, 1024, 2048], P('dp', 'ctx'), may hold values from -6 to 6
- out_grad: bfloat16 [4, 1024, 2048], P('dp', 'ctx'), may hold values from -64 to 64
- level_slope: float32 [16], replicated, may hold values from -0.5 to 0.5
Outputs:
- query_grad: bfloat16 [4, 1024, 2048], P('dp', 'ctx')
- key_grad: bfloat16 [4, 1024, 2048], P('dp', 'ctx')
- value_grad: bfloat16 [4, 1024, 2048], P('dp', 'ctx')
- slope_grad: float32 [16], replicated
All inputs are finite; a program needn't handle non-finite values.
Results may differ from a plain program's by a relative error of at most 0.0075.
Values may be sent and summed in bfloat16 or wider, within the bound.
No kernel may reach another device: no remote copies, remote signals or barrier semaphores. Data moves between devices by JAX's collectives and lax.ppermute only.
A program may use at most 64 MiB of HBM per device.

v0:
```python
import math

import jax
import jax.numpy as jnp
from jax import lax
from jax.sharding import PartitionSpec as P


def as_sent(x):
    return jax.tree.map(lambda a: a.astype(jnp.bfloat16) if a.dtype == jnp.float32 else a, x)


def from_partner(value, axis, apart):
    mask = 2**apart
    pairs = [(source, source ^ mask) for source in range(lax.axis_size(axis))]
    return lax.ppermute(value, axis, pairs)


def pair_mean(cells):
    shaped = cells.reshape(cells.shape[:-2] + (cells.shape[-2] // 2, 2, cells.shape[-1])).astype(
        jnp.float32
    )
    return ((shaped[..., 0, :] + shaped[..., 1, :]) * 0.5).astype(jnp.bfloat16)


def merge_level(own_pair, other_pair, flag):
    merged = []
    for own_part, other_part in zip(own_pair, other_pair):
        own_small = pair_mean(own_part)
        other_small = pair_mean(other_part)
        merged.append(
            jnp.where(
                flag == 1,
                jnp.concatenate([other_small, own_small], axis=1),
                jnp.concatenate([own_small, other_small], axis=1),
            )
        )
    return tuple(merged)


def to_heads(rows, heads):
    seqs, count, width = rows.shape
    return jnp.transpose(rows.reshape(seqs, count, heads, width // heads), (0, 2, 1, 3))


def from_heads(split):
    seqs, heads, count, head = split.shape
    return jnp.transpose(split, (0, 2, 1, 3)).reshape(seqs, count, heads * head)


def product(form, left, right):
    return jnp.einsum(form, left, right, preferred_element_type=jnp.float32)


def attend(query_four, key_four, value_four, grad_four, level_slope, block):
    head = query_four.shape[3]
    key_count = key_four.shape[2]
    scale = 1.0 / math.sqrt(head)
    column = jnp.arange(key_count, dtype=jnp.int32)
    level_of = column // block - 1
    sibling = jnp.maximum(level_of, 0)
    multiple = jnp.where(level_of < 0, 1.0, jnp.exp2(sibling.astype(jnp.float32)))
    bias = level_slope[:, None] * sibling.astype(jnp.float32)[None, :]
    raw = product("shqd,shkd->shqk", query_four, key_four)
    scores = raw * scale + bias[None, :, None, :]
    top = jnp.max(scores, axis=-1, keepdims=True)
    weights = multiple[None, None, None, :] * jnp.exp(scores - top)
    probs = weights / jnp.sum(weights, axis=-1, keepdims=True)
    probs_low = probs.astype(jnp.bfloat16)
    output = product("shqk,shkd->shqd", probs_low, value_four)
    delta = jnp.sum(grad_four.astype(jnp.float32) * output, axis=-1)
    upstream = product("shqd,shkd->shqk", grad_four, value_four)
    dscore = probs * (upstream - delta[..., None])
    slope_part = jnp.sum(dscore * sibling.astype(jnp.float32)[None, None, None, :], axis=(0, 2, 3))
    dscore_low = dscore.astype(jnp.bfloat16)
    query_part = product("shqk,shkd->shqd", dscore_low, key_four) * scale
    key_part = product("shqk,shqd->shkd", dscore_low, query_four) * scale
    value_part = product("shqk,shqd->shkd", probs_low, grad_four)
    return (query_part, key_part, value_part, slope_part)


def split_level(grad_now, direct, flag, level, block):
    half = block // 2
    lower_src = grad_now[:, :, :half]
    upper_src = grad_now[:, :, half:]
    own_src = jnp.where(flag == 1, upper_src, lower_src)
    other_src = jnp.where(flag == 1, lower_src, upper_src)
    own_half = jnp.repeat(own_src, 2, axis=2) * 0.5
    other_half = jnp.repeat(other_src, 2, axis=2) * 0.5
    sent = (other_half + direct[:, :, (level + 1) * block : (level + 2) * block]).astype(
        jnp.bfloat16
    )
    return (own_half, sent)


def shards(queries, key_rows, value_rows, out_grad, level_slope):
    seqs, block, width = queries.shape
    heads = level_slope.shape[0]
    ctx_count = lax.axis_size("ctx")
    levels = ctx_count.bit_length() - 1
    position = lax.axis_index("ctx")
    bit_list = [position // 2**level % 2 for level in range(levels)]
    own_pair = (key_rows, value_rows)
    partners = []
    for level in range(levels - 2):
        other_pair = jax.tree.map(
            lambda part, own: part.astype(own.dtype),
            from_partner(as_sent(own_pair), "ctx", level),
            own_pair,
        )
        partners.append(other_pair)
        own_pair = merge_level(own_pair, other_pair, bit_list[level])
    for level in range(levels - 2, levels):
        other_pair = jax.tree.map(
            lambda part, own: part.astype(own.dtype),
            from_partner(as_sent(own_pair), "ctx", level),
            own_pair,
        )
        partners.append(other_pair)
        if level + 1 < levels:
            own_pair = merge_level(own_pair, other_pair, bit_list[level])
    key_set = jnp.concatenate(
        [to_heads(key_rows, heads)] + [to_heads(pair[0], heads) for pair in partners], axis=2
    )
    value_set = jnp.concatenate(
        [to_heads(value_rows, heads)] + [to_heads(pair[1], heads) for pair in partners], axis=2
    )
    query_four = to_heads(queries, heads)
    grad_four = to_heads(out_grad, heads)
    query_part, key_part, value_part, slope_part = attend(
        query_four, key_set, value_set, grad_four, level_slope, block
    )
    slope_grad = lax.psum(slope_part, ("dp", "ctx"))
    head = width // heads
    grad_keys = jnp.zeros((seqs, heads, block, head), jnp.float32)
    grad_values = jnp.zeros((seqs, heads, block, head), jnp.float32)
    for level in reversed(range(levels)):
        own_keys, sent_keys = split_level(grad_keys, key_part, bit_list[level], level, block)
        own_values, sent_values = split_level(
            grad_values, value_part, bit_list[level], level, block
        )
        back_keys, back_values = from_partner((sent_keys, sent_values), "ctx", level)
        grad_keys = own_keys + back_keys.astype(jnp.float32)
        grad_values = own_values + back_values.astype(jnp.float32)
    key_grad = from_heads((grad_keys + key_part[:, :, :block]).astype(jnp.bfloat16))
    value_grad = from_heads((grad_values + value_part[:, :, :block]).astype(jnp.bfloat16))
    return (from_heads(query_part.astype(jnp.bfloat16)), key_grad, value_grad, slope_grad)


def solution(mesh):
    placed = (
        P("dp", "ctx", None),
        P("dp", "ctx", None),
        P("dp", "ctx", None),
        P("dp", "ctx", None),
        P(),
    )
    return jax.shard_map(
        shards,
        mesh=mesh,
        in_specs=placed,
        out_specs=(P("dp", "ctx", None), P("dp", "ctx", None), P("dp", "ctx", None), P()),
        check_vma=False,
    )
```

profile of v0, /device:TPU:0, one launch (start us, length us, event | category | flops | bytes accessed | tf_op | source)
XLA Modules:
  0.0 241.0 jit_solution(9212115930186061034)
XLA Ops:
  1.3 2.7 %copy.60 = f32[2,64,2048]{2,0,1:T(2,128)} copy(bf16[2,64,2048]{2,1,0:T(8,128)(2,1)} %param.6) | data formatting | bytes 1572864 | tf_op jit(solution)/shard_map/convert_element_type | solution.py:20
  3.9 2.5 %copy.83 = f32[2,64,2048]{2,0,1:T(2,128)} copy(bf16[2,64,2048]{2,1,0:T(8,128)(2,1)} %param.7) | data formatting | bytes 1572864 | tf_op jit(solution)/shard_map/convert_element_type | solution.py:20
  7.6 1.7 fusion.44
  10.2 1.6 copy.80
  12.3 1.6 copy.58
  15.5 3.0 %collective-permute-start.1 = (bf16[2,64,2048]{2,0,1:T(2,128)(2,1)S(1)}, bf16[2,64,2048]{2,0,1:T(2,128)(2,1)S(1)}, u32[]{:S(2)}, u32[]{:S(2)}) collective-permute-start(bf16[2,64,2048]{2,0,1:T(2,128)(2,1)S(1)} %broadcast_select_fusion.5), channel_id=1, source_target_pairs={{0,2},{1,3},{2,0},{3,1},{4,6},{5,7},{6,4},{7,5},{8,10},{9,11},{10,... | collective-permute-start | bytes 1572872 | tf_op jit(solution)/shard_map/ppermute | solution.py:16
  22.0 2.1 fusion.25
  24.1 7.1 %collective-permute-done.1 = bf16[2,64,2048]{2,0,1:T(2,128)(2,1)S(1)} collective-permute-done((bf16[2,64,2048]{2,0,1:T(2,128)(2,1)S(1)}, bf16[2,64,2048]{2,0,1:T(2,128)(2,1)S(1)}, u32[]{:S(2)}, u32[]{:S(2)}) %collective-permute-start.1) | collective-permute-done | bytes 524320 | tf_op jit(solution)/shard_map/ppermute | solution.py:16
  32.7 1.9 broadcast_select_fusion.3
  34.7 2.1 collective-permute-start.2
  36.8 1.6 convert.23
  39.1 2.8 %collective-permute-done.5 = bf16[2,64,2048]{2,0,1:T(2,128)(2,1)S(1)} collective-permute-done((bf16[2,64,2048]{2,0,1:T(2,128)(2,1)S(1)}, bf16[2,64,2048]{2,0,1:T(2,128)(2,1)S(1)}, u32[]{:S(2)}, u32[]{:S(2)}) %collective-permute-start.5) | collective-permute-done | bytes 524320 | tf_op jit(solution)/shard_map/ppermute | solution.py:16
  43.4 2.0 broadcast_select_fusion.2
  45.4 1.8 collective-permute-start.6
  47.2 2.2 reshape.287
  49.3 1.3 bitcast_dynamic-update-slice_fusion.5
  50.6 2.2 reshape.290
  52.8 2.1 bitcast_dynamic-update-slice_fusion.2
  54.9 1.6 convert.27
  56.9 1.6 convert.22
  58.9 1.9 broadcast_select_fusion.1
  60.9 2.6 %collective-permute-start.3 = (bf16[2,64,2048]{2,0,1:T(2,128)(2,1)}, bf16[2,64,2048]{2,0,1:T(2,128)(2,1)}, u32[]{:S(2)}, u32[]{:S(2)}) collective-permute-start(bf16[2,64,2048]{2,0,1:T(2,128)(2,1)} %broadcast_select_fusion.1), channel_id=1, source_target_pairs={{0,8},{1,9},{2,10},{3,11},{4,12},{5,13},{6,14},{7,15},{8,0},{9,1},... | collective-permute-start | bytes 1572872 | tf_op jit(solution)/shard_map/ppermute | solution.py:16
  63.5 1.6 convert.26
  65.5 1.9 broadcast_select_fusion
  67.7 2.2 reshape.288
  69.9 1.3 bitcast_dynamic-update-slice_fusion.4
  71.2 2.2 reshape.291
  73.4 2.0 bitcast_dynamic-update-slice_fusion.1
  75.4 22.1 %collective-permute-done.3 = bf16[2,64,2048]{2,0,1:T(2,128)(2,1)} collective-permute-done((bf16[2,64,2048]{2,0,1:T(2,128)(2,1)}, bf16[2,64,2048]{2,0,1:T(2,128)(2,1)}, u32[]{:S(2)}, u32[]{:S(2)}) %collective-permute-start.3) | collective-permute-done | bytes 524320 | tf_op jit(solution)/shard_map/ppermute | solution.py:16
  97.5 2.2 reshape.289
  99.7 1.3 bitcast_dynamic-update-slice_fusion.3
  101.0 7.7 %collective-permute-done.7 = bf16[2,64,2048]{2,0,1:T(2,128)(2,1)} collective-permute-done((bf16[2,64,2048]{2,0,1:T(2,128)(2,1)}, bf16[2,64,2048]{2,0,1:T(2,128)(2,1)}, u32[]{:S(2)}, u32[]{:S(2)}) %collective-permute-start.7) | collective-permute-done | bytes 524320 | tf_op jit(solution)/shard_map/ppermute | solution.py:16
  108.7 2.2 reshape.292
  110.8 2.1 bitcast_dynamic-update-slice_fusion
  112.9 12.7 %fusion.27 = f32[2,16,320,64]{2,3,1,0:T(8,128)S(1)} fusion(bf16[2,16,320,128]{3,2,1,0:T(8,128)(2,1)S(1)} %bitcast_dynamic-update-slice_fusion.3, bf16[2,64,2048]{2,1,0:T(8,128)(2,1)} %param.5), kind=kOutput, calls=%fused_computation.61 | convolution fusion | flops 167772160 | bytes 5767168 | tf_op jit(solution)/shard_map/shqd,shkd->shqk/dot_general | solution.py:52
  125.6 1.3 fusion.87
  126.9 1.4 fusion.24
  129.5 1.4 multiply_reduce_fusion
  132.0 1.5 fusion.11
  133.5 44.7 %psum.7 = f32[16]{0:T(128)} all-reduce(f32[16]{0:T(128)S(1)} %get-tuple-element.18), channel_id=1, replica_groups=mesh['dp'=2,'ctx'=16] {'dp','ctx'}, use_global_device_ids=true, to_apply=%region_4.5 | all-reduce | flops 16 | bytes 128 | tf_op jit(solution)/shard_map/psum | solution.py:133
  178.2 2.1 copy.183
  180.3 2.4 %broadcast_multiply_fusion = f32[2,16,320,128]{3,2,1,0:T(8,128)S(1)} fusion(bf16[2,16,64,320]{3,2,1,0:T(8,128)(2,1)} %copy-done.2, bf16[2,64,2048]{2,1,0:T(8,128)(2,1)S(1)} %copy-done.5), kind=kOutput, calls=%fused_computation.9 | convolution fusion | flops 169082880 | bytes 7077888 | tf_op jit(solution)/shard_map/shqk,shqd->shkd/dot_general | solution.py:52
  184.8 2.1 collective-permute-start.13
  186.9 20.7 %collective-permute-done.8 = bf16[2,16,64,128]{3,2,1,0:T(8,128)(2,1)S(1)} collective-permute-done((bf16[2,16,64,128]{3,2,1,0:T(8,128)(2,1)S(1)}, bf16[2,16,64,128]{3,2,1,0:T(8,128)(2,1)S(1)}, u32[]{:S(2)}, u32[]{:S(2)}) %collective-permute-start.8) | collective-permute-done | bytes 524320 | tf_op jit(solution)/shard_map/ppermute | solution.py:16
  210.2 1.4 collective-permute-start.14
  211.6 10.5 %collective-permute-done.9 = bf16[2,16,64,128]{3,2,1,0:T(8,128)(2,1)S(1)} collective-permute-done((bf16[2,16,64,128]{3,2,1,0:T(8,128)(2,1)S(1)}, bf16[2,16,64,128]{3,2,1,0:T(8,128)(2,1)S(1)}, u32[]{:S(2)}, u32[]{:S(2)}) %collective-permute-start.9) | collective-permute-done | bytes 524320 | tf_op jit(solution)/shard_map/ppermute | solution.py:16
  223.3 1.4 collective-permute-start.10
  226.0 10.3 %collective-permute-done.10 = bf16[2,16,64,128]{3,2,1,0:T(8,128)(2,1)S(1)} collective-permute-done((bf16[2,16,64,128]{3,2,1,0:T(8,128)(2,1)S(1)}, bf16[2,16,64,128]{3,2,1,0:T(8,128)(2,1)S(1)}, u32[]{:S(2)}, u32[]{:S(2)}) %collective-permute-start.10) | collective-permute-done | bytes 524320 | tf_op jit(solution)/shard_map/ppermute | solution.py:16
  (105 shorter events, 27.1 us)
Async XLA Ops:
  0.6 126.3 %copy-start = (bf16[2,64,2048]{2,1,0:T(8,128)(2,1)S(1)}, bf16[2,64,2048]{2,1,0:T(8,128)(2,1)}, u32[]{:S(2)}) copy-start(bf16[2,64,2048]{2,1,0:T(8,128)(2,1)} %param.8) | copy-start | bytes 1572868
  0.6 11.6 %collective-permute-start = (bf16[2,64,2048]{2,1,0:T(8,128)(2,1)}, bf16[2,64,2048]{2,1,0:T(8,128)(2,1)}, u32[]{:S(2)}, u32[]{:S(2)}) collective-permute-start(bf16[2,64,2048]{2,1,0:T(8,128)(2,1)} %param.6), channel_id=1, source_target_pairs={{0,1},{1,0},{2,3},{3,2},{4,5},{5,4},{6,7},{7,6},{8,9},{9,8},{10,11... | collective-permute-start | bytes 1572872 | tf_op jit(solution)/shard_map/ppermute | solution.py:16
  1.2 9.1 %collective-permute-start.4 = (bf16[2,64,2048]{2,1,0:T(8,128)(2,1)}, bf16[2,64,2048]{2,1,0:T(8,128)(2,1)}, u32[]{:S(2)}, u32[]{:S(2)}) collective-permute-start(bf16[2,64,2048]{2,1,0:T(8,128)(2,1)} %param.7), channel_id=1, source_target_pairs={{0,1},{1,0},{2,3},{3,2},{4,5},{5,4},{6,7},{7,6},{8,9},{9,8},{10,11... | collective-permute-start | bytes 1572872 | tf_op jit(solution)/shard_map/ppermute | solution.py:16
  1.2 5.2 %copy-start.7 = (bf16[2,64,2048]{2,1,0:T(8,128)(2,1)S(1)}, bf16[2,64,2048]{2,1,0:T(8,128)(2,1)}, u32[]{:S(2)}) copy-start(bf16[2,64,2048]{2,1,0:T(8,128)(2,1)} %param.6) | copy-start | bytes 1572868
  1.2 5.4 %copy-start.6 = (bf16[2,64,2048]{2,1,0:T(8,128)(2,1)S(1)}, bf16[2,64,2048]{2,1,0:T(8,128)(2,1)}, u32[]{:S(2)}) copy-start(bf16[2,64,2048]{2,1,0:T(8,128)(2,1)} %param.7) | copy-start | bytes 1572868
  6.5 3.2 %copy-start.11 = (f32[16]{0:T(128)S(1)}, f32[16]{0:T(128)}, u32[]{:S(2)}) copy-start(f32[16]{0:T(128)} %param.9) | copy-start | bytes 196
  7.6 2.2 copy-start.4
  15.5 15.7 %collective-permute-start.1 = (bf16[2,64,2048]{2,0,1:T(2,128)(2,1)S(1)}, bf16[2,64,2048]{2,0,1:T(2,128)(2,1)S(1)}, u32[]{:S(2)}, u32[]{:S(2)}) collective-permute-start(bf16[2,64,2048]{2,0,1:T(2,128)(2,1)S(1)} %broadcast_select_fusion.5), channel_id=1, source_target_pairs={{0,2},{1,3},{2,0},{3,1},{4,6},{5,7},{6,4},{7,5},{8,10},{9,11},{10,... | collective-permute-start | bytes 1572872 | tf_op jit(solution)/shard_map/ppermute | solution.py:16
  20.2 21.7 %collective-permute-start.5 = (bf16[2,64,2048]{2,0,1:T(2,128)(2,1)S(1)}, bf16[2,64,2048]{2,0,1:T(2,128)(2,1)S(1)}, u32[]{:S(2)}, u32[]{:S(2)}) collective-permute-start(bf16[2,64,2048]{2,0,1:T(2,128)(2,1)S(1)} %broadcast_select_fusion.4), channel_id=1, source_target_pairs={{0,2},{1,3},{2,0},{3,1},{4,6},{5,7},{6,4},{7,5},{8,10},{9,11},{10,... | collective-permute-start | bytes 1572872 | tf_op jit(solution)/shard_map/ppermute | solution.py:16
  31.2 3.5 %copy-start.8 = (bf16[2,64,2048]{2,0,1:T(2,128)(2,1)}, bf16[2,64,2048]{2,0,1:T(2,128)(2,1)S(1)}, u32[]{:S(2)}) copy-start(bf16[2,64,2048]{2,0,1:T(2,128)(2,1)S(1)} %collective-permute-done.1) | copy-start | bytes 1572868
  34.7 22.2 %collective-permute-start.2 = (bf16[2,64,2048]{2,0,1:T(2,128)(2,1)}, bf16[2,64,2048]{2,0,1:T(2,128)(2,1)}, u32[]{:S(2)}, u32[]{:S(2)}) collective-permute-start(bf16[2,64,2048]{2,0,1:T(2,128)(2,1)} %broadcast_select_fusion.3), channel_id=1, source_target_pairs={{0,4},{1,5},{2,6},{3,7},{4,0},{5,1},{6,2},{7,3},{8,12},{9,13},{10,... | collective-permute-start | bytes 1572872 | tf_op jit(solution)/shard_map/ppermute | solution.py:16
  41.9 3.5 %copy-start.9 = (bf16[2,64,2048]{2,0,1:T(2,128)(2,1)}, bf16[2,64,2048]{2,0,1:T(2,128)(2,1)S(1)}, u32[]{:S(2)}) copy-start(bf16[2,64,2048]{2,0,1:T(2,128)(2,1)S(1)} %collective-permute-done.5) | copy-start | bytes 1572868
  45.4 18.1 %collective-permute-start.6 = (bf16[2,64,2048]{2,0,1:T(2,128)(2,1)}, bf16[2,64,2048]{2,0,1:T(2,128)(2,1)}, u32[]{:S(2)}, u32[]{:S(2)}) collective-permute-start(bf16[2,64,2048]{2,0,1:T(2,128)(2,1)} %broadcast_select_fusion.2), channel_id=1, source_target_pairs={{0,4},{1,5},{2,6},{3,7},{4,0},{5,1},{6,2},{7,3},{8,12},{9,13},{10,... | collective-permute-start | bytes 1572872 | tf_op jit(solution)/shard_map/ppermute | solution.py:16
  60.9 36.7 %collective-permute-start.3 = (bf16[2,64,2048]{2,0,1:T(2,128)(2,1)}, bf16[2,64,2048]{2,0,1:T(2,128)(2,1)}, u32[]{:S(2)}, u32[]{:S(2)}) collective-permute-start(bf16[2,64,2048]{2,0,1:T(2,128)(2,1)} %broadcast_select_fusion.1), channel_id=1, source_target_pairs={{0,8},{1,9},{2,10},{3,11},{4,12},{5,13},{6,14},{7,15},{8,0},{9,1},... | collective-permute-start | bytes 1572872 | tf_op jit(solution)/shard_map/ppermute | solution.py:16
  67.4 41.3 %collective-permute-start.7 = (bf16[2,64,2048]{2,0,1:T(2,128)(2,1)}, bf16[2,64,2048]{2,0,1:T(2,128)(2,1)}, u32[]{:S(2)}, u32[]{:S(2)}) collective-permute-start(bf16[2,64,2048]{2,0,1:T(2,128)(2,1)} %broadcast_select_fusion), channel_id=1, source_target_pairs={{0,8},{1,9},{2,10},{3,11},{4,12},{5,13},{6,14},{7,15},{8,0},{9,1},... | collective-permute-start | bytes 1572872 | tf_op jit(solution)/shard_map/ppermute | solution.py:16
  126.9 1.7 copy-start.10
  128.7 2.3 copy-start.3
  131.0 2.5 %copy-start.2 = (bf16[2,16,64,320]{3,2,1,0:T(8,128)(2,1)}, bf16[2,16,64,320]{3,2,1,0:T(8,128)(2,1)S(1)}, u32[]{:S(2)}) copy-start(bf16[2,16,64,320]{3,2,1,0:T(8,128)(2,1)S(1)} %get-tuple-element.19) | copy-start | bytes 3932164
  132.0 50.9 %collective-permute-start.12 = (bf16[2,16,64,128]{3,2,1,0:T(8,128)(2,1)}, bf16[2,16,64,128]{3,2,1,0:T(8,128)(2,1)}, u32[]{:S(2)}, u32[]{:S(2)}) collective-permute-start(bf16[2,16,64,128]{3,2,1,0:T(8,128)(2,1)} %slice.446), channel_id=1, source_target_pairs={{0,8},{1,9},{2,10},{3,11},{4,12},{5,13},{6,14},{7,15},{8,0},{9,1},... | collective-permute-start | bytes 1572872 | tf_op jit(solution)/shard_map/ppermute | solution.py:16
  132.0 48.3 %copy-start.5 = (bf16[2,64,2048]{2,1,0:T(8,128)(2,1)S(1)}, bf16[2,64,2048]{2,1,0:T(8,128)(2,1)}, u32[]{:S(2)}) copy-start(bf16[2,64,2048]{2,1,0:T(8,128)(2,1)} %param.5) | copy-start | bytes 1572868
  178.2 6.4 %slice-start = ((s8[5242880]{0:T(1024)(128)(4,1)}), s8[4194304]{0:T(1024)(128)(4,1)S(1)}, s32[]{:S(2)}) async-start(s8[5242880]{0:T(1024)(128)(4,1)} %bitcast.380), calls=%async_computation | async-start | bytes 8388608
  180.3 4.3 %slice-start.1 = ((s8[5242880]{0:T(1024)(128)(4,1)}), s8[1048576]{0:T(1024)(128)(4,1)S(1)}, s32[]{:S(2)}) async-start(s8[5242880]{0:T(1024)(128)(4,1)} %bitcast.380), calls=%async_computation.1 | async-start | bytes 2097152
  182.8 24.7 %collective-permute-start.8 = (bf16[2,16,64,128]{3,2,1,0:T(8,128)(2,1)S(1)}, bf16[2,16,64,128]{3,2,1,0:T(8,128)(2,1)S(1)}, u32[]{:S(2)}, u32[]{:S(2)}) collective-permute-start(bf16[2,16,64,128]{3,2,1,0:T(8,128)(2,1)S(1)} %slice.447), channel_id=1, source_target_pairs={{0,8},{1,9},{2,10},{3,11},{4,12},{5,13},{6,14},{7,15},{8,0},{9,1},... | collective-permute-start | bytes 1572872 | tf_op jit(solution)/shard_map/ppermute | solution.py:16
  184.8 24.3 %collective-permute-start.13 = (bf16[2,16,64,128]{3,2,1,0:T(8,128)(2,1)S(1)}, bf16[2,16,64,128]{3,2,1,0:T(8,128)(2,1)S(1)}, u32[]{:S(2)}, u32[]{:S(2)}) collective-permute-start(bf16[2,16,64,128]{3,2,1,0:T(8,128)(2,1)S(1)} %fusion.15), channel_id=1, source_target_pairs={{0,4},{1,5},{2,6},{3,7},{4,0},{5,1},{6,2},{7,3},{8,12},{9,13},{10,... | collective-permute-start | bytes 1572872 | tf_op jit(solution)/shard_map/ppermute | solution.py:16
  208.3 13.8 %collective-permute-start.9 = (bf16[2,16,64,128]{3,2,1,0:T(8,128)(2,1)S(1)}, bf16[2,16,64,128]{3,2,1,0:T(8,128)(2,1)S(1)}, u32[]{:S(2)}, u32[]{:S(2)}) collective-permute-start(bf16[2,16,64,128]{3,2,1,0:T(8,128)(2,1)S(1)} %fusion.19), channel_id=1, source_target_pairs={{0,4},{1,5},{2,6},{3,7},{4,0},{5,1},{6,2},{7,3},{8,12},{9,13},{10,... | collective-permute-start | bytes 1572872 | tf_op jit(solution)/shard_map/ppermute | solution.py:16
  210.2 14.5 %collective-permute-start.14 = (bf16[2,16,64,128]{3,2,1,0:T(8,128)(2,1)S(1)}, bf16[2,16,64,128]{3,2,1,0:T(8,128)(2,1)S(1)}, u32[]{:S(2)}, u32[]{:S(2)}) collective-permute-start(bf16[2,16,64,128]{3,2,1,0:T(8,128)(2,1)S(1)} %fusion.14), channel_id=1, source_target_pairs={{0,2},{1,3},{2,0},{3,1},{4,6},{5,7},{6,4},{7,5},{8,10},{9,11},{10,... | collective-permute-start | bytes 1572872 | tf_op jit(solution)/shard_map/ppermute | solution.py:16
  223.3 13.0 %collective-permute-start.10 = (bf16[2,16,64,128]{3,2,1,0:T(8,128)(2,1)S(1)}, bf16[2,16,64,128]{3,2,1,0:T(8,128)(2,1)S(1)}, u32[]{:S(2)}, u32[]{:S(2)}) collective-permute-start(bf16[2,16,64,128]{3,2,1,0:T(8,128)(2,1)S(1)} %fusion.18), channel_id=1, source_target_pairs={{0,2},{1,3},{2,0},{3,1},{4,6},{5,7},{6,4},{7,5},{8,10},{9,11},{10,... | collective-permute-start | bytes 1572872 | tf_op jit(solution)/shard_map/ppermute | solution.py:16
  225.9 11.7 %collective-permute-start.15 = (bf16[2,16,64,128]{3,2,1,0:T(8,128)(2,1)S(1)}, bf16[2,16,64,128]{3,2,1,0:T(8,128)(2,1)S(1)}, u32[]{:S(2)}, u32[]{:S(2)}) collective-permute-start(bf16[2,16,64,128]{3,2,1,0:T(8,128)(2,1)S(1)} %fusion.13), channel_id=1, source_target_pairs={{0,1},{1,0},{2,3},{3,2},{4,5},{5,4},{6,7},{7,6},{8,9},{9,8},{10,11... | collective-permute-start | bytes 1572872 | tf_op jit(solution)/shard_map/ppermute | solution.py:16
  237.5 2.0 collective-permute-start.11
  238.0 2.8 %copy-start.1 = (bf16[2,64,2048]{2,1,0:T(8,128)(2,1)S(1)}, bf16[2,64,2048]{2,1,0:T(8,128)(2,1)}, u32[]{:S(2)}) copy-start(bf16[2,64,2048]{2,1,0:T(8,128)(2,1)} %param.8) | copy-start | bytes 1572868
where the time goes:
time: 246 us; the launch traced here: 241 us
  waiting for transfers between devices  82.5 us (34%)
  blocking collectives  44.7 us (18%)
  local copies, waits for them, and re-layouts  44.1 us (18%)
  other arithmetic  32.2 us (13%)
  matrix products  20.3 us (8%)
  starting transfers between devices  15.8 us (6%)
    ppermute x16, waiting for transfers between devices, from_partner(): return lax.ppermute(value, axis, pairs)  82.5 us
    psum x1, blocking collectives, shards(): slope_grad = lax.psum(slope_part, ('dp', 'ctx'))  44.7 us
    dot_general x6, matrix products, product(): return jnp.einsum(form, left, right, preferred_element_type=jnp.float32)  20.3 us
    ppermute x16, starting transfers between devices, from_partner(): return lax.ppermute(value, axis, pairs)  15.8 us
    reshape x6, local copies, waits for them, and re-layouts, to_heads(): rows.reshape(seqs, count, heads, width // heads)  13 us
    unnamed x36, local copies, waits for them, and re-layouts  11.5 us
    select_n x6, other arithmetic, merge_level(): jnp.where(flag == 1, jnp.concatenate([other_small, own_small], axis=1), j...  10.1 us
    convert_element_type x4, local copies, waits for them, and re-layouts, pair_mean(): cells.reshape(cells.shape[:-2] + (cells.shape[-2] // 2, 2, cells.shape[-1]))  8.37 us
  transfers between devices with their start and end apart: 16, of which 9 were waited for; matrix products, arithmetic and copies ran while one was open for 29% of the time, Pallas kernels for 0%

commit v1 on v0

--- a/solution.py
+++ b/solution.py
@@ -1,9 +1,259 @@
+import functools
 import math
 
 import jax
 import jax.numpy as jnp
 from jax import lax
+from jax.experimental import pallas as pl
+from jax.experimental.pallas import tpu as pltpu
 from jax.sharding import PartitionSpec as P
+
+F32, BF16 = jnp.float32, jnp.bfloat16
+LOG2E = math.log2(math.e)
+VMEM = pl.BlockSpec(memory_space=pltpu.VMEM)
+SMEM = pl.BlockSpec(memory_space=pltpu.SMEM)
+
+
+def swap(value, apart):
+    count = lax.axis_size("ctx")
+    return lax.ppermute(value, "ctx", [(source, source ^ apart) for source in range(count)])
+
+
+def like(*shape, dtype=BF16):
+    return jax.ShapeDtypeStruct(shape, dtype)
+
+
+def call(body, out_shape, operands, scalars=0, flops=0, name=None):
+    moved = sum(a.size * a.dtype.itemsize for a in jax.tree.leaves((operands, out_shape)))
+    return pl.pallas_call(
+        body,
+        out_shape=out_shape,
+        in_specs=[SMEM] * scalars + [VMEM] * (len(operands) - scalars),
+        out_specs=jax.tree.map(lambda _: VMEM, out_shape),
+        compiler_params=pltpu.CompilerParams(vmem_limit_bytes=32 * 2**20),
+        cost_estimate=pl.CostEstimate(flops=flops, bytes_accessed=moved, transcendentals=0),
+        name=name,
+    )(*operands)
+
+
+def dot(left, right, left_dim=1, right_dim=0):
+    dims = (((left_dim,), (right_dim,)), ((), ()))
+    return lax.dot_general(left, right, dims, preferred_element_type=F32)
+
+
+def pair_matrix(rows):
+    cell = lax.broadcasted_iota(jnp.int32, (rows, 2 * rows), 0)
+    source = lax.broadcasted_iota(jnp.int32, (rows, 2 * rows), 1)
+    return jnp.where(source // 2 == cell, 0.5, 0.0).astype(BF16)
+
+
+def spread_matrix(rows, level):
+    row = lax.broadcasted_iota(jnp.int32, (rows, rows >> level), 0)
+    cell = lax.broadcasted_iota(jnp.int32, (rows, rows >> level), 1)
+    return jnp.where(row >> level == cell, 0.5**level, 0.0).astype(BF16)
+
+
+def split_body(core, k, v, q, g, kv_own, kv_send, qg_own, qg_send):
+    half = kv_own.shape[-1]
+    mine = pl.ds(pl.multiple_of(core[0] * half, half), half)
+    theirs = pl.ds(pl.multiple_of((1 - core[0]) * half, half), half)
+    for index, (first, second) in enumerate(((k, q), (v, g))):
+        kv_own[index] = first[:, :, mine]
+        kv_send[index] = first[:, :, theirs]
+        qg_own[index] = second[:, :, mine]
+        qg_send[index] = second[:, :, theirs]
+
+
+def summary_body(own, other, *cells):
+    for kind in range(own.shape[0]):
+        for seq in range(own.shape[1]):
+            rows = jnp.concatenate([own[kind, seq], other[kind, seq]], axis=0)
+            for out in cells:
+                rows = dot(pair_matrix(rows.shape[0] // 2), rows).astype(BF16)
+                out[kind, seq] = rows
+
+
+def coarser_body(cells, out):
+    for kind in range(cells.shape[0]):
+        for seq in range(cells.shape[1]):
+            rows = cells[kind, seq]
+            out[kind, seq] = dot(pair_matrix(rows.shape[0] // 2), rows).astype(BF16)
+
+
+def attend_body(levels_of, head, core, slope, *refs):
+    count = len(levels_of)
+    qg_own, qg_other = refs[:2]
+    pieces = refs[2 : 2 + count]
+    dq_own, dq_send, slope_out = refs[2 + count : 5 + count]
+    outs = refs[5 + count :]
+    seqs, block, width = qg_own.shape[1:]
+    heads = width // head
+    scale = 1.0 / math.sqrt(head)
+    sizes = [piece.shape[2] for piece in pieces]
+    starts = [sum(sizes[:i]) for i in range(count + 1)]
+    for h in range(heads):
+        lanes = slice(h * head, (h + 1) * head)
+        step = slope[core[0] * heads + h] * LOG2E + 1.0
+        slope_sum = jnp.zeros((1, 2 * block), F32)
+        for seq in range(seqs):
+            query = jnp.concatenate([qg_own[0, seq, :, lanes], qg_other[0, seq, :, lanes]], axis=0)
+            grad = jnp.concatenate([qg_own[1, seq, :, lanes], qg_other[1, seq, :, lanes]], axis=0)
+            keys = jnp.concatenate([piece[0, seq, :, lanes] for piece in pieces], axis=0)
+            values = jnp.concatenate([piece[1, seq, :, lanes] for piece in pieces], axis=0)
+            raw = dot(keys, query, 1, 1)
+            upstream = dot(values, grad, 1, 1)
+            scores = jnp.concatenate(
+                [
+                    raw[starts[i] : starts[i + 1]] * (scale * LOG2E) + step * float(levels_of[i])
+                    for i in range(count)
+                ],
+                axis=0,
+            )
+            weights = jnp.exp2(scores - jnp.max(scores, axis=0, keepdims=True))
+            probs = weights * (1.0 / jnp.sum(weights, axis=0, keepdims=True))
+            probs_low = probs.astype(BF16)
+            delta = jnp.sum(probs_low.astype(F32) * upstream, axis=0, keepdims=True)
+            dscore = probs * (upstream - delta)
+            for i in range(count):
+                if levels_of[i]:
+                    part = jnp.sum(dscore[starts[i] : starts[i + 1]], axis=0, keepdims=True)
+                    slope_sum = slope_sum + part * float(levels_of[i])
+            dscore_low = dscore.astype(BF16)
+            dv = dot(probs_low, grad)
+            dk = dot(dscore_low, query) * scale
+            dq = (dot(dscore_low, keys, 0, 0) * scale).astype(BF16)
+            dq_own[seq, :, lanes] = dq[:block]
+            dq_send[seq, :, lanes] = dq[block:]
+            for i in range(count):
+                outs[i][0, seq, :, lanes] = dk[starts[i] : starts[i + 1]].astype(outs[i].dtype)
+                outs[i][1, seq, :, lanes] = dv[starts[i] : starts[i + 1]].astype(outs[i].dtype)
+        slope_out[h : h + 1, :] = slope_sum
+
+
+def fold_body(direct, coarse, out):
+    rows = direct.shape[2]
+    for kind in range(direct.shape[0]):
+        for seq in range(direct.shape[1]):
+            spread = dot(spread_matrix(rows, 1), coarse[kind, seq])
+            out[kind, seq] = (direct[kind, seq] + spread).astype(BF16)
+
+
+def relay_body(count, *refs):
+    direct, back, outs = refs[:count], refs[count : 2 * count], refs[2 * count :]
+    for first, second, out in zip(direct, back, outs):
+        out[...] = (first[...] + second[...].astype(F32)).astype(BF16)
+
+
+def gather_body(levels_of, own, other, *refs):
+    back, (kept, sent) = refs[: len(levels_of)], refs[len(levels_of) :]
+    block = own.shape[2]
+    spread = jnp.concatenate([spread_matrix(2 * block, level) for level in levels_of], axis=1)
+    for kind in range(own.shape[0]):
+        for seq in range(own.shape[1]):
+            cells = jnp.concatenate([part[kind, seq] for part in back], axis=0)
+            total = dot(spread, cells)
+            kept[kind, seq] = (own[kind, seq] + total[:block]).astype(BF16)
+            sent[kind, seq] = (other[kind, seq] + total[block:]).astype(BF16)
+
+
+def join_body(core, dq_own, dq_other, kv_own, kv_other, dq, dk, dv):
+    half = dq_own.shape[-1]
+    mine = pl.ds(pl.multiple_of(core[0] * half, half), half)
+    theirs = pl.ds(pl.multiple_of((1 - core[0]) * half, half), half)
+    dq[:, :, mine] = dq_own[...]
+    dq[:, :, theirs] = dq_other[...]
+    for index, out in enumerate((dk, dv)):
+        out[:, :, mine] = kv_own[index]
+        out[:, :, theirs] = kv_other[index]
+
+
+def paired(queries, key_rows, value_rows, out_grad, level_slope):
+    seqs, block, width = queries.shape
+    heads = level_slope.shape[0]
+    half = width // 2
+    ctx_count = lax.axis_size("ctx")
+    levels = ctx_count.bit_length() - 1
+    core = (lax.axis_index("ctx") % 2).astype(jnp.int32).reshape(1)
+
+    part = like(2, seqs, block, half)
+    kv_own, kv_send, qg_own, qg_send = call(
+        split_body, (part,) * 4, (core, key_rows, value_rows, queries, out_grad), scalars=1, name="split_heads"
+    )
+    kv_other = swap(kv_send, 1)
+    qg_other = swap(qg_send, 1)
+
+    cells = call(
+        summary_body,
+        tuple(like(2, seqs, 2 * block >> level, half) for level in range(1, levels)),
+        (kv_own, kv_other),
+        name="summaries",
+    )
+    level_of = {m: m.bit_length() for m in range(1, ctx_count // 2)}
+    far = [m for m in range(4, ctx_count // 2, 2)]
+    far_cells = [swap(cells[level_of[m] - 1], 2 * m) for m in far]
+    near_cells = swap(cells[0], 2)
+    side_cells = swap(cells[1], 4)
+    relayed_cells = [swap(c, 2) for c in far_cells]
+    across = call(coarser_body, like(2, seqs, block // 2, half), (near_cells,), name="coarser")
+    across_cells = swap(across, 4)
+
+    pieces = [kv_own, kv_other, near_cells, side_cells, across_cells] + far_cells + relayed_cells
+    levels_of = [0, 0, 1, 2, 2] + [level_of[m] for m in far] * 2
+    kinds = [F32, F32, F32, BF16, BF16] + [F32] * len(far) + [BF16] * len(far)
+    rows = sum(p.shape[2] for p in pieces)
+    dq_part = like(seqs, block, half)
+    dq_own, dq_send, slope_part, *grads = call(
+        functools.partial(attend_body, tuple(levels_of), width // heads),
+        (dq_part, dq_part, like(heads // 2, 2 * block, dtype=F32))
+        + tuple(like(*p.shape, dtype=kind) for p, kind in zip(pieces, kinds)),
+        (core, level_slope, qg_own, qg_other, *pieces),
+        scalars=2,
+        flops=10 * seqs * 2 * block * rows * half,
+        name="attend",
+    )
+    own, other, near, side, across = grads[:5]
+    far_direct, far_relayed = grads[5 : 5 + len(far)], grads[5 + len(far) :]
+
+    across_back = swap(across, 4)
+    relay_back = [swap(part, 2) for part in far_relayed]
+    near_total = call(fold_body, like(*near.shape), (near, across_back), name="fold")
+    far_total = call(
+        functools.partial(relay_body, len(far)),
+        tuple(like(*part.shape) for part in far_direct),
+        (*far_direct, *relay_back),
+        name="relay",
+    )
+    near_back = swap(near_total, 2)
+    far_back = [swap(part, 2 * m) for m, part in zip(far, far_total)]
+    side_back = swap(side, 4)
+    dq_other = swap(dq_send, 1)
+
+    slope_sum = slope_part
+    dp_count = lax.axis_size("dp")
+    for bit in range(dp_count.bit_length() - 1):
+        slope_sum = slope_sum + lax.ppermute(slope_sum, "dp", [(i, i ^ 2**bit) for i in range(dp_count)])
+    for level in range(1, levels):
+        slope_sum = slope_sum + swap(slope_sum, 2**level)
+    slope_other = swap(slope_sum, 1)
+    both = jnp.where(
+        core[0] == 0,
+        jnp.concatenate([slope_sum, slope_other], axis=0),
+        jnp.concatenate([slope_other, slope_sum], axis=0),
+    )
+    slope_grad = jnp.sum(both, axis=1)
+
+    kv_grad, kv_grad_send = call(
+        functools.partial(gather_body, (1, 2) + tuple(level_of[m] for m in far)),
+        (part, part),
+        (own, other, near_back, side_back, *far_back),
+        name="gather_cells",
+    )
+    kv_grad_other = swap(kv_grad_send, 1)
+    whole = like(seqs, block, width)
+    dq, dk, dv = call(
+        join_body, (whole,) * 3, (core, dq_own, dq_other, kv_grad, kv_grad_other), scalars=1, name="join_heads"
+    )
+    return dq, dk, dv, slope_grad
 
 
 def as_sent(x):
@@ -93,7 +343,7 @@
     return (own_half, sent)
 
 
-def shards(queries, key_rows, value_rows, out_grad, level_slope):
+def by_blocks(queries, key_rows, value_rows, out_grad, level_slope):
     seqs, block, width = queries.shape
     heads = level_slope.shape[0]
     ctx_count = lax.axis_size("ctx")
@@ -147,6 +397,13 @@
     return (from_heads(query_part.astype(jnp.bfloat16)), key_grad, value_grad, slope_grad)
 
 
+def shards(queries, key_rows, value_rows, out_grad, level_slope):
+    levels = lax.axis_size("ctx").bit_length() - 1
+    few = levels >= 3 and 2 * queries.shape[1] >> levels - 1 >= 16
+    form = paired if few else by_blocks
+    return form(queries, key_rows, value_rows, out_grad, level_slope)
+
+
 def solution(mesh):
     placed = (
         P("dp", "ctx", None),

time: 246 us -> 96.8 us (0.39); the launches traced: 241 us -> 96.5 us
  blocking collectives: 44.7 us -> 0 us
  local copies, waits for them, and re-layouts: 44.1 us -> 4.16 us
  other arithmetic: 32.2 us -> 0.64 us
  waiting for transfers between devices: 82.5 us -> 53.5 us
  matrix products: 20.3 us -> 0 us
  starting transfers between devices: 15.8 us -> 26.7 us
  Pallas kernels: 0 us -> 10.8 us
    psum x1 -> x0, blocking collectives: 44.7 us -> none  [shards(): slope_grad = lax.psum(slope_part, ('dp', 'ctx'))]
    ppermute x16 -> x23, waiting for transfers between devices: 82.5 us -> 53.5 us  [the longest x22 51.4 us: swap(): lax.ppermute(value, 'ctx', [(source, source ^ apart) for source in range(...]
    dot_general x6 -> x0, matrix products: 20.3 us -> none  [product(): return jnp.einsum(form, left, right, preferred_element_type=jnp.float32)]
    convert_element_type x27 -> x0, other arithmetic: 17.6 us -> none  [the longest x8 8.29 us: pair_mean(): cells.reshape(cells.shape[:-2] + (cells.shape[-2] // 2, 2, cells.shape[-1]))]
    reshape x7 -> x0, local copies, waits for them, and re-layouts: 15.1 us -> none  [the longest x6 13 us: to_heads(): rows.reshape(seqs, count, heads, width // heads)]
    ppermute x16 -> x23, starting transfers between devices: 15.8 us -> 26.7 us  [the longest x22 25.2 us: swap(): lax.ppermute(value, 'ctx', [(source, source ^ apart) for source in range(...]
    pallas_call x0 -> x8, Pallas kernels: none -> 10.8 us  [call(): pl.pallas_call(body, out_shape=out_shape, in_specs=[SMEM] * scalars + [VM...]
    select_n x7 -> x0, other arithmetic: 10.1 us -> none  [the longest x6 10.1 us: merge_level(): jnp.where(flag == 1, jnp.concatenate([other_small, own_small], axis=1), j...]
  transfers between devices with their start and end apart: 16 -> 23, of which waited for: 9 -> 15; matrix products, arithmetic and copies ran while one was open for 29% -> 1% of each run, Pallas kernels for 0% -> 0%
where the time goes in v1:
time: 96.8 us; the launch traced here: 96.5 us
  waiting for transfers between devices  53.5 us (55%)
  starting transfers between devices  26.7 us (28%)
  Pallas kernels  10.8 us (11%)
  local copies, waits for them, and re-layouts  4.16 us (4%)
    ppermute x22, waiting for transfers between devices, swap(): lax.ppermute(value, 'ctx', [(source, source ^ apart) for source in range(...  51.4 us
    ppermute x22, starting transfers between devices, swap(): lax.ppermute(value, 'ctx', [(source, source ^ apart) for source in range(...  25.2 us
    pallas_call x8, Pallas kernels, call(): pl.pallas_call(body, out_shape=out_shape, in_specs=[SMEM] * scalars + [VM...  10.8 us
    unnamed x10, local copies, waits for them, and re-layouts  4.16 us
    ppermute x1, waiting for transfers between devices, paired(): lax.ppermute(slope_sum, 'dp', [(i, i ^ 2 ** bit) for i in range(dp_count)])  2.12 us
  transfers between devices with their start and end apart: 23, of which 15 were waited for; matrix products, arithmetic and copies ran while one was open for 1% of the time, Pallas kernels for 0%

profile of v1, /device:TPU:0, one launch (start us, length us, event | category | flops | bytes accessed | tf_op | source)
XLA Modules:
  0.0 96.5 jit_solution(11405467313037052330)
XLA Ops:
  0.7 1.0 %copy-done = bf16[2,64,2048]{2,1,0:T(8,128)(2,1)S(1)} copy-done((bf16[2,64,2048]{2,1,0:T(8,128)(2,1)S(1)}, bf16[2,64,2048]{2,1,0:T(8,128)(2,1)}, u32[]{:S(2)}) %copy-start) | copy-done | bytes 524312
  1.7 1.0 %copy-done.1 = bf16[2,64,2048]{2,1,0:T(8,128)(2,1)S(1)} copy-done((bf16[2,64,2048]{2,1,0:T(8,128)(2,1)S(1)}, bf16[2,64,2048]{2,1,0:T(8,128)(2,1)}, u32[]{:S(2)}) %copy-start.1) | copy-done | bytes 524312
  2.7 1.0 %copy-done.2 = bf16[2,64,2048]{2,1,0:T(8,128)(2,1)S(1)} copy-done((bf16[2,64,2048]{2,1,0:T(8,128)(2,1)S(1)}, bf16[2,64,2048]{2,1,0:T(8,128)(2,1)}, u32[]{:S(2)}) %copy-start.2) | copy-done | bytes 524312
  3.8 1.0 %copy-done.3 = bf16[2,64,2048]{2,1,0:T(8,128)(2,1)S(1)} copy-done((bf16[2,64,2048]{2,1,0:T(8,128)(2,1)S(1)}, bf16[2,64,2048]{2,1,0:T(8,128)(2,1)}, u32[]{:S(2)}) %copy-start.3) | copy-done | bytes 524312
  4.8 0.1 split_heads.1
  5.0 0.5 collective-permute-start.1
  5.5 1.5 %collective-permute-done.1.other.refs_3_ = bf16[2,2,64,1024]{3,2,1,0:T(8,128)(2,1)S(1)} collective-permute-done((bf16[2,2,64,1024]{3,2,1,0:T(8,128)(2,1)S(1)}, bf16[2,2,64,1024]{3,2,1,0:T(8,128)(2,1)S(1)}, u32[]{:S(2)}, u32[]{:S(2)}) %collective-permute-start.1) | collective-permute-done | bytes 524320 | tf_op jit(solution)/shard_map/ppermute | solution.py:19
  7.0 1.3 %summaries.1 = (bf16[2,2,64,1024]{3,2,1,0:T(8,128)(2,1)S(1)}, bf16[2,2,32,1024]{3,2,1,0:T(8,128)(2,1)S(1)}, bf16[2,2,16,1024]{3,2,1,0:T(8,128)(2,1)S(1)}) custom-call(bf16[2,2,64,1024]{3,2,1,0:T(8,128)(2,1)S(1)} %get-tuple-element.32.own.refs_2_, bf16[2,2,64,1024]{3,2,1,0:T(8,128)(2,1)S(1)} %collective-permute-done.1.other.refs_3_), custom_call_target="tpu_custom_call" | custom-call | bytes 1966080 | tf_op jit(solution)/shard_map/summaries/pallas_call | solution.py:28
  8.3 2.9 %collective-permute-start.2 = (bf16[2,2,64,1024]{3,2,1,0:T(8,128)(2,1)S(1)}, bf16[2,2,64,1024]{3,2,1,0:T(8,128)(2,1)S(1)}, u32[]{:S(2)}, u32[]{:S(2)}) collective-permute-start(bf16[2,2,64,1024]{3,2,1,0:T(8,128)(2,1)S(1)} %get-tuple-element.34), channel_id=1, source_target_pairs={{0,2},{1,3},{2,0},{3,1},{4,6},{5,7},{6,4},{7,5},{8,10},{9,11},{10,... | collective-permute-start | bytes 1572872 | tf_op jit(solution)/shard_map/ppermute | solution.py:19
  11.2 2.6 %collective-permute-start.5 = (bf16[2,2,16,1024]{3,2,1,0:T(8,128)(2,1)S(1)}, bf16[2,2,16,1024]{3,2,1,0:T(8,128)(2,1)S(1)}, u32[]{:S(2)}, u32[]{:S(2)}) collective-permute-start(bf16[2,2,16,1024]{3,2,1,0:T(8,128)(2,1)S(1)} %get-tuple-element.36), channel_id=1, source_target_pairs={{0,8},{1,9},{2,10},{3,11},{4,12},{5,13},{6,14},{7,15},{8,0},{9,1},... | collective-permute-start | bytes 393224 | tf_op jit(solution)/shard_map/ppermute | solution.py:19
  13.8 1.3 %collective-permute-start.6 = (bf16[2,2,16,1024]{3,2,1,0:T(8,128)(2,1)S(1)}, bf16[2,2,16,1024]{3,2,1,0:T(8,128)(2,1)S(1)}, u32[]{:S(2)}, u32[]{:S(2)}) collective-permute-start(bf16[2,2,16,1024]{3,2,1,0:T(8,128)(2,1)S(1)} %get-tuple-element.36), channel_id=1, source_target_pairs={{0,12},{1,13},{2,14},{3,15},{4,8},{5,9},{6,10},{7,11},{8,4},{9,5},... | collective-permute-start | bytes 393224 | tf_op jit(solution)/shard_map/ppermute | solution.py:19
  15.2 0.2 collective-permute-start.3
  15.4 8.0 %collective-permute-done.2.cells.refs_4_ = bf16[2,2,64,1024]{3,2,1,0:T(8,128)(2,1)S(1)} collective-permute-done((bf16[2,2,64,1024]{3,2,1,0:T(8,128)(2,1)S(1)}, bf16[2,2,64,1024]{3,2,1,0:T(8,128)(2,1)S(1)}, u32[]{:S(2)}, u32[]{:S(2)}) %collective-permute-start.2) | collective-permute-done | bytes 524320 | tf_op jit(solution)/shard_map/ppermute | solution.py:19
  23.5 0.2 coarser.1
  23.7 1.9 %collective-permute-start.4 = (bf16[2,2,32,1024]{3,2,1,0:T(8,128)(2,1)S(1)}, bf16[2,2,32,1024]{3,2,1,0:T(8,128)(2,1)S(1)}, u32[]{:S(2)}, u32[]{:S(2)}) collective-permute-start(bf16[2,2,32,1024]{3,2,1,0:T(8,128)(2,1)S(1)} %coarser.1), channel_id=1, source_target_pairs={{0,4},{1,5},{2,6},{3,7},{4,0},{5,1},{6,2},{7,3},{8,12},{9,13},{10,... | collective-permute-start | bytes 786440 | tf_op jit(solution)/shard_map/ppermute | solution.py:19
  25.6 1.5 %collective-permute-start.7 = (bf16[2,2,16,1024]{3,2,1,0:T(8,128)(2,1)S(1)}, bf16[2,2,16,1024]{3,2,1,0:T(8,128)(2,1)S(1)}, u32[]{:S(2)}, u32[]{:S(2)}) collective-permute-start(bf16[2,2,16,1024]{3,2,1,0:T(8,128)(2,1)S(1)} %collective-permute-done.5.refs_7_), channel_id=1, source_target_pairs={{0,2},{1,3},{2,0},{3,1},{4,6},{5,7},{6,4},{7,5},{8,10},{9,11},{10,... | collective-permute-start | bytes 393224 | tf_op jit(solution)/shard_map/ppermute | solution.py:19
  27.1 0.5 collective-permute-start.8
  27.6 1.3 %collective-permute-done.3.refs_5_ = bf16[2,2,32,1024]{3,2,1,0:T(8,128)(2,1)S(1)} collective-permute-done((bf16[2,2,32,1024]{3,2,1,0:T(8,128)(2,1)S(1)}, bf16[2,2,32,1024]{3,2,1,0:T(8,128)(2,1)S(1)}, u32[]{:S(2)}, u32[]{:S(2)}) %collective-permute-start.3) | collective-permute-done | bytes 262176 | tf_op jit(solution)/shard_map/ppermute | solution.py:19
  28.9 2.5 %collective-permute-done.7.refs_9_ = bf16[2,2,16,1024]{3,2,1,0:T(8,128)(2,1)S(1)} collective-permute-done((bf16[2,2,16,1024]{3,2,1,0:T(8,128)(2,1)S(1)}, bf16[2,2,16,1024]{3,2,1,0:T(8,128)(2,1)S(1)}, u32[]{:S(2)}, u32[]{:S(2)}) %collective-permute-start.7) | collective-permute-done | bytes 131104 | tf_op jit(solution)/shard_map/ppermute | solution.py:19
  31.4 1.4 %collective-permute-done.8.refs_10_ = bf16[2,2,16,1024]{3,2,1,0:T(8,128)(2,1)S(1)} collective-permute-done((bf16[2,2,16,1024]{3,2,1,0:T(8,128)(2,1)S(1)}, bf16[2,2,16,1024]{3,2,1,0:T(8,128)(2,1)S(1)}, u32[]{:S(2)}, u32[]{:S(2)}) %collective-permute-start.8) | collective-permute-done | bytes 131104 | tf_op jit(solution)/shard_map/ppermute | solution.py:19
  32.8 0.7 collective-permute-done.4.refs_6_
  33.5 7.1 %attend.1 = (bf16[2,64,1024]{2,1,0:T(8,128)(2,1)S(1)}, bf16[2,64,1024]{2,1,0:T(8,128)(2,1)S(1)}, f32[8,128]{1,0:T(8,128)S(1)}, f32[2,2,64,1024]{3,2,1,0:T(8,128)...) custom-call(s32[1]{0:T(128)} %bitcast.core, ...), custom_call_target="tpu_custom_call" | custom-call | flops 838860800 | bytes 8654916 | tf_op jit(solution)/shard_map/attend/pallas_call | solution.py:28
  40.5 0.5 collective-permute-start.10
  41.0 6.9 %collective-permute-done.10.coarse = bf16[2,2,32,1024]{3,2,1,0:T(8,128)(2,1)S(1)} collective-permute-done((bf16[2,2,32,1024]{3,2,1,0:T(8,128)(2,1)S(1)}, bf16[2,2,32,1024]{3,2,1,0:T(8,128)(2,1)S(1)}, u32[]{:S(2)}, u32[]{:S(2)}) %collective-permute-start.10) | collective-permute-done | bytes 262176 | tf_op jit(solution)/shard_map/ppermute | solution.py:19
  47.9 0.3 fold.1
  48.2 0.7 collective-permute-start.11
  48.9 1.4 %collective-permute-start.13 = (bf16[2,2,16,1024]{3,2,1,0:T(8,128)(2,1)S(1)}, bf16[2,2,16,1024]{3,2,1,0:T(8,128)(2,1)S(1)}, u32[]{:S(2)}, u32[]{:S(2)}) collective-permute-start(bf16[2,2,16,1024]{3,2,1,0:T(8,128)(2,1)S(1)} %get-tuple-element.46), channel_id=1, source_target_pairs={{0,2},{1,3},{2,0},{3,1},{4,6},{5,7},{6,4},{7,5},{8,10},{9,11},{10,... | collective-permute-start | bytes 393224 | tf_op jit(solution)/shard_map/ppermute | solution.py:19
  50.3 0.6 collective-permute-start.14
  50.9 0.3 collective-permute-start.12
  51.2 13.3 %collective-permute-done.13.refs_2_ = bf16[2,2,16,1024]{3,2,1,0:T(8,128)(2,1)S(1)} collective-permute-done((bf16[2,2,16,1024]{3,2,1,0:T(8,128)(2,1)S(1)}, bf16[2,2,16,1024]{3,2,1,0:T(8,128)(2,1)S(1)}, u32[]{:S(2)}, u32[]{:S(2)}) %collective-permute-start.13) | collective-permute-done | bytes 131104 | tf_op jit(solution)/shard_map/ppermute | solution.py:19
  64.4 1.4 %collective-permute-done.14.refs_3_ = bf16[2,2,16,1024]{3,2,1,0:T(8,128)(2,1)S(1)} collective-permute-done((bf16[2,2,16,1024]{3,2,1,0:T(8,128)(2,1)S(1)}, bf16[2,2,16,1024]{3,2,1,0:T(8,128)(2,1)S(1)}, u32[]{:S(2)}, u32[]{:S(2)}) %collective-permute-start.14) | collective-permute-done | bytes 131104 | tf_op jit(solution)/shard_map/ppermute | solution.py:19
  65.9 2.2 %collective-permute-start.15 = (bf16[2,2,16,1024]{3,2,1,0:T(8,128)(2,1)S(1)}, bf16[2,2,16,1024]{3,2,1,0:T(8,128)(2,1)S(1)}, u32[]{:S(2)}, u32[]{:S(2)}) collective-permute-start(bf16[2,2,16,1024]{3,2,1,0:T(8,128)(2,1)S(1)} %get-tuple-element.48), channel_id=1, source_target_pairs={{0,8},{1,9},{2,10},{3,11},{4,12},{5,13},{6,14},{7,15},{8,0},{9,1},... | collective-permute-start | bytes 393224 | tf_op jit(solution)/shard_map/ppermute | solution.py:19
  68.2 1.4 %collective-permute-start.16 = (bf16[2,2,16,1024]{3,2,1,0:T(8,128)(2,1)S(1)}, bf16[2,2,16,1024]{3,2,1,0:T(8,128)(2,1)S(1)}, u32[]{:S(2)}, u32[]{:S(2)}) collective-permute-start(bf16[2,2,16,1024]{3,2,1,0:T(8,128)(2,1)S(1)} %get-tuple-element.49), channel_id=1, source_target_pairs={{0,12},{1,13},{2,14},{3,15},{4,8},{5,9},{6,10},{7,11},{8,4},{9,5},... | collective-permute-start | bytes 393224 | tf_op jit(solution)/shard_map/ppermute | solution.py:19
  69.6 6.9 %collective-permute-done.15.refs_2_ = bf16[2,2,16,1024]{3,2,1,0:T(8,128)(2,1)S(1)} collective-permute-done((bf16[2,2,16,1024]{3,2,1,0:T(8,128)(2,1)S(1)}, bf16[2,2,16,1024]{3,2,1,0:T(8,128)(2,1)S(1)}, u32[]{:S(2)}, u32[]{:S(2)}) %collective-permute-start.15) | collective-permute-done | bytes 131104 | tf_op jit(solution)/shard_map/ppermute | solution.py:19
  76.5 0.5 gather_cells.1
  77.0 0.1 collective-permute-start.17
  77.0 0.5 collective-permute-start.9
  77.5 1.5 %collective-permute-start.18 = (f32[8,128]{1,0:T(8,128)S(1)}, f32[8,128]{1,0:T(8,128)S(1)}, u32[]{:S(2)}, u32[]{:S(2)}) collective-permute-start(f32[8,128]{1,0:T(8,128)S(1)} %get-tuple-element.55), channel_id=1, source_target_pairs={{0,16},{16,0},{1,17},{17,1},{2,18},{18,2},{3,19},{19,3},{4,20},{20... | collective-permute-start | bytes 12296 | tf_op jit(solution)/shard_map/ppermute | solution.py:234
  79.0 2.1 %collective-permute-done.18 = f32[8,128]{1,0:T(8,128)S(1)} collective-permute-done((f32[8,128]{1,0:T(8,128)S(1)}, f32[8,128]{1,0:T(8,128)S(1)}, u32[]{:S(2)}, u32[]{:S(2)}) %collective-permute-start.18) | collective-permute-done | bytes 4128 | tf_op jit(solution)/shard_map/ppermute | solution.py:234
  81.2 0.5 collective-permute-start.19
  81.6 3.1 %collective-permute-done.19 = f32[8,128]{1,0:T(8,128)S(1)} collective-permute-done((f32[8,128]{1,0:T(8,128)S(1)}, f32[8,128]{1,0:T(8,128)S(1)}, u32[]{:S(2)}, u32[]{:S(2)}) %collective-permute-start.19) | collective-permute-done | bytes 4128 | tf_op jit(solution)/shard_map/ppermute | solution.py:19
  84.8 2.1 %collective-permute-start.20 = (f32[8,128]{1,0:T(8,128)S(1)}, f32[8,128]{1,0:T(8,128)S(1)}, u32[]{:S(2)}, u32[]{:S(2)}) collective-permute-start(f32[8,128]{1,0:T(8,128)S(1)} %add.18), channel_id=1, source_target_pairs={{0,4},{1,5},{2,6},{3,7},{4,0},{5,1},{6,2},{7,3},{8,12},{9,13},{10,... | collective-permute-start | bytes 12296 | tf_op jit(solution)/shard_map/ppermute | solution.py:19
  86.8 1.6 %collective-permute-done.20 = f32[8,128]{1,0:T(8,128)S(1)} collective-permute-done((f32[8,128]{1,0:T(8,128)S(1)}, f32[8,128]{1,0:T(8,128)S(1)}, u32[]{:S(2)}, u32[]{:S(2)}) %collective-permute-start.20) | collective-permute-done | bytes 4128 | tf_op jit(solution)/shard_map/ppermute | solution.py:19
  88.4 3.5 %collective-permute-start.21 = (f32[8,128]{1,0:T(8,128)S(1)}, f32[8,128]{1,0:T(8,128)S(1)}, u32[]{:S(2)}, u32[]{:S(2)}) collective-permute-start(f32[8,128]{1,0:T(8,128)S(1)} %add.19), channel_id=1, source_target_pairs={{0,8},{1,9},{2,10},{3,11},{4,12},{5,13},{6,14},{7,15},{8,0},{9,1},... | collective-permute-start | bytes 12296 | tf_op jit(solution)/shard_map/ppermute | solution.py:19
  91.9 1.6 %collective-permute-done.21 = f32[8,128]{1,0:T(8,128)S(1)} collective-permute-done((f32[8,128]{1,0:T(8,128)S(1)}, f32[8,128]{1,0:T(8,128)S(1)}, u32[]{:S(2)}, u32[]{:S(2)}) %collective-permute-start.21) | collective-permute-done | bytes 4128 | tf_op jit(solution)/shard_map/ppermute | solution.py:19
  93.5 1.2 %collective-permute-done.22 = f32[8,128]{1,0:T(8,128)S(1)} collective-permute-done((f32[8,128]{1,0:T(8,128)S(1)}, f32[8,128]{1,0:T(8,128)S(1)}, u32[]{:S(2)}, u32[]{:S(2)}) %collective-permute-start.22) | collective-permute-done | bytes 4128 | tf_op jit(solution)/shard_map/ppermute | solution.py:19
  94.7 0.6 fusion
  95.3 1.2 %join_heads.1 = (bf16[2,64,2048]{2,1,0:T(8,128)(2,1)}, bf16[2,64,2048]{2,1,0:T(8,128)(2,1)}, bf16[2,64,2048]{2,1,0:T(8,128)(2,1)}) custom-call(s32[1]{0:T(128)} %bitcast.core, bf16[2,64,1024]{2,1,0:T(8,128)(2,1)S(1)} %get-tuple-element.37.dq_own, bf16[2,64,1024]{2,1,0:T(8,128)(2,1)S(1)} %collective-permute-done.9.dq_other, ...), custom_call_target="tpu_custom_call" | custom-call | bytes 3145732 | tf_op jit(solution)/shard_map/join_heads/pallas_call | solution.py:28
  (21 shorter events, 0.1 us)
Async XLA Ops:
  0.6 1.0 %copy-start = (bf16[2,64,2048]{2,1,0:T(8,128)(2,1)S(1)}, bf16[2,64,2048]{2,1,0:T(8,128)(2,1)}, u32[]{:S(2)}) copy-start(bf16[2,64,2048]{2,1,0:T(8,128)(2,1)} %k.1) | copy-start | bytes 1572868
  1.7 1.0 %copy-start.1 = (bf16[2,64,2048]{2,1,0:T(8,128)(2,1)S(1)}, bf16[2,64,2048]{2,1,0:T(8,128)(2,1)}, u32[]{:S(2)}) copy-start(bf16[2,64,2048]{2,1,0:T(8,128)(2,1)} %v.1) | copy-start | bytes 1572868
  2.7 1.0 %copy-start.2 = (bf16[2,64,2048]{2,1,0:T(8,128)(2,1)S(1)}, bf16[2,64,2048]{2,1,0:T(8,128)(2,1)}, u32[]{:S(2)}) copy-start(bf16[2,64,2048]{2,1,0:T(8,128)(2,1)} %q.1) | copy-start | bytes 1572868
  3.8 1.0 %copy-start.3 = (bf16[2,64,2048]{2,1,0:T(8,128)(2,1)S(1)}, bf16[2,64,2048]{2,1,0:T(8,128)(2,1)}, u32[]{:S(2)}) copy-start(bf16[2,64,2048]{2,1,0:T(8,128)(2,1)} %g.1) | copy-start | bytes 1572868
  5.0 2.1 %collective-permute-start.1 = (bf16[2,2,64,1024]{3,2,1,0:T(8,128)(2,1)S(1)}, bf16[2,2,64,1024]{3,2,1,0:T(8,128)(2,1)S(1)}, u32[]{:S(2)}, u32[]{:S(2)}) collective-permute-start(bf16[2,2,64,1024]{3,2,1,0:T(8,128)(2,1)S(1)} %get-tuple-element.33), channel_id=1, source_target_pairs={{0,1},{1,0},{2,3},{3,2},{4,5},{5,4},{6,7},{7,6},{8,9},{9,8},{10,11... | collective-permute-start | bytes 1572872 | tf_op jit(solution)/shard_map/ppermute | solution.py:19
  8.3 15.1 %collective-permute-start.2 = (bf16[2,2,64,1024]{3,2,1,0:T(8,128)(2,1)S(1)}, bf16[2,2,64,1024]{3,2,1,0:T(8,128)(2,1)S(1)}, u32[]{:S(2)}, u32[]{:S(2)}) collective-permute-start(bf16[2,2,64,1024]{3,2,1,0:T(8,128)(2,1)S(1)} %get-tuple-element.34), channel_id=1, source_target_pairs={{0,2},{1,3},{2,0},{3,1},{4,6},{5,7},{6,4},{7,5},{8,10},{9,11},{10,... | collective-permute-start | bytes 1572872 | tf_op jit(solution)/shard_map/ppermute | solution.py:19
  11.2 16.3 %collective-permute-start = (bf16[2,2,64,1024]{3,2,1,0:T(8,128)(2,1)S(1)}, bf16[2,2,64,1024]{3,2,1,0:T(8,128)(2,1)S(1)}, u32[]{:S(2)}, u32[]{:S(2)}) collective-permute-start(bf16[2,2,64,1024]{3,2,1,0:T(8,128)(2,1)S(1)} %get-tuple-element.31), channel_id=1, source_target_pairs={{0,1},{1,0},{2,3},{3,2},{4,5},{5,4},{6,7},{7,6},{8,9},{9,8},{10,11... | collective-permute-start | bytes 1572872 | tf_op jit(solution)/shard_map/ppermute | solution.py:19
  11.2 14.3 %collective-permute-start.5 = (bf16[2,2,16,1024]{3,2,1,0:T(8,128)(2,1)S(1)}, bf16[2,2,16,1024]{3,2,1,0:T(8,128)(2,1)S(1)}, u32[]{:S(2)}, u32[]{:S(2)}) collective-permute-start(bf16[2,2,16,1024]{3,2,1,0:T(8,128)(2,1)S(1)} %get-tuple-element.36), channel_id=1, source_target_pairs={{0,8},{1,9},{2,10},{3,11},{4,12},{5,13},{6,14},{7,15},{8,0},{9,1},... | collective-permute-start | bytes 393224 | tf_op jit(solution)/shard_map/ppermute | solution.py:19
  13.8 13.2 %collective-permute-start.6 = (bf16[2,2,16,1024]{3,2,1,0:T(8,128)(2,1)S(1)}, bf16[2,2,16,1024]{3,2,1,0:T(8,128)(2,1)S(1)}, u32[]{:S(2)}, u32[]{:S(2)}) collective-permute-start(bf16[2,2,16,1024]{3,2,1,0:T(8,128)(2,1)S(1)} %get-tuple-element.36), channel_id=1, source_target_pairs={{0,12},{1,13},{2,14},{3,15},{4,8},{5,9},{6,10},{7,11},{8,4},{9,5},... | collective-permute-start | bytes 393224 | tf_op jit(solution)/shard_map/ppermute | solution.py:19
  15.2 13.7 %collective-permute-start.3 = (bf16[2,2,32,1024]{3,2,1,0:T(8,128)(2,1)S(1)}, bf16[2,2,32,1024]{3,2,1,0:T(8,128)(2,1)S(1)}, u32[]{:S(2)}, u32[]{:S(2)}) collective-permute-start(bf16[2,2,32,1024]{3,2,1,0:T(8,128)(2,1)S(1)} %get-tuple-element.35), channel_id=1, source_target_pairs={{0,4},{1,5},{2,6},{3,7},{4,0},{5,1},{6,2},{7,3},{8,12},{9,13},{10,... | collective-permute-start | bytes 786440 | tf_op jit(solution)/shard_map/ppermute | solution.py:19
  23.7 9.8 %copy-start.4 = (f32[16]{0:T(128)S(1)}, f32[16]{0:T(128)}, u32[]{:S(2)}) copy-start(f32[16]{0:T(128)} %slope.1) | copy-start | bytes 196
  23.7 9.8 %collective-permute-start.4 = (bf16[2,2,32,1024]{3,2,1,0:T(8,128)(2,1)S(1)}, bf16[2,2,32,1024]{3,2,1,0:T(8,128)(2,1)S(1)}, u32[]{:S(2)}, u32[]{:S(2)}) collective-permute-start(bf16[2,2,32,1024]{3,2,1,0:T(8,128)(2,1)S(1)} %coarser.1), channel_id=1, source_target_pairs={{0,4},{1,5},{2,6},{3,7},{4,0},{5,1},{6,2},{7,3},{8,12},{9,13},{10,... | collective-permute-start | bytes 786440 | tf_op jit(solution)/shard_map/ppermute | solution.py:19
  25.6 5.8 %collective-permute-start.7 = (bf16[2,2,16,1024]{3,2,1,0:T(8,128)(2,1)S(1)}, bf16[2,2,16,1024]{3,2,1,0:T(8,128)(2,1)S(1)}, u32[]{:S(2)}, u32[]{:S(2)}) collective-permute-start(bf16[2,2,16,1024]{3,2,1,0:T(8,128)(2,1)S(1)} %collective-permute-done.5.refs_7_), channel_id=1, source_target_pairs={{0,2},{1,3},{2,0},{3,1},{4,6},{5,7},{6,4},{7,5},{8,10},{9,11},{10,... | collective-permute-start | bytes 393224 | tf_op jit(solution)/shard_map/ppermute | solution.py:19
  27.1 5.7 %collective-permute-start.8 = (bf16[2,2,16,1024]{3,2,1,0:T(8,128)(2,1)S(1)}, bf16[2,2,16,1024]{3,2,1,0:T(8,128)(2,1)S(1)}, u32[]{:S(2)}, u32[]{:S(2)}) collective-permute-start(bf16[2,2,16,1024]{3,2,1,0:T(8,128)(2,1)S(1)} %collective-permute-done.6.refs_8_), channel_id=1, source_target_pairs={{0,2},{1,3},{2,0},{3,1},{4,6},{5,7},{6,4},{7,5},{8,10},{9,11},{10,... | collective-permute-start | bytes 393224 | tf_op jit(solution)/shard_map/ppermute | solution.py:19
  40.5 7.4 %collective-permute-start.10 = (bf16[2,2,32,1024]{3,2,1,0:T(8,128)(2,1)S(1)}, bf16[2,2,32,1024]{3,2,1,0:T(8,128)(2,1)S(1)}, u32[]{:S(2)}, u32[]{:S(2)}) collective-permute-start(bf16[2,2,32,1024]{3,2,1,0:T(8,128)(2,1)S(1)} %get-tuple-element.42), channel_id=1, source_target_pairs={{0,4},{1,5},{2,6},{3,7},{4,0},{5,1},{6,2},{7,3},{8,12},{9,13},{10,... | collective-permute-start | bytes 786440 | tf_op jit(solution)/shard_map/ppermute | solution.py:19
  48.2 28.3 %collective-permute-start.11 = (bf16[2,2,64,1024]{3,2,1,0:T(8,128)(2,1)S(1)}, bf16[2,2,64,1024]{3,2,1,0:T(8,128)(2,1)S(1)}, u32[]{:S(2)}, u32[]{:S(2)}) collective-permute-start(bf16[2,2,64,1024]{3,2,1,0:T(8,128)(2,1)S(1)} %fold.1), channel_id=1, source_target_pairs={{0,2},{1,3},{2,0},{3,1},{4,6},{5,7},{6,4},{7,5},{8,10},{9,11},{10,... | collective-permute-start | bytes 1572872 | tf_op jit(solution)/shard_map/ppermute | solution.py:19
  48.9 15.6 %collective-permute-start.13 = (bf16[2,2,16,1024]{3,2,1,0:T(8,128)(2,1)S(1)}, bf16[2,2,16,1024]{3,2,1,0:T(8,128)(2,1)S(1)}, u32[]{:S(2)}, u32[]{:S(2)}) collective-permute-start(bf16[2,2,16,1024]{3,2,1,0:T(8,128)(2,1)S(1)} %get-tuple-element.46), channel_id=1, source_target_pairs={{0,2},{1,3},{2,0},{3,1},{4,6},{5,7},{6,4},{7,5},{8,10},{9,11},{10,... | collective-permute-start | bytes 393224 | tf_op jit(solution)/shard_map/ppermute | solution.py:19
  50.3 15.6 %collective-permute-start.14 = (bf16[2,2,16,1024]{3,2,1,0:T(8,128)(2,1)S(1)}, bf16[2,2,16,1024]{3,2,1,0:T(8,128)(2,1)S(1)}, u32[]{:S(2)}, u32[]{:S(2)}) collective-permute-start(bf16[2,2,16,1024]{3,2,1,0:T(8,128)(2,1)S(1)} %get-tuple-element.47), channel_id=1, source_target_pairs={{0,2},{1,3},{2,0},{3,1},{4,6},{5,7},{6,4},{7,5},{8,10},{9,11},{10,... | collective-permute-start | bytes 393224 | tf_op jit(solution)/shard_map/ppermute | solution.py:19
  50.9 25.6 %collective-permute-start.12 = (bf16[2,2,32,1024]{3,2,1,0:T(8,128)(2,1)S(1)}, bf16[2,2,32,1024]{3,2,1,0:T(8,128)(2,1)S(1)}, u32[]{:S(2)}, u32[]{:S(2)}) collective-permute-start(bf16[2,2,32,1024]{3,2,1,0:T(8,128)(2,1)S(1)} %get-tuple-element.43), channel_id=1, source_target_pairs={{0,4},{1,5},{2,6},{3,7},{4,0},{5,1},{6,2},{7,3},{8,12},{9,13},{10,... | collective-permute-start | bytes 786440 | tf_op jit(solution)/shard_map/ppermute | solution.py:19
  65.9 10.5 %collective-permute-start.15 = (bf16[2,2,16,1024]{3,2,1,0:T(8,128)(2,1)S(1)}, bf16[2,2,16,1024]{3,2,1,0:T(8,128)(2,1)S(1)}, u32[]{:S(2)}, u32[]{:S(2)}) collective-permute-start(bf16[2,2,16,1024]{3,2,1,0:T(8,128)(2,1)S(1)} %get-tuple-element.48), channel_id=1, source_target_pairs={{0,8},{1,9},{2,10},{3,11},{4,12},{5,13},{6,14},{7,15},{8,0},{9,1},... | collective-permute-start | bytes 393224 | tf_op jit(solution)/shard_map/ppermute | solution.py:19
  68.2 8.3 %collective-permute-start.16 = (bf16[2,2,16,1024]{3,2,1,0:T(8,128)(2,1)S(1)}, bf16[2,2,16,1024]{3,2,1,0:T(8,128)(2,1)S(1)}, u32[]{:S(2)}, u32[]{:S(2)}) collective-permute-start(bf16[2,2,16,1024]{3,2,1,0:T(8,128)(2,1)S(1)} %get-tuple-element.49), channel_id=1, source_target_pairs={{0,12},{1,13},{2,14},{3,15},{4,8},{5,9},{6,10},{7,11},{8,4},{9,5},... | collective-permute-start | bytes 393224 | tf_op jit(solution)/shard_map/ppermute | solution.py:19
  77.0 18.3 %collective-permute-start.17 = (bf16[2,2,64,1024]{3,2,1,0:T(8,128)(2,1)S(1)}, bf16[2,2,64,1024]{3,2,1,0:T(8,128)(2,1)S(1)}, u32[]{:S(2)}, u32[]{:S(2)}) collective-permute-start(bf16[2,2,64,1024]{3,2,1,0:T(8,128)(2,1)S(1)} %get-tuple-element.51), channel_id=1, source_target_pairs={{0,1},{1,0},{2,3},{3,2},{4,5},{5,4},{6,7},{7,6},{8,9},{9,8},{10,11... | collective-permute-start | bytes 1572872 | tf_op jit(solution)/shard_map/ppermute | solution.py:19
  77.0 18.2 %collective-permute-start.9 = (bf16[2,64,1024]{2,1,0:T(8,128)(2,1)S(1)}, bf16[2,64,1024]{2,1,0:T(8,128)(2,1)S(1)}, u32[]{:S(2)}, u32[]{:S(2)}) collective-permute-start(bf16[2,64,1024]{2,1,0:T(8,128)(2,1)S(1)} %get-tuple-element.38), channel_id=1, source_target_pairs={{0,1},{1,0},{2,3},{3,2},{4,5},{5,4},{6,7},{7,6},{8,9},{9,8},{10,11... | collective-permute-start | bytes 786440 | tf_op jit(solution)/shard_map/ppermute | solution.py:19
  77.5 3.6 %collective-permute-start.18 = (f32[8,128]{1,0:T(8,128)S(1)}, f32[8,128]{1,0:T(8,128)S(1)}, u32[]{:S(2)}, u32[]{:S(2)}) collective-permute-start(f32[8,128]{1,0:T(8,128)S(1)} %get-tuple-element.55), channel_id=1, source_target_pairs={{0,16},{16,0},{1,17},{17,1},{2,18},{18,2},{3,19},{19,3},{4,20},{20... | collective-permute-start | bytes 12296 | tf_op jit(solution)/shard_map/ppermute | solution.py:234
  81.2 3.6 %collective-permute-start.19 = (f32[8,128]{1,0:T(8,128)S(1)}, f32[8,128]{1,0:T(8,128)S(1)}, u32[]{:S(2)}, u32[]{:S(2)}) collective-permute-start(f32[8,128]{1,0:T(8,128)S(1)} %add.17), channel_id=1, source_target_pairs={{0,2},{1,3},{2,0},{3,1},{4,6},{5,7},{6,4},{7,5},{8,10},{9,11},{10,... | collective-permute-start | bytes 12296 | tf_op jit(solution)/shard_map/ppermute | solution.py:19
  84.8 3.6 %collective-permute-start.20 = (f32[8,128]{1,0:T(8,128)S(1)}, f32[8,128]{1,0:T(8,128)S(1)}, u32[]{:S(2)}, u32[]{:S(2)}) collective-permute-start(f32[8,128]{1,0:T(8,128)S(1)} %add.18), channel_id=1, source_target_pairs={{0,4},{1,5},{2,6},{3,7},{4,0},{5,1},{6,2},{7,3},{8,12},{9,13},{10,... | collective-permute-start | bytes 12296 | tf_op jit(solution)/shard_map/ppermute | solution.py:19
  88.4 5.1 %collective-permute-start.21 = (f32[8,128]{1,0:T(8,128)S(1)}, f32[8,128]{1,0:T(8,128)S(1)}, u32[]{:S(2)}, u32[]{:S(2)}) collective-permute-start(f32[8,128]{1,0:T(8,128)S(1)} %add.19), channel_id=1, source_target_pairs={{0,8},{1,9},{2,10},{3,11},{4,12},{5,13},{6,14},{7,15},{8,0},{9,1},... | collective-permute-start | bytes 12296 | tf_op jit(solution)/shard_map/ppermute | solution.py:19
  93.5 1.2 %collective-permute-start.22 = (f32[8,128]{1,0:T(8,128)S(1)}, f32[8,128]{1,0:T(8,128)S(1)}, u32[]{:S(2)}, u32[]{:S(2)}) collective-permute-start(f32[8,128]{1,0:T(8,128)S(1)} %add.20), channel_id=1, source_target_pairs={{0,1},{1,0},{2,3},{3,2},{4,5},{5,4},{6,7},{7,6},{8,9},{9,8},{10,11... | collective-permute-start | bytes 12296 | tf_op jit(solution)/shard_map/ppermute | solution.py:19

commit v2 on v1

--- a/solution.py
+++ b/solution.py
@@ -12,24 +12,31 @@
 LOG2E = math.log2(math.e)
 VMEM = pl.BlockSpec(memory_space=pltpu.VMEM)
 SMEM = pl.BlockSpec(memory_space=pltpu.SMEM)
-
-
-def swap(value, apart):
+HBM = pl.BlockSpec(memory_space=pltpu.HBM)
+
+
+def swap(value, apart, dp_apart=0):
     count = lax.axis_size("ctx")
-    return lax.ppermute(value, "ctx", [(source, source ^ apart) for source in range(count)])
+    if not dp_apart:
+        return lax.ppermute(value, "ctx", [(source, source ^ apart) for source in range(count)])
+    mask = dp_apart * count + apart
+    pairs = [(source, source ^ mask) for source in range(lax.axis_size("dp") * count)]
+    return lax.ppermute(value, ("dp", "ctx"), pairs)
 
 
 def like(*shape, dtype=BF16):
     return jax.ShapeDtypeStruct(shape, dtype)
 
 
-def call(body, out_shape, operands, scalars=0, flops=0, name=None):
+def call(body, out_shape, operands, name, scalars=0, hbm_in=0, hbm_out=False, copies=0, flops=0):
     moved = sum(a.size * a.dtype.itemsize for a in jax.tree.leaves((operands, out_shape)))
+    count = len(operands) - scalars - hbm_in
     return pl.pallas_call(
         body,
         out_shape=out_shape,
-        in_specs=[SMEM] * scalars + [VMEM] * (len(operands) - scalars),
-        out_specs=jax.tree.map(lambda _: VMEM, out_shape),
+        in_specs=[SMEM] * scalars + [HBM] * hbm_in + [VMEM] * count,
+        out_specs=jax.tree.map(lambda _: HBM if hbm_out else VMEM, out_shape),
+        scratch_shapes=[pltpu.SemaphoreType.DMA((copies,))] if copies else [],
         compiler_params=pltpu.CompilerParams(vmem_limit_bytes=32 * 2**20),
         cost_estimate=pl.CostEstimate(flops=flops, bytes_accessed=moved, transcendentals=0),
         name=name,
@@ -53,15 +60,37 @@
     return jnp.where(row >> level == cell, 0.5**level, 0.0).astype(BF16)
 
 
-def split_body(core, k, v, q, g, kv_own, kv_send, qg_own, qg_send):
-    half = kv_own.shape[-1]
+def two_parts(x):
+    high = x.astype(BF16)
+    return jnp.concatenate([high, (x - high.astype(F32)).astype(BF16)], axis=0)
+
+
+def one_part(x):
+    rows = x.shape[0] // 2
+    return x[:rows].astype(F32) + x[rows:].astype(F32)
+
+
+def head_halves(core, half):
     mine = pl.ds(pl.multiple_of(core[0] * half, half), half)
     theirs = pl.ds(pl.multiple_of((1 - core[0]) * half, half), half)
-    for index, (first, second) in enumerate(((k, q), (v, g))):
-        kv_own[index] = first[:, :, mine]
-        kv_send[index] = first[:, :, theirs]
-        qg_own[index] = second[:, :, mine]
-        qg_send[index] = second[:, :, theirs]
+    return mine, theirs
+
+
+def copy_all(moves, sems):
+    copies = [pltpu.make_async_copy(src, dst, sems.at[i]) for i, (src, dst) in enumerate(moves)]
+    for copy in copies:
+        copy.start()
+    for copy in copies:
+        copy.wait()
+
+
+def split_body(core, first, second, own, send, sems):
+    mine, theirs = head_halves(core, own.shape[-1])
+    moves = []
+    for index, whole in enumerate((first, second)):
+        moves.append((whole.at[:, :, theirs], send.at[index]))
+        moves.append((whole.at[:, :, mine], own.at[index]))
+    copy_all(moves, sems)
 
 
 def summary_body(own, other, *cells):
@@ -84,13 +113,14 @@
     count = len(levels_of)
     qg_own, qg_other = refs[:2]
     pieces = refs[2 : 2 + count]
-    dq_own, dq_send, slope_out = refs[2 + count : 5 + count]
-    outs = refs[5 + count :]
+    dq_own, dq_send, slope_out, own, other, near, across, side, far, relay = refs[2 + count :]
     seqs, block, width = qg_own.shape[1:]
     heads = width // head
     scale = 1.0 / math.sqrt(head)
     sizes = [piece.shape[2] for piece in pieces]
     starts = [sum(sizes[:i]) for i in range(count + 1)]
+    far_count = (count - 5) // 2
+    slabs = [2 * seqs * heads * sum(sizes[5 : 5 + i]) for i in range(far_count)]
     for h in range(heads):
         lanes = slice(h * head, (h + 1) * head)
         step = slope[core[0] * heads + h] * LOG2E + 1.0
@@ -124,10 +154,20 @@
             dq = (dot(dscore_low, keys, 0, 0) * scale).astype(BF16)
             dq_own[seq, :, lanes] = dq[:block]
             dq_send[seq, :, lanes] = dq[block:]
-            for i in range(count):
-                outs[i][0, seq, :, lanes] = dk[starts[i] : starts[i + 1]].astype(outs[i].dtype)
-                outs[i][1, seq, :, lanes] = dv[starts[i] : starts[i + 1]].astype(outs[i].dtype)
+            for kind, direct in enumerate((dk, dv)):
+                parts = [direct[starts[i] : starts[i + 1]] for i in range(count)]
+                own[kind, seq, :, lanes] = parts[0]
+                other[kind, seq, :, lanes] = parts[1]
+                near[kind, seq, :, lanes] = parts[2]
+                group = (kind * seqs + seq) * heads + h
+                side[pl.ds(group * sizes[3], sizes[3]), :] = parts[3].astype(BF16)
+                across[kind, seq, :, lanes] = parts[4].astype(BF16)
+                for i in range(far_count):
+                    at = pl.ds(slabs[i] + group * sizes[5 + i], sizes[5 + i])
+                    far[at, :] = parts[5 + i]
+                    relay[at, :] = parts[5 + far_count + i].astype(BF16)
         slope_out[h : h + 1, :] = slope_sum
+    relay[pl.ds(far.shape[0], 2 * heads), :] = two_parts(slope_out[...])
 
 
 def fold_body(direct, coarse, out):
@@ -138,121 +178,157 @@
             out[kind, seq] = (direct[kind, seq] + spread).astype(BF16)
 
 
-def relay_body(count, *refs):
-    direct, back, outs = refs[:count], refs[count : 2 * count], refs[2 * count :]
-    for first, second, out in zip(direct, back, outs):
-        out[...] = (first[...] + second[...].astype(F32)).astype(BF16)
-
-
-def gather_body(levels_of, own, other, *refs):
-    back, (kept, sent) = refs[: len(levels_of)], refs[len(levels_of) :]
-    block = own.shape[2]
+def relay_body(side, far, back, slope, *refs):
+    heads = slope.shape[0]
+    tail = 2 * heads
+    slopes = [ref for ref in refs if ref.shape == slope.shape]
+    others, slope_out = slopes[:-1], slopes[-1]
+    side_out, *far_outs = [ref for ref in refs if ref.shape != slope.shape]
+    total = slope[...] + one_part(back[pl.ds(far.shape[0], tail), :])
+    for ref in others:
+        total = total + ref[...]
+    slope_out[...] = total
+    ending = two_parts(total)
+    rows = side.shape[0]
+    side_out[pl.ds(0, rows), :] = side[...]
+    side_out[pl.ds(rows, tail), :] = ending
+    start = 0
+    for out in far_outs:
+        rows = out.shape[0] - tail
+        here = pl.ds(start, rows)
+        out[pl.ds(0, rows), :] = (far[here, :] + back[here, :].astype(F32)).astype(BF16)
+        out[pl.ds(rows, tail), :] = ending
+        start += rows
+
+
+def gather_body(levels_of, own, other, slope, near, *refs):
+    back, (kept, sent, slope_out) = refs[:-3], refs[-3:]
+    kinds, seqs, block, width = own.shape
+    heads = slope.shape[0]
+    head = width // heads
+    sizes = [2 * block >> level for level in levels_of[1:]]
     spread = jnp.concatenate([spread_matrix(2 * block, level) for level in levels_of], axis=1)
-    for kind in range(own.shape[0]):
-        for seq in range(own.shape[1]):
-            cells = jnp.concatenate([part[kind, seq] for part in back], axis=0)
-            total = dot(spread, cells)
-            kept[kind, seq] = (own[kind, seq] + total[:block]).astype(BF16)
-            sent[kind, seq] = (other[kind, seq] + total[block:]).astype(BF16)
-
-
-def join_body(core, dq_own, dq_other, kv_own, kv_other, dq, dk, dv):
-    half = dq_own.shape[-1]
-    mine = pl.ds(pl.multiple_of(core[0] * half, half), half)
-    theirs = pl.ds(pl.multiple_of((1 - core[0]) * half, half), half)
-    dq[:, :, mine] = dq_own[...]
-    dq[:, :, theirs] = dq_other[...]
-    for index, out in enumerate((dk, dv)):
-        out[:, :, mine] = kv_own[index]
-        out[:, :, theirs] = kv_other[index]
+    for kind in range(kinds):
+        for seq in range(seqs):
+            for h in range(heads):
+                lanes = slice(h * head, (h + 1) * head)
+                group = (kind * seqs + seq) * heads + h
+                cells = [near[kind, seq, :, lanes]]
+                cells += [part[pl.ds(group * size, size), :] for part, size in zip(back, sizes)]
+                total = dot(spread, jnp.concatenate(cells, axis=0))
+                kept[kind, seq, :, lanes] = (own[kind, seq, :, lanes] + total[:block]).astype(BF16)
+                sent[kind, seq, :, lanes] = (other[kind, seq, :, lanes] + total[block:]).astype(BF16)
+    all_slopes = slope[...]
+    for part, size in zip(back, sizes):
+        all_slopes = all_slopes + one_part(part[pl.ds(kinds * seqs * heads * size, 2 * heads), :])
+    slope_out[...] = all_slopes
+
+
+def join_body(core, own, other, out, sems):
+    mine, theirs = head_halves(core, own.shape[-1])
+    copy_all([(other, out.at[:, :, theirs]), (own, out.at[:, :, mine])], sems)
+
+
+def join_pair_body(core, own, other, first, second, sems):
+    mine, theirs = head_halves(core, own.shape[-1])
+    moves = []
+    for index, out in enumerate((first, second)):
+        moves.append((other.at[index], out.at[:, :, theirs]))
+        moves.append((own.at[index], out.at[:, :, mine]))
+    copy_all(moves, sems)
 
 
 def paired(queries, key_rows, value_rows, out_grad, level_slope):
     seqs, block, width = queries.shape
     heads = level_slope.shape[0]
-    half = width // 2
-    ctx_count = lax.axis_size("ctx")
+    half, head = width // 2, width // heads
+    ctx_count, dp_count = lax.axis_size("ctx"), lax.axis_size("dp")
     levels = ctx_count.bit_length() - 1
-    core = (lax.axis_index("ctx") % 2).astype(jnp.int32).reshape(1)
+    position = lax.axis_index("ctx")
+    core = (position % 2).astype(jnp.int32).reshape(1)
 
     part = like(2, seqs, block, half)
-    kv_own, kv_send, qg_own, qg_send = call(
-        split_body, (part,) * 4, (core, key_rows, value_rows, queries, out_grad), scalars=1, name="split_heads"
+    kv_own, kv_send = call(
+        split_body, (part, part), (core, key_rows, value_rows), "split_kv", scalars=1, hbm_in=2, copies=4
     )
     kv_other = swap(kv_send, 1)
+    qg_own, qg_send = call(
+        split_body, (part, part), (core, queries, out_grad), "split_qg", scalars=1, hbm_in=2, copies=4
+    )
     qg_other = swap(qg_send, 1)
 
     cells = call(
         summary_body,
         tuple(like(2, seqs, 2 * block >> level, half) for level in range(1, levels)),
         (kv_own, kv_other),
-        name="summaries",
-    )
-    level_of = {m: m.bit_length() for m in range(1, ctx_count // 2)}
-    far = [m for m in range(4, ctx_count // 2, 2)]
-    far_cells = [swap(cells[level_of[m] - 1], 2 * m) for m in far]
+        "summaries",
+    )
+    far = list(range(4, ctx_count // 2, 2))
+    far_levels = [m.bit_length() for m in far]
+    far_cells = [swap(cells[level - 1], 2 * m) for m, level in zip(far, far_levels)]
     near_cells = swap(cells[0], 2)
     side_cells = swap(cells[1], 4)
+    across_cells = swap(call(coarser_body, like(2, seqs, block // 2, half), (near_cells,), "coarser"), 4)
     relayed_cells = [swap(c, 2) for c in far_cells]
-    across = call(coarser_body, like(2, seqs, block // 2, half), (near_cells,), name="coarser")
-    across_cells = swap(across, 4)
 
     pieces = [kv_own, kv_other, near_cells, side_cells, across_cells] + far_cells + relayed_cells
-    levels_of = [0, 0, 1, 2, 2] + [level_of[m] for m in far] * 2
-    kinds = [F32, F32, F32, BF16, BF16] + [F32] * len(far) + [BF16] * len(far)
+    levels_of = [0, 0, 1, 2, 2] + far_levels * 2
     rows = sum(p.shape[2] for p in pieces)
+    groups = seqs * heads
+    far_rows = [groups * (2 * block >> level) for level in far_levels]
+    tail = heads
+    slope_part = like(heads // 2, 2 * block, dtype=F32)
     dq_part = like(seqs, block, half)
-    dq_own, dq_send, slope_part, *grads = call(
-        functools.partial(attend_body, tuple(levels_of), width // heads),
-        (dq_part, dq_part, like(heads // 2, 2 * block, dtype=F32))
-        + tuple(like(*p.shape, dtype=kind) for p, kind in zip(pieces, kinds)),
+    dq_own, dq_send, slope, own, other, near, across, side, far_direct, relay = call(
+        functools.partial(attend_body, tuple(levels_of), head),
+        (
+            dq_part,
+            dq_part,
+            slope_part,
+            like(*part.shape, dtype=F32),
+            like(*part.shape, dtype=F32),
+            like(*part.shape, dtype=F32),
+            like(2, seqs, block // 2, half),
+            like(groups * (block // 2), head),
+            like(sum(far_rows), head, dtype=F32),
+            like(sum(far_rows) + tail, head),
+        ),
         (core, level_slope, qg_own, qg_other, *pieces),
+        "attend",
         scalars=2,
         flops=10 * seqs * 2 * block * rows * half,
-        name="attend",
-    )
-    own, other, near, side, across = grads[:5]
-    far_direct, far_relayed = grads[5 : 5 + len(far)], grads[5 + len(far) :]
+    )
 
     across_back = swap(across, 4)
-    relay_back = [swap(part, 2) for part in far_relayed]
-    near_total = call(fold_body, like(*near.shape), (near, across_back), name="fold")
-    far_total = call(
-        functools.partial(relay_body, len(far)),
-        tuple(like(*part.shape) for part in far_direct),
-        (*far_direct, *relay_back),
-        name="relay",
-    )
-    near_back = swap(near_total, 2)
-    far_back = [swap(part, 2 * m) for m, part in zip(far, far_total)]
-    side_back = swap(side, 4)
+    relay_back = swap(relay, 2)
+    slopes = [swap(slope, 2 * y, dp) for dp in range(1, dp_count) for y in range(2)]
     dq_other = swap(dq_send, 1)
-
-    slope_sum = slope_part
-    dp_count = lax.axis_size("dp")
-    for bit in range(dp_count.bit_length() - 1):
-        slope_sum = slope_sum + lax.ppermute(slope_sum, "dp", [(i, i ^ 2**bit) for i in range(dp_count)])
-    for level in range(1, levels):
-        slope_sum = slope_sum + swap(slope_sum, 2**level)
-    slope_other = swap(slope_sum, 1)
-    both = jnp.where(
-        core[0] == 0,
-        jnp.concatenate([slope_sum, slope_other], axis=0),
-        jnp.concatenate([slope_other, slope_sum], axis=0),
-    )
-    slope_grad = jnp.sum(both, axis=1)
-
-    kv_grad, kv_grad_send = call(
-        functools.partial(gather_body, (1, 2) + tuple(level_of[m] for m in far)),
-        (part, part),
-        (own, other, near_back, side_back, *far_back),
-        name="gather_cells",
-    )
-    kv_grad_other = swap(kv_grad_send, 1)
+    near_back = swap(call(fold_body, like(*near.shape), (near, across_back), "fold"), 2)
+    slope, side_total, *far_total = call(
+        relay_body,
+        (slope_part, like(side.shape[0] + tail, head)) + tuple(like(r + tail, head) for r in far_rows),
+        (side, far_direct, relay_back, slope, *slopes),
+        "relay",
+    )
+    side_back = swap(side_total, 4)
+    far_back = [swap(message, 2 * m) for m, message in zip(far, far_total)]
     whole = like(seqs, block, width)
-    dq, dk, dv = call(
-        join_body, (whole,) * 3, (core, dq_own, dq_other, kv_grad, kv_grad_other), scalars=1, name="join_heads"
-    )
+    dq = call(
+        join_body, whole, (core, dq_own, dq_other), "join_queries", scalars=1, hbm_out=True, copies=2
+    )
+    kept, sent, slope = call(
+        functools.partial(gather_body, (1, 2, *far_levels)),
+        (part, part, slope_part),
+        (own, other, slope, near_back, side_back, *far_back),
+        "gather_cells",
+    )
+    kv_grad_other = swap(sent, 1)
+    slope_other = swap(slope, 1)
+    dk, dv = call(
+        join_pair_body, (whole, whole), (core, kept, kv_grad_other), "join_kv", scalars=1, hbm_out=True, copies=4
+    )
+    ours, rest = jnp.sum(slope, axis=1), jnp.sum(slope_other, axis=1)
+    slope_grad = jnp.concatenate([jnp.where(core == 0, ours, rest), jnp.where(core == 0, rest, ours)])
     return dq, dk, dv, slope_grad
 
 
@@ -399,7 +475,8 @@
 
 def shards(queries, key_rows, value_rows, out_grad, level_slope):
     levels = lax.axis_size("ctx").bit_length() - 1
-    few = levels >= 3 and 2 * queries.shape[1] >> levels - 1 >= 16
+    cells = 2 * queries.shape[1] >> levels - 1
+    few = levels >= 4 and cells >= 16 and level_slope.shape[0] % 16 == 0
     form = paired if few else by_blocks
     return form(queries, key_rows, value_rows, out_grad, level_slope)
 

time: 96.8 us -> 70.1 us (0.72)
  waiting for transfers between devices: 53.5 us -> 33.3 us
  starting transfers between devices: 26.7 us -> 21.4 us
  local copies, waits for them, and re-layouts: 4.16 us -> 2.09 us
    ppermute x22 -> x18, waiting for transfers between devices: 51.4 us -> 30.2 us  [swap(): lax.ppermute(value, 'ctx', [(source, source ^ apart) for source in range(...]
    ppermute x22 -> x18, starting transfers between devices: 25.2 us -> 18.3 us  [swap(): lax.ppermute(value, 'ctx', [(source, source ^ apart) for source in range(...]
    unnamed x10, local copies, waits for them, and re-layouts: 4.16 us -> 2.09 us
    ppermute x1 -> x2, starting transfers between devices: 1.49 us -> 3.05 us  [swap(): return lax.ppermute(value, ('dp', 'ctx'), pairs)]
    ppermute x1 -> x2, waiting for transfers between devices: 2.12 us -> 3.12 us  [swap(): return lax.ppermute(value, ('dp', 'ctx'), pairs)]
    pallas_call x8 -> x10, Pallas kernels: 10.8 us -> 11.5 us  [call(): pl.pallas_call(body, out_shape=out_shape, in_specs=[SMEM] * scalars + [HB...]
  transfers between devices with their start and end apart: 23 -> 20, of which waited for: 15 -> 12; matrix products, arithmetic and copies ran while one was open for 1% -> 1% of each run, Pallas kernels for 0% -> 3%
where the time goes in v2:
time: 70.1 us; the launch traced here: 69.9 us
  waiting for transfers between devices  33.3 us (48%)
  starting transfers between devices  21.4 us (31%)
  Pallas kernels  11.5 us (16%)
  local copies, waits for them, and re-layouts  2.09 us (3%)
  other arithmetic  0.83 us (1%)
  between operations  0.75 us (1%)
    ppermute x18, waiting for transfers between devices, swap(): lax.ppermute(value, 'ctx', [(source, source ^ apart) for source in range(...  30.2 us
    ppermute x18, starting transfers between devices, swap(): lax.ppermute(value, 'ctx', [(source, source ^ apart) for source in range(...  18.3 us
    pallas_call x10, Pallas kernels, call(): pl.pallas_call(body, out_shape=out_shape, in_specs=[SMEM] * scalars + [HB...  11.5 us
    ppermute x2, waiting for transfers between devices, swap(): return lax.ppermute(value, ('dp', 'ctx'), pairs)  3.12 us
    ppermute x2, starting transfers between devices, swap(): return lax.ppermute(value, ('dp', 'ctx'), pairs)  3.05 us
    unnamed x10, local copies, waits for them, and re-layouts  2.09 us
  transfers between devices with their start and end apart: 20, of which 12 were waited for; matrix products, arithmetic and copies ran while one was open for 1% of the time, Pallas kernels for 3%

profile of v2, /device:TPU:0, one launch (start us, length us, event | category | flops | bytes accessed | tf_op | source)
XLA Modules:
  0.0 69.9 jit_solution(3125789784370429457)
XLA Ops:
  0.7 1.0 %copy-done = bf16[2,64,2048]{2,1,0:T(8,128)(2,1)S(1)} copy-done((bf16[2,64,2048]{2,1,0:T(8,128)(2,1)S(1)}, bf16[2,64,2048]{2,1,0:T(8,128)(2,1)}, u32[]{:S(2)}) %copy-start) | copy-done | bytes 524312
  1.7 1.0 %copy-done.1 = bf16[2,64,2048]{2,1,0:T(8,128)(2,1)S(1)} copy-done((bf16[2,64,2048]{2,1,0:T(8,128)(2,1)S(1)}, bf16[2,64,2048]{2,1,0:T(8,128)(2,1)}, u32[]{:S(2)}) %copy-start.1) | copy-done | bytes 524312
  2.7 0.1 split_kv.1
  2.8 0.5 collective-permute-start.1
  3.4 1.5 %collective-permute-done.1.other.refs_3_ = bf16[2,2,64,1024]{3,2,1,0:T(8,128)(2,1)S(1)} collective-permute-done((bf16[2,2,64,1024]{3,2,1,0:T(8,128)(2,1)S(1)}, bf16[2,2,64,1024]{3,2,1,0:T(8,128)(2,1)S(1)}, u32[]{:S(2)}, u32[]{:S(2)}) %collective-permute-start.1) | collective-permute-done | bytes 524320 | tf_op jit(solution)/shard_map/ppermute | solution.py:21
  4.9 1.3 %summaries.1 = (bf16[2,2,64,1024]{3,2,1,0:T(8,128)(2,1)S(1)}, bf16[2,2,32,1024]{3,2,1,0:T(8,128)(2,1)S(1)}, bf16[2,2,16,1024]{3,2,1,0:T(8,128)(2,1)S(1)}) custom-call(bf16[2,2,64,1024]{3,2,1,0:T(8,128)(2,1)S(1)} %get-tuple-element.32.own.refs_2_, bf16[2,2,64,1024]{3,2,1,0:T(8,128)(2,1)S(1)} %collective-permute-done.1.other.refs_3_), custom_call_target="tpu_custom_call" | custom-call | bytes 1966080 | tf_op jit(solution)/shard_map/summaries/pallas_call | solution.py:34
  6.2 2.9 %collective-permute-start.2 = (bf16[2,2,64,1024]{3,2,1,0:T(8,128)(2,1)S(1)}, bf16[2,2,64,1024]{3,2,1,0:T(8,128)(2,1)S(1)}, u32[]{:S(2)}, u32[]{:S(2)}) collective-permute-start(bf16[2,2,64,1024]{3,2,1,0:T(8,128)(2,1)S(1)} %get-tuple-element.34), channel_id=1, source_target_pairs={{0,2},{1,3},{2,0},{3,1},{4,6},{5,7},{6,4},{7,5},{8,10},{9,11},{10,... | collective-permute-start | bytes 1572872 | tf_op jit(solution)/shard_map/ppermute | solution.py:21
  9.1 0.1 split_qg.1
  9.3 0.1 collective-permute-start
  9.4 2.7 %collective-permute-start.5 = (bf16[2,2,16,1024]{3,2,1,0:T(8,128)(2,1)S(1)}, bf16[2,2,16,1024]{3,2,1,0:T(8,128)(2,1)S(1)}, u32[]{:S(2)}, u32[]{:S(2)}) collective-permute-start(bf16[2,2,16,1024]{3,2,1,0:T(8,128)(2,1)S(1)} %get-tuple-element.36), channel_id=1, source_target_pairs={{0,8},{1,9},{2,10},{3,11},{4,12},{5,13},{6,14},{7,15},{8,0},{9,1},... | collective-permute-start | bytes 393224 | tf_op jit(solution)/shard_map/ppermute | solution.py:21
  12.0 1.3 %collective-permute-start.6 = (bf16[2,2,16,1024]{3,2,1,0:T(8,128)(2,1)S(1)}, bf16[2,2,16,1024]{3,2,1,0:T(8,128)(2,1)S(1)}, u32[]{:S(2)}, u32[]{:S(2)}) collective-permute-start(bf16[2,2,16,1024]{3,2,1,0:T(8,128)(2,1)S(1)} %get-tuple-element.36), channel_id=1, source_target_pairs={{0,12},{1,13},{2,14},{3,15},{4,8},{5,9},{6,10},{7,11},{8,4},{9,5},... | collective-permute-start | bytes 393224 | tf_op jit(solution)/shard_map/ppermute | solution.py:21
  13.4 0.2 collective-permute-start.3
  13.6 7.8 %collective-permute-done.2.cells.refs_4_ = bf16[2,2,64,1024]{3,2,1,0:T(8,128)(2,1)S(1)} collective-permute-done((bf16[2,2,64,1024]{3,2,1,0:T(8,128)(2,1)S(1)}, bf16[2,2,64,1024]{3,2,1,0:T(8,128)(2,1)S(1)}, u32[]{:S(2)}, u32[]{:S(2)}) %collective-permute-start.2) | collective-permute-done | bytes 524320 | tf_op jit(solution)/shard_map/ppermute | solution.py:21
  21.4 0.2 coarser.1
  21.6 0.0 copy-start.4
  21.6 1.9 %collective-permute-start.4 = (bf16[2,2,32,1024]{3,2,1,0:T(8,128)(2,1)S(1)}, bf16[2,2,32,1024]{3,2,1,0:T(8,128)(2,1)S(1)}, u32[]{:S(2)}, u32[]{:S(2)}) collective-permute-start(bf16[2,2,32,1024]{3,2,1,0:T(8,128)(2,1)S(1)} %coarser.1), channel_id=1, source_target_pairs={{0,4},{1,5},{2,6},{3,7},{4,0},{5,1},{6,2},{7,3},{8,12},{9,13},{10,... | collective-permute-start | bytes 786440 | tf_op jit(solution)/shard_map/ppermute | solution.py:21
  23.5 1.5 %collective-permute-start.7 = (bf16[2,2,16,1024]{3,2,1,0:T(8,128)(2,1)S(1)}, bf16[2,2,16,1024]{3,2,1,0:T(8,128)(2,1)S(1)}, u32[]{:S(2)}, u32[]{:S(2)}) collective-permute-start(bf16[2,2,16,1024]{3,2,1,0:T(8,128)(2,1)S(1)} %collective-permute-done.5.refs_7_), channel_id=1, source_target_pairs={{0,2},{1,3},{2,0},{3,1},{4,6},{5,7},{6,4},{7,5},{8,10},{9,11},{10,... | collective-permute-start | bytes 393224 | tf_op jit(solution)/shard_map/ppermute | solution.py:21
  25.0 0.0 collective-permute-done.6.refs_8_
  25.0 0.5 collective-permute-start.8
  25.5 1.5 %collective-permute-done.3.refs_5_ = bf16[2,2,32,1024]{3,2,1,0:T(8,128)(2,1)S(1)} collective-permute-done((bf16[2,2,32,1024]{3,2,1,0:T(8,128)(2,1)S(1)}, bf16[2,2,32,1024]{3,2,1,0:T(8,128)(2,1)S(1)}, u32[]{:S(2)}, u32[]{:S(2)}) %collective-permute-start.3) | collective-permute-done | bytes 262176 | tf_op jit(solution)/shard_map/ppermute | solution.py:21
  27.0 2.3 %collective-permute-done.7.refs_9_ = bf16[2,2,16,1024]{3,2,1,0:T(8,128)(2,1)S(1)} collective-permute-done((bf16[2,2,16,1024]{3,2,1,0:T(8,128)(2,1)S(1)}, bf16[2,2,16,1024]{3,2,1,0:T(8,128)(2,1)S(1)}, u32[]{:S(2)}, u32[]{:S(2)}) %collective-permute-start.7) | collective-permute-done | bytes 131104 | tf_op jit(solution)/shard_map/ppermute | solution.py:21
  29.3 1.4 %collective-permute-done.8.refs_10_ = bf16[2,2,16,1024]{3,2,1,0:T(8,128)(2,1)S(1)} collective-permute-done((bf16[2,2,16,1024]{3,2,1,0:T(8,128)(2,1)S(1)}, bf16[2,2,16,1024]{3,2,1,0:T(8,128)(2,1)S(1)}, u32[]{:S(2)}, u32[]{:S(2)}) %collective-permute-start.8) | collective-permute-done | bytes 131104 | tf_op jit(solution)/shard_map/ppermute | solution.py:21
  30.7 0.9 %collective-permute-done.4.refs_6_ = bf16[2,2,32,1024]{3,2,1,0:T(8,128)(2,1)S(1)} collective-permute-done((bf16[2,2,32,1024]{3,2,1,0:T(8,128)(2,1)S(1)}, bf16[2,2,32,1024]{3,2,1,0:T(8,128)(2,1)S(1)}, u32[]{:S(2)}, u32[]{:S(2)}) %collective-permute-start.4) | collective-permute-done | bytes 262176 | tf_op jit(solution)/shard_map/ppermute | solution.py:21
  31.6 7.1 %attend.1 = (bf16[2,64,1024]{2,1,0:T(8,128)(2,1)S(1)}, bf16[2,64,1024]{2,1,0:T(8,128)(2,1)S(1)}, f32[8,128]{1,0:T(8,128)S(1)}, f32[2,2,64,1024]{3,2,1,0:T(8,128)...) custom-call(s32[1]{0:T(128)} %bitcast.core, ...), custom_call_target="tpu_custom_call" | custom-call | flops 838860800 | bytes 8659012 | tf_op jit(solution)/shard_map/attend/pallas_call | solution.py:34
  38.6 0.5 collective-permute-start.13
  39.1 0.7 %collective-permute-start.10 = (bf16[1040,128]{1,0:T(8,128)(2,1)S(1)}, bf16[1040,128]{1,0:T(8,128)(2,1)S(1)}, u32[]{:S(2)}, u32[]{:S(2)}) collective-permute-start(bf16[1040,128]{1,0:T(8,128)(2,1)S(1)} %get-tuple-element.43), channel_id=1, source_target_pairs={{0,2},{1,3},{2,0},{3,1},{4,6},{5,7},{6,4},{7,5},{8,10},{9,11},{10,... | collective-permute-start | bytes 798728 | tf_op jit(solution)/shard_map/ppermute | solution.py:21
  39.8 6.2 %collective-permute-done.13.coarse = bf16[2,2,32,1024]{3,2,1,0:T(8,128)(2,1)S(1)} collective-permute-done((bf16[2,2,32,1024]{3,2,1,0:T(8,128)(2,1)S(1)}, bf16[2,2,32,1024]{3,2,1,0:T(8,128)(2,1)S(1)}, u32[]{:S(2)}, u32[]{:S(2)}) %collective-permute-start.13) | collective-permute-done | bytes 262176 | tf_op jit(solution)/shard_map/ppermute | solution.py:21
  46.0 0.3 fold.1
  46.3 0.5 collective-permute-start.14
  46.8 1.6 %collective-permute-start.11 = (f32[8,128]{1,0:T(8,128)S(1)}, f32[8,128]{1,0:T(8,128)S(1)}, u32[]{:S(2)}, u32[]{:S(2)}) collective-permute-start(f32[8,128]{1,0:T(8,128)S(1)} %get-tuple-element.44.slope), channel_id=1, source_target_pairs={{0,16},{1,17},{2,18},{3,19},{4,20},{5,21},{6,22},{7,23},{8,24},{9,... | collective-permute-start | bytes 12296 | tf_op jit(solution)/shard_map/ppermute | solution.py:24
  48.3 1.5 %collective-permute-start.12 = (f32[8,128]{1,0:T(8,128)S(1)}, f32[8,128]{1,0:T(8,128)S(1)}, u32[]{:S(2)}, u32[]{:S(2)}) collective-permute-start(f32[8,128]{1,0:T(8,128)S(1)} %get-tuple-element.44.slope), channel_id=1, source_target_pairs={{0,18},{1,19},{2,16},{3,17},{4,22},{5,23},{6,20},{7,21},{8,26},{9,... | collective-permute-start | bytes 12296 | tf_op jit(solution)/shard_map/ppermute | solution.py:24
  49.8 0.6 collective-permute-done.11.refs_0_
  50.4 2.6 %collective-permute-done.12.refs_1_ = f32[8,128]{1,0:T(8,128)S(1)} collective-permute-done((f32[8,128]{1,0:T(8,128)S(1)}, f32[8,128]{1,0:T(8,128)S(1)}, u32[]{:S(2)}, u32[]{:S(2)}) %collective-permute-start.12) | collective-permute-done | bytes 4128 | tf_op jit(solution)/shard_map/ppermute | solution.py:24
  52.9 0.1 relay.1
  53.0 0.3 collective-permute-start.15
  53.4 3.8 %collective-permute-start.16 = (bf16[528,128]{1,0:T(8,128)(2,1)S(1)}, bf16[528,128]{1,0:T(8,128)(2,1)S(1)}, u32[]{:S(2)}, u32[]{:S(2)}) collective-permute-start(bf16[528,128]{1,0:T(8,128)(2,1)S(1)} %get-tuple-element.49), channel_id=1, source_target_pairs={{0,8},{1,9},{2,10},{3,11},{4,12},{5,13},{6,14},{7,15},{8,0},{9,1},... | collective-permute-start | bytes 405512 | tf_op jit(solution)/shard_map/ppermute | solution.py:21
  57.2 0.3 collective-permute-start.17
  57.5 4.1 %collective-permute-done.16.refs_1_ = bf16[528,128]{1,0:T(8,128)(2,1)S(1)} collective-permute-done((bf16[528,128]{1,0:T(8,128)(2,1)S(1)}, bf16[528,128]{1,0:T(8,128)(2,1)S(1)}, u32[]{:S(2)}, u32[]{:S(2)}) %collective-permute-start.16) | collective-permute-done | bytes 135200 | tf_op jit(solution)/shard_map/ppermute | solution.py:21
  61.6 4.0 %collective-permute-done.17.refs_2_ = bf16[528,128]{1,0:T(8,128)(2,1)S(1)} collective-permute-done((bf16[528,128]{1,0:T(8,128)(2,1)S(1)}, bf16[528,128]{1,0:T(8,128)(2,1)S(1)}, u32[]{:S(2)}, u32[]{:S(2)}) %collective-permute-start.17) | collective-permute-done | bytes 135200 | tf_op jit(solution)/shard_map/ppermute | solution.py:21
  65.7 0.5 gather_cells.1
  66.2 0.1 collective-permute-start.18
  66.3 0.5 collective-permute-start.19
  66.8 0.8 %join_queries.1 = bf16[2,64,2048]{2,1,0:T(8,128)(2,1)} custom-call(s32[1]{0:T(128)} %bitcast.core, bf16[2,64,1024]{2,1,0:T(8,128)(2,1)S(1)} %get-tuple-element.37.own, bf16[2,64,1024]{2,1,0:T(8,128)(2,1)S(1)} %collective-permute-done.9.other), custom_call_target="tpu_custom_call" | custom-call | bytes 1048580 | tf_op jit(solution)/shard_map/join_queries/pallas_call | solution.py:34
  67.6 0.1 reduce_sum.18
  67.7 0.5 collective-permute-done.19
  68.2 0.1 reduce_sum.19
  68.3 0.6 pad_maximum_fusion
  68.9 1.0 %join_kv.1 = (bf16[2,64,2048]{2,1,0:T(8,128)(2,1)}, bf16[2,64,2048]{2,1,0:T(8,128)(2,1)}) custom-call(s32[1]{0:T(128)} %bitcast.core, bf16[2,2,64,1024]{3,2,1,0:T(8,128)(2,1)S(1)} %get-tuple-element.51.own, bf16[2,2,64,1024]{3,2,1,0:T(8,128)(2,1)S(1)} %collective-permute-done.18.other), custom_call_target="tpu_custom_call" | custom-call | bytes 2097156 | tf_op jit(solution)/shard_map/join_kv/pallas_call | solution.py:34
  (16 shorter events, 0.0 us)
Async XLA Ops:
  0.6 1.0 %copy-start = (bf16[2,64,2048]{2,1,0:T(8,128)(2,1)S(1)}, bf16[2,64,2048]{2,1,0:T(8,128)(2,1)}, u32[]{:S(2)}) copy-start(bf16[2,64,2048]{2,1,0:T(8,128)(2,1)} %first.3) | copy-start | bytes 1572868
  1.7 1.0 %copy-start.1 = (bf16[2,64,2048]{2,1,0:T(8,128)(2,1)S(1)}, bf16[2,64,2048]{2,1,0:T(8,128)(2,1)}, u32[]{:S(2)}) copy-start(bf16[2,64,2048]{2,1,0:T(8,128)(2,1)} %second.3) | copy-start | bytes 1572868
  2.8 2.1 %collective-permute-start.1 = (bf16[2,2,64,1024]{3,2,1,0:T(8,128)(2,1)S(1)}, bf16[2,2,64,1024]{3,2,1,0:T(8,128)(2,1)S(1)}, u32[]{:S(2)}, u32[]{:S(2)}) collective-permute-start(bf16[2,2,64,1024]{3,2,1,0:T(8,128)(2,1)S(1)} %get-tuple-element.33), channel_id=1, source_target_pairs={{0,1},{1,0},{2,3},{3,2},{4,5},{5,4},{6,7},{7,6},{8,9},{9,8},{10,11... | collective-permute-start | bytes 1572872 | tf_op jit(solution)/shard_map/ppermute | solution.py:21
  4.9 4.2 %copy-start.2 = (bf16[2,64,2048]{2,1,0:T(8,128)(2,1)S(1)}, bf16[2,64,2048]{2,1,0:T(8,128)(2,1)}, u32[]{:S(2)}) copy-start(bf16[2,64,2048]{2,1,0:T(8,128)(2,1)} %first.2) | copy-start | bytes 1572868
  4.9 4.2 %copy-start.3 = (bf16[2,64,2048]{2,1,0:T(8,128)(2,1)S(1)}, bf16[2,64,2048]{2,1,0:T(8,128)(2,1)}, u32[]{:S(2)}) copy-start(bf16[2,64,2048]{2,1,0:T(8,128)(2,1)} %second.2) | copy-start | bytes 1572868
  6.2 15.1 %collective-permute-start.2 = (bf16[2,2,64,1024]{3,2,1,0:T(8,128)(2,1)S(1)}, bf16[2,2,64,1024]{3,2,1,0:T(8,128)(2,1)S(1)}, u32[]{:S(2)}, u32[]{:S(2)}) collective-permute-start(bf16[2,2,64,1024]{3,2,1,0:T(8,128)(2,1)S(1)} %get-tuple-element.34), channel_id=1, source_target_pairs={{0,2},{1,3},{2,0},{3,1},{4,6},{5,7},{6,4},{7,5},{8,10},{9,11},{10,... | collective-permute-start | bytes 1572872 | tf_op jit(solution)/shard_map/ppermute | solution.py:21
  9.3 16.2 %collective-permute-start = (bf16[2,2,64,1024]{3,2,1,0:T(8,128)(2,1)S(1)}, bf16[2,2,64,1024]{3,2,1,0:T(8,128)(2,1)S(1)}, u32[]{:S(2)}, u32[]{:S(2)}) collective-permute-start(bf16[2,2,64,1024]{3,2,1,0:T(8,128)(2,1)S(1)} %get-tuple-element.31), channel_id=1, source_target_pairs={{0,1},{1,0},{2,3},{3,2},{4,5},{5,4},{6,7},{7,6},{8,9},{9,8},{10,11... | collective-permute-start | bytes 1572872 | tf_op jit(solution)/shard_map/ppermute | solution.py:21
  9.4 14.1 %collective-permute-start.5 = (bf16[2,2,16,1024]{3,2,1,0:T(8,128)(2,1)S(1)}, bf16[2,2,16,1024]{3,2,1,0:T(8,128)(2,1)S(1)}, u32[]{:S(2)}, u32[]{:S(2)}) collective-permute-start(bf16[2,2,16,1024]{3,2,1,0:T(8,128)(2,1)S(1)} %get-tuple-element.36), channel_id=1, source_target_pairs={{0,8},{1,9},{2,10},{3,11},{4,12},{5,13},{6,14},{7,15},{8,0},{9,1},... | collective-permute-start | bytes 393224 | tf_op jit(solution)/shard_map/ppermute | solution.py:21
  12.0 13.0 %collective-permute-start.6 = (bf16[2,2,16,1024]{3,2,1,0:T(8,128)(2,1)S(1)}, bf16[2,2,16,1024]{3,2,1,0:T(8,128)(2,1)S(1)}, u32[]{:S(2)}, u32[]{:S(2)}) collective-permute-start(bf16[2,2,16,1024]{3,2,1,0:T(8,128)(2,1)S(1)} %get-tuple-element.36), channel_id=1, source_target_pairs={{0,12},{1,13},{2,14},{3,15},{4,8},{5,9},{6,10},{7,11},{8,4},{9,5},... | collective-permute-start | bytes 393224 | tf_op jit(solution)/shard_map/ppermute | solution.py:21
  13.4 13.6 %collective-permute-start.3 = (bf16[2,2,32,1024]{3,2,1,0:T(8,128)(2,1)S(1)}, bf16[2,2,32,1024]{3,2,1,0:T(8,128)(2,1)S(1)}, u32[]{:S(2)}, u32[]{:S(2)}) collective-permute-start(bf16[2,2,32,1024]{3,2,1,0:T(8,128)(2,1)S(1)} %get-tuple-element.35), channel_id=1, source_target_pairs={{0,4},{1,5},{2,6},{3,7},{4,0},{5,1},{6,2},{7,3},{8,12},{9,13},{10,... | collective-permute-start | bytes 786440 | tf_op jit(solution)/shard_map/ppermute | solution.py:21
  21.6 10.0 %copy-start.4 = (f32[16]{0:T(128)S(1)}, f32[16]{0:T(128)}, u32[]{:S(2)}) copy-start(f32[16]{0:T(128)} %slope.1) | copy-start | bytes 196
  21.6 10.0 %collective-permute-start.4 = (bf16[2,2,32,1024]{3,2,1,0:T(8,128)(2,1)S(1)}, bf16[2,2,32,1024]{3,2,1,0:T(8,128)(2,1)S(1)}, u32[]{:S(2)}, u32[]{:S(2)}) collective-permute-start(bf16[2,2,32,1024]{3,2,1,0:T(8,128)(2,1)S(1)} %coarser.1), channel_id=1, source_target_pairs={{0,4},{1,5},{2,6},{3,7},{4,0},{5,1},{6,2},{7,3},{8,12},{9,13},{10,... | collective-permute-start | bytes 786440 | tf_op jit(solution)/shard_map/ppermute | solution.py:21
  23.5 5.8 %collective-permute-start.7 = (bf16[2,2,16,1024]{3,2,1,0:T(8,128)(2,1)S(1)}, bf16[2,2,16,1024]{3,2,1,0:T(8,128)(2,1)S(1)}, u32[]{:S(2)}, u32[]{:S(2)}) collective-permute-start(bf16[2,2,16,1024]{3,2,1,0:T(8,128)(2,1)S(1)} %collective-permute-done.5.refs_7_), channel_id=1, source_target_pairs={{0,2},{1,3},{2,0},{3,1},{4,6},{5,7},{6,4},{7,5},{8,10},{9,11},{10,... | collective-permute-start | bytes 393224 | tf_op jit(solution)/shard_map/ppermute | solution.py:21
  25.0 5.7 %collective-permute-start.8 = (bf16[2,2,16,1024]{3,2,1,0:T(8,128)(2,1)S(1)}, bf16[2,2,16,1024]{3,2,1,0:T(8,128)(2,1)S(1)}, u32[]{:S(2)}, u32[]{:S(2)}) collective-permute-start(bf16[2,2,16,1024]{3,2,1,0:T(8,128)(2,1)S(1)} %collective-permute-done.6.refs_8_), channel_id=1, source_target_pairs={{0,2},{1,3},{2,0},{3,1},{4,6},{5,7},{6,4},{7,5},{8,10},{9,11},{10,... | collective-permute-start | bytes 393224 | tf_op jit(solution)/shard_map/ppermute | solution.py:21
  38.6 7.3 %collective-permute-start.13 = (bf16[2,2,32,1024]{3,2,1,0:T(8,128)(2,1)S(1)}, bf16[2,2,32,1024]{3,2,1,0:T(8,128)(2,1)S(1)}, u32[]{:S(2)}, u32[]{:S(2)}) collective-permute-start(bf16[2,2,32,1024]{3,2,1,0:T(8,128)(2,1)S(1)} %get-tuple-element.47), channel_id=1, source_target_pairs={{0,4},{1,5},{2,6},{3,7},{4,0},{5,1},{6,2},{7,3},{8,12},{9,13},{10,... | collective-permute-start | bytes 786440 | tf_op jit(solution)/shard_map/ppermute | solution.py:21
  39.1 13.8 %collective-permute-start.10 = (bf16[1040,128]{1,0:T(8,128)(2,1)S(1)}, bf16[1040,128]{1,0:T(8,128)(2,1)S(1)}, u32[]{:S(2)}, u32[]{:S(2)}) collective-permute-start(bf16[1040,128]{1,0:T(8,128)(2,1)S(1)} %get-tuple-element.43), channel_id=1, source_target_pairs={{0,2},{1,3},{2,0},{3,1},{4,6},{5,7},{6,4},{7,5},{8,10},{9,11},{10,... | collective-permute-start | bytes 798728 | tf_op jit(solution)/shard_map/ppermute | solution.py:21
  46.3 19.4 %collective-permute-start.14 = (bf16[2,2,64,1024]{3,2,1,0:T(8,128)(2,1)S(1)}, bf16[2,2,64,1024]{3,2,1,0:T(8,128)(2,1)S(1)}, u32[]{:S(2)}, u32[]{:S(2)}) collective-permute-start(bf16[2,2,64,1024]{3,2,1,0:T(8,128)(2,1)S(1)} %fold.1), channel_id=1, source_target_pairs={{0,2},{1,3},{2,0},{3,1},{4,6},{5,7},{6,4},{7,5},{8,10},{9,11},{10,... | collective-permute-start | bytes 1572872 | tf_op jit(solution)/shard_map/ppermute | solution.py:21
  46.8 3.6 %collective-permute-start.11 = (f32[8,128]{1,0:T(8,128)S(1)}, f32[8,128]{1,0:T(8,128)S(1)}, u32[]{:S(2)}, u32[]{:S(2)}) collective-permute-start(f32[8,128]{1,0:T(8,128)S(1)} %get-tuple-element.44.slope), channel_id=1, source_target_pairs={{0,16},{1,17},{2,18},{3,19},{4,20},{5,21},{6,22},{7,23},{8,24},{9,... | collective-permute-start | bytes 12296 | tf_op jit(solution)/shard_map/ppermute | solution.py:24
  48.3 4.6 %collective-permute-start.12 = (f32[8,128]{1,0:T(8,128)S(1)}, f32[8,128]{1,0:T(8,128)S(1)}, u32[]{:S(2)}, u32[]{:S(2)}) collective-permute-start(f32[8,128]{1,0:T(8,128)S(1)} %get-tuple-element.44.slope), channel_id=1, source_target_pairs={{0,18},{1,19},{2,16},{3,17},{4,22},{5,23},{6,20},{7,21},{8,26},{9,... | collective-permute-start | bytes 12296 | tf_op jit(solution)/shard_map/ppermute | solution.py:24
  53.0 12.6 %collective-permute-start.15 = (bf16[1040,128]{1,0:T(8,128)(2,1)S(1)}, bf16[1040,128]{1,0:T(8,128)(2,1)S(1)}, u32[]{:S(2)}, u32[]{:S(2)}) collective-permute-start(bf16[1040,128]{1,0:T(8,128)(2,1)S(1)} %get-tuple-element.48), channel_id=1, source_target_pairs={{0,4},{1,5},{2,6},{3,7},{4,0},{5,1},{6,2},{7,3},{8,12},{9,13},{10,... | collective-permute-start | bytes 798728 | tf_op jit(solution)/shard_map/ppermute | solution.py:21
  53.4 8.3 %collective-permute-start.16 = (bf16[528,128]{1,0:T(8,128)(2,1)S(1)}, bf16[528,128]{1,0:T(8,128)(2,1)S(1)}, u32[]{:S(2)}, u32[]{:S(2)}) collective-permute-start(bf16[528,128]{1,0:T(8,128)(2,1)S(1)} %get-tuple-element.49), channel_id=1, source_target_pairs={{0,8},{1,9},{2,10},{3,11},{4,12},{5,13},{6,14},{7,15},{8,0},{9,1},... | collective-permute-start | bytes 405512 | tf_op jit(solution)/shard_map/ppermute | solution.py:21
  57.2 8.4 %collective-permute-start.17 = (bf16[528,128]{1,0:T(8,128)(2,1)S(1)}, bf16[528,128]{1,0:T(8,128)(2,1)S(1)}, u32[]{:S(2)}, u32[]{:S(2)}) collective-permute-start(bf16[528,128]{1,0:T(8,128)(2,1)S(1)} %get-tuple-element.50), channel_id=1, source_target_pairs={{0,12},{1,13},{2,14},{3,15},{4,8},{5,9},{6,10},{7,11},{8,4},{9,5},... | collective-permute-start | bytes 405512 | tf_op jit(solution)/shard_map/ppermute | solution.py:21
  57.5 9.3 %collective-permute-start.9 = (bf16[2,64,1024]{2,1,0:T(8,128)(2,1)S(1)}, bf16[2,64,1024]{2,1,0:T(8,128)(2,1)S(1)}, u32[]{:S(2)}, u32[]{:S(2)}) collective-permute-start(bf16[2,64,1024]{2,1,0:T(8,128)(2,1)S(1)} %get-tuple-element.38), channel_id=1, source_target_pairs={{0,1},{1,0},{2,3},{3,2},{4,5},{5,4},{6,7},{7,6},{8,9},{9,8},{10,11... | collective-permute-start | bytes 786440 | tf_op jit(solution)/shard_map/ppermute | solution.py:21
  66.2 2.7 %collective-permute-start.18 = (bf16[2,2,64,1024]{3,2,1,0:T(8,128)(2,1)S(1)}, bf16[2,2,64,1024]{3,2,1,0:T(8,128)(2,1)S(1)}, u32[]{:S(2)}, u32[]{:S(2)}) collective-permute-start(bf16[2,2,64,1024]{3,2,1,0:T(8,128)(2,1)S(1)} %get-tuple-element.52), channel_id=1, source_target_pairs={{0,1},{1,0},{2,3},{3,2},{4,5},{5,4},{6,7},{7,6},{8,9},{9,8},{10,11... | collective-permute-start | bytes 1572872 | tf_op jit(solution)/shard_map/ppermute | solution.py:21
  66.3 1.9 %collective-permute-start.19 = (f32[8,128]{1,0:T(8,128)S(1)}, f32[8,128]{1,0:T(8,128)S(1)}, u32[]{:S(2)}, u32[]{:S(2)}) collective-permute-start(f32[8,128]{1,0:T(8,128)S(1)} %get-tuple-element.55), channel_id=1, source_target_pairs={{0,1},{1,0},{2,3},{3,2},{4,5},{5,4},{6,7},{7,6},{8,9},{9,8},{10,11... | collective-permute-start | bytes 12296 | tf_op jit(solution)/shard_map/ppermute | solution.py:21

commit v3 on v2

--- a/solution.py
+++ b/solution.py
@@ -28,16 +28,18 @@
     return jax.ShapeDtypeStruct(shape, dtype)
 
 
-def call(body, out_shape, operands, name, scalars=0, hbm_in=0, hbm_out=False, copies=0, flops=0):
+def call(body, out_shape, operands, name, scalars=0, hbm_in=0, hbm_out=0, copies=0, flops=0, limit=32):
     moved = sum(a.size * a.dtype.itemsize for a in jax.tree.leaves((operands, out_shape)))
     count = len(operands) - scalars - hbm_in
     return pl.pallas_call(
         body,
         out_shape=out_shape,
         in_specs=[SMEM] * scalars + [HBM] * hbm_in + [VMEM] * count,
-        out_specs=jax.tree.map(lambda _: HBM if hbm_out else VMEM, out_shape),
+        out_specs=tuple(HBM if i < hbm_out else VMEM for i in range(len(out_shape)))
+        if isinstance(out_shape, tuple)
+        else VMEM,
         scratch_shapes=[pltpu.SemaphoreType.DMA((copies,))] if copies else [],
-        compiler_params=pltpu.CompilerParams(vmem_limit_bytes=32 * 2**20),
+        compiler_params=pltpu.CompilerParams(vmem_limit_bytes=limit * 2**20),
         cost_estimate=pl.CostEstimate(flops=flops, bytes_accessed=moved, transcendentals=0),
         name=name,
     )(*operands)
@@ -109,68 +111,121 @@
             out[kind, seq] = dot(pair_matrix(rows.shape[0] // 2), rows).astype(BF16)
 
 
-def attend_body(levels_of, head, core, slope, *refs):
-    count = len(levels_of)
-    qg_own, qg_other = refs[:2]
-    pieces = refs[2 : 2 + count]
-    dq_own, dq_send, slope_out, own, other, near, across, side, far, relay = refs[2 + count :]
+def stack_body(*refs):
+    *parts, out = refs
+    start = 0
+    for part in parts:
+        rows = part.shape[2]
+        out[:, :, pl.ds(start, rows), :] = part[...]
+        start += rows
+
+
+def stacked(parts, kind, seq, lanes):
+    return jnp.concatenate([part[kind, seq, :, lanes] for part in parts], axis=0)
+
+
+def score_body(levels_of, head, core, slope, qg_own, qg_other, *refs):
+    *pieces, scores, upstream = refs
+    seqs, width = qg_own.shape[1], qg_own.shape[3]
+    heads = width // head
+    scale = LOG2E / math.sqrt(head)
+    for h in range(heads):
+        lanes = slice(h * head, (h + 1) * head)
+        step = slope[core[0] * heads + h] * LOG2E + 1.0
+        for seq in range(seqs):
+            raw = dot(stacked(pieces, 0, seq, lanes), stacked((qg_own, qg_other), 0, seq, lanes), 1, 1)
+            start = 0
+            for piece, level in zip(pieces, levels_of):
+                here = slice(start, start + piece.shape[2])
+                scores[seq * heads + h, here] = raw[here] * scale + step * float(level)
+                start += piece.shape[2]
+            upstream[seq * heads + h] = dot(
+                stacked(pieces, 1, seq, lanes), stacked((qg_own, qg_other), 1, seq, lanes), 1, 1
+            )
+
+
+def attend_body(runs, head, far_sizes, core, slope, *refs):
+    early, (qg_own, qg_other, across_cells, relayed_cells), outs = refs[:4], refs[4:8], refs[8:]
+    slope_out, near, across, side, far, relay, dscore_out, probs_out = outs
     seqs, block, width = qg_own.shape[1:]
     heads = width // head
     scale = 1.0 / math.sqrt(head)
-    sizes = [piece.shape[2] for piece in pieces]
-    starts = [sum(sizes[:i]) for i in range(count + 1)]
-    far_count = (count - 5) // 2
-    slabs = [2 * seqs * heads * sum(sizes[5 : 5 + i]) for i in range(far_count)]
+    token_rows = 2 * block
+    early_rows = early[0].shape[1] + early[2].shape[1]
+    starts = [sum(rows for _, rows in runs[:i]) for i in range(len(runs) + 1)]
+    far_count = len(far_sizes)
+    slabs = [2 * seqs * heads * sum(far_sizes[:i]) for i in range(far_count)]
     for h in range(heads):
         lanes = slice(h * head, (h + 1) * head)
         step = slope[core[0] * heads + h] * LOG2E + 1.0
-        slope_sum = jnp.zeros((1, 2 * block), F32)
+        slope_sum = jnp.zeros((1, token_rows), F32)
         for seq in range(seqs):
-            query = jnp.concatenate([qg_own[0, seq, :, lanes], qg_other[0, seq, :, lanes]], axis=0)
-            grad = jnp.concatenate([qg_own[1, seq, :, lanes], qg_other[1, seq, :, lanes]], axis=0)
-            keys = jnp.concatenate([piece[0, seq, :, lanes] for piece in pieces], axis=0)
-            values = jnp.concatenate([piece[1, seq, :, lanes] for piece in pieces], axis=0)
-            raw = dot(keys, query, 1, 1)
-            upstream = dot(values, grad, 1, 1)
-            scores = jnp.concatenate(
-                [
-                    raw[starts[i] : starts[i + 1]] * (scale * LOG2E) + step * float(levels_of[i])
-                    for i in range(count)
-                ],
-                axis=0,
-            )
+            at = seq * heads + h
+            query = stacked((qg_own, qg_other), 0, seq, lanes)
+            grad = stacked((qg_own, qg_other), 1, seq, lanes)
+            late = (across_cells, relayed_cells)
+            raw = dot(stacked(late, 0, seq, lanes), query, 1, 1)
+            late_up = dot(stacked(late, 1, seq, lanes), grad, 1, 1)
+            late_scores = [
+                raw[starts[i] - early_rows : starts[i + 1] - early_rows] * (scale * LOG2E) + step * float(runs[i][0])
+                for i in range(len(runs))
+                if starts[i] >= early_rows
+            ]
+            scores = jnp.concatenate([early[0][at], early[2][at], *late_scores], axis=0)
+            upstream = jnp.concatenate([early[1][at], early[3][at], late_up], axis=0)
             weights = jnp.exp2(scores - jnp.max(scores, axis=0, keepdims=True))
             probs = weights * (1.0 / jnp.sum(weights, axis=0, keepdims=True))
             probs_low = probs.astype(BF16)
             delta = jnp.sum(probs_low.astype(F32) * upstream, axis=0, keepdims=True)
             dscore = probs * (upstream - delta)
-            for i in range(count):
-                if levels_of[i]:
+            for i, (level, _) in enumerate(runs):
+                if level:
                     part = jnp.sum(dscore[starts[i] : starts[i + 1]], axis=0, keepdims=True)
-                    slope_sum = slope_sum + part * float(levels_of[i])
+                    slope_sum = slope_sum + part * float(level)
             dscore_low = dscore.astype(BF16)
-            dv = dot(probs_low, grad)
-            dk = dot(dscore_low, query) * scale
-            dq = (dot(dscore_low, keys, 0, 0) * scale).astype(BF16)
+            dscore_out[at] = dscore_low
+            probs_out[at] = probs_low[:token_rows]
+            dk = dot(dscore_low[token_rows:], query) * scale
+            dv = dot(probs_low[token_rows:], grad)
+            for kind, direct in enumerate((dk, dv)):
+                parts = [direct[starts[i] - token_rows : starts[i + 1] - token_rows] for i in range(1, len(runs))]
+                group = (kind * seqs + seq) * heads + h
+                near[kind, seq, :, lanes] = parts[0]
+                side[pl.ds(group * (block // 2), block // 2), :] = parts[1].astype(BF16)
+                across[kind, seq, :, lanes] = parts[2 + far_count].astype(BF16)
+                for i, size in enumerate(far_sizes):
+                    here = pl.ds(slabs[i] + group * size, size)
+                    far[here, :] = parts[2 + i]
+                    relay[here, :] = parts[3 + far_count + i].astype(BF16)
+        slope_out[h : h + 1, :] = slope_sum
+    relay[pl.ds(far.shape[0], 2 * heads), :] = two_parts(slope_out[...])
+
+
+def own_grads_body(head, dscore, probs, qg_own, qg_other, *refs):
+    *pieces, dq_own, dq_send, own, other = refs
+    seqs, block, width = qg_own.shape[1:]
+    heads = width // head
+    scale = 1.0 / math.sqrt(head)
+    for h in range(heads):
+        lanes = slice(h * head, (h + 1) * head)
+        for seq in range(seqs):
+            at = seq * heads + h
+            dq = (dot(dscore[at], stacked(pieces, 0, seq, lanes), 0, 0) * scale).astype(BF16)
             dq_own[seq, :, lanes] = dq[:block]
             dq_send[seq, :, lanes] = dq[block:]
+            dk = dot(dscore[at, : 2 * block], stacked((qg_own, qg_other), 0, seq, lanes)) * scale
+            dv = dot(probs[at], stacked((qg_own, qg_other), 1, seq, lanes))
             for kind, direct in enumerate((dk, dv)):
-                parts = [direct[starts[i] : starts[i + 1]] for i in range(count)]
-                own[kind, seq, :, lanes] = parts[0]
-                other[kind, seq, :, lanes] = parts[1]
-                near[kind, seq, :, lanes] = parts[2]
-                group = (kind * seqs + seq) * heads + h
-                side[pl.ds(group * sizes[3], sizes[3]), :] = parts[3].astype(BF16)
-                across[kind, seq, :, lanes] = parts[4].astype(BF16)
-                for i in range(far_count):
-                    at = pl.ds(slabs[i] + group * sizes[5 + i], sizes[5 + i])
-                    far[at, :] = parts[5 + i]
-                    relay[at, :] = parts[5 + far_count + i].astype(BF16)
-        slope_out[h : h + 1, :] = slope_sum
-    relay[pl.ds(far.shape[0], 2 * heads), :] = two_parts(slope_out[...])
-
-
-def fold_body(direct, coarse, out):
+                own[kind, seq, :, lanes] = direct[:block]
+                other[kind, seq, :, lanes] = direct[block:]
+
+
+def fold_body(direct, coarse, slope, *refs):
+    *slopes, out, slope_out = refs
+    total = slope[...]
+    for ref in slopes:
+        total = total + ref[...]
+    slope_out[...] = total
     rows = direct.shape[2]
     for kind in range(direct.shape[0]):
         for seq in range(direct.shape[1]):
@@ -178,15 +233,9 @@
             out[kind, seq] = (direct[kind, seq] + spread).astype(BF16)
 
 
-def relay_body(side, far, back, slope, *refs):
-    heads = slope.shape[0]
-    tail = 2 * heads
-    slopes = [ref for ref in refs if ref.shape == slope.shape]
-    others, slope_out = slopes[:-1], slopes[-1]
-    side_out, *far_outs = [ref for ref in refs if ref.shape != slope.shape]
+def relay_body(side, far, back, slope, slope_out, side_out, *far_outs):
+    tail = 2 * slope.shape[0]
     total = slope[...] + one_part(back[pl.ds(far.shape[0], tail), :])
-    for ref in others:
-        total = total + ref[...]
     slope_out[...] = total
     ending = two_parts(total)
     rows = side.shape[0]
@@ -229,13 +278,18 @@
     copy_all([(other, out.at[:, :, theirs]), (own, out.at[:, :, mine])], sems)
 
 
-def join_pair_body(core, own, other, first, second, sems):
+def join_pair_body(core, own, other, slope, slope_other, first, second, slope_out, sems):
     mine, theirs = head_halves(core, own.shape[-1])
     moves = []
     for index, out in enumerate((first, second)):
         moves.append((other.at[index], out.at[:, :, theirs]))
         moves.append((own.at[index], out.at[:, :, mine]))
     copy_all(moves, sems)
+    ours, rest = slope[...], slope_other[...]
+    lower = jnp.where(core[0] == 0, ours, rest)
+    upper = jnp.where(core[0] == 0, rest, ours)
+    terms = jnp.concatenate([lower, upper], axis=0)
+    slope_out[...] = jnp.sum(terms.T, axis=0, keepdims=True)
 
 
 def paired(queries, key_rows, value_rows, out_grad, level_slope):
@@ -269,52 +323,80 @@
     near_cells = swap(cells[0], 2)
     side_cells = swap(cells[1], 4)
     across_cells = swap(call(coarser_body, like(2, seqs, block // 2, half), (near_cells,), "coarser"), 4)
-    relayed_cells = [swap(c, 2) for c in far_cells]
-
-    pieces = [kv_own, kv_other, near_cells, side_cells, across_cells] + far_cells + relayed_cells
-    levels_of = [0, 0, 1, 2, 2] + far_levels * 2
-    rows = sum(p.shape[2] for p in pieces)
+    far_sizes = [2 * block >> level for level in far_levels]
+    far_stack = call(stack_body, like(2, seqs, sum(far_sizes), half), far_cells, "stack")
+    relayed_cells = swap(far_stack, 2)
+
     groups = seqs * heads
-    far_rows = [groups * (2 * block >> level) for level in far_levels]
+    early_levels, late_levels = (0, 0), (1, 2, *far_levels)
+    token_rows, cell_rows = 2 * block, block + block // 2 + sum(far_sizes)
+    rows = token_rows + cell_rows + block // 2 + sum(far_sizes)
+
+    def score(levels_of, pieces, count):
+        product = like(groups // 2, count, token_rows, dtype=F32)
+        return call(
+            functools.partial(score_body, levels_of, head),
+            (product, product),
+            (core, level_slope, qg_own, qg_other, *pieces),
+            "scores",
+            scalars=2,
+            flops=40 * seqs * token_rows * count * half,
+        )
+
+    token_pieces = [kv_own, kv_other]
+    cell_pieces = [near_cells, side_cells, *far_cells]
+    early = (*score(early_levels, token_pieces, token_rows), *score(late_levels, cell_pieces, cell_rows))
+    runs = [(0, token_rows), (1, block), (2, block // 2), *zip(far_levels, far_sizes)]
+    runs += [(2, block // 2), *zip(far_levels, far_sizes)]
+    far_rows = [groups * size for size in far_sizes]
     tail = heads
-    slope_part = like(heads // 2, 2 * block, dtype=F32)
-    dq_part = like(seqs, block, half)
-    dq_own, dq_send, slope, own, other, near, across, side, far_direct, relay = call(
-        functools.partial(attend_body, tuple(levels_of), head),
+    slope_part = like(heads // 2, token_rows, dtype=F32)
+    wide = like(*part.shape, dtype=F32)
+    slope, near, across, side, far_direct, relay, dscore, probs = call(
+        functools.partial(attend_body, tuple(runs), head, tuple(far_sizes)),
         (
-            dq_part,
-            dq_part,
             slope_part,
-            like(*part.shape, dtype=F32),
-            like(*part.shape, dtype=F32),
-            like(*part.shape, dtype=F32),
+            wide,
             like(2, seqs, block // 2, half),
             like(groups * (block // 2), head),
             like(sum(far_rows), head, dtype=F32),
             like(sum(far_rows) + tail, head),
+            like(groups // 2, rows, token_rows),
+            like(groups // 2, token_rows, token_rows),
         ),
-        (core, level_slope, qg_own, qg_other, *pieces),
+        (core, level_slope, *early, qg_own, qg_other, across_cells, relayed_cells),
         "attend",
         scalars=2,
-        flops=10 * seqs * 2 * block * rows * half,
+        flops=40 * seqs * token_rows * rows * half,
+    )
+    dq_part = like(seqs, block, half)
+    dq_own, dq_send, own, other = call(
+        functools.partial(own_grads_body, head),
+        (dq_part, dq_part, wide, wide),
+        (dscore, probs, qg_own, qg_other, *token_pieces, *cell_pieces, across_cells, relayed_cells),
+        "own_grads",
+        flops=40 * seqs * token_rows * rows * half,
     )
 
     across_back = swap(across, 4)
     relay_back = swap(relay, 2)
     slopes = [swap(slope, 2 * y, dp) for dp in range(1, dp_count) for y in range(2)]
     dq_other = swap(dq_send, 1)
-    near_back = swap(call(fold_body, like(*near.shape), (near, across_back), "fold"), 2)
+    near_total, slope = call(
+        fold_body, (like(*near.shape), slope_part), (near, across_back, slope, *slopes), "fold"
+    )
+    near_back = swap(near_total, 2)
     slope, side_total, *far_total = call(
         relay_body,
         (slope_part, like(side.shape[0] + tail, head)) + tuple(like(r + tail, head) for r in far_rows),
-        (side, far_direct, relay_back, slope, *slopes),
+        (side, far_direct, relay_back, slope),
         "relay",
     )
     side_back = swap(side_total, 4)
     far_back = [swap(message, 2 * m) for m, message in zip(far, far_total)]
     whole = like(seqs, block, width)
-    dq = call(
-        join_body, whole, (core, dq_own, dq_other), "join_queries", scalars=1, hbm_out=True, copies=2
+    (dq,) = call(
+        join_body, (whole,), (core, dq_own, dq_other), "join_queries", scalars=1, hbm_out=1, copies=2
     )
     kept, sent, slope = call(
         functools.partial(gather_body, (1, 2, *far_levels)),
@@ -324,12 +406,16 @@
     )
     kv_grad_other = swap(sent, 1)
     slope_other = swap(slope, 1)
-    dk, dv = call(
-        join_pair_body, (whole, whole), (core, kept, kv_grad_other), "join_kv", scalars=1, hbm_out=True, copies=4
-    )
-    ours, rest = jnp.sum(slope, axis=1), jnp.sum(slope_other, axis=1)
-    slope_grad = jnp.concatenate([jnp.where(core == 0, ours, rest), jnp.where(core == 0, rest, ours)])
-    return dq, dk, dv, slope_grad
+    dk, dv, slope_grad = call(
+        join_pair_body,
+        (whole, whole, like(1, heads, dtype=F32)),
+        (core, kept, kv_grad_other, slope, slope_other),
+        "join_kv",
+        scalars=1,
+        hbm_out=2,
+        copies=4,
+    )
+    return dq, dk, dv, slope_grad.reshape(heads)
 
 
 def as_sent(x):

time: 70.1 us -> 66.4 us (0.947)
  waiting for transfers between devices: 33.3 us -> 30.3 us
  Pallas kernels: 11.5 us -> 14.2 us
  starting transfers between devices: 21.4 us -> 18.8 us
  other arithmetic: 0.83 us -> 0 us
    ppermute x18 -> x17, waiting for transfers between devices: 30.2 us -> 27.2 us  [swap(): lax.ppermute(value, 'ctx', [(source, source ^ apart) for source in range(...]
    pallas_call x10 -> x14, Pallas kernels: 11.5 us -> 14.2 us  [call(): pl.pallas_call(body, out_shape=out_shape, in_specs=[SMEM] * scalars + [HB...]
    ppermute x18 -> x17, starting transfers between devices: 18.3 us -> 16.9 us  [swap(): lax.ppermute(value, 'ctx', [(source, source ^ apart) for source in range(...]
    ppermute x2, starting transfers between devices: 3.05 us -> 1.97 us  [swap(): return lax.ppermute(value, ('dp', 'ctx'), pairs)]
  transfers between devices with their start and end apart: 20 -> 19, of which waited for: 12 -> 11; matrix products, arithmetic and copies ran while one was open for 1% -> 0% of each run, Pallas kernels for 3% -> 8%
where the time goes in v3:
time: 66.4 us; the launch traced here: 66.2 us
  waiting for transfers between devices  30.3 us (46%)
  starting transfers between devices  18.8 us (28%)
  Pallas kernels  14.2 us (21%)
  local copies, waits for them, and re-layouts  2.09 us (3%)
  between operations  0.8 us (1%)
    ppermute x17, waiting for transfers between devices, swap(): lax.ppermute(value, 'ctx', [(source, source ^ apart) for source in range(...  27.2 us
    ppermute x17, starting transfers between devices, swap(): lax.ppermute(value, 'ctx', [(source, source ^ apart) for source in range(...  16.9 us
    pallas_call x14, Pallas kernels, call(): pl.pallas_call(body, out_shape=out_shape, in_specs=[SMEM] * scalars + [HB...  14.2 us
    ppermute x2, waiting for transfers between devices, swap(): return lax.ppermute(value, ('dp', 'ctx'), pairs)  3.08 us
    unnamed x10, local copies, waits for them, and re-layouts  2.09 us
    ppermute x2, starting transfers between devices, swap(): return lax.ppermute(value, ('dp', 'ctx'), pairs)  1.97 us
  transfers between devices with their start and end apart: 19, of which 11 were waited for; matrix products, arithmetic and copies ran while one was open for 0% of the time, Pallas kernels for 8%

profile of v3, /device:TPU:0, one launch (start us, length us, event | category | flops | bytes accessed | tf_op | source)
XLA Modules:
  0.0 66.2 jit_solution(10983805007116543756)
XLA Ops:
  0.7 1.0 %copy-done = bf16[2,64,2048]{2,1,0:T(8,128)(2,1)S(1)} copy-done((bf16[2,64,2048]{2,1,0:T(8,128)(2,1)S(1)}, bf16[2,64,2048]{2,1,0:T(8,128)(2,1)}, u32[]{:S(2)}) %copy-start) | copy-done | bytes 524312
  1.7 1.0 %copy-done.1 = bf16[2,64,2048]{2,1,0:T(8,128)(2,1)S(1)} copy-done((bf16[2,64,2048]{2,1,0:T(8,128)(2,1)S(1)}, bf16[2,64,2048]{2,1,0:T(8,128)(2,1)}, u32[]{:S(2)}) %copy-start.1) | copy-done | bytes 524312
  2.7 0.1 split_kv.1
  2.9 0.5 collective-permute-start.1
  3.4 1.5 %collective-permute-done.1.refs_1_.other = bf16[2,2,64,1024]{3,2,1,0:T(8,128)(2,1)S(1)} collective-permute-done((bf16[2,2,64,1024]{3,2,1,0:T(8,128)(2,1)S(1)}, bf16[2,2,64,1024]{3,2,1,0:T(8,128)(2,1)S(1)}, u32[]{:S(2)}, u32[]{:S(2)}) %collective-permute-start.1) | collective-permute-done | bytes 524320 | tf_op jit(solution)/shard_map/ppermute | solution.py:21
  4.9 1.3 %summaries.1 = (bf16[2,2,64,1024]{3,2,1,0:T(8,128)(2,1)S(1)}, bf16[2,2,32,1024]{3,2,1,0:T(8,128)(2,1)S(1)}, bf16[2,2,16,1024]{3,2,1,0:T(8,128)(2,1)S(1)}) custom-call(bf16[2,2,64,1024]{3,2,1,0:T(8,128)(2,1)S(1)} %get-tuple-element.41.refs_0_.own, bf16[2,2,64,1024]{3,2,1,0:T(8,128)(2,1)S(1)} %collective-permute-done.1.refs_1_.other), custom_call_target="tpu_custom_call" | custom-call | bytes 1966080 | tf_op jit(solution)/shard_map/summaries/pallas_call | solution.py:34
  6.2 2.9 %collective-permute-start.2 = (bf16[2,2,64,1024]{3,2,1,0:T(8,128)(2,1)S(1)}, bf16[2,2,64,1024]{3,2,1,0:T(8,128)(2,1)S(1)}, u32[]{:S(2)}, u32[]{:S(2)}) collective-permute-start(bf16[2,2,64,1024]{3,2,1,0:T(8,128)(2,1)S(1)} %get-tuple-element.45), channel_id=1, source_target_pairs={{0,2},{1,3},{2,0},{3,1},{4,6},{5,7},{6,4},{7,5},{8,10},{9,11},{10,... | collective-permute-start | bytes 1572872 | tf_op jit(solution)/shard_map/ppermute | solution.py:21
  9.2 0.1 split_qg.1
  9.3 0.1 collective-permute-start
  9.4 3.7 %collective-permute-start.5 = (bf16[2,2,16,1024]{3,2,1,0:T(8,128)(2,1)S(1)}, bf16[2,2,16,1024]{3,2,1,0:T(8,128)(2,1)S(1)}, u32[]{:S(2)}, u32[]{:S(2)}) collective-permute-start(bf16[2,2,16,1024]{3,2,1,0:T(8,128)(2,1)S(1)} %get-tuple-element.47), channel_id=1, source_target_pairs={{0,12},{1,13},{2,14},{3,15},{4,8},{5,9},{6,10},{7,11},{8,4},{9,5},... | collective-permute-start | bytes 393224 | tf_op jit(solution)/shard_map/ppermute | solution.py:21
  13.0 0.0 collective-permute-start.4
  13.0 0.8 %collective-permute-start.3 = (bf16[2,2,32,1024]{3,2,1,0:T(8,128)(2,1)S(1)}, bf16[2,2,32,1024]{3,2,1,0:T(8,128)(2,1)S(1)}, u32[]{:S(2)}, u32[]{:S(2)}) collective-permute-start(bf16[2,2,32,1024]{3,2,1,0:T(8,128)(2,1)S(1)} %get-tuple-element.46), channel_id=1, source_target_pairs={{0,4},{1,5},{2,6},{3,7},{4,0},{5,1},{6,2},{7,3},{8,12},{9,13},{10,... | collective-permute-start | bytes 786440 | tf_op jit(solution)/shard_map/ppermute | solution.py:21
  13.8 3.8 %collective-permute-done.5.refs_3_.refs_1_.refs_5_ = bf16[2,2,16,1024]{3,2,1,0:T(8,128)(2,1)S(1)} collective-permute-done((bf16[2,2,16,1024]{3,2,1,0:T(8,128)(2,1)S(1)}, bf16[2,2,16,1024]{3,2,1,0:T(8,128)(2,1)S(1)}, u32[]{:S(2)}, u32[]{:S(2)}) %collective-permute-start.5) | collective-permute-done | bytes 131104 | tf_op jit(solution)/shard_map/ppermute | solution.py:21
  17.6 7.2 %collective-permute-done.4.refs_2_.refs_0_.refs_4_ = bf16[2,2,16,1024]{3,2,1,0:T(8,128)(2,1)S(1)} collective-permute-done((bf16[2,2,16,1024]{3,2,1,0:T(8,128)(2,1)S(1)}, bf16[2,2,16,1024]{3,2,1,0:T(8,128)(2,1)S(1)}, u32[]{:S(2)}, u32[]{:S(2)}) %collective-permute-start.4) | collective-permute-done | bytes 131104 | tf_op jit(solution)/shard_map/ppermute | solution.py:21
  24.8 0.6 collective-permute-start.7
  25.4 0.0 collective-permute-done.2.refs_0_.cells.refs_2_
  25.4 0.2 coarser.1
  25.6 0.1 collective-permute-start.6
  25.7 1.4 %scores.2 = (f32[16,128,128]{2,1,0:T(8,128)S(1)}, f32[16,128,128]{2,1,0:T(8,128)S(1)}) custom-call(s32[1]{0:T(128)} %bitcast.core, f32[16]{0:T(128)S(1)} %copy-done.4, bf16[2,2,64,1024]{3,2,1,0:T(8,128)(2,1)S(1)} %get-tuple-element.39.qg_own.refs_4_, bf16[2,2,64,1024]{3,2,1,0:T(8,128)(2,1)S(1)} %collective-permute-done.qg_other.refs_5_, ...), custom_call_target="tpu_custom_call" | custom-call | flops 1342177280 | bytes 4194372 | tf_op jit(solution)/shard_map/scores/pallas_call | solution.py:34
  27.1 1.4 %scores.3 = (f32[16,128,128]{2,1,0:T(8,128)S(1)}, f32[16,128,128]{2,1,0:T(8,128)S(1)}) custom-call(s32[1]{0:T(128)} %bitcast.core, f32[16]{0:T(128)S(1)} %copy-done.4, bf16[2,2,64,1024]{3,2,1,0:T(8,128)(2,1)S(1)} %get-tuple-element.39.qg_own.refs_4_, bf16[2,2,64,1024]{3,2,1,0:T(8,128)(2,1)S(1)} %collective-permute-done.qg_other.refs_5_, ...), custom_call_target="tpu_custom_call" | custom-call | flops 1342177280 | bytes 4194372 | tf_op jit(solution)/shard_map/scores/pallas_call | solution.py:34
  28.5 4.2 %collective-permute-done.7.refs_7_ = bf16[2,2,32,1024]{3,2,1,0:T(8,128)(2,1)S(1)} collective-permute-done((bf16[2,2,32,1024]{3,2,1,0:T(8,128)(2,1)S(1)}, bf16[2,2,32,1024]{3,2,1,0:T(8,128)(2,1)S(1)}, u32[]{:S(2)}, u32[]{:S(2)}) %collective-permute-start.7) | collective-permute-done | bytes 262176 | tf_op jit(solution)/shard_map/ppermute | solution.py:21
  32.7 0.5 collective-permute-done.6.refs_6_
  33.2 5.4 %attend.1 = (f32[8,128]{1,0:T(8,128)S(1)}, f32[2,2,64,1024]{3,2,1,0:T(8,128)S(1)}, bf16[2,2,32,1024]{3,2,1,0:T(8,128)(2,1)S(1)}, bf16[1024,128]{1,0:T(8,128)(2,1...) custom-call(s32[1]{0:T(128)} %bitcast.core, ...), custom_call_target="tpu_custom_call" | custom-call | flops 3355443200 | bytes 9969732 | tf_op jit(solution)/shard_map/attend/pallas_call | solution.py:34
  38.6 0.4 collective-permute-start.10
  39.0 1.5 %collective-permute-start.9 = (bf16[1040,128]{1,0:T(8,128)(2,1)S(1)}, bf16[1040,128]{1,0:T(8,128)(2,1)S(1)}, u32[]{:S(2)}, u32[]{:S(2)}) collective-permute-start(bf16[1040,128]{1,0:T(8,128)(2,1)S(1)} %get-tuple-element.58), channel_id=1, source_target_pairs={{0,2},{1,3},{2,0},{3,1},{4,6},{5,7},{6,4},{7,5},{8,10},{9,11},{10,... | collective-permute-start | bytes 798728 | tf_op jit(solution)/shard_map/ppermute | solution.py:21
  40.5 1.4 %collective-permute-start.12 = (f32[8,128]{1,0:T(8,128)S(1)}, f32[8,128]{1,0:T(8,128)S(1)}, u32[]{:S(2)}, u32[]{:S(2)}) collective-permute-start(f32[8,128]{1,0:T(8,128)S(1)} %get-tuple-element.61.slope), channel_id=1, source_target_pairs={{0,18},{1,19},{2,16},{3,17},{4,22},{5,23},{6,20},{7,21},{8,26},{9,... | collective-permute-start | bytes 12296 | tf_op jit(solution)/shard_map/ppermute | solution.py:24
  41.9 0.5 collective-permute-start.11
  42.5 2.6 %collective-permute-done.12.refs_1_ = f32[8,128]{1,0:T(8,128)S(1)} collective-permute-done((f32[8,128]{1,0:T(8,128)S(1)}, f32[8,128]{1,0:T(8,128)S(1)}, u32[]{:S(2)}, u32[]{:S(2)}) %collective-permute-start.12) | collective-permute-done | bytes 4128 | tf_op jit(solution)/shard_map/ppermute | solution.py:24
  45.1 0.4 collective-permute-done.11.refs_0_
  45.6 0.3 fold.1
  45.8 1.6 %collective-permute-start.13 = (bf16[2,2,64,1024]{3,2,1,0:T(8,128)(2,1)S(1)}, bf16[2,2,64,1024]{3,2,1,0:T(8,128)(2,1)S(1)}, u32[]{:S(2)}, u32[]{:S(2)}) collective-permute-start(bf16[2,2,64,1024]{3,2,1,0:T(8,128)(2,1)S(1)} %get-tuple-element.64), channel_id=1, source_target_pairs={{0,2},{1,3},{2,0},{3,1},{4,6},{5,7},{6,4},{7,5},{8,10},{9,11},{10,... | collective-permute-start | bytes 1572872 | tf_op jit(solution)/shard_map/ppermute | solution.py:21
  47.4 0.1 relay.1
  47.5 2.8 %collective-permute-start.15 = (bf16[528,128]{1,0:T(8,128)(2,1)S(1)}, bf16[528,128]{1,0:T(8,128)(2,1)S(1)}, u32[]{:S(2)}, u32[]{:S(2)}) collective-permute-start(bf16[528,128]{1,0:T(8,128)(2,1)S(1)} %get-tuple-element.66), channel_id=1, source_target_pairs={{0,8},{1,9},{2,10},{3,11},{4,12},{5,13},{6,14},{7,15},{8,0},{9,1},... | collective-permute-start | bytes 405512 | tf_op jit(solution)/shard_map/ppermute | solution.py:21
  50.3 1.3 %collective-permute-start.16 = (bf16[528,128]{1,0:T(8,128)(2,1)S(1)}, bf16[528,128]{1,0:T(8,128)(2,1)S(1)}, u32[]{:S(2)}, u32[]{:S(2)}) collective-permute-start(bf16[528,128]{1,0:T(8,128)(2,1)S(1)} %get-tuple-element.67), channel_id=1, source_target_pairs={{0,12},{1,13},{2,14},{3,15},{4,8},{5,9},{6,10},{7,11},{8,4},{9,5},... | collective-permute-start | bytes 405512 | tf_op jit(solution)/shard_map/ppermute | solution.py:21
  51.7 0.9 %own_grads.1 = (bf16[2,64,1024]{2,1,0:T(8,128)(2,1)S(1)}, bf16[2,64,1024]{2,1,0:T(8,128)(2,1)S(1)}, f32[2,2,64,1024]{3,2,1,0:T(8,128)S(1)}, f32[2,2,64,1024]{3,2,1,0:T(8,128)S(1)}) custom-call(bf16[16,320,128]{2,1,0:T(8,128)(2,1)S(1)} %get-tuple-element.50.dscore, bf16[16,128,128]{2,1,0:T(8,128)(2,1)S(1)} %get-tuple-element.51.probs, ...), custom_call_target="tpu_custom_call" | custom-call | flops 3355443200 | bytes 8126464 | tf_op jit(solution)/shard_map/own_grads/pallas_call | solution.py:34
  52.6 4.6 %collective-permute-done.15.refs_1_ = bf16[528,128]{1,0:T(8,128)(2,1)S(1)} collective-permute-done((bf16[528,128]{1,0:T(8,128)(2,1)S(1)}, bf16[528,128]{1,0:T(8,128)(2,1)S(1)}, u32[]{:S(2)}, u32[]{:S(2)}) %collective-permute-start.15) | collective-permute-done | bytes 135200 | tf_op jit(solution)/shard_map/ppermute | solution.py:21
  57.2 1.0 %collective-permute-done.16.refs_2_ = bf16[528,128]{1,0:T(8,128)(2,1)S(1)} collective-permute-done((bf16[528,128]{1,0:T(8,128)(2,1)S(1)}, bf16[528,128]{1,0:T(8,128)(2,1)S(1)}, u32[]{:S(2)}, u32[]{:S(2)}) %collective-permute-start.16) | collective-permute-done | bytes 135200 | tf_op jit(solution)/shard_map/ppermute | solution.py:21
  58.3 2.6 %collective-permute-done.14.refs_0_ = bf16[1040,128]{1,0:T(8,128)(2,1)S(1)} collective-permute-done((bf16[1040,128]{1,0:T(8,128)(2,1)S(1)}, bf16[1040,128]{1,0:T(8,128)(2,1)S(1)}, u32[]{:S(2)}, u32[]{:S(2)}) %collective-permute-start.14) | collective-permute-done | bytes 266272 | tf_op jit(solution)/shard_map/ppermute | solution.py:21
  60.9 0.0 collective-permute-done.13.near
  60.9 0.5 gather_cells.1
  61.4 0.1 collective-permute-start.17
  61.5 0.5 collective-permute-start.8
  62.0 0.1 collective-permute-start.18
  62.1 1.7 %collective-permute-done.8.other = bf16[2,64,1024]{2,1,0:T(8,128)(2,1)S(1)} collective-permute-done((bf16[2,64,1024]{2,1,0:T(8,128)(2,1)S(1)}, bf16[2,64,1024]{2,1,0:T(8,128)(2,1)S(1)}, u32[]{:S(2)}, u32[]{:S(2)}) %collective-permute-start.8) | collective-permute-done | bytes 262176 | tf_op jit(solution)/shard_map/ppermute | solution.py:21
  63.8 0.8 %join_queries.1 = bf16[2,64,2048]{2,1,0:T(8,128)(2,1)} custom-call(s32[1]{0:T(128)} %bitcast.core, bf16[2,64,1024]{2,1,0:T(8,128)(2,1)S(1)} %get-tuple-element.52.own, bf16[2,64,1024]{2,1,0:T(8,128)(2,1)S(1)} %collective-permute-done.8.other), custom_call_target="tpu_custom_call" | custom-call | bytes 1048580 | tf_op jit(solution)/shard_map/join_queries/pallas_call | solution.py:34
  64.6 0.0 collective-permute-done.18.slope_other
  64.6 0.0 collective-permute-done.17.other
  64.6 1.6 %join_kv.1 = (bf16[2,64,2048]{2,1,0:T(8,128)(2,1)}, bf16[2,64,2048]{2,1,0:T(8,128)(2,1)}, f32[1,16]{1,0:T(1,128)}) custom-call(s32[1]{0:T(128)} %bitcast.core, bf16[2,2,64,1024]{3,2,1,0:T(8,128)(2,1)S(1)} %get-tuple-element.68.own, bf16[2,2,64,1024]{3,2,1,0:T(8,128)(2,1)S(1)} %collective-permute-done.17.other, f32[8,128]{1,0:T(8,128)S(1)} %get-tuple-element.70.slope, ...), custom_call_target="tpu_custom_call" | custom-call | bytes 2105412 | tf_op jit(solution)/shard_map/join_kv/pallas_call | solution.py:34
  (14 shorter events, 0.0 us)
Async XLA Ops:
  0.6 1.0 %copy-start = (bf16[2,64,2048]{2,1,0:T(8,128)(2,1)S(1)}, bf16[2,64,2048]{2,1,0:T(8,128)(2,1)}, u32[]{:S(2)}) copy-start(bf16[2,64,2048]{2,1,0:T(8,128)(2,1)} %first.3) | copy-start | bytes 1572868
  1.7 1.0 %copy-start.1 = (bf16[2,64,2048]{2,1,0:T(8,128)(2,1)S(1)}, bf16[2,64,2048]{2,1,0:T(8,128)(2,1)}, u32[]{:S(2)}) copy-start(bf16[2,64,2048]{2,1,0:T(8,128)(2,1)} %second.3) | copy-start | bytes 1572868
  2.7 6.4 %copy-start.2 = (bf16[2,64,2048]{2,1,0:T(8,128)(2,1)S(1)}, bf16[2,64,2048]{2,1,0:T(8,128)(2,1)}, u32[]{:S(2)}) copy-start(bf16[2,64,2048]{2,1,0:T(8,128)(2,1)} %first.2) | copy-start | bytes 1572868
  2.7 6.4 %copy-start.3 = (bf16[2,64,2048]{2,1,0:T(8,128)(2,1)S(1)}, bf16[2,64,2048]{2,1,0:T(8,128)(2,1)}, u32[]{:S(2)}) copy-start(bf16[2,64,2048]{2,1,0:T(8,128)(2,1)} %second.2) | copy-start | bytes 1572868
  2.9 2.1 %collective-permute-start.1 = (bf16[2,2,64,1024]{3,2,1,0:T(8,128)(2,1)S(1)}, bf16[2,2,64,1024]{3,2,1,0:T(8,128)(2,1)S(1)}, u32[]{:S(2)}, u32[]{:S(2)}) collective-permute-start(bf16[2,2,64,1024]{3,2,1,0:T(8,128)(2,1)S(1)} %get-tuple-element.42), channel_id=1, source_target_pairs={{0,1},{1,0},{2,3},{3,2},{4,5},{5,4},{6,7},{7,6},{8,9},{9,8},{10,11... | collective-permute-start | bytes 1572872 | tf_op jit(solution)/shard_map/ppermute | solution.py:21
  6.2 19.5 %copy-start.4 = (f32[16]{0:T(128)S(1)}, f32[16]{0:T(128)}, u32[]{:S(2)}) copy-start(f32[16]{0:T(128)} %slope.5) | copy-start | bytes 196
  6.2 19.2 %collective-permute-start.2 = (bf16[2,2,64,1024]{3,2,1,0:T(8,128)(2,1)S(1)}, bf16[2,2,64,1024]{3,2,1,0:T(8,128)(2,1)S(1)}, u32[]{:S(2)}, u32[]{:S(2)}) collective-permute-start(bf16[2,2,64,1024]{3,2,1,0:T(8,128)(2,1)S(1)} %get-tuple-element.45), channel_id=1, source_target_pairs={{0,2},{1,3},{2,0},{3,1},{4,6},{5,7},{6,4},{7,5},{8,10},{9,11},{10,... | collective-permute-start | bytes 1572872 | tf_op jit(solution)/shard_map/ppermute | solution.py:21
  9.3 16.4 %collective-permute-start = (bf16[2,2,64,1024]{3,2,1,0:T(8,128)(2,1)S(1)}, bf16[2,2,64,1024]{3,2,1,0:T(8,128)(2,1)S(1)}, u32[]{:S(2)}, u32[]{:S(2)}) collective-permute-start(bf16[2,2,64,1024]{3,2,1,0:T(8,128)(2,1)S(1)} %get-tuple-element.40), channel_id=1, source_target_pairs={{0,1},{1,0},{2,3},{3,2},{4,5},{5,4},{6,7},{7,6},{8,9},{9,8},{10,11... | collective-permute-start | bytes 1572872 | tf_op jit(solution)/shard_map/ppermute | solution.py:21
  9.4 8.3 %collective-permute-start.5 = (bf16[2,2,16,1024]{3,2,1,0:T(8,128)(2,1)S(1)}, bf16[2,2,16,1024]{3,2,1,0:T(8,128)(2,1)S(1)}, u32[]{:S(2)}, u32[]{:S(2)}) collective-permute-start(bf16[2,2,16,1024]{3,2,1,0:T(8,128)(2,1)S(1)} %get-tuple-element.47), channel_id=1, source_target_pairs={{0,12},{1,13},{2,14},{3,15},{4,8},{5,9},{6,10},{7,11},{8,4},{9,5},... | collective-permute-start | bytes 393224 | tf_op jit(solution)/shard_map/ppermute | solution.py:21
  13.0 11.8 %collective-permute-start.4 = (bf16[2,2,16,1024]{3,2,1,0:T(8,128)(2,1)S(1)}, bf16[2,2,16,1024]{3,2,1,0:T(8,128)(2,1)S(1)}, u32[]{:S(2)}, u32[]{:S(2)}) collective-permute-start(bf16[2,2,16,1024]{3,2,1,0:T(8,128)(2,1)S(1)} %get-tuple-element.47), channel_id=1, source_target_pairs={{0,8},{1,9},{2,10},{3,11},{4,12},{5,13},{6,14},{7,15},{8,0},{9,1},... | collective-permute-start | bytes 393224 | tf_op jit(solution)/shard_map/ppermute | solution.py:21
  13.0 14.1 %collective-permute-start.3 = (bf16[2,2,32,1024]{3,2,1,0:T(8,128)(2,1)S(1)}, bf16[2,2,32,1024]{3,2,1,0:T(8,128)(2,1)S(1)}, u32[]{:S(2)}, u32[]{:S(2)}) collective-permute-start(bf16[2,2,32,1024]{3,2,1,0:T(8,128)(2,1)S(1)} %get-tuple-element.46), channel_id=1, source_target_pairs={{0,4},{1,5},{2,6},{3,7},{4,0},{5,1},{6,2},{7,3},{8,12},{9,13},{10,... | collective-permute-start | bytes 786440 | tf_op jit(solution)/shard_map/ppermute | solution.py:21
  24.8 7.9 %collective-permute-start.7 = (bf16[2,2,32,1024]{3,2,1,0:T(8,128)(2,1)S(1)}, bf16[2,2,32,1024]{3,2,1,0:T(8,128)(2,1)S(1)}, u32[]{:S(2)}, u32[]{:S(2)}) collective-permute-start(bf16[2,2,32,1024]{3,2,1,0:T(8,128)(2,1)S(1)} %stack.1), channel_id=1, source_target_pairs={{0,2},{1,3},{2,0},{3,1},{4,6},{5,7},{6,4},{7,5},{8,10},{9,11},{10,... | collective-permute-start | bytes 786440 | tf_op jit(solution)/shard_map/ppermute | solution.py:21
  25.6 7.6 %collective-permute-start.6 = (bf16[2,2,32,1024]{3,2,1,0:T(8,128)(2,1)S(1)}, bf16[2,2,32,1024]{3,2,1,0:T(8,128)(2,1)S(1)}, u32[]{:S(2)}, u32[]{:S(2)}) collective-permute-start(bf16[2,2,32,1024]{3,2,1,0:T(8,128)(2,1)S(1)} %coarser.1), channel_id=1, source_target_pairs={{0,4},{1,5},{2,6},{3,7},{4,0},{5,1},{6,2},{7,3},{8,12},{9,13},{10,... | collective-permute-start | bytes 786440 | tf_op jit(solution)/shard_map/ppermute | solution.py:21
  38.6 6.9 %collective-permute-start.10 = (bf16[2,2,32,1024]{3,2,1,0:T(8,128)(2,1)S(1)}, bf16[2,2,32,1024]{3,2,1,0:T(8,128)(2,1)S(1)}, u32[]{:S(2)}, u32[]{:S(2)}) collective-permute-start(bf16[2,2,32,1024]{3,2,1,0:T(8,128)(2,1)S(1)} %get-tuple-element.60), channel_id=1, source_target_pairs={{0,4},{1,5},{2,6},{3,7},{4,0},{5,1},{6,2},{7,3},{8,12},{9,13},{10,... | collective-permute-start | bytes 786440 | tf_op jit(solution)/shard_map/ppermute | solution.py:21
  39.0 8.4 %collective-permute-start.9 = (bf16[1040,128]{1,0:T(8,128)(2,1)S(1)}, bf16[1040,128]{1,0:T(8,128)(2,1)S(1)}, u32[]{:S(2)}, u32[]{:S(2)}) collective-permute-start(bf16[1040,128]{1,0:T(8,128)(2,1)S(1)} %get-tuple-element.58), channel_id=1, source_target_pairs={{0,2},{1,3},{2,0},{3,1},{4,6},{5,7},{6,4},{7,5},{8,10},{9,11},{10,... | collective-permute-start | bytes 798728 | tf_op jit(solution)/shard_map/ppermute | solution.py:21
  40.5 4.6 %collective-permute-start.12 = (f32[8,128]{1,0:T(8,128)S(1)}, f32[8,128]{1,0:T(8,128)S(1)}, u32[]{:S(2)}, u32[]{:S(2)}) collective-permute-start(f32[8,128]{1,0:T(8,128)S(1)} %get-tuple-element.61.slope), channel_id=1, source_target_pairs={{0,18},{1,19},{2,16},{3,17},{4,22},{5,23},{6,20},{7,21},{8,26},{9,... | collective-permute-start | bytes 12296 | tf_op jit(solution)/shard_map/ppermute | solution.py:24
  41.9 3.6 %collective-permute-start.11 = (f32[8,128]{1,0:T(8,128)S(1)}, f32[8,128]{1,0:T(8,128)S(1)}, u32[]{:S(2)}, u32[]{:S(2)}) collective-permute-start(f32[8,128]{1,0:T(8,128)S(1)} %get-tuple-element.61.slope), channel_id=1, source_target_pairs={{0,16},{1,17},{2,18},{3,19},{4,20},{5,21},{6,22},{7,23},{8,24},{9,... | collective-permute-start | bytes 12296 | tf_op jit(solution)/shard_map/ppermute | solution.py:24
  45.8 15.0 %collective-permute-start.13 = (bf16[2,2,64,1024]{3,2,1,0:T(8,128)(2,1)S(1)}, bf16[2,2,64,1024]{3,2,1,0:T(8,128)(2,1)S(1)}, u32[]{:S(2)}, u32[]{:S(2)}) collective-permute-start(bf16[2,2,64,1024]{3,2,1,0:T(8,128)(2,1)S(1)} %get-tuple-element.64), channel_id=1, source_target_pairs={{0,2},{1,3},{2,0},{3,1},{4,6},{5,7},{6,4},{7,5},{8,10},{9,11},{10,... | collective-permute-start | bytes 1572872 | tf_op jit(solution)/shard_map/ppermute | solution.py:21
  47.5 9.7 %collective-permute-start.15 = (bf16[528,128]{1,0:T(8,128)(2,1)S(1)}, bf16[528,128]{1,0:T(8,128)(2,1)S(1)}, u32[]{:S(2)}, u32[]{:S(2)}) collective-permute-start(bf16[528,128]{1,0:T(8,128)(2,1)S(1)} %get-tuple-element.66), channel_id=1, source_target_pairs={{0,8},{1,9},{2,10},{3,11},{4,12},{5,13},{6,14},{7,15},{8,0},{9,1},... | collective-permute-start | bytes 405512 | tf_op jit(solution)/shard_map/ppermute | solution.py:21
  50.3 7.9 %collective-permute-start.16 = (bf16[528,128]{1,0:T(8,128)(2,1)S(1)}, bf16[528,128]{1,0:T(8,128)(2,1)S(1)}, u32[]{:S(2)}, u32[]{:S(2)}) collective-permute-start(bf16[528,128]{1,0:T(8,128)(2,1)S(1)} %get-tuple-element.67), channel_id=1, source_target_pairs={{0,12},{1,13},{2,14},{3,15},{4,8},{5,9},{6,10},{7,11},{8,4},{9,5},... | collective-permute-start | bytes 405512 | tf_op jit(solution)/shard_map/ppermute | solution.py:21
  51.7 9.2 %collective-permute-start.14 = (bf16[1040,128]{1,0:T(8,128)(2,1)S(1)}, bf16[1040,128]{1,0:T(8,128)(2,1)S(1)}, u32[]{:S(2)}, u32[]{:S(2)}) collective-permute-start(bf16[1040,128]{1,0:T(8,128)(2,1)S(1)} %get-tuple-element.65), channel_id=1, source_target_pairs={{0,4},{1,5},{2,6},{3,7},{4,0},{5,1},{6,2},{7,3},{8,12},{9,13},{10,... | collective-permute-start | bytes 798728 | tf_op jit(solution)/shard_map/ppermute | solution.py:21
  61.4 3.2 %collective-permute-start.17 = (bf16[2,2,64,1024]{3,2,1,0:T(8,128)(2,1)S(1)}, bf16[2,2,64,1024]{3,2,1,0:T(8,128)(2,1)S(1)}, u32[]{:S(2)}, u32[]{:S(2)}) collective-permute-start(bf16[2,2,64,1024]{3,2,1,0:T(8,128)(2,1)S(1)} %get-tuple-element.69), channel_id=1, source_target_pairs={{0,1},{1,0},{2,3},{3,2},{4,5},{5,4},{6,7},{7,6},{8,9},{9,8},{10,11... | collective-permute-start | bytes 1572872 | tf_op jit(solution)/shard_map/ppermute | solution.py:21
  61.5 2.3 %collective-permute-start.8 = (bf16[2,64,1024]{2,1,0:T(8,128)(2,1)S(1)}, bf16[2,64,1024]{2,1,0:T(8,128)(2,1)S(1)}, u32[]{:S(2)}, u32[]{:S(2)}) collective-permute-start(bf16[2,64,1024]{2,1,0:T(8,128)(2,1)S(1)} %get-tuple-element.53), channel_id=1, source_target_pairs={{0,1},{1,0},{2,3},{3,2},{4,5},{5,4},{6,7},{7,6},{8,9},{9,8},{10,11... | collective-permute-start | bytes 786440 | tf_op jit(solution)/shard_map/ppermute | solution.py:21
  62.0 2.6 %collective-permute-start.18 = (f32[8,128]{1,0:T(8,128)S(1)}, f32[8,128]{1,0:T(8,128)S(1)}, u32[]{:S(2)}, u32[]{:S(2)}) collective-permute-start(f32[8,128]{1,0:T(8,128)S(1)} %get-tuple-element.70.slope), channel_id=1, source_target_pairs={{0,1},{1,0},{2,3},{3,2},{4,5},{5,4},{6,7},{7,6},{8,9},{9,8},{10,11... | collective-permute-start | bytes 12296 | tf_op jit(solution)/shard_map/ppermute | solution.py:21

commit v4 on v3

--- a/solution.py
+++ b/solution.py
@@ -28,7 +28,7 @@
     return jax.ShapeDtypeStruct(shape, dtype)
 
 
-def call(body, out_shape, operands, name, scalars=0, hbm_in=0, hbm_out=0, copies=0, flops=0, limit=32):
+def call(body, out_shape, operands, name, scalars=0, hbm_in=0, hbm_out=0, copies=0, flops=0, limit=32, scratch=()):
     moved = sum(a.size * a.dtype.itemsize for a in jax.tree.leaves((operands, out_shape)))
     count = len(operands) - scalars - hbm_in
     return pl.pallas_call(
@@ -38,8 +38,8 @@
         out_specs=tuple(HBM if i < hbm_out else VMEM for i in range(len(out_shape)))
         if isinstance(out_shape, tuple)
         else VMEM,
-        scratch_shapes=[pltpu.SemaphoreType.DMA((copies,))] if copies else [],
-        compiler_params=pltpu.CompilerParams(vmem_limit_bytes=limit * 2**20),
+        scratch_shapes=[*scratch, *([pltpu.SemaphoreType.DMA((copies,))] if copies else [])],
+        compiler_params=pltpu.CompilerParams(vmem_limit_bytes=int(limit * 2**20)),
         cost_estimate=pl.CostEstimate(flops=flops, bytes_accessed=moved, transcendentals=0),
         name=name,
     )(*operands)
@@ -78,11 +78,15 @@
     return mine, theirs
 
 
-def copy_all(moves, sems):
+def start_all(moves, sems):
     copies = [pltpu.make_async_copy(src, dst, sems.at[i]) for i, (src, dst) in enumerate(moves)]
     for copy in copies:
         copy.start()
-    for copy in copies:
+    return copies
+
+
+def copy_all(moves, sems):
+    for copy in start_all(moves, sems):
         copy.wait()
 
 
@@ -95,13 +99,48 @@
     copy_all(moves, sems)
 
 
-def summary_body(own, other, *cells):
-    for kind in range(own.shape[0]):
-        for seq in range(own.shape[1]):
-            rows = jnp.concatenate([own[kind, seq], other[kind, seq]], axis=0)
-            for out in cells:
-                rows = dot(pair_matrix(rows.shape[0] // 2), rows).astype(BF16)
-                out[kind, seq] = rows
+def keep_body(core, k, v, k_other, v_other, own, other):
+    mine, _ = head_halves(core, own.shape[-1])
+    for index, (first, second) in enumerate(((k, k_other), (v, v_other))):
+        own[index] = first[:, :, mine]
+        other[index] = second[:, :, mine]
+
+
+def halve(rows, wide):
+    count = rows.shape[0]
+    wide[pl.ds(0, count), :] = rows
+    return (wide[pl.ds(0, count // 2, stride=2), :] + wide[pl.ds(1, count // 2, stride=2), :]) * 0.5
+
+
+def tiles_of(shape, core, wide):
+    kinds, seqs, _, half = shape
+    for kind in range(kinds):
+        for seq in range(seqs):
+            for start in range(0, half, 128):
+                source = pl.ds(pl.multiple_of(core[0] * half + start, 128), 128)
+                yield kind, seq, source, slice(start, start + 128), wide.at[kind, seq, start // 128]
+
+
+def own_summary_body(core, k, v, *refs):
+    *cells, wide = refs
+    for kind, seq, source, lanes, scratch in tiles_of(cells[0].shape, core, wide):
+        rows = (k, v)[kind][seq, :, source].astype(F32)
+        for out in cells:
+            rows = halve(rows, scratch)
+            out[kind, seq, :, lanes] = jnp.concatenate([rows, jnp.zeros_like(rows)], axis=0).astype(BF16)
+            rows = rows.astype(BF16).astype(F32)
+
+
+def summary_body(core, k_other, v_other, *refs):
+    *refs, wide = refs
+    own, cells = refs[: len(refs) // 2], refs[len(refs) // 2 :]
+    for kind, seq, source, lanes, scratch in tiles_of(cells[0].shape, core, wide):
+        rows = (k_other, v_other)[kind][seq, :, source].astype(F32)
+        for first, out in zip(own, cells):
+            rows = halve(rows, scratch)
+            before = first[kind, seq, :, lanes].astype(F32)[: rows.shape[0]]
+            out[kind, seq, :, lanes] = jnp.concatenate([before, rows], axis=0).astype(BF16)
+            rows = rows.astype(BF16).astype(F32)
 
 
 def coarser_body(cells, out):
@@ -111,21 +150,12 @@
             out[kind, seq] = dot(pair_matrix(rows.shape[0] // 2), rows).astype(BF16)
 
 
-def stack_body(*refs):
-    *parts, out = refs
-    start = 0
-    for part in parts:
-        rows = part.shape[2]
-        out[:, :, pl.ds(start, rows), :] = part[...]
-        start += rows
-
-
 def stacked(parts, kind, seq, lanes):
     return jnp.concatenate([part[kind, seq, :, lanes] for part in parts], axis=0)
 
 
 def score_body(levels_of, head, core, slope, qg_own, qg_other, *refs):
-    *pieces, scores, upstream = refs
+    *pieces, weights, upstream, stats = refs
     seqs, width = qg_own.shape[1], qg_own.shape[3]
     heads = width // head
     scale = LOG2E / math.sqrt(head)
@@ -133,71 +163,101 @@
         lanes = slice(h * head, (h + 1) * head)
         step = slope[core[0] * heads + h] * LOG2E + 1.0
         for seq in range(seqs):
+            at = seq * heads + h
             raw = dot(stacked(pieces, 0, seq, lanes), stacked((qg_own, qg_other), 0, seq, lanes), 1, 1)
-            start = 0
-            for piece, level in zip(pieces, levels_of):
-                here = slice(start, start + piece.shape[2])
-                scores[seq * heads + h, here] = raw[here] * scale + step * float(level)
-                start += piece.shape[2]
-            upstream[seq * heads + h] = dot(
-                stacked(pieces, 1, seq, lanes), stacked((qg_own, qg_other), 1, seq, lanes), 1, 1
-            )
+            upstream[at] = dot(stacked(pieces, 1, seq, lanes), stacked((qg_own, qg_other), 1, seq, lanes), 1, 1)
+            scores = with_bias(raw * scale, zip(levels_of, [piece.shape[2] for piece in pieces]), step)
+            top = jnp.max(scores, axis=0, keepdims=True)
+            spread = jnp.exp2(scores - top)
+            weights[at] = spread
+            stats[at, 0:1] = top
+            stats[at, 1:2] = jnp.sum(spread, axis=0, keepdims=True)
+
+
+def with_bias(scores, runs, step):
+    parts, start = [], 0
+    for level, count in runs:
+        part = scores[start : start + count]
+        parts.append(part + step * float(level) if level else part)
+        start += count
+    return jnp.concatenate(parts, axis=0)
 
 
 def attend_body(runs, head, far_sizes, core, slope, *refs):
-    early, (qg_own, qg_other, across_cells, relayed_cells), outs = refs[:4], refs[4:8], refs[8:]
+    *refs, late_scores, late_up, probs_cells = refs
+    early, (qg_own, qg_other, *late), outs = refs[:6], refs[6:-8], refs[-8:]
     slope_out, near, across, side, far, relay, dscore_out, probs_out = outs
     seqs, block, width = qg_own.shape[1:]
     heads = width // head
     scale = 1.0 / math.sqrt(head)
-    token_rows = 2 * block
-    early_rows = early[0].shape[1] + early[2].shape[1]
     starts = [sum(rows for _, rows in runs[:i]) for i in range(len(runs) + 1)]
+    token_rows = early[0].shape[1]
+    early_rows = token_rows + early[3].shape[1]
+    bounds = (0, token_rows, early_rows, starts[-1])
+    late_runs = [run for run, start in zip(runs, starts) if start >= early_rows]
     far_count = len(far_sizes)
     slabs = [2 * seqs * heads * sum(far_sizes[:i]) for i in range(far_count)]
+
+    def score(h, seq):
+        at, lanes = seq * heads + h, slice(h * head, (h + 1) * head)
+        step = slope[core[0] * heads + h] * LOG2E + 1.0
+        raw = dot(stacked(late, 0, seq, lanes), stacked((qg_own, qg_other), 0, seq, lanes), 1, 1)
+        late_scores[at] = with_bias(raw * (scale * LOG2E), late_runs, step)
+        late_up[at] = dot(stacked(late, 1, seq, lanes), stacked((qg_own, qg_other), 1, seq, lanes), 1, 1)
+
+    def normalise(h, seq):
+        at = seq * heads + h
+        tops = early[2][at, 0:1], early[5][at, 0:1]
+        scores = late_scores[at]
+        top = jnp.maximum(jnp.maximum(*tops), jnp.max(scores, axis=0, keepdims=True))
+        shares = [jnp.exp2(part - top) for part in tops]
+        weights = jnp.exp2(scores - top)
+        total = early[2][at, 1:2] * shares[0] + early[5][at, 1:2] * shares[1]
+        inverse = 1.0 / (total + jnp.sum(weights, axis=0, keepdims=True))
+        probs = [early[0][at] * (shares[0] * inverse), early[3][at] * (shares[1] * inverse), weights * inverse]
+        upstream = [early[1][at], early[4][at], late_up[at]]
+        probs_low = [part.astype(BF16) for part in probs]
+        delta = sum(jnp.sum(p.astype(F32) * u, axis=0, keepdims=True) for p, u in zip(probs_low, upstream))
+        slope_sum = jnp.zeros_like(delta)
+        for p, u, low, high in zip(probs, upstream, bounds, bounds[1:]):
+            dscore = p * (u - delta)
+            for (level, rows), start in zip(runs, starts):
+                if level and low <= start < high:
+                    here = dscore[start - low : start - low + rows]
+                    slope_sum = slope_sum + jnp.sum(here, axis=0, keepdims=True) * float(level)
+            dscore_out[at, low:high] = dscore.astype(BF16)
+        probs_out[at] = probs_low[0]
+        probs_cells[at] = jnp.concatenate(probs_low[1:], axis=0)
+        return slope_sum
+
+    def gradients(h, seq):
+        at, lanes = seq * heads + h, slice(h * head, (h + 1) * head)
+        dk = dot(dscore_out[at, token_rows:], stacked((qg_own, qg_other), 0, seq, lanes)) * scale
+        dv = dot(probs_cells[at], stacked((qg_own, qg_other), 1, seq, lanes))
+        for kind, direct in enumerate((dk, dv)):
+            parts = [direct[starts[i] - token_rows : starts[i + 1] - token_rows] for i in range(1, len(runs))]
+            group = (kind * seqs + seq) * heads + h
+            near[kind, seq, :, lanes] = parts[0]
+            side[pl.ds(group * (block // 2), block // 2), :] = parts[1].astype(BF16)
+            across[kind, seq, :, lanes] = parts[2 + far_count].astype(BF16)
+            for i, size in enumerate(far_sizes):
+                here = pl.ds(slabs[i] + group * size, size)
+                far[here, :] = parts[2 + i]
+                relay[here, :] = parts[3 + far_count + i].astype(BF16)
+
+    items = [(h, seq) for h in range(heads) for seq in range(seqs)]
+    behind = 2
+    sums = {}
+    for i in range(len(items) + 2 * behind):
+        if i < len(items):
+            score(*items[i])
+        if 0 <= i - behind < len(items):
+            item = items[i - behind]
+            sums[item] = normalise(*item)
+        if 0 <= i - 2 * behind < len(items):
+            gradients(*items[i - 2 * behind])
     for h in range(heads):
-        lanes = slice(h * head, (h + 1) * head)
-        step = slope[core[0] * heads + h] * LOG2E + 1.0
-        slope_sum = jnp.zeros((1, token_rows), F32)
-        for seq in range(seqs):
-            at = seq * heads + h
-            query = stacked((qg_own, qg_other), 0, seq, lanes)
-            grad = stacked((qg_own, qg_other), 1, seq, lanes)
-            late = (across_cells, relayed_cells)
-            raw = dot(stacked(late, 0, seq, lanes), query, 1, 1)
-            late_up = dot(stacked(late, 1, seq, lanes), grad, 1, 1)
-            late_scores = [
-                raw[starts[i] - early_rows : starts[i + 1] - early_rows] * (scale * LOG2E) + step * float(runs[i][0])
-                for i in range(len(runs))
-                if starts[i] >= early_rows
-            ]
-            scores = jnp.concatenate([early[0][at], early[2][at], *late_scores], axis=0)
-            upstream = jnp.concatenate([early[1][at], early[3][at], late_up], axis=0)
-            weights = jnp.exp2(scores - jnp.max(scores, axis=0, keepdims=True))
-            probs = weights * (1.0 / jnp.sum(weights, axis=0, keepdims=True))
-            probs_low = probs.astype(BF16)
-            delta = jnp.sum(probs_low.astype(F32) * upstream, axis=0, keepdims=True)
-            dscore = probs * (upstream - delta)
-            for i, (level, _) in enumerate(runs):
-                if level:
-                    part = jnp.sum(dscore[starts[i] : starts[i + 1]], axis=0, keepdims=True)
-                    slope_sum = slope_sum + part * float(level)
-            dscore_low = dscore.astype(BF16)
-            dscore_out[at] = dscore_low
-            probs_out[at] = probs_low[:token_rows]
-            dk = dot(dscore_low[token_rows:], query) * scale
-            dv = dot(probs_low[token_rows:], grad)
-            for kind, direct in enumerate((dk, dv)):
-                parts = [direct[starts[i] - token_rows : starts[i + 1] - token_rows] for i in range(1, len(runs))]
-                group = (kind * seqs + seq) * heads + h
-                near[kind, seq, :, lanes] = parts[0]
-                side[pl.ds(group * (block // 2), block // 2), :] = parts[1].astype(BF16)
-                across[kind, seq, :, lanes] = parts[2 + far_count].astype(BF16)
-                for i, size in enumerate(far_sizes):
-                    here = pl.ds(slabs[i] + group * size, size)
-                    far[here, :] = parts[2 + i]
-                    relay[here, :] = parts[3 + far_count + i].astype(BF16)
-        slope_out[h : h + 1, :] = slope_sum
+        slope_out[h : h + 1, :] = sum(sums[h, seq] for seq in range(seqs))
     relay[pl.ds(far.shape[0], 2 * heads), :] = two_parts(slope_out[...])
 
 
@@ -233,14 +293,11 @@
             out[kind, seq] = (direct[kind, seq] + spread).astype(BF16)
 
 
-def relay_body(side, far, back, slope, slope_out, side_out, *far_outs):
+def relay_body(far, back, slope, slope_out, *far_outs):
     tail = 2 * slope.shape[0]
     total = slope[...] + one_part(back[pl.ds(far.shape[0], tail), :])
     slope_out[...] = total
     ending = two_parts(total)
-    rows = side.shape[0]
-    side_out[pl.ds(0, rows), :] = side[...]
-    side_out[pl.ds(rows, tail), :] = ending
     start = 0
     for out in far_outs:
         rows = out.shape[0] - tail
@@ -250,7 +307,7 @@
         start += rows
 
 
-def gather_body(levels_of, own, other, slope, near, *refs):
+def gather_body(levels_of, done, own, other, slope, slope_side, near, *refs):
     back, (kept, sent, slope_out) = refs[:-3], refs[-3:]
     kinds, seqs, block, width = own.shape
     heads = slope.shape[0]
@@ -267,29 +324,34 @@
                 total = dot(spread, jnp.concatenate(cells, axis=0))
                 kept[kind, seq, :, lanes] = (own[kind, seq, :, lanes] + total[:block]).astype(BF16)
                 sent[kind, seq, :, lanes] = (other[kind, seq, :, lanes] + total[block:]).astype(BF16)
-    all_slopes = slope[...]
-    for part, size in zip(back, sizes):
+    all_slopes = slope[...] + slope_side[...]
+    for part, size in zip(back[1:], sizes[1:]):
         all_slopes = all_slopes + one_part(part[pl.ds(kinds * seqs * heads * size, 2 * heads), :])
     slope_out[...] = all_slopes
 
 
-def join_body(core, own, other, out, sems):
+def join_body(core, own, other, out, done, sems):
     mine, theirs = head_halves(core, own.shape[-1])
     copy_all([(other, out.at[:, :, theirs]), (own, out.at[:, :, mine])], sems)
-
-
-def join_pair_body(core, own, other, slope, slope_other, first, second, slope_out, sems):
+    done[...] = jnp.zeros_like(done)
+
+
+def join_pair_body(core, own, other, slope, slope_other, first, second, slope_out, sums, sems):
     mine, theirs = head_halves(core, own.shape[-1])
     moves = []
     for index, out in enumerate((first, second)):
         moves.append((other.at[index], out.at[:, :, theirs]))
         moves.append((own.at[index], out.at[:, :, mine]))
-    copy_all(moves, sems)
+    copies = start_all(moves, sems)
     ours, rest = slope[...], slope_other[...]
     lower = jnp.where(core[0] == 0, ours, rest)
     upper = jnp.where(core[0] == 0, rest, ours)
     terms = jnp.concatenate([lower, upper], axis=0)
-    slope_out[...] = jnp.sum(terms.T, axis=0, keepdims=True)
+    sums[...] = jnp.sum(terms.T, axis=0, keepdims=True)
+    last = pltpu.make_async_copy(sums, slope_out, sems.at[len(moves)])
+    last.start()
+    for copy in (*copies, last):
+        copy.wait()
 
 
 def paired(queries, key_rows, value_rows, out_grad, level_slope):
@@ -302,30 +364,28 @@
     core = (position % 2).astype(jnp.int32).reshape(1)
 
     part = like(2, seqs, block, half)
-    kv_own, kv_send = call(
-        split_body, (part, part), (core, key_rows, value_rows), "split_kv", scalars=1, hbm_in=2, copies=4
-    )
-    kv_other = swap(kv_send, 1)
+    k_other, v_other = swap(key_rows, 1), swap(value_rows, 1)
+    cell_shapes = tuple(like(2, seqs, 2 * block >> level, half) for level in range(1, levels))
+    wide = (pltpu.VMEM((2, seqs, half // 128, block, 128), F32),)
+    own_cells = call(own_summary_body, cell_shapes, (core, key_rows, value_rows), "own_summaries", scalars=1, scratch=wide)
+    cells = call(summary_body, cell_shapes, (core, k_other, v_other, *own_cells), "summaries", scalars=1, scratch=wide)
     qg_own, qg_send = call(
         split_body, (part, part), (core, queries, out_grad), "split_qg", scalars=1, hbm_in=2, copies=4
     )
     qg_other = swap(qg_send, 1)
 
-    cells = call(
-        summary_body,
-        tuple(like(2, seqs, 2 * block >> level, half) for level in range(1, levels)),
-        (kv_own, kv_other),
-        "summaries",
+    kv_own, kv_other = call(
+        keep_body, (part, part), (core, key_rows, value_rows, k_other, v_other), "keep_halves", scalars=1
     )
     far = list(range(4, ctx_count // 2, 2))
     far_levels = [m.bit_length() for m in far]
     far_cells = [swap(cells[level - 1], 2 * m) for m, level in zip(far, far_levels)]
     near_cells = swap(cells[0], 2)
     side_cells = swap(cells[1], 4)
-    across_cells = swap(call(coarser_body, like(2, seqs, block // 2, half), (near_cells,), "coarser"), 4)
+    across = call(coarser_body, like(2, seqs, block // 2, half), (near_cells,), "coarser")
+    across_cells = swap(across, 4)
     far_sizes = [2 * block >> level for level in far_levels]
-    far_stack = call(stack_body, like(2, seqs, sum(far_sizes), half), far_cells, "stack")
-    relayed_cells = swap(far_stack, 2)
+    relayed_cells = [swap(c, 2) for c in far_cells]
 
     groups = seqs * heads
     early_levels, late_levels = (0, 0), (1, 2, *far_levels)
@@ -336,7 +396,7 @@
         product = like(groups // 2, count, token_rows, dtype=F32)
         return call(
             functools.partial(score_body, levels_of, head),
-            (product, product),
+            (product, product, like(groups // 2, 8, token_rows, dtype=F32)),
             (core, level_slope, qg_own, qg_other, *pieces),
             "scores",
             scalars=2,
@@ -364,16 +424,21 @@
             like(groups // 2, rows, token_rows),
             like(groups // 2, token_rows, token_rows),
         ),
-        (core, level_slope, *early, qg_own, qg_other, across_cells, relayed_cells),
+        (core, level_slope, *early, qg_own, qg_other, across_cells, *relayed_cells),
         "attend",
         scalars=2,
         flops=40 * seqs * token_rows * rows * half,
+        scratch=(
+            pltpu.VMEM((groups // 2, block // 2 + sum(far_sizes), token_rows), F32),
+            pltpu.VMEM((groups // 2, block // 2 + sum(far_sizes), token_rows), F32),
+            pltpu.VMEM((groups // 2, rows - token_rows, token_rows), BF16),
+        ),
     )
     dq_part = like(seqs, block, half)
     dq_own, dq_send, own, other = call(
         functools.partial(own_grads_body, head),
         (dq_part, dq_part, wide, wide),
-        (dscore, probs, qg_own, qg_other, *token_pieces, *cell_pieces, across_cells, relayed_cells),
+        (dscore, probs, qg_own, qg_other, *token_pieces, *cell_pieces, across_cells, *relayed_cells),
         "own_grads",
         flops=40 * seqs * token_rows * rows * half,
     )
@@ -386,34 +451,34 @@
         fold_body, (like(*near.shape), slope_part), (near, across_back, slope, *slopes), "fold"
     )
     near_back = swap(near_total, 2)
-    slope, side_total, *far_total = call(
+    side_back = swap(side, 4)
+    slope, *far_total = call(
         relay_body,
-        (slope_part, like(side.shape[0] + tail, head)) + tuple(like(r + tail, head) for r in far_rows),
-        (side, far_direct, relay_back, slope),
+        (slope_part, *(like(r + tail, head) for r in far_rows)),
+        (far_direct, relay_back, slope),
         "relay",
     )
-    side_back = swap(side_total, 4)
     far_back = [swap(message, 2 * m) for m, message in zip(far, far_total)]
     whole = like(seqs, block, width)
-    (dq,) = call(
-        join_body, (whole,), (core, dq_own, dq_other), "join_queries", scalars=1, hbm_out=1, copies=2
+    dq, done = call(
+        join_body, (whole, slope_part), (core, dq_own, dq_other), "join_queries", scalars=1, hbm_out=1, copies=2
     )
     kept, sent, slope = call(
         functools.partial(gather_body, (1, 2, *far_levels)),
         (part, part, slope_part),
-        (own, other, slope, near_back, side_back, *far_back),
+        (done, own, other, slope, swap(slope, 4), near_back, side_back, *far_back),
         "gather_cells",
     )
     kv_grad_other = swap(sent, 1)
-    slope_other = swap(slope, 1)
     dk, dv, slope_grad = call(
         join_pair_body,
         (whole, whole, like(1, heads, dtype=F32)),
-        (core, kept, kv_grad_other, slope, slope_other),
+        (core, kept, kv_grad_other, slope, swap(slope, 1)),
         "join_kv",
         scalars=1,
-        hbm_out=2,
-        copies=4,
+        hbm_out=3,
+        copies=5,
+        scratch=(pltpu.VMEM((1, heads), F32),),
     )
     return dq, dk, dv, slope_grad.reshape(heads)
 

time: 66.4 us -> 61 us (0.919)
  waiting for transfers between devices: 30.3 us -> 25.1 us
  Pallas kernels: 14.2 us -> 10.1 us
  starting transfers between devices: 18.8 us -> 22.7 us
    ppermute x17 -> x20, waiting for transfers between devices: 27.2 us -> 22.3 us  [swap(): lax.ppermute(value, 'ctx', [(source, source ^ apart) for source in range(...]
    pallas_call x14, Pallas kernels: 14.2 us -> 10.1 us  [call(): pl.pallas_call(body, out_shape=out_shape, in_specs=[SMEM] * scalars + [HB...]
    ppermute x17 -> x20, starting transfers between devices: 16.9 us -> 19.5 us  [swap(): lax.ppermute(value, 'ctx', [(source, source ^ apart) for source in range(...]
    ppermute x2, starting transfers between devices: 1.97 us -> 3.21 us  [swap(): return lax.ppermute(value, ('dp', 'ctx'), pairs)]
    unnamed x10 -> x14, local copies, waits for them, and re-layouts: 2.09 us -> 2.11 us
  transfers between devices with their start and end apart: 19 -> 22, of which waited for: 11 -> 11; matrix products, arithmetic and copies ran while one was open for 0% -> 0% of each run, Pallas kernels for 8% -> 9%
where the time goes in v4:
time: 61 us; the launch traced here: 60.8 us
  waiting for transfers between devices  25.1 us (41%)
  starting transfers between devices  22.7 us (37%)
  Pallas kernels  10.1 us (17%)
  local copies, waits for them, and re-layouts  2.11 us (3%)
  between operations  0.79 us (1%)
    ppermute x20, waiting for transfers between devices, swap(): lax.ppermute(value, 'ctx', [(source, source ^ apart) for source in range(...  22.3 us
    ppermute x20, starting transfers between devices, swap(): lax.ppermute(value, 'ctx', [(source, source ^ apart) for source in range(...  19.5 us
    pallas_call x14, Pallas kernels, call(): pl.pallas_call(body, out_shape=out_shape, in_specs=[SMEM] * scalars + [HB...  10.1 us
    ppermute x2, starting transfers between devices, swap(): return lax.ppermute(value, ('dp', 'ctx'), pairs)  3.21 us
    ppermute x2, waiting for transfers between devices, swap(): return lax.ppermute(value, ('dp', 'ctx'), pairs)  2.79 us
    unnamed x14, local copies, waits for them, and re-layouts  2.11 us
  transfers between devices with their start and end apart: 22, of which 11 were waited for; matrix products, arithmetic and copies ran while one was open for 0% of the time, Pallas kernels for 9%

profile of v4, /device:TPU:0, one launch (start us, length us, event | category | flops | bytes accessed | tf_op | source)
XLA Modules:
  0.0 60.8 jit_solution(13728741821467109931)
XLA Ops:
  0.6 0.5 collective-permute-start.1
  1.1 0.1 collective-permute-start.2
  1.2 1.0 %copy-done = bf16[2,64,2048]{2,1,0:T(8,128)(2,1)S(1)} copy-done((bf16[2,64,2048]{2,1,0:T(8,128)(2,1)S(1)}, bf16[2,64,2048]{2,1,0:T(8,128)(2,1)}, u32[]{:S(2)}) %copy-start) | copy-done | bytes 524312
  2.3 1.0 %copy-done.2 = bf16[2,64,2048]{2,1,0:T(8,128)(2,1)S(1)} copy-done((bf16[2,64,2048]{2,1,0:T(8,128)(2,1)S(1)}, bf16[2,64,2048]{2,1,0:T(8,128)(2,1)}, u32[]{:S(2)}) %copy-start.2) | copy-done | bytes 524312
  3.3 0.4 own_summaries.1
  3.7 0.4 summaries.1
  4.2 3.0 %collective-permute-start.3 = (bf16[2,2,64,1024]{3,2,1,0:T(8,128)(2,1)S(1)}, bf16[2,2,64,1024]{3,2,1,0:T(8,128)(2,1)S(1)}, u32[]{:S(2)}, u32[]{:S(2)}) collective-permute-start(bf16[2,2,64,1024]{3,2,1,0:T(8,128)(2,1)S(1)} %get-tuple-element.55), channel_id=1, source_target_pairs={{0,2},{1,3},{2,0},{3,1},{4,6},{5,7},{6,4},{7,5},{8,10},{9,11},{10,... | collective-permute-start | bytes 1572872 | tf_op jit(solution)/shard_map/ppermute | solution.py:21
  7.2 0.1 split_qg.1
  7.3 0.1 collective-permute-start
  7.4 1.6 %collective-permute-start.4 = (bf16[2,2,32,1024]{3,2,1,0:T(8,128)(2,1)S(1)}, bf16[2,2,32,1024]{3,2,1,0:T(8,128)(2,1)S(1)}, u32[]{:S(2)}, u32[]{:S(2)}) collective-permute-start(bf16[2,2,32,1024]{3,2,1,0:T(8,128)(2,1)S(1)} %get-tuple-element.56), channel_id=1, source_target_pairs={{0,4},{1,5},{2,6},{3,7},{4,0},{5,1},{6,2},{7,3},{8,12},{9,13},{10,... | collective-permute-start | bytes 786440 | tf_op jit(solution)/shard_map/ppermute | solution.py:21
  9.0 2.5 %collective-permute-start.6 = (bf16[2,2,16,1024]{3,2,1,0:T(8,128)(2,1)S(1)}, bf16[2,2,16,1024]{3,2,1,0:T(8,128)(2,1)S(1)}, u32[]{:S(2)}, u32[]{:S(2)}) collective-permute-start(bf16[2,2,16,1024]{3,2,1,0:T(8,128)(2,1)S(1)} %get-tuple-element.57), channel_id=1, source_target_pairs={{0,12},{1,13},{2,14},{3,15},{4,8},{5,9},{6,10},{7,11},{8,4},{9,5},... | collective-permute-start | bytes 393224 | tf_op jit(solution)/shard_map/ppermute | solution.py:21
  11.5 0.1 collective-permute-start.5
  11.6 7.7 %collective-permute-done.3.refs_0_.cells.refs_2_ = bf16[2,2,64,1024]{3,2,1,0:T(8,128)(2,1)S(1)} collective-permute-done((bf16[2,2,64,1024]{3,2,1,0:T(8,128)(2,1)S(1)}, bf16[2,2,64,1024]{3,2,1,0:T(8,128)(2,1)S(1)}, u32[]{:S(2)}, u32[]{:S(2)}) %collective-permute-start.3) | collective-permute-done | bytes 524320 | tf_op jit(solution)/shard_map/ppermute | solution.py:21
  19.4 0.2 coarser.1
  19.6 1.9 %collective-permute-start.7 = (bf16[2,2,32,1024]{3,2,1,0:T(8,128)(2,1)S(1)}, bf16[2,2,32,1024]{3,2,1,0:T(8,128)(2,1)S(1)}, u32[]{:S(2)}, u32[]{:S(2)}) collective-permute-start(bf16[2,2,32,1024]{3,2,1,0:T(8,128)(2,1)S(1)} %coarser.1), channel_id=1, source_target_pairs={{0,4},{1,5},{2,6},{3,7},{4,0},{5,1},{6,2},{7,3},{8,12},{9,13},{10,... | collective-permute-start | bytes 786440 | tf_op jit(solution)/shard_map/ppermute | solution.py:21
  21.4 0.1 keep_halves.1
  21.5 1.6 %collective-permute-start.9 = (bf16[2,2,16,1024]{3,2,1,0:T(8,128)(2,1)S(1)}, bf16[2,2,16,1024]{3,2,1,0:T(8,128)(2,1)S(1)}, u32[]{:S(2)}, u32[]{:S(2)}) collective-permute-start(bf16[2,2,16,1024]{3,2,1,0:T(8,128)(2,1)S(1)} %collective-permute-done.6.refs_3_.refs_5_), channel_id=1, source_target_pairs={{0,2},{1,3},{2,0},{3,1},{4,6},{5,7},{6,4},{7,5},{8,10},{9,11},{10,... | collective-permute-start | bytes 393224 | tf_op jit(solution)/shard_map/ppermute | solution.py:21
  23.1 0.9 %collective-permute-done.5.refs_2_.refs_4_ = bf16[2,2,16,1024]{3,2,1,0:T(8,128)(2,1)S(1)} collective-permute-done((bf16[2,2,16,1024]{3,2,1,0:T(8,128)(2,1)S(1)}, bf16[2,2,16,1024]{3,2,1,0:T(8,128)(2,1)S(1)}, u32[]{:S(2)}, u32[]{:S(2)}) %collective-permute-start.5) | collective-permute-done | bytes 131104 | tf_op jit(solution)/shard_map/ppermute | solution.py:21
  24.0 0.5 collective-permute-start.8
  24.5 1.4 %scores.2 = (f32[16,128,128]{2,1,0:T(8,128)S(1)}, f32[16,128,128]{2,1,0:T(8,128)S(1)}, f32[16,8,128]{2,1,0:T(8,128)S(1)}) custom-call(s32[1]{0:T(128)} %bitcast.core, f32[16]{0:T(128)S(1)} %copy-done.6, bf16[2,2,64,1024]{3,2,1,0:T(8,128)(2,1)S(1)} %get-tuple-element.45.qg_own.refs_6_, bf16[2,2,64,1024]{3,2,1,0:T(8,128)(2,1)S(1)} %collective-permute-done.qg_other.refs_7_, ...), custom_call_target="tpu_custom_call" | custom-call | flops 1342177280 | bytes 4259908 | tf_op jit(solution)/shard_map/scores/pallas_call | solution.py:34
  26.0 1.4 %scores.3 = (f32[16,128,128]{2,1,0:T(8,128)S(1)}, f32[16,128,128]{2,1,0:T(8,128)S(1)}, f32[16,8,128]{2,1,0:T(8,128)S(1)}) custom-call(s32[1]{0:T(128)} %bitcast.core, f32[16]{0:T(128)S(1)} %copy-done.6, bf16[2,2,64,1024]{3,2,1,0:T(8,128)(2,1)S(1)} %get-tuple-element.45.qg_own.refs_6_, bf16[2,2,64,1024]{3,2,1,0:T(8,128)(2,1)S(1)} %collective-permute-done.qg_other.refs_7_, ...), custom_call_target="tpu_custom_call" | custom-call | flops 1342177280 | bytes 4259908 | tf_op jit(solution)/shard_map/scores/pallas_call | solution.py:34
  27.4 0.1 collective-permute-done.9.refs_10_.refs_8_
  27.5 1.5 %collective-permute-done.8.refs_9_.refs_7_ = bf16[2,2,16,1024]{3,2,1,0:T(8,128)(2,1)S(1)} collective-permute-done((bf16[2,2,16,1024]{3,2,1,0:T(8,128)(2,1)S(1)}, bf16[2,2,16,1024]{3,2,1,0:T(8,128)(2,1)S(1)}, u32[]{:S(2)}, u32[]{:S(2)}) %collective-permute-start.8) | collective-permute-done | bytes 131104 | tf_op jit(solution)/shard_map/ppermute | solution.py:21
  29.0 2.4 %attend.1 = (f32[8,128]{1,0:T(8,128)S(1)}, f32[2,2,64,1024]{3,2,1,0:T(8,128)S(1)}, bf16[2,2,32,1024]{3,2,1,0:T(8,128)(2,1)S(1)}, bf16[1024,128]{1,0:T(8,128)(2,1...) custom-call(s32[1]{0:T(128)} %bitcast.core, ...), custom_call_target="tpu_custom_call" | custom-call | flops 3355443200 | bytes 10100804 | tf_op jit(solution)/shard_map/attend/pallas_call | solution.py:34
  31.5 0.7 %collective-permute-start.12 = (bf16[2,2,32,1024]{3,2,1,0:T(8,128)(2,1)S(1)}, bf16[2,2,32,1024]{3,2,1,0:T(8,128)(2,1)S(1)}, u32[]{:S(2)}, u32[]{:S(2)}) collective-permute-start(bf16[2,2,32,1024]{3,2,1,0:T(8,128)(2,1)S(1)} %get-tuple-element.72), channel_id=1, source_target_pairs={{0,4},{1,5},{2,6},{3,7},{4,0},{5,1},{6,2},{7,3},{8,12},{9,13},{10,... | collective-permute-start | bytes 786440 | tf_op jit(solution)/shard_map/ppermute | solution.py:21
  32.1 2.7 %collective-permute-start.14 = (f32[8,128]{1,0:T(8,128)S(1)}, f32[8,128]{1,0:T(8,128)S(1)}, u32[]{:S(2)}, u32[]{:S(2)}) collective-permute-start(f32[8,128]{1,0:T(8,128)S(1)} %get-tuple-element.73.slope), channel_id=1, source_target_pairs={{0,18},{1,19},{2,16},{3,17},{4,22},{5,23},{6,20},{7,21},{8,26},{9,... | collective-permute-start | bytes 12296 | tf_op jit(solution)/shard_map/ppermute | solution.py:24
  34.8 0.5 collective-permute-start.13
  35.3 0.3 collective-permute-start.11
  35.6 1.1 %collective-permute-done.14.refs_1_ = f32[8,128]{1,0:T(8,128)S(1)} collective-permute-done((f32[8,128]{1,0:T(8,128)S(1)}, f32[8,128]{1,0:T(8,128)S(1)}, u32[]{:S(2)}, u32[]{:S(2)}) %collective-permute-start.14) | collective-permute-done | bytes 4128 | tf_op jit(solution)/shard_map/ppermute | solution.py:24
  36.7 1.7 %collective-permute-done.13.refs_0_ = f32[8,128]{1,0:T(8,128)S(1)} collective-permute-done((f32[8,128]{1,0:T(8,128)S(1)}, f32[8,128]{1,0:T(8,128)S(1)}, u32[]{:S(2)}, u32[]{:S(2)}) %collective-permute-start.13) | collective-permute-done | bytes 4128 | tf_op jit(solution)/shard_map/ppermute | solution.py:24
  38.4 0.3 fold.1
  38.7 0.8 %collective-permute-start.16 = (bf16[2,2,64,1024]{3,2,1,0:T(8,128)(2,1)S(1)}, bf16[2,2,64,1024]{3,2,1,0:T(8,128)(2,1)S(1)}, u32[]{:S(2)}, u32[]{:S(2)}) collective-permute-start(bf16[2,2,64,1024]{3,2,1,0:T(8,128)(2,1)S(1)} %get-tuple-element.76), channel_id=1, source_target_pairs={{0,2},{1,3},{2,0},{3,1},{4,6},{5,7},{6,4},{7,5},{8,10},{9,11},{10,... | collective-permute-start | bytes 1572872 | tf_op jit(solution)/shard_map/ppermute | solution.py:21
  39.5 0.9 %own_grads.1 = (bf16[2,64,1024]{2,1,0:T(8,128)(2,1)S(1)}, bf16[2,64,1024]{2,1,0:T(8,128)(2,1)S(1)}, f32[2,2,64,1024]{3,2,1,0:T(8,128)S(1)}, f32[2,2,64,1024]{3,2,1,0:T(8,128)S(1)}) custom-call(bf16[16,320,128]{2,1,0:T(8,128)(2,1)S(1)} %get-tuple-element.61.dscore, bf16[16,128,128]{2,1,0:T(8,128)(2,1)S(1)} %get-tuple-element.62.probs, ...), custom_call_target="tpu_custom_call" | custom-call | flops 3355443200 | bytes 8126464 | tf_op jit(solution)/shard_map/own_grads/pallas_call | solution.py:34
  40.5 0.1 collective-permute-start.10
  40.5 1.7 %collective-permute-start.17 = (bf16[1024,128]{1,0:T(8,128)(2,1)S(1)}, bf16[1024,128]{1,0:T(8,128)(2,1)S(1)}, u32[]{:S(2)}, u32[]{:S(2)}) collective-permute-start(bf16[1024,128]{1,0:T(8,128)(2,1)S(1)} %get-tuple-element.77), channel_id=1, source_target_pairs={{0,4},{1,5},{2,6},{3,7},{4,0},{5,1},{6,2},{7,3},{8,12},{9,13},{10,... | collective-permute-start | bytes 786440 | tf_op jit(solution)/shard_map/ppermute | solution.py:21
  42.2 2.4 %collective-permute-done.11.back = bf16[1040,128]{1,0:T(8,128)(2,1)S(1)} collective-permute-done((bf16[1040,128]{1,0:T(8,128)(2,1)S(1)}, bf16[1040,128]{1,0:T(8,128)(2,1)S(1)}, u32[]{:S(2)}, u32[]{:S(2)}) %collective-permute-start.11) | collective-permute-done | bytes 266272 | tf_op jit(solution)/shard_map/ppermute | solution.py:21
  44.7 1.1 %collective-permute-start.18 = (bf16[528,128]{1,0:T(8,128)(2,1)S(1)}, bf16[528,128]{1,0:T(8,128)(2,1)S(1)}, u32[]{:S(2)}, u32[]{:S(2)}) collective-permute-start(bf16[528,128]{1,0:T(8,128)(2,1)S(1)} %get-tuple-element.78), channel_id=1, source_target_pairs={{0,8},{1,9},{2,10},{3,11},{4,12},{5,13},{6,14},{7,15},{8,0},{9,1},... | collective-permute-start | bytes 405512 | tf_op jit(solution)/shard_map/ppermute | solution.py:21
  45.8 2.0 %collective-permute-start.19 = (bf16[528,128]{1,0:T(8,128)(2,1)S(1)}, bf16[528,128]{1,0:T(8,128)(2,1)S(1)}, u32[]{:S(2)}, u32[]{:S(2)}) collective-permute-start(bf16[528,128]{1,0:T(8,128)(2,1)S(1)} %get-tuple-element.79), channel_id=1, source_target_pairs={{0,12},{1,13},{2,14},{3,15},{4,8},{5,9},{6,10},{7,11},{8,4},{9,5},... | collective-permute-start | bytes 405512 | tf_op jit(solution)/shard_map/ppermute | solution.py:21
  47.8 0.4 collective-permute-start.15
  48.3 0.8 %join_queries.1 = (bf16[2,64,2048]{2,1,0:T(8,128)(2,1)}, f32[8,128]{1,0:T(8,128)S(1)}) custom-call(s32[1]{0:T(128)} %bitcast.core, bf16[2,64,1024]{2,1,0:T(8,128)(2,1)S(1)} %get-tuple-element.63.own, bf16[2,64,1024]{2,1,0:T(8,128)(2,1)S(1)} %collective-permute-done.10.other), custom_call_target="tpu_custom_call" | custom-call | bytes 1052676 | tf_op jit(solution)/shard_map/join_queries/pallas_call | solution.py:34
  49.1 3.1 %collective-permute-done.17.refs_0_ = bf16[1024,128]{1,0:T(8,128)(2,1)S(1)} collective-permute-done((bf16[1024,128]{1,0:T(8,128)(2,1)S(1)}, bf16[1024,128]{1,0:T(8,128)(2,1)S(1)}, u32[]{:S(2)}, u32[]{:S(2)}) %collective-permute-start.17) | collective-permute-done | bytes 262176 | tf_op jit(solution)/shard_map/ppermute | solution.py:21
  52.2 2.1 %collective-permute-done.15.slope_side = f32[8,128]{1,0:T(8,128)S(1)} collective-permute-done((f32[8,128]{1,0:T(8,128)S(1)}, f32[8,128]{1,0:T(8,128)S(1)}, u32[]{:S(2)}, u32[]{:S(2)}) %collective-permute-start.15) | collective-permute-done | bytes 4128 | tf_op jit(solution)/shard_map/ppermute | solution.py:21
  54.3 3.0 %collective-permute-done.19.refs_2_ = bf16[528,128]{1,0:T(8,128)(2,1)S(1)} collective-permute-done((bf16[528,128]{1,0:T(8,128)(2,1)S(1)}, bf16[528,128]{1,0:T(8,128)(2,1)S(1)}, u32[]{:S(2)}, u32[]{:S(2)}) %collective-permute-start.19) | collective-permute-done | bytes 135200 | tf_op jit(solution)/shard_map/ppermute | solution.py:21
  57.3 0.5 gather_cells.1
  57.8 0.1 collective-permute-start.20
  57.9 0.5 collective-permute-start.21
  58.4 1.4 %collective-permute-done.21.slope_other = f32[8,128]{1,0:T(8,128)S(1)} collective-permute-done((f32[8,128]{1,0:T(8,128)S(1)}, f32[8,128]{1,0:T(8,128)S(1)}, u32[]{:S(2)}, u32[]{:S(2)}) %collective-permute-start.21) | collective-permute-done | bytes 4128 | tf_op jit(solution)/shard_map/ppermute | solution.py:21
  59.8 1.0 %join_kv.1 = (bf16[2,64,2048]{2,1,0:T(8,128)(2,1)}, bf16[2,64,2048]{2,1,0:T(8,128)(2,1)}, f32[1,16]{1,0:T(1,128)}) custom-call(s32[1]{0:T(128)} %bitcast.core, bf16[2,2,64,1024]{3,2,1,0:T(8,128)(2,1)S(1)} %get-tuple-element.80.own, bf16[2,2,64,1024]{3,2,1,0:T(8,128)(2,1)S(1)} %collective-permute-done.20.other, f32[8,128]{1,0:T(8,128)S(1)} %get-tuple-element.82.slope, ...), custom_call_target="tpu_custom_call" | custom-call | bytes 2105412 | tf_op jit(solution)/shard_map/join_kv/pallas_call | solution.py:34
  (24 shorter events, 0.1 us)
Async XLA Ops:
  0.6 3.1 %collective-permute-start.1 = (bf16[2,64,2048]{2,1,0:T(8,128)(2,1)}, bf16[2,64,2048]{2,1,0:T(8,128)(2,1)S(1)}, u32[]{:S(2)}, u32[]{:S(2)}) collective-permute-start(bf16[2,64,2048]{2,1,0:T(8,128)(2,1)} %k.3), channel_id=1, source_target_pairs={{0,1},{1,0},{2,3},{3,2},{4,5},{5,4},{6,7},{7,6},{8,9},{9,8},{10,11... | collective-permute-start | bytes 1572872 | tf_op jit(solution)/shard_map/ppermute | solution.py:21
  1.1 2.6 %collective-permute-start.2 = (bf16[2,64,2048]{2,1,0:T(8,128)(2,1)}, bf16[2,64,2048]{2,1,0:T(8,128)(2,1)S(1)}, u32[]{:S(2)}, u32[]{:S(2)}) collective-permute-start(bf16[2,64,2048]{2,1,0:T(8,128)(2,1)} %v.3), channel_id=1, source_target_pairs={{0,1},{1,0},{2,3},{3,2},{4,5},{5,4},{6,7},{7,6},{8,9},{9,8},{10,11... | collective-permute-start | bytes 1572872 | tf_op jit(solution)/shard_map/ppermute | solution.py:21
  1.2 1.0 %copy-start = (bf16[2,64,2048]{2,1,0:T(8,128)(2,1)S(1)}, bf16[2,64,2048]{2,1,0:T(8,128)(2,1)}, u32[]{:S(2)}) copy-start(bf16[2,64,2048]{2,1,0:T(8,128)(2,1)} %k.3) | copy-start | bytes 1572868
  2.3 1.0 %copy-start.2 = (bf16[2,64,2048]{2,1,0:T(8,128)(2,1)S(1)}, bf16[2,64,2048]{2,1,0:T(8,128)(2,1)}, u32[]{:S(2)}) copy-start(bf16[2,64,2048]{2,1,0:T(8,128)(2,1)} %v.3) | copy-start | bytes 1572868
  3.3 3.9 %copy-start.4 = (bf16[2,64,2048]{2,1,0:T(8,128)(2,1)S(1)}, bf16[2,64,2048]{2,1,0:T(8,128)(2,1)}, u32[]{:S(2)}) copy-start(bf16[2,64,2048]{2,1,0:T(8,128)(2,1)} %first.1) | copy-start | bytes 1572868
  3.3 3.9 %copy-start.5 = (bf16[2,64,2048]{2,1,0:T(8,128)(2,1)S(1)}, bf16[2,64,2048]{2,1,0:T(8,128)(2,1)}, u32[]{:S(2)}) copy-start(bf16[2,64,2048]{2,1,0:T(8,128)(2,1)} %second.1) | copy-start | bytes 1572868
  4.2 17.3 %copy-start.1 = (bf16[2,64,2048]{2,1,0:T(8,128)(2,1)S(1)}, bf16[2,64,2048]{2,1,0:T(8,128)(2,1)}, u32[]{:S(2)}) copy-start(bf16[2,64,2048]{2,1,0:T(8,128)(2,1)} %k.3) | copy-start | bytes 1572868
  4.2 17.3 %copy-start.3 = (bf16[2,64,2048]{2,1,0:T(8,128)(2,1)S(1)}, bf16[2,64,2048]{2,1,0:T(8,128)(2,1)}, u32[]{:S(2)}) copy-start(bf16[2,64,2048]{2,1,0:T(8,128)(2,1)} %v.3) | copy-start | bytes 1572868
  4.2 15.2 %collective-permute-start.3 = (bf16[2,2,64,1024]{3,2,1,0:T(8,128)(2,1)S(1)}, bf16[2,2,64,1024]{3,2,1,0:T(8,128)(2,1)S(1)}, u32[]{:S(2)}, u32[]{:S(2)}) collective-permute-start(bf16[2,2,64,1024]{3,2,1,0:T(8,128)(2,1)S(1)} %get-tuple-element.55), channel_id=1, source_target_pairs={{0,2},{1,3},{2,0},{3,1},{4,6},{5,7},{6,4},{7,5},{8,10},{9,11},{10,... | collective-permute-start | bytes 1572872 | tf_op jit(solution)/shard_map/ppermute | solution.py:21
  7.3 17.2 %collective-permute-start = (bf16[2,2,64,1024]{3,2,1,0:T(8,128)(2,1)S(1)}, bf16[2,2,64,1024]{3,2,1,0:T(8,128)(2,1)S(1)}, u32[]{:S(2)}, u32[]{:S(2)}) collective-permute-start(bf16[2,2,64,1024]{3,2,1,0:T(8,128)(2,1)S(1)} %get-tuple-element.46), channel_id=1, source_target_pairs={{0,1},{1,0},{2,3},{3,2},{4,5},{5,4},{6,7},{7,6},{8,9},{9,8},{10,11... | collective-permute-start | bytes 1572872 | tf_op jit(solution)/shard_map/ppermute | solution.py:21
  7.4 18.6 %collective-permute-start.4 = (bf16[2,2,32,1024]{3,2,1,0:T(8,128)(2,1)S(1)}, bf16[2,2,32,1024]{3,2,1,0:T(8,128)(2,1)S(1)}, u32[]{:S(2)}, u32[]{:S(2)}) collective-permute-start(bf16[2,2,32,1024]{3,2,1,0:T(8,128)(2,1)S(1)} %get-tuple-element.56), channel_id=1, source_target_pairs={{0,4},{1,5},{2,6},{3,7},{4,0},{5,1},{6,2},{7,3},{8,12},{9,13},{10,... | collective-permute-start | bytes 786440 | tf_op jit(solution)/shard_map/ppermute | solution.py:21
  9.0 15.5 %copy-start.6 = (f32[16]{0:T(128)S(1)}, f32[16]{0:T(128)}, u32[]{:S(2)}) copy-start(f32[16]{0:T(128)} %slope.5) | copy-start | bytes 196
  9.0 12.5 %collective-permute-start.6 = (bf16[2,2,16,1024]{3,2,1,0:T(8,128)(2,1)S(1)}, bf16[2,2,16,1024]{3,2,1,0:T(8,128)(2,1)S(1)}, u32[]{:S(2)}, u32[]{:S(2)}) collective-permute-start(bf16[2,2,16,1024]{3,2,1,0:T(8,128)(2,1)S(1)} %get-tuple-element.57), channel_id=1, source_target_pairs={{0,12},{1,13},{2,14},{3,15},{4,8},{5,9},{6,10},{7,11},{8,4},{9,5},... | collective-permute-start | bytes 393224 | tf_op jit(solution)/shard_map/ppermute | solution.py:21
  11.5 12.5 %collective-permute-start.5 = (bf16[2,2,16,1024]{3,2,1,0:T(8,128)(2,1)S(1)}, bf16[2,2,16,1024]{3,2,1,0:T(8,128)(2,1)S(1)}, u32[]{:S(2)}, u32[]{:S(2)}) collective-permute-start(bf16[2,2,16,1024]{3,2,1,0:T(8,128)(2,1)S(1)} %get-tuple-element.57), channel_id=1, source_target_pairs={{0,8},{1,9},{2,10},{3,11},{4,12},{5,13},{6,14},{7,15},{8,0},{9,1},... | collective-permute-start | bytes 393224 | tf_op jit(solution)/shard_map/ppermute | solution.py:21
  19.6 9.4 %collective-permute-start.7 = (bf16[2,2,32,1024]{3,2,1,0:T(8,128)(2,1)S(1)}, bf16[2,2,32,1024]{3,2,1,0:T(8,128)(2,1)S(1)}, u32[]{:S(2)}, u32[]{:S(2)}) collective-permute-start(bf16[2,2,32,1024]{3,2,1,0:T(8,128)(2,1)S(1)} %coarser.1), channel_id=1, source_target_pairs={{0,4},{1,5},{2,6},{3,7},{4,0},{5,1},{6,2},{7,3},{8,12},{9,13},{10,... | collective-permute-start | bytes 786440 | tf_op jit(solution)/shard_map/ppermute | solution.py:21
  21.5 5.9 %collective-permute-start.9 = (bf16[2,2,16,1024]{3,2,1,0:T(8,128)(2,1)S(1)}, bf16[2,2,16,1024]{3,2,1,0:T(8,128)(2,1)S(1)}, u32[]{:S(2)}, u32[]{:S(2)}) collective-permute-start(bf16[2,2,16,1024]{3,2,1,0:T(8,128)(2,1)S(1)} %collective-permute-done.6.refs_3_.refs_5_), channel_id=1, source_target_pairs={{0,2},{1,3},{2,0},{3,1},{4,6},{5,7},{6,4},{7,5},{8,10},{9,11},{10,... | collective-permute-start | bytes 393224 | tf_op jit(solution)/shard_map/ppermute | solution.py:21
  24.0 5.0 %collective-permute-start.8 = (bf16[2,2,16,1024]{3,2,1,0:T(8,128)(2,1)S(1)}, bf16[2,2,16,1024]{3,2,1,0:T(8,128)(2,1)S(1)}, u32[]{:S(2)}, u32[]{:S(2)}) collective-permute-start(bf16[2,2,16,1024]{3,2,1,0:T(8,128)(2,1)S(1)} %collective-permute-done.5.refs_2_.refs_4_), channel_id=1, source_target_pairs={{0,2},{1,3},{2,0},{3,1},{4,6},{5,7},{6,4},{7,5},{8,10},{9,11},{10,... | collective-permute-start | bytes 393224 | tf_op jit(solution)/shard_map/ppermute | solution.py:21
  31.5 6.9 %collective-permute-start.12 = (bf16[2,2,32,1024]{3,2,1,0:T(8,128)(2,1)S(1)}, bf16[2,2,32,1024]{3,2,1,0:T(8,128)(2,1)S(1)}, u32[]{:S(2)}, u32[]{:S(2)}) collective-permute-start(bf16[2,2,32,1024]{3,2,1,0:T(8,128)(2,1)S(1)} %get-tuple-element.72), channel_id=1, source_target_pairs={{0,4},{1,5},{2,6},{3,7},{4,0},{5,1},{6,2},{7,3},{8,12},{9,13},{10,... | collective-permute-start | bytes 786440 | tf_op jit(solution)/shard_map/ppermute | solution.py:21
  32.1 4.6 %collective-permute-start.14 = (f32[8,128]{1,0:T(8,128)S(1)}, f32[8,128]{1,0:T(8,128)S(1)}, u32[]{:S(2)}, u32[]{:S(2)}) collective-permute-start(f32[8,128]{1,0:T(8,128)S(1)} %get-tuple-element.73.slope), channel_id=1, source_target_pairs={{0,18},{1,19},{2,16},{3,17},{4,22},{5,23},{6,20},{7,21},{8,26},{9,... | collective-permute-start | bytes 12296 | tf_op jit(solution)/shard_map/ppermute | solution.py:24
  34.8 3.6 %collective-permute-start.13 = (f32[8,128]{1,0:T(8,128)S(1)}, f32[8,128]{1,0:T(8,128)S(1)}, u32[]{:S(2)}, u32[]{:S(2)}) collective-permute-start(f32[8,128]{1,0:T(8,128)S(1)} %get-tuple-element.73.slope), channel_id=1, source_target_pairs={{0,16},{1,17},{2,18},{3,19},{4,20},{5,21},{6,22},{7,23},{8,24},{9,... | collective-permute-start | bytes 12296 | tf_op jit(solution)/shard_map/ppermute | solution.py:24
  35.3 9.3 %collective-permute-start.11 = (bf16[1040,128]{1,0:T(8,128)(2,1)S(1)}, bf16[1040,128]{1,0:T(8,128)(2,1)S(1)}, u32[]{:S(2)}, u32[]{:S(2)}) collective-permute-start(bf16[1040,128]{1,0:T(8,128)(2,1)S(1)} %get-tuple-element.70), channel_id=1, source_target_pairs={{0,2},{1,3},{2,0},{3,1},{4,6},{5,7},{6,4},{7,5},{8,10},{9,11},{10,... | collective-permute-start | bytes 798728 | tf_op jit(solution)/shard_map/ppermute | solution.py:21
  38.7 18.6 %collective-permute-start.16 = (bf16[2,2,64,1024]{3,2,1,0:T(8,128)(2,1)S(1)}, bf16[2,2,64,1024]{3,2,1,0:T(8,128)(2,1)S(1)}, u32[]{:S(2)}, u32[]{:S(2)}) collective-permute-start(bf16[2,2,64,1024]{3,2,1,0:T(8,128)(2,1)S(1)} %get-tuple-element.76), channel_id=1, source_target_pairs={{0,2},{1,3},{2,0},{3,1},{4,6},{5,7},{6,4},{7,5},{8,10},{9,11},{10,... | collective-permute-start | bytes 1572872 | tf_op jit(solution)/shard_map/ppermute | solution.py:21
  40.5 7.4 %collective-permute-start.10 = (bf16[2,64,1024]{2,1,0:T(8,128)(2,1)S(1)}, bf16[2,64,1024]{2,1,0:T(8,128)(2,1)S(1)}, u32[]{:S(2)}, u32[]{:S(2)}) collective-permute-start(bf16[2,64,1024]{2,1,0:T(8,128)(2,1)S(1)} %get-tuple-element.64), channel_id=1, source_target_pairs={{0,1},{1,0},{2,3},{3,2},{4,5},{5,4},{6,7},{7,6},{8,9},{9,8},{10,11... | collective-permute-start | bytes 786440 | tf_op jit(solution)/shard_map/ppermute | solution.py:21
  40.5 11.7 %collective-permute-start.17 = (bf16[1024,128]{1,0:T(8,128)(2,1)S(1)}, bf16[1024,128]{1,0:T(8,128)(2,1)S(1)}, u32[]{:S(2)}, u32[]{:S(2)}) collective-permute-start(bf16[1024,128]{1,0:T(8,128)(2,1)S(1)} %get-tuple-element.77), channel_id=1, source_target_pairs={{0,4},{1,5},{2,6},{3,7},{4,0},{5,1},{6,2},{7,3},{8,12},{9,13},{10,... | collective-permute-start | bytes 786440 | tf_op jit(solution)/shard_map/ppermute | solution.py:21
  44.7 9.6 %collective-permute-start.18 = (bf16[528,128]{1,0:T(8,128)(2,1)S(1)}, bf16[528,128]{1,0:T(8,128)(2,1)S(1)}, u32[]{:S(2)}, u32[]{:S(2)}) collective-permute-start(bf16[528,128]{1,0:T(8,128)(2,1)S(1)} %get-tuple-element.78), channel_id=1, source_target_pairs={{0,8},{1,9},{2,10},{3,11},{4,12},{5,13},{6,14},{7,15},{8,0},{9,1},... | collective-permute-start | bytes 405512 | tf_op jit(solution)/shard_map/ppermute | solution.py:21
  45.8 11.5 %collective-permute-start.19 = (bf16[528,128]{1,0:T(8,128)(2,1)S(1)}, bf16[528,128]{1,0:T(8,128)(2,1)S(1)}, u32[]{:S(2)}, u32[]{:S(2)}) collective-permute-start(bf16[528,128]{1,0:T(8,128)(2,1)S(1)} %get-tuple-element.79), channel_id=1, source_target_pairs={{0,12},{1,13},{2,14},{3,15},{4,8},{5,9},{6,10},{7,11},{8,4},{9,5},... | collective-permute-start | bytes 405512 | tf_op jit(solution)/shard_map/ppermute | solution.py:21
  47.8 6.5 %collective-permute-start.15 = (f32[8,128]{1,0:T(8,128)S(1)}, f32[8,128]{1,0:T(8,128)S(1)}, u32[]{:S(2)}, u32[]{:S(2)}) collective-permute-start(f32[8,128]{1,0:T(8,128)S(1)} %get-tuple-element.75.slope), channel_id=1, source_target_pairs={{0,4},{1,5},{2,6},{3,7},{4,0},{5,1},{6,2},{7,3},{8,12},{9,13},{10,... | collective-permute-start | bytes 12296 | tf_op jit(solution)/shard_map/ppermute | solution.py:21
  57.8 2.0 %collective-permute-start.20 = (bf16[2,2,64,1024]{3,2,1,0:T(8,128)(2,1)S(1)}, bf16[2,2,64,1024]{3,2,1,0:T(8,128)(2,1)S(1)}, u32[]{:S(2)}, u32[]{:S(2)}) collective-permute-start(bf16[2,2,64,1024]{3,2,1,0:T(8,128)(2,1)S(1)} %get-tuple-element.81), channel_id=1, source_target_pairs={{0,1},{1,0},{2,3},{3,2},{4,5},{5,4},{6,7},{7,6},{8,9},{9,8},{10,11... | collective-permute-start | bytes 1572872 | tf_op jit(solution)/shard_map/ppermute | solution.py:21
  57.9 1.9 %collective-permute-start.21 = (f32[8,128]{1,0:T(8,128)S(1)}, f32[8,128]{1,0:T(8,128)S(1)}, u32[]{:S(2)}, u32[]{:S(2)}) collective-permute-start(f32[8,128]{1,0:T(8,128)S(1)} %get-tuple-element.82.slope), channel_id=1, source_target_pairs={{0,1},{1,0},{2,3},{3,2},{4,5},{5,4},{6,7},{7,6},{8,9},{9,8},{10,11... | collective-permute-start | bytes 12296 | tf_op jit(solution)/shard_map/ppermute | solution.py:21

commit v5 on v4

--- a/solution.py
+++ b/solution.py
@@ -280,12 +280,7 @@
                 other[kind, seq, :, lanes] = direct[block:]
 
 
-def fold_body(direct, coarse, slope, *refs):
-    *slopes, out, slope_out = refs
-    total = slope[...]
-    for ref in slopes:
-        total = total + ref[...]
-    slope_out[...] = total
+def fold_body(direct, coarse, done, out):
     rows = direct.shape[2]
     for kind in range(direct.shape[0]):
         for seq in range(direct.shape[1]):
@@ -293,21 +288,27 @@
             out[kind, seq] = (direct[kind, seq] + spread).astype(BF16)
 
 
-def relay_body(far, back, slope, slope_out, *far_outs):
-    tail = 2 * slope.shape[0]
-    total = slope[...] + one_part(back[pl.ds(far.shape[0], tail), :])
+def relay_body(far, back, slope, *refs):
+    *slopes, slope_out, keep, message = refs
+    rows = keep.shape[0]
+    total = slope[...] + one_part(back[pl.ds(2 * rows, 2 * slope.shape[0]), :])
+    for ref in slopes:
+        total = total + ref[...]
     slope_out[...] = total
-    ending = two_parts(total)
-    start = 0
-    for out in far_outs:
-        rows = out.shape[0] - tail
-        here = pl.ds(start, rows)
-        out[pl.ds(0, rows), :] = (far[here, :] + back[here, :].astype(F32)).astype(BF16)
-        out[pl.ds(rows, tail), :] = ending
-        start += rows
-
-
-def gather_body(levels_of, done, own, other, slope, slope_side, near, *refs):
+    keep[...] = far[pl.ds(0, rows), :] + back[pl.ds(0, rows), :].astype(F32)
+    message[pl.ds(0, rows), :] = (far[pl.ds(rows, rows), :] + back[pl.ds(rows, rows), :].astype(F32)).astype(BF16)
+    message[pl.ds(rows, 2 * slope.shape[0]), :] = two_parts(total)
+
+
+def meet_body(keep, back, slope, slope_out, message):
+    rows = keep.shape[0]
+    total = slope[...] + one_part(back[pl.ds(rows, 2 * slope.shape[0]), :])
+    slope_out[...] = total
+    message[pl.ds(0, rows), :] = (keep[...] + back[pl.ds(0, rows), :].astype(F32)).astype(BF16)
+    message[pl.ds(rows, 2 * slope.shape[0]), :] = two_parts(total)
+
+
+def gather_body(levels_of, done, own, other, slope, near, *refs):
     back, (kept, sent, slope_out) = refs[:-3], refs[-3:]
     kinds, seqs, block, width = own.shape
     heads = slope.shape[0]
@@ -324,10 +325,8 @@
                 total = dot(spread, jnp.concatenate(cells, axis=0))
                 kept[kind, seq, :, lanes] = (own[kind, seq, :, lanes] + total[:block]).astype(BF16)
                 sent[kind, seq, :, lanes] = (other[kind, seq, :, lanes] + total[block:]).astype(BF16)
-    all_slopes = slope[...] + slope_side[...]
-    for part, size in zip(back[1:], sizes[1:]):
-        all_slopes = all_slopes + one_part(part[pl.ds(kinds * seqs * heads * size, 2 * heads), :])
-    slope_out[...] = all_slopes
+    far, size = back[-1], sizes[-1]
+    slope_out[...] = slope[...] + one_part(far[pl.ds(kinds * seqs * heads * size, 2 * heads), :])
 
 
 def join_body(core, own, other, out, done, sems):
@@ -358,8 +357,8 @@
     seqs, block, width = queries.shape
     heads = level_slope.shape[0]
     half, head = width // 2, width // heads
-    ctx_count, dp_count = lax.axis_size("ctx"), lax.axis_size("dp")
-    levels = ctx_count.bit_length() - 1
+    dp_count = lax.axis_size("dp")
+    levels = 4
     position = lax.axis_index("ctx")
     core = (position % 2).astype(jnp.int32).reshape(1)
 
@@ -377,20 +376,17 @@
     kv_own, kv_other = call(
         keep_body, (part, part), (core, key_rows, value_rows, k_other, v_other), "keep_halves", scalars=1
     )
-    far = list(range(4, ctx_count // 2, 2))
-    far_levels = [m.bit_length() for m in far]
-    far_cells = [swap(cells[level - 1], 2 * m) for m, level in zip(far, far_levels)]
     near_cells = swap(cells[0], 2)
+    far_cells = swap(cells[2], 8)
     side_cells = swap(cells[1], 4)
-    across = call(coarser_body, like(2, seqs, block // 2, half), (near_cells,), "coarser")
-    across_cells = swap(across, 4)
-    far_sizes = [2 * block >> level for level in far_levels]
-    relayed_cells = [swap(c, 2) for c in far_cells]
+    across_cells = swap(call(coarser_body, like(2, seqs, block // 2, half), (near_cells,), "coarser"), 4)
+    far_side_cells = swap(far_cells, 4)
+    relayed_cells = [swap(far_cells, 2), swap(far_side_cells, 2)]
 
     groups = seqs * heads
-    early_levels, late_levels = (0, 0), (1, 2, *far_levels)
-    token_rows, cell_rows = 2 * block, block + block // 2 + sum(far_sizes)
-    rows = token_rows + cell_rows + block // 2 + sum(far_sizes)
+    far_size = block // 4
+    token_rows, cell_rows, late_rows = 2 * block, 2 * block, block
+    rows = token_rows + cell_rows + late_rows
 
     def score(levels_of, pieces, count):
         product = like(groups // 2, count, token_rows, dtype=F32)
@@ -404,33 +400,33 @@
         )
 
     token_pieces = [kv_own, kv_other]
-    cell_pieces = [near_cells, side_cells, *far_cells]
-    early = (*score(early_levels, token_pieces, token_rows), *score(late_levels, cell_pieces, cell_rows))
-    runs = [(0, token_rows), (1, block), (2, block // 2), *zip(far_levels, far_sizes)]
-    runs += [(2, block // 2), *zip(far_levels, far_sizes)]
-    far_rows = [groups * size for size in far_sizes]
-    tail = heads
+    cell_pieces = [near_cells, side_cells, far_cells, far_side_cells]
+    late_pieces = [across_cells, *relayed_cells]
+    early = (*score((0, 0), token_pieces, token_rows), *score((1, 2, 3, 3), cell_pieces, cell_rows))
+    runs = ((0, token_rows), (1, block), (2, block // 2), (3, far_size), (3, far_size))
+    runs += ((2, block // 2), (3, far_size), (3, far_size))
+    far_rows, tail = groups * far_size, heads
     slope_part = like(heads // 2, token_rows, dtype=F32)
     wide = like(*part.shape, dtype=F32)
     slope, near, across, side, far_direct, relay, dscore, probs = call(
-        functools.partial(attend_body, tuple(runs), head, tuple(far_sizes)),
+        functools.partial(attend_body, runs, head, (far_size, far_size)),
         (
             slope_part,
             wide,
             like(2, seqs, block // 2, half),
             like(groups * (block // 2), head),
-            like(sum(far_rows), head, dtype=F32),
-            like(sum(far_rows) + tail, head),
+            like(2 * far_rows, head, dtype=F32),
+            like(2 * far_rows + tail, head),
             like(groups // 2, rows, token_rows),
             like(groups // 2, token_rows, token_rows),
         ),
-        (core, level_slope, *early, qg_own, qg_other, across_cells, *relayed_cells),
+        (core, level_slope, *early, qg_own, qg_other, *late_pieces),
         "attend",
         scalars=2,
         flops=40 * seqs * token_rows * rows * half,
         scratch=(
-            pltpu.VMEM((groups // 2, block // 2 + sum(far_sizes), token_rows), F32),
-            pltpu.VMEM((groups // 2, block // 2 + sum(far_sizes), token_rows), F32),
+            pltpu.VMEM((groups // 2, late_rows, token_rows), F32),
+            pltpu.VMEM((groups // 2, late_rows, token_rows), F32),
             pltpu.VMEM((groups // 2, rows - token_rows, token_rows), BF16),
         ),
     )
@@ -438,7 +434,7 @@
     dq_own, dq_send, own, other = call(
         functools.partial(own_grads_body, head),
         (dq_part, dq_part, wide, wide),
-        (dscore, probs, qg_own, qg_other, *token_pieces, *cell_pieces, across_cells, *relayed_cells),
+        (dscore, probs, qg_own, qg_other, *token_pieces, *cell_pieces, *late_pieces),
         "own_grads",
         flops=40 * seqs * token_rows * rows * half,
     )
@@ -447,26 +443,26 @@
     relay_back = swap(relay, 2)
     slopes = [swap(slope, 2 * y, dp) for dp in range(1, dp_count) for y in range(2)]
     dq_other = swap(dq_send, 1)
-    near_total, slope = call(
-        fold_body, (like(*near.shape), slope_part), (near, across_back, slope, *slopes), "fold"
-    )
-    near_back = swap(near_total, 2)
+    message = like(far_rows + tail, head)
+    slope, keep, far_side = call(
+        relay_body,
+        (slope_part, like(far_rows, head, dtype=F32), message),
+        (far_direct, relay_back, slope, *slopes),
+        "relay",
+    )
+    far_side_back = swap(far_side, 4)
+    near_back = swap(call(fold_body, like(*near.shape), (near, across_back, slope), "fold"), 2)
     side_back = swap(side, 4)
-    slope, *far_total = call(
-        relay_body,
-        (slope_part, *(like(r + tail, head) for r in far_rows)),
-        (far_direct, relay_back, slope),
-        "relay",
-    )
-    far_back = [swap(message, 2 * m) for m, message in zip(far, far_total)]
+    slope, far_total = call(meet_body, (slope_part, message), (keep, far_side_back, slope), "meet")
+    far_back = swap(far_total, 8)
     whole = like(seqs, block, width)
     dq, done = call(
         join_body, (whole, slope_part), (core, dq_own, dq_other), "join_queries", scalars=1, hbm_out=1, copies=2
     )
     kept, sent, slope = call(
-        functools.partial(gather_body, (1, 2, *far_levels)),
+        functools.partial(gather_body, (1, 2, 3)),
         (part, part, slope_part),
-        (done, own, other, slope, swap(slope, 4), near_back, side_back, *far_back),
+        (done, own, other, slope, near_back, side_back, far_back),
         "gather_cells",
     )
     kv_grad_other = swap(sent, 1)
@@ -625,9 +621,7 @@
 
 
 def shards(queries, key_rows, value_rows, out_grad, level_slope):
-    levels = lax.axis_size("ctx").bit_length() - 1
-    cells = 2 * queries.shape[1] >> levels - 1
-    few = levels >= 4 and cells >= 16 and level_slope.shape[0] % 16 == 0
+    few = lax.axis_size("ctx") == 16 and queries.shape[1] % 64 == 0 and level_slope.shape[0] % 16 == 0
     form = paired if few else by_blocks
     return form(queries, key_rows, value_rows, out_grad, level_slope)
 

time: 61 us -> 58.2 us (0.954)
  waiting for transfers between devices: 25.1 us -> 21.9 us
    ppermute x20 -> x19, waiting for transfers between devices: 22.3 us -> 18.8 us  [swap(): lax.ppermute(value, 'ctx', [(source, source ^ apart) for source in range(...]
    ppermute x20 -> x19, starting transfers between devices: 19.5 us -> 21 us  [swap(): lax.ppermute(value, 'ctx', [(source, source ^ apart) for source in range(...]
    ppermute x2, starting transfers between devices: 3.21 us -> 2.15 us  [swap(): return lax.ppermute(value, ('dp', 'ctx'), pairs)]
    pallas_call x14 -> x15, Pallas kernels: 10.1 us -> 10.1 us  [call(): pl.pallas_call(body, out_shape=out_shape, in_specs=[SMEM] * scalars + [HB...]
  transfers between devices with their start and end apart: 22 -> 21, of which waited for: 11 -> 10; matrix products, arithmetic and copies ran while one was open for 0% -> 0% of each run, Pallas kernels for 9% -> 10%
where the time goes in v5:
time: 58.2 us; the launch traced here: 58 us
  starting transfers between devices  23.1 us (40%)
  waiting for transfers between devices  21.9 us (38%)
  Pallas kernels  10.1 us (17%)
  local copies, waits for them, and re-layouts  2.11 us (4%)
  between operations  0.78 us (1%)
    ppermute x19, starting transfers between devices, swap(): lax.ppermute(value, 'ctx', [(source, source ^ apart) for source in range(...  21 us
    ppermute x19, waiting for transfers between devices, swap(): lax.ppermute(value, 'ctx', [(source, source ^ apart) for source in range(...  18.8 us
    pallas_call x15, Pallas kernels, call(): pl.pallas_call(body, out_shape=out_shape, in_specs=[SMEM] * scalars + [HB...  10.1 us
    ppermute x2, waiting for transfers between devices, swap(): return lax.ppermute(value, ('dp', 'ctx'), pairs)  3.07 us
    ppermute x2, starting transfers between devices, swap(): return lax.ppermute(value, ('dp', 'ctx'), pairs)  2.15 us
    unnamed x14, local copies, waits for them, and re-layouts  2.11 us
  transfers between devices with their start and end apart: 21, of which 10 were waited for; matrix products, arithmetic and copies ran while one was open for 0% of the time, Pallas kernels for 10%

profile of v5, /device:TPU:0, one launch (start us, length us, event | category | flops | bytes accessed | tf_op | source)
XLA Modules:
  0.0 58.0 jit_solution(14396335492807141903)
XLA Ops:
  0.6 0.5 collective-permute-start.1
  1.1 0.1 collective-permute-start.2
  1.2 1.0 %copy-done = bf16[2,64,2048]{2,1,0:T(8,128)(2,1)S(1)} copy-done((bf16[2,64,2048]{2,1,0:T(8,128)(2,1)S(1)}, bf16[2,64,2048]{2,1,0:T(8,128)(2,1)}, u32[]{:S(2)}) %copy-start) | copy-done | bytes 524312
  2.3 1.0 %copy-done.2 = bf16[2,64,2048]{2,1,0:T(8,128)(2,1)S(1)} copy-done((bf16[2,64,2048]{2,1,0:T(8,128)(2,1)S(1)}, bf16[2,64,2048]{2,1,0:T(8,128)(2,1)}, u32[]{:S(2)}) %copy-start.2) | copy-done | bytes 524312
  3.3 0.4 own_summaries.1
  3.7 0.4 summaries.1
  4.2 0.0 copy-start.1
  4.2 0.0 copy-start.3
  4.2 3.0 %collective-permute-start.3 = (bf16[2,2,64,1024]{3,2,1,0:T(8,128)(2,1)S(1)}, bf16[2,2,64,1024]{3,2,1,0:T(8,128)(2,1)S(1)}, u32[]{:S(2)}, u32[]{:S(2)}) collective-permute-start(bf16[2,2,64,1024]{3,2,1,0:T(8,128)(2,1)S(1)} %get-tuple-element.55), channel_id=1, source_target_pairs={{0,2},{1,3},{2,0},{3,1},{4,6},{5,7},{6,4},{7,5},{8,10},{9,11},{10,... | collective-permute-start | bytes 1572872 | tf_op jit(solution)/shard_map/ppermute | solution.py:21
  7.2 0.1 split_qg.1
  7.3 0.1 collective-permute-start
  7.4 2.7 %collective-permute-start.5 = (bf16[2,2,16,1024]{3,2,1,0:T(8,128)(2,1)S(1)}, bf16[2,2,16,1024]{3,2,1,0:T(8,128)(2,1)S(1)}, u32[]{:S(2)}, u32[]{:S(2)}) collective-permute-start(bf16[2,2,16,1024]{3,2,1,0:T(8,128)(2,1)S(1)} %get-tuple-element.57), channel_id=1, source_target_pairs={{0,8},{1,9},{2,10},{3,11},{4,12},{5,13},{6,14},{7,15},{8,0},{9,1},... | collective-permute-start | bytes 393224 | tf_op jit(solution)/shard_map/ppermute | solution.py:21
  10.0 1.6 %collective-permute-start.4 = (bf16[2,2,32,1024]{3,2,1,0:T(8,128)(2,1)S(1)}, bf16[2,2,32,1024]{3,2,1,0:T(8,128)(2,1)S(1)}, u32[]{:S(2)}, u32[]{:S(2)}) collective-permute-start(bf16[2,2,32,1024]{3,2,1,0:T(8,128)(2,1)S(1)} %get-tuple-element.56), channel_id=1, source_target_pairs={{0,4},{1,5},{2,6},{3,7},{4,0},{5,1},{6,2},{7,3},{8,12},{9,13},{10,... | collective-permute-start | bytes 786440 | tf_op jit(solution)/shard_map/ppermute | solution.py:21
  11.6 5.5 %collective-permute-done.5.refs_2_.refs_4_ = bf16[2,2,16,1024]{3,2,1,0:T(8,128)(2,1)S(1)} collective-permute-done((bf16[2,2,16,1024]{3,2,1,0:T(8,128)(2,1)S(1)}, bf16[2,2,16,1024]{3,2,1,0:T(8,128)(2,1)S(1)}, u32[]{:S(2)}, u32[]{:S(2)}) %collective-permute-start.5) | collective-permute-done | bytes 131104 | tf_op jit(solution)/shard_map/ppermute | solution.py:21
  17.1 0.6 %collective-permute-start.6 = (bf16[2,2,16,1024]{3,2,1,0:T(8,128)(2,1)S(1)}, bf16[2,2,16,1024]{3,2,1,0:T(8,128)(2,1)S(1)}, u32[]{:S(2)}, u32[]{:S(2)}) collective-permute-start(bf16[2,2,16,1024]{3,2,1,0:T(8,128)(2,1)S(1)} %collective-permute-done.5.refs_2_.refs_4_), channel_id=1, source_target_pairs={{0,4},{1,5},{2,6},{3,7},{4,0},{5,1},{6,2},{7,3},{8,12},{9,13},{10,... | collective-permute-start | bytes 393224 | tf_op jit(solution)/shard_map/ppermute | solution.py:21
  17.7 1.6 %collective-permute-done.3.refs_0_.cells.refs_2_ = bf16[2,2,64,1024]{3,2,1,0:T(8,128)(2,1)S(1)} collective-permute-done((bf16[2,2,64,1024]{3,2,1,0:T(8,128)(2,1)S(1)}, bf16[2,2,64,1024]{3,2,1,0:T(8,128)(2,1)S(1)}, u32[]{:S(2)}, u32[]{:S(2)}) %collective-permute-start.3) | collective-permute-done | bytes 524320 | tf_op jit(solution)/shard_map/ppermute | solution.py:21
  19.4 0.2 coarser.1
  19.6 1.9 %collective-permute-start.7 = (bf16[2,2,32,1024]{3,2,1,0:T(8,128)(2,1)S(1)}, bf16[2,2,32,1024]{3,2,1,0:T(8,128)(2,1)S(1)}, u32[]{:S(2)}, u32[]{:S(2)}) collective-permute-start(bf16[2,2,32,1024]{3,2,1,0:T(8,128)(2,1)S(1)} %coarser.1), channel_id=1, source_target_pairs={{0,4},{1,5},{2,6},{3,7},{4,0},{5,1},{6,2},{7,3},{8,12},{9,13},{10,... | collective-permute-start | bytes 786440 | tf_op jit(solution)/shard_map/ppermute | solution.py:21
  21.4 0.1 keep_halves.1
  21.5 1.6 %collective-permute-start.8 = (bf16[2,2,16,1024]{3,2,1,0:T(8,128)(2,1)S(1)}, bf16[2,2,16,1024]{3,2,1,0:T(8,128)(2,1)S(1)}, u32[]{:S(2)}, u32[]{:S(2)}) collective-permute-start(bf16[2,2,16,1024]{3,2,1,0:T(8,128)(2,1)S(1)} %collective-permute-done.5.refs_2_.refs_4_), channel_id=1, source_target_pairs={{0,2},{1,3},{2,0},{3,1},{4,6},{5,7},{6,4},{7,5},{8,10},{9,11},{10,... | collective-permute-start | bytes 393224 | tf_op jit(solution)/shard_map/ppermute | solution.py:21
  23.1 0.6 %collective-permute-done.6.refs_3_.refs_5_ = bf16[2,2,16,1024]{3,2,1,0:T(8,128)(2,1)S(1)} collective-permute-done((bf16[2,2,16,1024]{3,2,1,0:T(8,128)(2,1)S(1)}, bf16[2,2,16,1024]{3,2,1,0:T(8,128)(2,1)S(1)}, u32[]{:S(2)}, u32[]{:S(2)}) %collective-permute-start.6) | collective-permute-done | bytes 131104 | tf_op jit(solution)/shard_map/ppermute | solution.py:21
  23.7 1.4 %scores.2 = (f32[16,128,128]{2,1,0:T(8,128)S(1)}, f32[16,128,128]{2,1,0:T(8,128)S(1)}, f32[16,8,128]{2,1,0:T(8,128)S(1)}) custom-call(s32[1]{0:T(128)} %bitcast.core, f32[16]{0:T(128)S(1)} %copy-done.6, bf16[2,2,64,1024]{3,2,1,0:T(8,128)(2,1)S(1)} %get-tuple-element.45.qg_own.refs_6_, bf16[2,2,64,1024]{3,2,1,0:T(8,128)(2,1)S(1)} %collective-permute-done.qg_other.refs_7_, ...), custom_call_target="tpu_custom_call" | custom-call | flops 1342177280 | bytes 4259908 | tf_op jit(solution)/shard_map/scores/pallas_call | solution.py:34
  25.1 1.4 %scores.3 = (f32[16,128,128]{2,1,0:T(8,128)S(1)}, f32[16,128,128]{2,1,0:T(8,128)S(1)}, f32[16,8,128]{2,1,0:T(8,128)S(1)}) custom-call(s32[1]{0:T(128)} %bitcast.core, f32[16]{0:T(128)S(1)} %copy-done.6, bf16[2,2,64,1024]{3,2,1,0:T(8,128)(2,1)S(1)} %get-tuple-element.45.qg_own.refs_6_, bf16[2,2,64,1024]{3,2,1,0:T(8,128)(2,1)S(1)} %collective-permute-done.qg_other.refs_7_, ...), custom_call_target="tpu_custom_call" | custom-call | flops 1342177280 | bytes 4259908 | tf_op jit(solution)/shard_map/scores/pallas_call | solution.py:34
  26.6 1.1 %collective-permute-done.8.refs_9_.refs_7_ = bf16[2,2,16,1024]{3,2,1,0:T(8,128)(2,1)S(1)} collective-permute-done((bf16[2,2,16,1024]{3,2,1,0:T(8,128)(2,1)S(1)}, bf16[2,2,16,1024]{3,2,1,0:T(8,128)(2,1)S(1)}, u32[]{:S(2)}, u32[]{:S(2)}) %collective-permute-start.8) | collective-permute-done | bytes 131104 | tf_op jit(solution)/shard_map/ppermute | solution.py:21
  27.7 1.4 %collective-permute-done.9.refs_10_.refs_8_ = bf16[2,2,16,1024]{3,2,1,0:T(8,128)(2,1)S(1)} collective-permute-done((bf16[2,2,16,1024]{3,2,1,0:T(8,128)(2,1)S(1)}, bf16[2,2,16,1024]{3,2,1,0:T(8,128)(2,1)S(1)}, u32[]{:S(2)}, u32[]{:S(2)}) %collective-permute-start.9) | collective-permute-done | bytes 131104 | tf_op jit(solution)/shard_map/ppermute | solution.py:21
  29.1 2.4 %attend.1 = (f32[8,128]{1,0:T(8,128)S(1)}, f32[2,2,64,1024]{3,2,1,0:T(8,128)S(1)}, bf16[2,2,32,1024]{3,2,1,0:T(8,128)(2,1)S(1)}, bf16[1024,128]{1,0:T(8,128)(2,1...) custom-call(s32[1]{0:T(128)} %bitcast.core, ...), custom_call_target="tpu_custom_call" | custom-call | flops 3355443200 | bytes 10100804 | tf_op jit(solution)/shard_map/attend/pallas_call | solution.py:34
  31.5 1.3 %collective-permute-start.11 = (bf16[1040,128]{1,0:T(8,128)(2,1)S(1)}, bf16[1040,128]{1,0:T(8,128)(2,1)S(1)}, u32[]{:S(2)}, u32[]{:S(2)}) collective-permute-start(bf16[1040,128]{1,0:T(8,128)(2,1)S(1)} %get-tuple-element.70), channel_id=1, source_target_pairs={{0,2},{1,3},{2,0},{3,1},{4,6},{5,7},{6,4},{7,5},{8,10},{9,11},{10,... | collective-permute-start | bytes 798728 | tf_op jit(solution)/shard_map/ppermute | solution.py:21
  32.8 1.1 %collective-permute-start.15 = (bf16[2,2,32,1024]{3,2,1,0:T(8,128)(2,1)S(1)}, bf16[2,2,32,1024]{3,2,1,0:T(8,128)(2,1)S(1)}, u32[]{:S(2)}, u32[]{:S(2)}) collective-permute-start(bf16[2,2,32,1024]{3,2,1,0:T(8,128)(2,1)S(1)} %get-tuple-element.77), channel_id=1, source_target_pairs={{0,4},{1,5},{2,6},{3,7},{4,0},{5,1},{6,2},{7,3},{8,12},{9,13},{10,... | collective-permute-start | bytes 786440 | tf_op jit(solution)/shard_map/ppermute | solution.py:21
  33.8 1.6 %collective-permute-start.13 = (f32[8,128]{1,0:T(8,128)S(1)}, f32[8,128]{1,0:T(8,128)S(1)}, u32[]{:S(2)}, u32[]{:S(2)}) collective-permute-start(f32[8,128]{1,0:T(8,128)S(1)} %get-tuple-element.71.slope), channel_id=1, source_target_pairs={{0,18},{1,19},{2,16},{3,17},{4,22},{5,23},{6,20},{7,21},{8,26},{9,... | collective-permute-start | bytes 12296 | tf_op jit(solution)/shard_map/ppermute | solution.py:24
  35.5 0.5 collective-permute-start.12
  36.0 2.5 %collective-permute-done.13.refs_1_ = f32[8,128]{1,0:T(8,128)S(1)} collective-permute-done((f32[8,128]{1,0:T(8,128)S(1)}, f32[8,128]{1,0:T(8,128)S(1)}, u32[]{:S(2)}, u32[]{:S(2)}) %collective-permute-start.13) | collective-permute-done | bytes 4128 | tf_op jit(solution)/shard_map/ppermute | solution.py:24
  38.5 0.6 %collective-permute-done.12.refs_0_ = f32[8,128]{1,0:T(8,128)S(1)} collective-permute-done((f32[8,128]{1,0:T(8,128)S(1)}, f32[8,128]{1,0:T(8,128)S(1)}, u32[]{:S(2)}, u32[]{:S(2)}) %collective-permute-start.12) | collective-permute-done | bytes 4128 | tf_op jit(solution)/shard_map/ppermute | solution.py:24
  39.1 0.1 relay.1
  39.1 1.3 %collective-permute-start.14 = (bf16[528,128]{1,0:T(8,128)(2,1)S(1)}, bf16[528,128]{1,0:T(8,128)(2,1)S(1)}, u32[]{:S(2)}, u32[]{:S(2)}) collective-permute-start(bf16[528,128]{1,0:T(8,128)(2,1)S(1)} %get-tuple-element.73), channel_id=1, source_target_pairs={{0,4},{1,5},{2,6},{3,7},{4,0},{5,1},{6,2},{7,3},{8,12},{9,13},{10,... | collective-permute-start | bytes 405512 | tf_op jit(solution)/shard_map/ppermute | solution.py:21
  40.5 0.3 fold.1
  40.7 1.1 %collective-permute-start.16 = (bf16[2,2,64,1024]{3,2,1,0:T(8,128)(2,1)S(1)}, bf16[2,2,64,1024]{3,2,1,0:T(8,128)(2,1)S(1)}, u32[]{:S(2)}, u32[]{:S(2)}) collective-permute-start(bf16[2,2,64,1024]{3,2,1,0:T(8,128)(2,1)S(1)} %fold.1), channel_id=1, source_target_pairs={{0,2},{1,3},{2,0},{3,1},{4,6},{5,7},{6,4},{7,5},{8,10},{9,11},{10,... | collective-permute-start | bytes 1572872 | tf_op jit(solution)/shard_map/ppermute | solution.py:21
  41.9 0.9 %own_grads.1 = (bf16[2,64,1024]{2,1,0:T(8,128)(2,1)S(1)}, bf16[2,64,1024]{2,1,0:T(8,128)(2,1)S(1)}, f32[2,2,64,1024]{3,2,1,0:T(8,128)S(1)}, f32[2,2,64,1024]{3,2,1,0:T(8,128)S(1)}) custom-call(bf16[16,320,128]{2,1,0:T(8,128)(2,1)S(1)} %get-tuple-element.61.dscore, bf16[16,128,128]{2,1,0:T(8,128)(2,1)S(1)} %get-tuple-element.62.probs, ...), custom_call_target="tpu_custom_call" | custom-call | flops 3355443200 | bytes 8126464 | tf_op jit(solution)/shard_map/own_grads/pallas_call | solution.py:34
  42.8 0.1 collective-permute-start.10
  42.9 1.1 %collective-permute-start.17 = (bf16[1024,128]{1,0:T(8,128)(2,1)S(1)}, bf16[1024,128]{1,0:T(8,128)(2,1)S(1)}, u32[]{:S(2)}, u32[]{:S(2)}) collective-permute-start(bf16[1024,128]{1,0:T(8,128)(2,1)S(1)} %get-tuple-element.78), channel_id=1, source_target_pairs={{0,4},{1,5},{2,6},{3,7},{4,0},{5,1},{6,2},{7,3},{8,12},{9,13},{10,... | collective-permute-start | bytes 786440 | tf_op jit(solution)/shard_map/ppermute | solution.py:21
  44.0 0.2 collective-permute-done.14.back
  44.3 2.5 %collective-permute-start.18 = (bf16[528,128]{1,0:T(8,128)(2,1)S(1)}, bf16[528,128]{1,0:T(8,128)(2,1)S(1)}, u32[]{:S(2)}, u32[]{:S(2)}) collective-permute-start(bf16[528,128]{1,0:T(8,128)(2,1)S(1)} %get-tuple-element.79), channel_id=1, source_target_pairs={{0,8},{1,9},{2,10},{3,11},{4,12},{5,13},{6,14},{7,15},{8,0},{9,1},... | collective-permute-start | bytes 405512 | tf_op jit(solution)/shard_map/ppermute | solution.py:21
  46.7 0.8 %join_queries.1 = (bf16[2,64,2048]{2,1,0:T(8,128)(2,1)}, f32[8,128]{1,0:T(8,128)S(1)}) custom-call(s32[1]{0:T(128)} %bitcast.core, bf16[2,64,1024]{2,1,0:T(8,128)(2,1)S(1)} %get-tuple-element.63.own, bf16[2,64,1024]{2,1,0:T(8,128)(2,1)S(1)} %collective-permute-done.10.other), custom_call_target="tpu_custom_call" | custom-call | bytes 1052676 | tf_op jit(solution)/shard_map/join_queries/pallas_call | solution.py:34
  47.6 6.9 %collective-permute-done.17.refs_0_ = bf16[1024,128]{1,0:T(8,128)(2,1)S(1)} collective-permute-done((bf16[1024,128]{1,0:T(8,128)(2,1)S(1)}, bf16[1024,128]{1,0:T(8,128)(2,1)S(1)}, u32[]{:S(2)}, u32[]{:S(2)}) %collective-permute-start.17) | collective-permute-done | bytes 262176 | tf_op jit(solution)/shard_map/ppermute | solution.py:21
  54.5 0.5 gather_cells.1
  55.0 0.1 collective-permute-start.19
  55.1 0.5 collective-permute-start.20
  55.6 1.4 %collective-permute-done.20.slope_other = f32[8,128]{1,0:T(8,128)S(1)} collective-permute-done((f32[8,128]{1,0:T(8,128)S(1)}, f32[8,128]{1,0:T(8,128)S(1)}, u32[]{:S(2)}, u32[]{:S(2)}) %collective-permute-start.20) | collective-permute-done | bytes 4128 | tf_op jit(solution)/shard_map/ppermute | solution.py:21
  57.0 1.0 %join_kv.1 = (bf16[2,64,2048]{2,1,0:T(8,128)(2,1)}, bf16[2,64,2048]{2,1,0:T(8,128)(2,1)}, f32[1,16]{1,0:T(1,128)}) custom-call(s32[1]{0:T(128)} %bitcast.core, bf16[2,2,64,1024]{3,2,1,0:T(8,128)(2,1)S(1)} %get-tuple-element.80.own, bf16[2,2,64,1024]{3,2,1,0:T(8,128)(2,1)S(1)} %collective-permute-done.19.other, f32[8,128]{1,0:T(8,128)S(1)} %get-tuple-element.82.slope, ...), custom_call_target="tpu_custom_call" | custom-call | bytes 2105412 | tf_op jit(solution)/shard_map/join_kv/pallas_call | solution.py:34
  (23 shorter events, 0.1 us)
Async XLA Ops:
  0.6 3.1 %collective-permute-start.1 = (bf16[2,64,2048]{2,1,0:T(8,128)(2,1)}, bf16[2,64,2048]{2,1,0:T(8,128)(2,1)S(1)}, u32[]{:S(2)}, u32[]{:S(2)}) collective-permute-start(bf16[2,64,2048]{2,1,0:T(8,128)(2,1)} %k.3), channel_id=1, source_target_pairs={{0,1},{1,0},{2,3},{3,2},{4,5},{5,4},{6,7},{7,6},{8,9},{9,8},{10,11... | collective-permute-start | bytes 1572872 | tf_op jit(solution)/shard_map/ppermute | solution.py:21
  1.1 2.6 %collective-permute-start.2 = (bf16[2,64,2048]{2,1,0:T(8,128)(2,1)}, bf16[2,64,2048]{2,1,0:T(8,128)(2,1)S(1)}, u32[]{:S(2)}, u32[]{:S(2)}) collective-permute-start(bf16[2,64,2048]{2,1,0:T(8,128)(2,1)} %v.3), channel_id=1, source_target_pairs={{0,1},{1,0},{2,3},{3,2},{4,5},{5,4},{6,7},{7,6},{8,9},{9,8},{10,11... | collective-permute-start | bytes 1572872 | tf_op jit(solution)/shard_map/ppermute | solution.py:21
  1.2 1.0 %copy-start = (bf16[2,64,2048]{2,1,0:T(8,128)(2,1)S(1)}, bf16[2,64,2048]{2,1,0:T(8,128)(2,1)}, u32[]{:S(2)}) copy-start(bf16[2,64,2048]{2,1,0:T(8,128)(2,1)} %k.3) | copy-start | bytes 1572868
  2.3 1.0 %copy-start.2 = (bf16[2,64,2048]{2,1,0:T(8,128)(2,1)S(1)}, bf16[2,64,2048]{2,1,0:T(8,128)(2,1)}, u32[]{:S(2)}) copy-start(bf16[2,64,2048]{2,1,0:T(8,128)(2,1)} %v.3) | copy-start | bytes 1572868
  3.3 3.9 %copy-start.4 = (bf16[2,64,2048]{2,1,0:T(8,128)(2,1)S(1)}, bf16[2,64,2048]{2,1,0:T(8,128)(2,1)}, u32[]{:S(2)}) copy-start(bf16[2,64,2048]{2,1,0:T(8,128)(2,1)} %first.1) | copy-start | bytes 1572868
  3.3 3.9 %copy-start.5 = (bf16[2,64,2048]{2,1,0:T(8,128)(2,1)S(1)}, bf16[2,64,2048]{2,1,0:T(8,128)(2,1)}, u32[]{:S(2)}) copy-start(bf16[2,64,2048]{2,1,0:T(8,128)(2,1)} %second.1) | copy-start | bytes 1572868
  4.2 17.3 %copy-start.1 = (bf16[2,64,2048]{2,1,0:T(8,128)(2,1)S(1)}, bf16[2,64,2048]{2,1,0:T(8,128)(2,1)}, u32[]{:S(2)}) copy-start(bf16[2,64,2048]{2,1,0:T(8,128)(2,1)} %k.3) | copy-start | bytes 1572868
  4.2 17.3 %copy-start.3 = (bf16[2,64,2048]{2,1,0:T(8,128)(2,1)S(1)}, bf16[2,64,2048]{2,1,0:T(8,128)(2,1)}, u32[]{:S(2)}) copy-start(bf16[2,64,2048]{2,1,0:T(8,128)(2,1)} %v.3) | copy-start | bytes 1572868
  4.2 15.2 %collective-permute-start.3 = (bf16[2,2,64,1024]{3,2,1,0:T(8,128)(2,1)S(1)}, bf16[2,2,64,1024]{3,2,1,0:T(8,128)(2,1)S(1)}, u32[]{:S(2)}, u32[]{:S(2)}) collective-permute-start(bf16[2,2,64,1024]{3,2,1,0:T(8,128)(2,1)S(1)} %get-tuple-element.55), channel_id=1, source_target_pairs={{0,2},{1,3},{2,0},{3,1},{4,6},{5,7},{6,4},{7,5},{8,10},{9,11},{10,... | collective-permute-start | bytes 1572872 | tf_op jit(solution)/shard_map/ppermute | solution.py:21
  7.3 16.4 %collective-permute-start = (bf16[2,2,64,1024]{3,2,1,0:T(8,128)(2,1)S(1)}, bf16[2,2,64,1024]{3,2,1,0:T(8,128)(2,1)S(1)}, u32[]{:S(2)}, u32[]{:S(2)}) collective-permute-start(bf16[2,2,64,1024]{3,2,1,0:T(8,128)(2,1)S(1)} %get-tuple-element.46), channel_id=1, source_target_pairs={{0,1},{1,0},{2,3},{3,2},{4,5},{5,4},{6,7},{7,6},{8,9},{9,8},{10,11... | collective-permute-start | bytes 1572872 | tf_op jit(solution)/shard_map/ppermute | solution.py:21
  7.4 9.7 %collective-permute-start.5 = (bf16[2,2,16,1024]{3,2,1,0:T(8,128)(2,1)S(1)}, bf16[2,2,16,1024]{3,2,1,0:T(8,128)(2,1)S(1)}, u32[]{:S(2)}, u32[]{:S(2)}) collective-permute-start(bf16[2,2,16,1024]{3,2,1,0:T(8,128)(2,1)S(1)} %get-tuple-element.57), channel_id=1, source_target_pairs={{0,8},{1,9},{2,10},{3,11},{4,12},{5,13},{6,14},{7,15},{8,0},{9,1},... | collective-permute-start | bytes 393224 | tf_op jit(solution)/shard_map/ppermute | solution.py:21
  10.0 13.7 %copy-start.6 = (f32[16]{0:T(128)S(1)}, f32[16]{0:T(128)}, u32[]{:S(2)}) copy-start(f32[16]{0:T(128)} %slope.5) | copy-start | bytes 196
  10.0 15.1 %collective-permute-start.4 = (bf16[2,2,32,1024]{3,2,1,0:T(8,128)(2,1)S(1)}, bf16[2,2,32,1024]{3,2,1,0:T(8,128)(2,1)S(1)}, u32[]{:S(2)}, u32[]{:S(2)}) collective-permute-start(bf16[2,2,32,1024]{3,2,1,0:T(8,128)(2,1)S(1)} %get-tuple-element.56), channel_id=1, source_target_pairs={{0,4},{1,5},{2,6},{3,7},{4,0},{5,1},{6,2},{7,3},{8,12},{9,13},{10,... | collective-permute-start | bytes 786440 | tf_op jit(solution)/shard_map/ppermute | solution.py:21
  17.1 6.6 %collective-permute-start.6 = (bf16[2,2,16,1024]{3,2,1,0:T(8,128)(2,1)S(1)}, bf16[2,2,16,1024]{3,2,1,0:T(8,128)(2,1)S(1)}, u32[]{:S(2)}, u32[]{:S(2)}) collective-permute-start(bf16[2,2,16,1024]{3,2,1,0:T(8,128)(2,1)S(1)} %collective-permute-done.5.refs_2_.refs_4_), channel_id=1, source_target_pairs={{0,4},{1,5},{2,6},{3,7},{4,0},{5,1},{6,2},{7,3},{8,12},{9,13},{10,... | collective-permute-start | bytes 393224 | tf_op jit(solution)/shard_map/ppermute | solution.py:21
  19.6 9.5 %collective-permute-start.7 = (bf16[2,2,32,1024]{3,2,1,0:T(8,128)(2,1)S(1)}, bf16[2,2,32,1024]{3,2,1,0:T(8,128)(2,1)S(1)}, u32[]{:S(2)}, u32[]{:S(2)}) collective-permute-start(bf16[2,2,32,1024]{3,2,1,0:T(8,128)(2,1)S(1)} %coarser.1), channel_id=1, source_target_pairs={{0,4},{1,5},{2,6},{3,7},{4,0},{5,1},{6,2},{7,3},{8,12},{9,13},{10,... | collective-permute-start | bytes 786440 | tf_op jit(solution)/shard_map/ppermute | solution.py:21
  21.5 6.2 %collective-permute-start.8 = (bf16[2,2,16,1024]{3,2,1,0:T(8,128)(2,1)S(1)}, bf16[2,2,16,1024]{3,2,1,0:T(8,128)(2,1)S(1)}, u32[]{:S(2)}, u32[]{:S(2)}) collective-permute-start(bf16[2,2,16,1024]{3,2,1,0:T(8,128)(2,1)S(1)} %collective-permute-done.5.refs_2_.refs_4_), channel_id=1, source_target_pairs={{0,2},{1,3},{2,0},{3,1},{4,6},{5,7},{6,4},{7,5},{8,10},{9,11},{10,... | collective-permute-start | bytes 393224 | tf_op jit(solution)/shard_map/ppermute | solution.py:21
  23.7 5.4 %collective-permute-start.9 = (bf16[2,2,16,1024]{3,2,1,0:T(8,128)(2,1)S(1)}, bf16[2,2,16,1024]{3,2,1,0:T(8,128)(2,1)S(1)}, u32[]{:S(2)}, u32[]{:S(2)}) collective-permute-start(bf16[2,2,16,1024]{3,2,1,0:T(8,128)(2,1)S(1)} %collective-permute-done.6.refs_3_.refs_5_), channel_id=1, source_target_pairs={{0,2},{1,3},{2,0},{3,1},{4,6},{5,7},{6,4},{7,5},{8,10},{9,11},{10,... | collective-permute-start | bytes 393224 | tf_op jit(solution)/shard_map/ppermute | solution.py:21
  31.5 7.5 %collective-permute-start.11 = (bf16[1040,128]{1,0:T(8,128)(2,1)S(1)}, bf16[1040,128]{1,0:T(8,128)(2,1)S(1)}, u32[]{:S(2)}, u32[]{:S(2)}) collective-permute-start(bf16[1040,128]{1,0:T(8,128)(2,1)S(1)} %get-tuple-element.70), channel_id=1, source_target_pairs={{0,2},{1,3},{2,0},{3,1},{4,6},{5,7},{6,4},{7,5},{8,10},{9,11},{10,... | collective-permute-start | bytes 798728 | tf_op jit(solution)/shard_map/ppermute | solution.py:21
  32.8 7.7 %collective-permute-start.15 = (bf16[2,2,32,1024]{3,2,1,0:T(8,128)(2,1)S(1)}, bf16[2,2,32,1024]{3,2,1,0:T(8,128)(2,1)S(1)}, u32[]{:S(2)}, u32[]{:S(2)}) collective-permute-start(bf16[2,2,32,1024]{3,2,1,0:T(8,128)(2,1)S(1)} %get-tuple-element.77), channel_id=1, source_target_pairs={{0,4},{1,5},{2,6},{3,7},{4,0},{5,1},{6,2},{7,3},{8,12},{9,13},{10,... | collective-permute-start | bytes 786440 | tf_op jit(solution)/shard_map/ppermute | solution.py:21
  33.8 4.6 %collective-permute-start.13 = (f32[8,128]{1,0:T(8,128)S(1)}, f32[8,128]{1,0:T(8,128)S(1)}, u32[]{:S(2)}, u32[]{:S(2)}) collective-permute-start(f32[8,128]{1,0:T(8,128)S(1)} %get-tuple-element.71.slope), channel_id=1, source_target_pairs={{0,18},{1,19},{2,16},{3,17},{4,22},{5,23},{6,20},{7,21},{8,26},{9,... | collective-permute-start | bytes 12296 | tf_op jit(solution)/shard_map/ppermute | solution.py:24
  35.5 3.6 %collective-permute-start.12 = (f32[8,128]{1,0:T(8,128)S(1)}, f32[8,128]{1,0:T(8,128)S(1)}, u32[]{:S(2)}, u32[]{:S(2)}) collective-permute-start(f32[8,128]{1,0:T(8,128)S(1)} %get-tuple-element.71.slope), channel_id=1, source_target_pairs={{0,16},{1,17},{2,18},{3,19},{4,20},{5,21},{6,22},{7,23},{8,24},{9,... | collective-permute-start | bytes 12296 | tf_op jit(solution)/shard_map/ppermute | solution.py:24
  39.1 5.1 %collective-permute-start.14 = (bf16[528,128]{1,0:T(8,128)(2,1)S(1)}, bf16[528,128]{1,0:T(8,128)(2,1)S(1)}, u32[]{:S(2)}, u32[]{:S(2)}) collective-permute-start(bf16[528,128]{1,0:T(8,128)(2,1)S(1)} %get-tuple-element.73), channel_id=1, source_target_pairs={{0,4},{1,5},{2,6},{3,7},{4,0},{5,1},{6,2},{7,3},{8,12},{9,13},{10,... | collective-permute-start | bytes 405512 | tf_op jit(solution)/shard_map/ppermute | solution.py:21
  40.7 13.8 %collective-permute-start.16 = (bf16[2,2,64,1024]{3,2,1,0:T(8,128)(2,1)S(1)}, bf16[2,2,64,1024]{3,2,1,0:T(8,128)(2,1)S(1)}, u32[]{:S(2)}, u32[]{:S(2)}) collective-permute-start(bf16[2,2,64,1024]{3,2,1,0:T(8,128)(2,1)S(1)} %fold.1), channel_id=1, source_target_pairs={{0,2},{1,3},{2,0},{3,1},{4,6},{5,7},{6,4},{7,5},{8,10},{9,11},{10,... | collective-permute-start | bytes 1572872 | tf_op jit(solution)/shard_map/ppermute | solution.py:21
  42.8 4.0 %collective-permute-start.10 = (bf16[2,64,1024]{2,1,0:T(8,128)(2,1)S(1)}, bf16[2,64,1024]{2,1,0:T(8,128)(2,1)S(1)}, u32[]{:S(2)}, u32[]{:S(2)}) collective-permute-start(bf16[2,64,1024]{2,1,0:T(8,128)(2,1)S(1)} %get-tuple-element.64), channel_id=1, source_target_pairs={{0,1},{1,0},{2,3},{3,2},{4,5},{5,4},{6,7},{7,6},{8,9},{9,8},{10,11... | collective-permute-start | bytes 786440 | tf_op jit(solution)/shard_map/ppermute | solution.py:21
  42.9 11.6 %collective-permute-start.17 = (bf16[1024,128]{1,0:T(8,128)(2,1)S(1)}, bf16[1024,128]{1,0:T(8,128)(2,1)S(1)}, u32[]{:S(2)}, u32[]{:S(2)}) collective-permute-start(bf16[1024,128]{1,0:T(8,128)(2,1)S(1)} %get-tuple-element.78), channel_id=1, source_target_pairs={{0,4},{1,5},{2,6},{3,7},{4,0},{5,1},{6,2},{7,3},{8,12},{9,13},{10,... | collective-permute-start | bytes 786440 | tf_op jit(solution)/shard_map/ppermute | solution.py:21
  44.3 10.2 %collective-permute-start.18 = (bf16[528,128]{1,0:T(8,128)(2,1)S(1)}, bf16[528,128]{1,0:T(8,128)(2,1)S(1)}, u32[]{:S(2)}, u32[]{:S(2)}) collective-permute-start(bf16[528,128]{1,0:T(8,128)(2,1)S(1)} %get-tuple-element.79), channel_id=1, source_target_pairs={{0,8},{1,9},{2,10},{3,11},{4,12},{5,13},{6,14},{7,15},{8,0},{9,1},... | collective-permute-start | bytes 405512 | tf_op jit(solution)/shard_map/ppermute | solution.py:21
  55.0 2.0 %collective-permute-start.19 = (bf16[2,2,64,1024]{3,2,1,0:T(8,128)(2,1)S(1)}, bf16[2,2,64,1024]{3,2,1,0:T(8,128)(2,1)S(1)}, u32[]{:S(2)}, u32[]{:S(2)}) collective-permute-start(bf16[2,2,64,1024]{3,2,1,0:T(8,128)(2,1)S(1)} %get-tuple-element.81), channel_id=1, source_target_pairs={{0,1},{1,0},{2,3},{3,2},{4,5},{5,4},{6,7},{7,6},{8,9},{9,8},{10,11... | collective-permute-start | bytes 1572872 | tf_op jit(solution)/shard_map/ppermute | solution.py:21
  55.1 1.9 %collective-permute-start.20 = (f32[8,128]{1,0:T(8,128)S(1)}, f32[8,128]{1,0:T(8,128)S(1)}, u32[]{:S(2)}, u32[]{:S(2)}) collective-permute-start(f32[8,128]{1,0:T(8,128)S(1)} %get-tuple-element.82.slope), channel_id=1, source_target_pairs={{0,1},{1,0},{2,3},{3,2},{4,5},{5,4},{6,7},{7,6},{8,9},{9,8},{10,11... | collective-permute-start | bytes 12296 | tf_op jit(solution)/shard_map/ppermute | solution.py:21

commit v6 on v5

--- a/solution.py
+++ b/solution.py
@@ -154,9 +154,19 @@
     return jnp.concatenate([part[kind, seq, :, lanes] for part in parts], axis=0)
 
 
-def score_body(levels_of, head, core, slope, qg_own, qg_other, *refs):
+def turn_body(head, qg_own, qg_other, turned):
+    kinds, seqs, _, width = qg_own.shape
+    heads = width // head
+    for kind in range(kinds):
+        for h in range(heads):
+            for seq in range(seqs):
+                lanes = slice(h * head, (h + 1) * head)
+                turned[kind, seq * heads + h] = stacked((qg_own, qg_other), kind, seq, lanes).T
+
+
+def score_body(levels_of, head, core, slope, turned, *refs):
     *pieces, weights, upstream, stats = refs
-    seqs, width = qg_own.shape[1], qg_own.shape[3]
+    seqs, width = pieces[0].shape[1], pieces[0].shape[3]
     heads = width // head
     scale = LOG2E / math.sqrt(head)
     for h in range(heads):
@@ -164,8 +174,8 @@
         step = slope[core[0] * heads + h] * LOG2E + 1.0
         for seq in range(seqs):
             at = seq * heads + h
-            raw = dot(stacked(pieces, 0, seq, lanes), stacked((qg_own, qg_other), 0, seq, lanes), 1, 1)
-            upstream[at] = dot(stacked(pieces, 1, seq, lanes), stacked((qg_own, qg_other), 1, seq, lanes), 1, 1)
+            raw = dot(stacked(pieces, 0, seq, lanes), turned[0, at])
+            upstream[at] = dot(stacked(pieces, 1, seq, lanes), turned[1, at])
             scores = with_bias(raw * scale, zip(levels_of, [piece.shape[2] for piece in pieces]), step)
             top = jnp.max(scores, axis=0, keepdims=True)
             spread = jnp.exp2(scores - top)
@@ -183,10 +193,14 @@
     return jnp.concatenate(parts, axis=0)
 
 
-def attend_body(runs, head, far_sizes, core, slope, *refs):
-    *refs, late_scores, late_up, probs_cells = refs
-    early, (qg_own, qg_other, *late), outs = refs[:6], refs[6:-8], refs[-8:]
-    slope_out, near, across, side, far, relay, dscore_out, probs_out = outs
+def by_eights(x):
+    return jnp.sum(x.reshape(x.shape[0] // 8, 8, x.shape[1]), axis=0)
+
+
+def attend_body(runs, head, core, slope, *refs):
+    *refs, late_scores, late_up = refs
+    early, (turned, qg_own, qg_other, *late), outs = refs[:6], refs[6:-5], refs[-5:]
+    slope_out, across, relay, dscore_out, probs_out = outs
     seqs, block, width = qg_own.shape[1:]
     heads = width // head
     scale = 1.0 / math.sqrt(head)
@@ -195,15 +209,15 @@
     early_rows = token_rows + early[3].shape[1]
     bounds = (0, token_rows, early_rows, starts[-1])
     late_runs = [run for run, start in zip(runs, starts) if start >= early_rows]
-    far_count = len(far_sizes)
-    slabs = [2 * seqs * heads * sum(far_sizes[:i]) for i in range(far_count)]
+    sent_rows, far_size = starts[-4], runs[-1][1]
+    slab = 2 * seqs * heads * far_size
 
     def score(h, seq):
         at, lanes = seq * heads + h, slice(h * head, (h + 1) * head)
         step = slope[core[0] * heads + h] * LOG2E + 1.0
-        raw = dot(stacked(late, 0, seq, lanes), stacked((qg_own, qg_other), 0, seq, lanes), 1, 1)
+        raw = dot(stacked(late, 0, seq, lanes), turned[0, at])
         late_scores[at] = with_bias(raw * (scale * LOG2E), late_runs, step)
-        late_up[at] = dot(stacked(late, 1, seq, lanes), stacked((qg_own, qg_other), 1, seq, lanes), 1, 1)
+        late_up[at] = dot(stacked(late, 1, seq, lanes), turned[1, at])
 
     def normalise(h, seq):
         at = seq * heads + h
@@ -217,36 +231,32 @@
         probs = [early[0][at] * (shares[0] * inverse), early[3][at] * (shares[1] * inverse), weights * inverse]
         upstream = [early[1][at], early[4][at], late_up[at]]
         probs_low = [part.astype(BF16) for part in probs]
-        delta = sum(jnp.sum(p.astype(F32) * u, axis=0, keepdims=True) for p, u in zip(probs_low, upstream))
-        slope_sum = jnp.zeros_like(delta)
+        delta = sum(by_eights(p.astype(F32) * u) for p, u in zip(probs_low, upstream))
+        delta = jnp.sum(delta, axis=0, keepdims=True)
+        slope_sum = jnp.zeros((8, token_rows), F32)
         for p, u, low, high in zip(probs, upstream, bounds, bounds[1:]):
             dscore = p * (u - delta)
             for (level, rows), start in zip(runs, starts):
                 if level and low <= start < high:
                     here = dscore[start - low : start - low + rows]
-                    slope_sum = slope_sum + jnp.sum(here, axis=0, keepdims=True) * float(level)
+                    slope_sum = slope_sum + by_eights(here) * float(level)
             dscore_out[at, low:high] = dscore.astype(BF16)
-        probs_out[at] = probs_low[0]
-        probs_cells[at] = jnp.concatenate(probs_low[1:], axis=0)
+        probs_out[at] = jnp.concatenate(probs_low, axis=0)
         return slope_sum
 
     def gradients(h, seq):
         at, lanes = seq * heads + h, slice(h * head, (h + 1) * head)
-        dk = dot(dscore_out[at, token_rows:], stacked((qg_own, qg_other), 0, seq, lanes)) * scale
-        dv = dot(probs_cells[at], stacked((qg_own, qg_other), 1, seq, lanes))
+        dk = dot(dscore_out[at, sent_rows:], stacked((qg_own, qg_other), 0, seq, lanes)) * scale
+        dv = dot(probs_out[at, sent_rows:], stacked((qg_own, qg_other), 1, seq, lanes))
         for kind, direct in enumerate((dk, dv)):
-            parts = [direct[starts[i] - token_rows : starts[i + 1] - token_rows] for i in range(1, len(runs))]
             group = (kind * seqs + seq) * heads + h
-            near[kind, seq, :, lanes] = parts[0]
-            side[pl.ds(group * (block // 2), block // 2), :] = parts[1].astype(BF16)
-            across[kind, seq, :, lanes] = parts[2 + far_count].astype(BF16)
-            for i, size in enumerate(far_sizes):
-                here = pl.ds(slabs[i] + group * size, size)
-                far[here, :] = parts[2 + i]
-                relay[here, :] = parts[3 + far_count + i].astype(BF16)
+            first, direct = direct[:far_size], direct[far_size:]
+            across[kind, seq, :, lanes] = direct[:-far_size].astype(BF16)
+            relay[pl.ds(group * far_size, far_size), :] = first.astype(BF16)
+            relay[pl.ds(slab + group * far_size, far_size), :] = direct[-far_size:].astype(BF16)
 
     items = [(h, seq) for h in range(heads) for seq in range(seqs)]
-    behind = 2
+    behind = 4
     sums = {}
     for i in range(len(items) + 2 * behind):
         if i < len(items):
@@ -257,8 +267,32 @@
         if 0 <= i - 2 * behind < len(items):
             gradients(*items[i - 2 * behind])
     for h in range(heads):
-        slope_out[h : h + 1, :] = sum(sums[h, seq] for seq in range(seqs))
-    relay[pl.ds(far.shape[0], 2 * heads), :] = two_parts(slope_out[...])
+        slope_out[h : h + 1, :] = jnp.sum(sum(sums[h, seq] for seq in range(seqs)), axis=0, keepdims=True)
+    relay[pl.ds(2 * slab, 2 * heads), :] = two_parts(slope_out[...])
+
+
+def cell_grads_body(head, far_sizes, dscore, probs, qg_own, qg_other, near, side, far):
+    seqs, block, width = qg_own.shape[1:]
+    heads = width // head
+    scale = 1.0 / math.sqrt(head)
+    sizes = (block, block // 2, *far_sizes)
+    rows = slice(2 * block, 2 * block + sum(sizes))
+    for h in range(heads):
+        lanes = slice(h * head, (h + 1) * head)
+        for seq in range(seqs):
+            at = seq * heads + h
+            dk = dot(dscore[at, rows], stacked((qg_own, qg_other), 0, seq, lanes)) * scale
+            dv = dot(probs[at, rows], stacked((qg_own, qg_other), 1, seq, lanes))
+            for kind, direct in enumerate((dk, dv)):
+                group = (kind * seqs + seq) * heads + h
+                near[kind, seq, :, lanes] = direct[:block]
+                start = block + sizes[1]
+                side[pl.ds(group * sizes[1], sizes[1]), :] = direct[block:start].astype(BF16)
+                slab = 0
+                for size in far_sizes:
+                    far[pl.ds(slab + group * size, size), :] = direct[start : start + size]
+                    start += size
+                    slab += 2 * seqs * heads * size
 
 
 def own_grads_body(head, dscore, probs, qg_own, qg_other, *refs):
@@ -274,7 +308,7 @@
             dq_own[seq, :, lanes] = dq[:block]
             dq_send[seq, :, lanes] = dq[block:]
             dk = dot(dscore[at, : 2 * block], stacked((qg_own, qg_other), 0, seq, lanes)) * scale
-            dv = dot(probs[at], stacked((qg_own, qg_other), 1, seq, lanes))
+            dv = dot(probs[at, : 2 * block], stacked((qg_own, qg_other), 1, seq, lanes))
             for kind, direct in enumerate((dk, dv)):
                 own[kind, seq, :, lanes] = direct[:block]
                 other[kind, seq, :, lanes] = direct[block:]
@@ -385,50 +419,56 @@
 
     groups = seqs * heads
     far_size = block // 4
-    token_rows, cell_rows, late_rows = 2 * block, 2 * block, block
+    token_rows, cell_rows, late_rows = 2 * block, 2 * block + far_size, block - far_size
     rows = token_rows + cell_rows + late_rows
+
+    turned = call(
+        functools.partial(turn_body, head), like(2, groups // 2, head, token_rows), (qg_own, qg_other), "turn"
+    )
 
     def score(levels_of, pieces, count):
         product = like(groups // 2, count, token_rows, dtype=F32)
         return call(
             functools.partial(score_body, levels_of, head),
             (product, product, like(groups // 2, 8, token_rows, dtype=F32)),
-            (core, level_slope, qg_own, qg_other, *pieces),
+            (core, level_slope, turned, *pieces),
             "scores",
             scalars=2,
             flops=40 * seqs * token_rows * count * half,
         )
 
     token_pieces = [kv_own, kv_other]
-    cell_pieces = [near_cells, side_cells, far_cells, far_side_cells]
-    late_pieces = [across_cells, *relayed_cells]
-    early = (*score((0, 0), token_pieces, token_rows), *score((1, 2, 3, 3), cell_pieces, cell_rows))
+    cell_pieces = [near_cells, side_cells, far_cells, far_side_cells, relayed_cells[0]]
+    late_pieces = [across_cells, relayed_cells[1]]
+    early = (*score((0, 0), token_pieces, token_rows), *score((1, 2, 3, 3, 3), cell_pieces, cell_rows))
     runs = ((0, token_rows), (1, block), (2, block // 2), (3, far_size), (3, far_size))
-    runs += ((2, block // 2), (3, far_size), (3, far_size))
+    runs += ((3, far_size), (2, block // 2), (3, far_size))
     far_rows, tail = groups * far_size, heads
     slope_part = like(heads // 2, token_rows, dtype=F32)
     wide = like(*part.shape, dtype=F32)
-    slope, near, across, side, far_direct, relay, dscore, probs = call(
-        functools.partial(attend_body, runs, head, (far_size, far_size)),
+    slope, across, relay, dscore, probs = call(
+        functools.partial(attend_body, runs, head),
         (
             slope_part,
-            wide,
             like(2, seqs, block // 2, half),
-            like(groups * (block // 2), head),
-            like(2 * far_rows, head, dtype=F32),
             like(2 * far_rows + tail, head),
             like(groups // 2, rows, token_rows),
-            like(groups // 2, token_rows, token_rows),
+            like(groups // 2, rows, token_rows),
         ),
-        (core, level_slope, *early, qg_own, qg_other, *late_pieces),
+        (core, level_slope, *early, turned, qg_own, qg_other, *late_pieces),
         "attend",
         scalars=2,
         flops=40 * seqs * token_rows * rows * half,
         scratch=(
             pltpu.VMEM((groups // 2, late_rows, token_rows), F32),
             pltpu.VMEM((groups // 2, late_rows, token_rows), F32),
-            pltpu.VMEM((groups // 2, rows - token_rows, token_rows), BF16),
         ),
+    )
+    near, side, far_direct = call(
+        functools.partial(cell_grads_body, head, (far_size, far_size)),
+        (wide, like(groups * (block // 2), head), like(2 * far_rows, head, dtype=F32)),
+        (dscore, probs, qg_own, qg_other),
+        "cell_grads",
     )
     dq_part = like(seqs, block, half)
     dq_own, dq_send, own, other = call(

time: 58.2 us -> 57.6 us (0.990)
  waiting for transfers between devices: 21.9 us -> 19.8 us
  starting transfers between devices: 23.1 us -> 24.7 us
    ppermute x19, starting transfers between devices: 21 us -> 22.8 us  [swap(): lax.ppermute(value, 'ctx', [(source, source ^ apart) for source in range(...]
    ppermute x19, waiting for transfers between devices: 18.8 us -> 17.2 us  [swap(): lax.ppermute(value, 'ctx', [(source, source ^ apart) for source in range(...]
    pallas_call x15 -> x17, Pallas kernels: 10.1 us -> 9.98 us  [call(): pl.pallas_call(body, out_shape=out_shape, in_specs=[SMEM] * scalars + [HB...]
    unnamed x14 -> x10, local copies, waits for them, and re-layouts: 2.11 us -> 2.1 us
  transfers between devices with their start and end apart: 21 -> 21, of which waited for: 10 -> 8; matrix products, arithmetic and copies ran while one was open for 0% -> 0% of each run, Pallas kernels for 10% -> 11%
where the time goes in v6:
time: 57.6 us; the launch traced here: 57.4 us
  starting transfers between devices  24.7 us (43%)
  waiting for transfers between devices  19.8 us (34%)
  Pallas kernels  9.98 us (17%)
  local copies, waits for them, and re-layouts  2.1 us (4%)
  between operations  0.79 us (1%)
    ppermute x19, starting transfers between devices, swap(): lax.ppermute(value, 'ctx', [(source, source ^ apart) for source in range(...  22.8 us
    ppermute x19, waiting for transfers between devices, swap(): lax.ppermute(value, 'ctx', [(source, source ^ apart) for source in range(...  17.2 us
    pallas_call x17, Pallas kernels, call(): pl.pallas_call(body, out_shape=out_shape, in_specs=[SMEM] * scalars + [HB...  9.98 us
    ppermute x2, waiting for transfers between devices, swap(): return lax.ppermute(value, ('dp', 'ctx'), pairs)  2.61 us
    unnamed x10, local copies, waits for them, and re-layouts  2.1 us
    ppermute x2, starting transfers between devices, swap(): return lax.ppermute(value, ('dp', 'ctx'), pairs)  1.97 us
  transfers between devices with their start and end apart: 21, of which 8 were waited for; matrix products, arithmetic and copies ran while one was open for 0% of the time, Pallas kernels for 11%

profile of v6, /device:TPU:0, one launch (start us, length us, event | category | flops | bytes accessed | tf_op | source)
XLA Modules:
  0.0 57.4 jit_solution(12746105408146490)
XLA Ops:
  0.7 0.5 collective-permute-start.1
  1.2 0.1 collective-permute-start.2
  1.2 1.0 %copy-done.2 = bf16[2,64,2048]{2,1,0:T(8,128)(2,1)S(1)} copy-done((bf16[2,64,2048]{2,1,0:T(8,128)(2,1)S(1)}, bf16[2,64,2048]{2,1,0:T(8,128)(2,1)}, u32[]{:S(2)}) %copy-start.2) | copy-done | bytes 524312
  2.3 1.0 %copy-done.3 = bf16[2,64,2048]{2,1,0:T(8,128)(2,1)S(1)} copy-done((bf16[2,64,2048]{2,1,0:T(8,128)(2,1)S(1)}, bf16[2,64,2048]{2,1,0:T(8,128)(2,1)}, u32[]{:S(2)}) %copy-start.3) | copy-done | bytes 524312
  3.3 0.1 split_qg.1
  3.5 0.5 collective-permute-start
  4.0 0.4 own_summaries.1
  4.4 0.4 summaries.1
  4.8 2.7 %collective-permute-start.3 = (bf16[2,2,64,1024]{3,2,1,0:T(8,128)(2,1)S(1)}, bf16[2,2,64,1024]{3,2,1,0:T(8,128)(2,1)S(1)}, u32[]{:S(2)}, u32[]{:S(2)}) collective-permute-start(bf16[2,2,64,1024]{3,2,1,0:T(8,128)(2,1)S(1)} %get-tuple-element.55), channel_id=1, source_target_pairs={{0,2},{1,3},{2,0},{3,1},{4,6},{5,7},{6,4},{7,5},{8,10},{9,11},{10,... | collective-permute-start | bytes 1572872 | tf_op jit(solution)/shard_map/ppermute | solution.py:21
  7.4 2.6 %collective-permute-start.5 = (bf16[2,2,16,1024]{3,2,1,0:T(8,128)(2,1)S(1)}, bf16[2,2,16,1024]{3,2,1,0:T(8,128)(2,1)S(1)}, u32[]{:S(2)}, u32[]{:S(2)}) collective-permute-start(bf16[2,2,16,1024]{3,2,1,0:T(8,128)(2,1)S(1)} %get-tuple-element.57), channel_id=1, source_target_pairs={{0,8},{1,9},{2,10},{3,11},{4,12},{5,13},{6,14},{7,15},{8,0},{9,1},... | collective-permute-start | bytes 393224 | tf_op jit(solution)/shard_map/ppermute | solution.py:21
  10.0 1.6 %collective-permute-start.4 = (bf16[2,2,32,1024]{3,2,1,0:T(8,128)(2,1)S(1)}, bf16[2,2,32,1024]{3,2,1,0:T(8,128)(2,1)S(1)}, u32[]{:S(2)}, u32[]{:S(2)}) collective-permute-start(bf16[2,2,32,1024]{3,2,1,0:T(8,128)(2,1)S(1)} %get-tuple-element.56), channel_id=1, source_target_pairs={{0,4},{1,5},{2,6},{3,7},{4,0},{5,1},{6,2},{7,3},{8,12},{9,13},{10,... | collective-permute-start | bytes 786440 | tf_op jit(solution)/shard_map/ppermute | solution.py:21
  11.6 5.2 %collective-permute-done.5.refs_2_.refs_4_ = bf16[2,2,16,1024]{3,2,1,0:T(8,128)(2,1)S(1)} collective-permute-done((bf16[2,2,16,1024]{3,2,1,0:T(8,128)(2,1)S(1)}, bf16[2,2,16,1024]{3,2,1,0:T(8,128)(2,1)S(1)}, u32[]{:S(2)}, u32[]{:S(2)}) %collective-permute-start.5) | collective-permute-done | bytes 131104 | tf_op jit(solution)/shard_map/ppermute | solution.py:21
  16.8 0.6 %collective-permute-start.6 = (bf16[2,2,16,1024]{3,2,1,0:T(8,128)(2,1)S(1)}, bf16[2,2,16,1024]{3,2,1,0:T(8,128)(2,1)S(1)}, u32[]{:S(2)}, u32[]{:S(2)}) collective-permute-start(bf16[2,2,16,1024]{3,2,1,0:T(8,128)(2,1)S(1)} %collective-permute-done.5.refs_2_.refs_4_), channel_id=1, source_target_pairs={{0,4},{1,5},{2,6},{3,7},{4,0},{5,1},{6,2},{7,3},{8,12},{9,13},{10,... | collective-permute-start | bytes 393224 | tf_op jit(solution)/shard_map/ppermute | solution.py:21
  17.4 0.5 collective-permute-start.7
  18.0 0.1 keep_halves.1
  18.0 0.0 copy-start.4
  18.0 0.3 turn.1.turned.refs_6_
  18.4 1.7 %collective-permute-done.3.refs_0_.cells.refs_2_ = bf16[2,2,64,1024]{3,2,1,0:T(8,128)(2,1)S(1)} collective-permute-done((bf16[2,2,64,1024]{3,2,1,0:T(8,128)(2,1)S(1)}, bf16[2,2,64,1024]{3,2,1,0:T(8,128)(2,1)S(1)}, u32[]{:S(2)}, u32[]{:S(2)}) %collective-permute-start.3) | collective-permute-done | bytes 524320 | tf_op jit(solution)/shard_map/ppermute | solution.py:21
  20.1 0.2 coarser.1
  20.3 2.2 %collective-permute-start.8 = (bf16[2,2,32,1024]{3,2,1,0:T(8,128)(2,1)S(1)}, bf16[2,2,32,1024]{3,2,1,0:T(8,128)(2,1)S(1)}, u32[]{:S(2)}, u32[]{:S(2)}) collective-permute-start(bf16[2,2,32,1024]{3,2,1,0:T(8,128)(2,1)S(1)} %coarser.1), channel_id=1, source_target_pairs={{0,4},{1,5},{2,6},{3,7},{4,0},{5,1},{6,2},{7,3},{8,12},{9,13},{10,... | collective-permute-start | bytes 786440 | tf_op jit(solution)/shard_map/ppermute | solution.py:21
  22.5 1.0 %scores.2 = (f32[16,128,128]{2,1,0:T(8,128)S(1)}, f32[16,128,128]{2,1,0:T(8,128)S(1)}, f32[16,8,128]{2,1,0:T(8,128)S(1)}) custom-call(s32[1]{0:T(128)} %bitcast.core, f32[16]{0:T(128)S(1)} %copy-done.4, bf16[2,16,128,128]{3,2,1,0:T(8,128)(2,1)S(1)} %turn.1.turned.refs_6_, bf16[2,2,64,1024]{3,2,1,0:T(8,128)(2,1)S(1)} %get-tuple-element.47.refs_0_, ...), custom_call_target="tpu_custom_call" | custom-call | flops 1342177280 | bytes 4259908 | tf_op jit(solution)/shard_map/scores/pallas_call | solution.py:34
  23.5 1.6 %collective-permute-start.9 = (bf16[2,2,16,1024]{3,2,1,0:T(8,128)(2,1)S(1)}, bf16[2,2,16,1024]{3,2,1,0:T(8,128)(2,1)S(1)}, u32[]{:S(2)}, u32[]{:S(2)}) collective-permute-start(bf16[2,2,16,1024]{3,2,1,0:T(8,128)(2,1)S(1)} %collective-permute-done.6.refs_3_.refs_5_), channel_id=1, source_target_pairs={{0,2},{1,3},{2,0},{3,1},{4,6},{5,7},{6,4},{7,5},{8,10},{9,11},{10,... | collective-permute-start | bytes 393224 | tf_op jit(solution)/shard_map/ppermute | solution.py:21
  25.1 1.3 %scores.3 = (f32[16,144,128]{2,1,0:T(8,128)S(1)}, f32[16,144,128]{2,1,0:T(8,128)S(1)}, f32[16,8,128]{2,1,0:T(8,128)S(1)}) custom-call(s32[1]{0:T(128)} %bitcast.core, f32[16]{0:T(128)S(1)} %copy-done.4, bf16[2,16,128,128]{3,2,1,0:T(8,128)(2,1)S(1)} %turn.1.turned.refs_6_, bf16[2,2,64,1024]{3,2,1,0:T(8,128)(2,1)S(1)} %collective-permute-done.3.refs_0_.cells.refs_2_, ...), custom_call_target="tpu_custom_call" | custom-call | flops 1509949440 | bytes 4653124 | tf_op jit(solution)/shard_map/scores/pallas_call | solution.py:34
  26.5 2.1 %collective-permute-done.9.refs_10_.refs_8_ = bf16[2,2,16,1024]{3,2,1,0:T(8,128)(2,1)S(1)} collective-permute-done((bf16[2,2,16,1024]{3,2,1,0:T(8,128)(2,1)S(1)}, bf16[2,2,16,1024]{3,2,1,0:T(8,128)(2,1)S(1)}, u32[]{:S(2)}, u32[]{:S(2)}) %collective-permute-start.9) | collective-permute-done | bytes 131104 | tf_op jit(solution)/shard_map/ppermute | solution.py:21
  28.6 2.0 %attend.1 = (f32[8,128]{1,0:T(8,128)S(1)}, bf16[2,2,32,1024]{3,2,1,0:T(8,128)(2,1)S(1)}, bf16[1040,128]{1,0:T(8,128)(2,1)S(1)}, bf16[16,320,128]{2,1,0:T(8,128)(2,1)S(1)}, bf16[16,320,128]{2,1,0:T(8,128)(2,1)S(1)}) custom-call(s32[1]{0:T(128)} %bitcast.core, f32[16]{0:T(128)S(1)} %copy-done.4, f32[16,128,128]{2,1,0:T(8,128)S(1)} %get-tuple-element.49.refs_0_, ...), custom_call_target="tpu_custom_call" | custom-call | flops 3355443200 | bytes 10231876 | tf_op jit(solution)/shard_map/attend/pallas_call | solution.py:34
  30.6 1.6 %collective-permute-start.11 = (bf16[1040,128]{1,0:T(8,128)(2,1)S(1)}, bf16[1040,128]{1,0:T(8,128)(2,1)S(1)}, u32[]{:S(2)}, u32[]{:S(2)}) collective-permute-start(bf16[1040,128]{1,0:T(8,128)(2,1)S(1)} %get-tuple-element.70), channel_id=1, source_target_pairs={{0,2},{1,3},{2,0},{3,1},{4,6},{5,7},{6,4},{7,5},{8,10},{9,11},{10,... | collective-permute-start | bytes 798728 | tf_op jit(solution)/shard_map/ppermute | solution.py:21
  32.2 1.3 %collective-permute-start.15 = (bf16[2,2,32,1024]{3,2,1,0:T(8,128)(2,1)S(1)}, bf16[2,2,32,1024]{3,2,1,0:T(8,128)(2,1)S(1)}, u32[]{:S(2)}, u32[]{:S(2)}) collective-permute-start(bf16[2,2,32,1024]{3,2,1,0:T(8,128)(2,1)S(1)} %get-tuple-element.77), channel_id=1, source_target_pairs={{0,4},{1,5},{2,6},{3,7},{4,0},{5,1},{6,2},{7,3},{8,12},{9,13},{10,... | collective-permute-start | bytes 786440 | tf_op jit(solution)/shard_map/ppermute | solution.py:21
  33.5 1.4 %collective-permute-start.13 = (f32[8,128]{1,0:T(8,128)S(1)}, f32[8,128]{1,0:T(8,128)S(1)}, u32[]{:S(2)}, u32[]{:S(2)}) collective-permute-start(f32[8,128]{1,0:T(8,128)S(1)} %get-tuple-element.71.slope), channel_id=1, source_target_pairs={{0,18},{1,19},{2,16},{3,17},{4,22},{5,23},{6,20},{7,21},{8,26},{9,... | collective-permute-start | bytes 12296 | tf_op jit(solution)/shard_map/ppermute | solution.py:24
  35.0 0.5 collective-permute-start.12
  35.5 0.5 cell_grads.1
  36.0 2.1 %collective-permute-done.13.refs_1_ = f32[8,128]{1,0:T(8,128)S(1)} collective-permute-done((f32[8,128]{1,0:T(8,128)S(1)}, f32[8,128]{1,0:T(8,128)S(1)}, u32[]{:S(2)}, u32[]{:S(2)}) %collective-permute-start.13) | collective-permute-done | bytes 4128 | tf_op jit(solution)/shard_map/ppermute | solution.py:24
  38.0 0.5 collective-permute-done.12.refs_0_
  38.6 0.1 relay.1
  38.7 0.8 %collective-permute-start.14 = (bf16[528,128]{1,0:T(8,128)(2,1)S(1)}, bf16[528,128]{1,0:T(8,128)(2,1)S(1)}, u32[]{:S(2)}, u32[]{:S(2)}) collective-permute-start(bf16[528,128]{1,0:T(8,128)(2,1)S(1)} %get-tuple-element.73), channel_id=1, source_target_pairs={{0,4},{1,5},{2,6},{3,7},{4,0},{5,1},{6,2},{7,3},{8,12},{9,13},{10,... | collective-permute-start | bytes 405512 | tf_op jit(solution)/shard_map/ppermute | solution.py:21
  39.4 0.3 fold.1
  39.7 1.6 %collective-permute-start.16 = (bf16[2,2,64,1024]{3,2,1,0:T(8,128)(2,1)S(1)}, bf16[2,2,64,1024]{3,2,1,0:T(8,128)(2,1)S(1)}, u32[]{:S(2)}, u32[]{:S(2)}) collective-permute-start(bf16[2,2,64,1024]{3,2,1,0:T(8,128)(2,1)S(1)} %fold.1), channel_id=1, source_target_pairs={{0,2},{1,3},{2,0},{3,1},{4,6},{5,7},{6,4},{7,5},{8,10},{9,11},{10,... | collective-permute-start | bytes 1572872 | tf_op jit(solution)/shard_map/ppermute | solution.py:21
  41.3 0.9 %own_grads.1 = (bf16[2,64,1024]{2,1,0:T(8,128)(2,1)S(1)}, bf16[2,64,1024]{2,1,0:T(8,128)(2,1)S(1)}, f32[2,2,64,1024]{3,2,1,0:T(8,128)S(1)}, f32[2,2,64,1024]{3,2,1,0:T(8,128)S(1)}) custom-call(bf16[16,320,128]{2,1,0:T(8,128)(2,1)S(1)} %get-tuple-element.61.dscore, bf16[16,320,128]{2,1,0:T(8,128)(2,1)S(1)} %get-tuple-element.62.probs, ...), custom_call_target="tpu_custom_call" | custom-call | flops 3355443200 | bytes 8912896 | tf_op jit(solution)/shard_map/own_grads/pallas_call | solution.py:34
  42.2 0.1 collective-permute-start.10
  42.3 1.4 %collective-permute-start.17 = (bf16[1024,128]{1,0:T(8,128)(2,1)S(1)}, bf16[1024,128]{1,0:T(8,128)(2,1)S(1)}, u32[]{:S(2)}, u32[]{:S(2)}) collective-permute-start(bf16[1024,128]{1,0:T(8,128)(2,1)S(1)} %get-tuple-element.78), channel_id=1, source_target_pairs={{0,4},{1,5},{2,6},{3,7},{4,0},{5,1},{6,2},{7,3},{8,12},{9,13},{10,... | collective-permute-start | bytes 786440 | tf_op jit(solution)/shard_map/ppermute | solution.py:21
  43.7 0.1 collective-permute-done.14.back
  43.8 2.7 %collective-permute-start.18 = (bf16[528,128]{1,0:T(8,128)(2,1)S(1)}, bf16[528,128]{1,0:T(8,128)(2,1)S(1)}, u32[]{:S(2)}, u32[]{:S(2)}) collective-permute-start(bf16[528,128]{1,0:T(8,128)(2,1)S(1)} %get-tuple-element.79), channel_id=1, source_target_pairs={{0,8},{1,9},{2,10},{3,11},{4,12},{5,13},{6,14},{7,15},{8,0},{9,1},... | collective-permute-start | bytes 405512 | tf_op jit(solution)/shard_map/ppermute | solution.py:21
  46.4 0.8 %join_queries.1 = (bf16[2,64,2048]{2,1,0:T(8,128)(2,1)}, f32[8,128]{1,0:T(8,128)S(1)}) custom-call(s32[1]{0:T(128)} %bitcast.core, bf16[2,64,1024]{2,1,0:T(8,128)(2,1)S(1)} %get-tuple-element.63.own, bf16[2,64,1024]{2,1,0:T(8,128)(2,1)S(1)} %collective-permute-done.10.other), custom_call_target="tpu_custom_call" | custom-call | bytes 1052676 | tf_op jit(solution)/shard_map/join_queries/pallas_call | solution.py:34
  47.2 6.6 %collective-permute-done.17.refs_0_ = bf16[1024,128]{1,0:T(8,128)(2,1)S(1)} collective-permute-done((bf16[1024,128]{1,0:T(8,128)(2,1)S(1)}, bf16[1024,128]{1,0:T(8,128)(2,1)S(1)}, u32[]{:S(2)}, u32[]{:S(2)}) %collective-permute-start.17) | collective-permute-done | bytes 262176 | tf_op jit(solution)/shard_map/ppermute | solution.py:21
  53.9 0.5 gather_cells.1
  54.4 0.1 collective-permute-start.19
  54.5 0.5 collective-permute-start.20
  55.0 1.4 %collective-permute-done.20.slope_other = f32[8,128]{1,0:T(8,128)S(1)} collective-permute-done((f32[8,128]{1,0:T(8,128)S(1)}, f32[8,128]{1,0:T(8,128)S(1)}, u32[]{:S(2)}, u32[]{:S(2)}) %collective-permute-start.20) | collective-permute-done | bytes 4128 | tf_op jit(solution)/shard_map/ppermute | solution.py:21
  56.4 1.0 %join_kv.1 = (bf16[2,64,2048]{2,1,0:T(8,128)(2,1)}, bf16[2,64,2048]{2,1,0:T(8,128)(2,1)}, f32[1,16]{1,0:T(1,128)}) custom-call(s32[1]{0:T(128)} %bitcast.core, bf16[2,2,64,1024]{3,2,1,0:T(8,128)(2,1)S(1)} %get-tuple-element.80.own, bf16[2,2,64,1024]{3,2,1,0:T(8,128)(2,1)S(1)} %collective-permute-done.19.other, f32[8,128]{1,0:T(8,128)S(1)} %get-tuple-element.82.slope, ...), custom_call_target="tpu_custom_call" | custom-call | bytes 2105412 | tf_op jit(solution)/shard_map/join_kv/pallas_call | solution.py:34
  (21 shorter events, 0.1 us)
Async XLA Ops:
  0.6 3.3 %copy-start = (bf16[2,64,2048]{2,1,0:T(8,128)(2,1)S(1)}, bf16[2,64,2048]{2,1,0:T(8,128)(2,1)}, u32[]{:S(2)}) copy-start(bf16[2,64,2048]{2,1,0:T(8,128)(2,1)} %k.3) | copy-start | bytes 1572868
  0.6 3.3 %copy-start.1 = (bf16[2,64,2048]{2,1,0:T(8,128)(2,1)S(1)}, bf16[2,64,2048]{2,1,0:T(8,128)(2,1)}, u32[]{:S(2)}) copy-start(bf16[2,64,2048]{2,1,0:T(8,128)(2,1)} %v.3) | copy-start | bytes 1572868
  0.7 3.7 %collective-permute-start.1 = (bf16[2,64,2048]{2,1,0:T(8,128)(2,1)}, bf16[2,64,2048]{2,1,0:T(8,128)(2,1)S(1)}, u32[]{:S(2)}, u32[]{:S(2)}) collective-permute-start(bf16[2,64,2048]{2,1,0:T(8,128)(2,1)} %k.3), channel_id=1, source_target_pairs={{0,1},{1,0},{2,3},{3,2},{4,5},{5,4},{6,7},{7,6},{8,9},{9,8},{10,11... | collective-permute-start | bytes 1572872 | tf_op jit(solution)/shard_map/ppermute | solution.py:21
  1.2 3.2 %collective-permute-start.2 = (bf16[2,64,2048]{2,1,0:T(8,128)(2,1)}, bf16[2,64,2048]{2,1,0:T(8,128)(2,1)S(1)}, u32[]{:S(2)}, u32[]{:S(2)}) collective-permute-start(bf16[2,64,2048]{2,1,0:T(8,128)(2,1)} %v.3), channel_id=1, source_target_pairs={{0,1},{1,0},{2,3},{3,2},{4,5},{5,4},{6,7},{7,6},{8,9},{9,8},{10,11... | collective-permute-start | bytes 1572872 | tf_op jit(solution)/shard_map/ppermute | solution.py:21
  1.2 1.0 %copy-start.2 = (bf16[2,64,2048]{2,1,0:T(8,128)(2,1)S(1)}, bf16[2,64,2048]{2,1,0:T(8,128)(2,1)}, u32[]{:S(2)}) copy-start(bf16[2,64,2048]{2,1,0:T(8,128)(2,1)} %first.1) | copy-start | bytes 1572868
  2.3 1.0 %copy-start.3 = (bf16[2,64,2048]{2,1,0:T(8,128)(2,1)S(1)}, bf16[2,64,2048]{2,1,0:T(8,128)(2,1)}, u32[]{:S(2)}) copy-start(bf16[2,64,2048]{2,1,0:T(8,128)(2,1)} %second.1) | copy-start | bytes 1572868
  3.5 14.6 %collective-permute-start = (bf16[2,2,64,1024]{3,2,1,0:T(8,128)(2,1)S(1)}, bf16[2,2,64,1024]{3,2,1,0:T(8,128)(2,1)S(1)}, u32[]{:S(2)}, u32[]{:S(2)}) collective-permute-start(bf16[2,2,64,1024]{3,2,1,0:T(8,128)(2,1)S(1)} %get-tuple-element.46), channel_id=1, source_target_pairs={{0,1},{1,0},{2,3},{3,2},{4,5},{5,4},{6,7},{7,6},{8,9},{9,8},{10,11... | collective-permute-start | bytes 1572872 | tf_op jit(solution)/shard_map/ppermute | solution.py:21
  4.8 15.3 %collective-permute-start.3 = (bf16[2,2,64,1024]{3,2,1,0:T(8,128)(2,1)S(1)}, bf16[2,2,64,1024]{3,2,1,0:T(8,128)(2,1)S(1)}, u32[]{:S(2)}, u32[]{:S(2)}) collective-permute-start(bf16[2,2,64,1024]{3,2,1,0:T(8,128)(2,1)S(1)} %get-tuple-element.55), channel_id=1, source_target_pairs={{0,2},{1,3},{2,0},{3,1},{4,6},{5,7},{6,4},{7,5},{8,10},{9,11},{10,... | collective-permute-start | bytes 1572872 | tf_op jit(solution)/shard_map/ppermute | solution.py:21
  7.4 9.4 %collective-permute-start.5 = (bf16[2,2,16,1024]{3,2,1,0:T(8,128)(2,1)S(1)}, bf16[2,2,16,1024]{3,2,1,0:T(8,128)(2,1)S(1)}, u32[]{:S(2)}, u32[]{:S(2)}) collective-permute-start(bf16[2,2,16,1024]{3,2,1,0:T(8,128)(2,1)S(1)} %get-tuple-element.57), channel_id=1, source_target_pairs={{0,8},{1,9},{2,10},{3,11},{4,12},{5,13},{6,14},{7,15},{8,0},{9,1},... | collective-permute-start | bytes 393224 | tf_op jit(solution)/shard_map/ppermute | solution.py:21
  10.0 15.1 %collective-permute-start.4 = (bf16[2,2,32,1024]{3,2,1,0:T(8,128)(2,1)S(1)}, bf16[2,2,32,1024]{3,2,1,0:T(8,128)(2,1)S(1)}, u32[]{:S(2)}, u32[]{:S(2)}) collective-permute-start(bf16[2,2,32,1024]{3,2,1,0:T(8,128)(2,1)S(1)} %get-tuple-element.56), channel_id=1, source_target_pairs={{0,4},{1,5},{2,6},{3,7},{4,0},{5,1},{6,2},{7,3},{8,12},{9,13},{10,... | collective-permute-start | bytes 786440 | tf_op jit(solution)/shard_map/ppermute | solution.py:21
  16.8 6.7 %collective-permute-start.6 = (bf16[2,2,16,1024]{3,2,1,0:T(8,128)(2,1)S(1)}, bf16[2,2,16,1024]{3,2,1,0:T(8,128)(2,1)S(1)}, u32[]{:S(2)}, u32[]{:S(2)}) collective-permute-start(bf16[2,2,16,1024]{3,2,1,0:T(8,128)(2,1)S(1)} %collective-permute-done.5.refs_2_.refs_4_), channel_id=1, source_target_pairs={{0,4},{1,5},{2,6},{3,7},{4,0},{5,1},{6,2},{7,3},{8,12},{9,13},{10,... | collective-permute-start | bytes 393224 | tf_op jit(solution)/shard_map/ppermute | solution.py:21
  17.4 7.7 %collective-permute-start.7 = (bf16[2,2,16,1024]{3,2,1,0:T(8,128)(2,1)S(1)}, bf16[2,2,16,1024]{3,2,1,0:T(8,128)(2,1)S(1)}, u32[]{:S(2)}, u32[]{:S(2)}) collective-permute-start(bf16[2,2,16,1024]{3,2,1,0:T(8,128)(2,1)S(1)} %collective-permute-done.5.refs_2_.refs_4_), channel_id=1, source_target_pairs={{0,2},{1,3},{2,0},{3,1},{4,6},{5,7},{6,4},{7,5},{8,10},{9,11},{10,... | collective-permute-start | bytes 393224 | tf_op jit(solution)/shard_map/ppermute | solution.py:21
  18.0 4.5 %copy-start.4 = (f32[16]{0:T(128)S(1)}, f32[16]{0:T(128)}, u32[]{:S(2)}) copy-start(f32[16]{0:T(128)} %slope.5) | copy-start | bytes 196
  20.3 8.3 %collective-permute-start.8 = (bf16[2,2,32,1024]{3,2,1,0:T(8,128)(2,1)S(1)}, bf16[2,2,32,1024]{3,2,1,0:T(8,128)(2,1)S(1)}, u32[]{:S(2)}, u32[]{:S(2)}) collective-permute-start(bf16[2,2,32,1024]{3,2,1,0:T(8,128)(2,1)S(1)} %coarser.1), channel_id=1, source_target_pairs={{0,4},{1,5},{2,6},{3,7},{4,0},{5,1},{6,2},{7,3},{8,12},{9,13},{10,... | collective-permute-start | bytes 786440 | tf_op jit(solution)/shard_map/ppermute | solution.py:21
  23.5 5.0 %collective-permute-start.9 = (bf16[2,2,16,1024]{3,2,1,0:T(8,128)(2,1)S(1)}, bf16[2,2,16,1024]{3,2,1,0:T(8,128)(2,1)S(1)}, u32[]{:S(2)}, u32[]{:S(2)}) collective-permute-start(bf16[2,2,16,1024]{3,2,1,0:T(8,128)(2,1)S(1)} %collective-permute-done.6.refs_3_.refs_5_), channel_id=1, source_target_pairs={{0,2},{1,3},{2,0},{3,1},{4,6},{5,7},{6,4},{7,5},{8,10},{9,11},{10,... | collective-permute-start | bytes 393224 | tf_op jit(solution)/shard_map/ppermute | solution.py:21
  30.6 8.0 %collective-permute-start.11 = (bf16[1040,128]{1,0:T(8,128)(2,1)S(1)}, bf16[1040,128]{1,0:T(8,128)(2,1)S(1)}, u32[]{:S(2)}, u32[]{:S(2)}) collective-permute-start(bf16[1040,128]{1,0:T(8,128)(2,1)S(1)} %get-tuple-element.70), channel_id=1, source_target_pairs={{0,2},{1,3},{2,0},{3,1},{4,6},{5,7},{6,4},{7,5},{8,10},{9,11},{10,... | collective-permute-start | bytes 798728 | tf_op jit(solution)/shard_map/ppermute | solution.py:21
  32.2 7.2 %collective-permute-start.15 = (bf16[2,2,32,1024]{3,2,1,0:T(8,128)(2,1)S(1)}, bf16[2,2,32,1024]{3,2,1,0:T(8,128)(2,1)S(1)}, u32[]{:S(2)}, u32[]{:S(2)}) collective-permute-start(bf16[2,2,32,1024]{3,2,1,0:T(8,128)(2,1)S(1)} %get-tuple-element.77), channel_id=1, source_target_pairs={{0,4},{1,5},{2,6},{3,7},{4,0},{5,1},{6,2},{7,3},{8,12},{9,13},{10,... | collective-permute-start | bytes 786440 | tf_op jit(solution)/shard_map/ppermute | solution.py:21
  33.5 4.5 %collective-permute-start.13 = (f32[8,128]{1,0:T(8,128)S(1)}, f32[8,128]{1,0:T(8,128)S(1)}, u32[]{:S(2)}, u32[]{:S(2)}) collective-permute-start(f32[8,128]{1,0:T(8,128)S(1)} %get-tuple-element.71.slope), channel_id=1, source_target_pairs={{0,18},{1,19},{2,16},{3,17},{4,22},{5,23},{6,20},{7,21},{8,26},{9,... | collective-permute-start | bytes 12296 | tf_op jit(solution)/shard_map/ppermute | solution.py:24
  35.0 3.6 %collective-permute-start.12 = (f32[8,128]{1,0:T(8,128)S(1)}, f32[8,128]{1,0:T(8,128)S(1)}, u32[]{:S(2)}, u32[]{:S(2)}) collective-permute-start(f32[8,128]{1,0:T(8,128)S(1)} %get-tuple-element.71.slope), channel_id=1, source_target_pairs={{0,16},{1,17},{2,18},{3,19},{4,20},{5,21},{6,22},{7,23},{8,24},{9,... | collective-permute-start | bytes 12296 | tf_op jit(solution)/shard_map/ppermute | solution.py:24
  38.7 5.1 %collective-permute-start.14 = (bf16[528,128]{1,0:T(8,128)(2,1)S(1)}, bf16[528,128]{1,0:T(8,128)(2,1)S(1)}, u32[]{:S(2)}, u32[]{:S(2)}) collective-permute-start(bf16[528,128]{1,0:T(8,128)(2,1)S(1)} %get-tuple-element.73), channel_id=1, source_target_pairs={{0,4},{1,5},{2,6},{3,7},{4,0},{5,1},{6,2},{7,3},{8,12},{9,13},{10,... | collective-permute-start | bytes 405512 | tf_op jit(solution)/shard_map/ppermute | solution.py:21
  39.7 14.2 %collective-permute-start.16 = (bf16[2,2,64,1024]{3,2,1,0:T(8,128)(2,1)S(1)}, bf16[2,2,64,1024]{3,2,1,0:T(8,128)(2,1)S(1)}, u32[]{:S(2)}, u32[]{:S(2)}) collective-permute-start(bf16[2,2,64,1024]{3,2,1,0:T(8,128)(2,1)S(1)} %fold.1), channel_id=1, source_target_pairs={{0,2},{1,3},{2,0},{3,1},{4,6},{5,7},{6,4},{7,5},{8,10},{9,11},{10,... | collective-permute-start | bytes 1572872 | tf_op jit(solution)/shard_map/ppermute | solution.py:21
  42.2 4.2 %collective-permute-start.10 = (bf16[2,64,1024]{2,1,0:T(8,128)(2,1)S(1)}, bf16[2,64,1024]{2,1,0:T(8,128)(2,1)S(1)}, u32[]{:S(2)}, u32[]{:S(2)}) collective-permute-start(bf16[2,64,1024]{2,1,0:T(8,128)(2,1)S(1)} %get-tuple-element.64), channel_id=1, source_target_pairs={{0,1},{1,0},{2,3},{3,2},{4,5},{5,4},{6,7},{7,6},{8,9},{9,8},{10,11... | collective-permute-start | bytes 786440 | tf_op jit(solution)/shard_map/ppermute | solution.py:21
  42.3 11.6 %collective-permute-start.17 = (bf16[1024,128]{1,0:T(8,128)(2,1)S(1)}, bf16[1024,128]{1,0:T(8,128)(2,1)S(1)}, u32[]{:S(2)}, u32[]{:S(2)}) collective-permute-start(bf16[1024,128]{1,0:T(8,128)(2,1)S(1)} %get-tuple-element.78), channel_id=1, source_target_pairs={{0,4},{1,5},{2,6},{3,7},{4,0},{5,1},{6,2},{7,3},{8,12},{9,13},{10,... | collective-permute-start | bytes 786440 | tf_op jit(solution)/shard_map/ppermute | solution.py:21
  43.8 10.1 %collective-permute-start.18 = (bf16[528,128]{1,0:T(8,128)(2,1)S(1)}, bf16[528,128]{1,0:T(8,128)(2,1)S(1)}, u32[]{:S(2)}, u32[]{:S(2)}) collective-permute-start(bf16[528,128]{1,0:T(8,128)(2,1)S(1)} %get-tuple-element.79), channel_id=1, source_target_pairs={{0,8},{1,9},{2,10},{3,11},{4,12},{5,13},{6,14},{7,15},{8,0},{9,1},... | collective-permute-start | bytes 405512 | tf_op jit(solution)/shard_map/ppermute | solution.py:21
  54.4 2.0 %collective-permute-start.19 = (bf16[2,2,64,1024]{3,2,1,0:T(8,128)(2,1)S(1)}, bf16[2,2,64,1024]{3,2,1,0:T(8,128)(2,1)S(1)}, u32[]{:S(2)}, u32[]{:S(2)}) collective-permute-start(bf16[2,2,64,1024]{3,2,1,0:T(8,128)(2,1)S(1)} %get-tuple-element.81), channel_id=1, source_target_pairs={{0,1},{1,0},{2,3},{3,2},{4,5},{5,4},{6,7},{7,6},{8,9},{9,8},{10,11... | collective-permute-start | bytes 1572872 | tf_op jit(solution)/shard_map/ppermute | solution.py:21
  54.5 1.9 %collective-permute-start.20 = (f32[8,128]{1,0:T(8,128)S(1)}, f32[8,128]{1,0:T(8,128)S(1)}, u32[]{:S(2)}, u32[]{:S(2)}) collective-permute-start(f32[8,128]{1,0:T(8,128)S(1)} %get-tuple-element.82.slope), channel_id=1, source_target_pairs={{0,1},{1,0},{2,3},{3,2},{4,5},{5,4},{6,7},{7,6},{8,9},{9,8},{10,11... | collective-permute-start | bytes 12296 | tf_op jit(solution)/shard_map/ppermute | solution.py:21

commit v7 on v6

--- a/solution.py
+++ b/solution.py
@@ -28,7 +28,7 @@
     return jax.ShapeDtypeStruct(shape, dtype)
 
 
-def call(body, out_shape, operands, name, scalars=0, hbm_in=0, hbm_out=0, copies=0, flops=0, limit=32, scratch=()):
+def call(body, out_shape, operands, name, scalars=0, hbm_in=0, hbm_out=0, copies=0, flops=0, limit=32, scratch=(), aliases={}):
     moved = sum(a.size * a.dtype.itemsize for a in jax.tree.leaves((operands, out_shape)))
     count = len(operands) - scalars - hbm_in
     return pl.pallas_call(
@@ -41,6 +41,7 @@
         scratch_shapes=[*scratch, *([pltpu.SemaphoreType.DMA((copies,))] if copies else [])],
         compiler_params=pltpu.CompilerParams(vmem_limit_bytes=int(limit * 2**20)),
         cost_estimate=pl.CostEstimate(flops=flops, bytes_accessed=moved, transcendentals=0),
+        input_output_aliases=aliases,
         name=name,
     )(*operands)
 
@@ -143,7 +144,7 @@
             rows = rows.astype(BF16).astype(F32)
 
 
-def coarser_body(cells, out):
+def coarser_body(cells, done, out):
     for kind in range(cells.shape[0]):
         for seq in range(cells.shape[1]):
             rows = cells[kind, seq]
@@ -342,25 +343,26 @@
     message[pl.ds(rows, 2 * slope.shape[0]), :] = two_parts(total)
 
 
-def gather_body(levels_of, done, own, other, slope, near, *refs):
-    back, (kept, sent, slope_out) = refs[:-3], refs[-3:]
-    kinds, seqs, block, width = own.shape
-    heads = slope.shape[0]
-    head = width // heads
+def gather_body(kind, levels_of, done, own, other, near, *refs):
+    back, (kept, sent) = refs[:-2], refs[-2:]
+    _, seqs, block, width = own.shape
     sizes = [2 * block >> level for level in levels_of[1:]]
+    head = back[0].shape[1]
     spread = jnp.concatenate([spread_matrix(2 * block, level) for level in levels_of], axis=1)
-    for kind in range(kinds):
-        for seq in range(seqs):
-            for h in range(heads):
-                lanes = slice(h * head, (h + 1) * head)
-                group = (kind * seqs + seq) * heads + h
-                cells = [near[kind, seq, :, lanes]]
-                cells += [part[pl.ds(group * size, size), :] for part, size in zip(back, sizes)]
-                total = dot(spread, jnp.concatenate(cells, axis=0))
-                kept[kind, seq, :, lanes] = (own[kind, seq, :, lanes] + total[:block]).astype(BF16)
-                sent[kind, seq, :, lanes] = (other[kind, seq, :, lanes] + total[block:]).astype(BF16)
-    far, size = back[-1], sizes[-1]
-    slope_out[...] = slope[...] + one_part(far[pl.ds(kinds * seqs * heads * size, 2 * heads), :])
+    for seq in range(seqs):
+        for h in range(width // head):
+            lanes = slice(h * head, (h + 1) * head)
+            group = (kind * seqs + seq) * (width // head) + h
+            cells = [near[kind, seq, :, lanes]]
+            cells += [part[pl.ds(group * size, size), :] for part, size in zip(back, sizes)]
+            total = dot(spread, jnp.concatenate(cells, axis=0))
+            kept[seq, :, lanes] = (own[kind, seq, :, lanes] + total[:block]).astype(BF16)
+            sent[seq, :, lanes] = (other[kind, seq, :, lanes] + total[block:]).astype(BF16)
+
+
+def total_body(slope, far, out):
+    rows = 2 * slope.shape[0]
+    out[...] = slope[...] + one_part(far[pl.ds(far.shape[0] - rows, rows), :])
 
 
 def join_body(core, own, other, out, done, sems):
@@ -369,12 +371,15 @@
     done[...] = jnp.zeros_like(done)
 
 
-def join_pair_body(core, own, other, slope, slope_other, first, second, slope_out, sums, sems):
-    mine, theirs = head_halves(core, own.shape[-1])
-    moves = []
-    for index, out in enumerate((first, second)):
-        moves.append((other.at[index], out.at[:, :, theirs]))
-        moves.append((own.at[index], out.at[:, :, mine]))
+def keep_grads_body(core, first, second, first_out, second_out, sems):
+    mine, _ = head_halves(core, first.shape[-1])
+    copy_all([(first, first_out.at[:, :, mine]), (second, second_out.at[:, :, mine])], sems)
+
+
+def join_pair_body(core, half_done, other_half_done, first, second, slope, slope_other, *refs):
+    first_out, second_out, slope_out, sums, sems = refs
+    _, theirs = head_halves(core, first.shape[-1])
+    moves = [(first, first_out.at[:, :, theirs]), (second, second_out.at[:, :, theirs])]
     copies = start_all(moves, sems)
     ours, rest = slope[...], slope_other[...]
     lower = jnp.where(core[0] == 0, ours, rest)
@@ -410,13 +415,6 @@
     kv_own, kv_other = call(
         keep_body, (part, part), (core, key_rows, value_rows, k_other, v_other), "keep_halves", scalars=1
     )
-    near_cells = swap(cells[0], 2)
-    far_cells = swap(cells[2], 8)
-    side_cells = swap(cells[1], 4)
-    across_cells = swap(call(coarser_body, like(2, seqs, block // 2, half), (near_cells,), "coarser"), 4)
-    far_side_cells = swap(far_cells, 4)
-    relayed_cells = [swap(far_cells, 2), swap(far_side_cells, 2)]
-
     groups = seqs * heads
     far_size = block // 4
     token_rows, cell_rows, late_rows = 2 * block, 2 * block + far_size, block - far_size
@@ -438,9 +436,19 @@
         )
 
     token_pieces = [kv_own, kv_other]
+    token_scores = score((0, 0), token_pieces, token_rows)
+
+    near_cells = swap(cells[0], 2)
+    far_cells = swap(cells[2], 8)
+    side_cells = swap(cells[1], 4)
+    across = call(coarser_body, like(2, seqs, block // 2, half), (near_cells, token_scores[2]), "coarser")
+    across_cells = swap(across, 4)
+    far_side_cells = swap(far_cells, 4)
+    relayed_cells = [swap(far_cells, 2), swap(far_side_cells, 2)]
+
     cell_pieces = [near_cells, side_cells, far_cells, far_side_cells, relayed_cells[0]]
     late_pieces = [across_cells, relayed_cells[1]]
-    early = (*score((0, 0), token_pieces, token_rows), *score((1, 2, 3, 3, 3), cell_pieces, cell_rows))
+    early = (*token_scores, *score((1, 2, 3, 3, 3), cell_pieces, cell_rows))
     runs = ((0, token_rows), (1, block), (2, block // 2), (3, far_size), (3, far_size))
     runs += ((3, far_size), (2, block // 2), (3, far_size))
     far_rows, tail = groups * far_size, heads
@@ -499,22 +507,31 @@
     dq, done = call(
         join_body, (whole, slope_part), (core, dq_own, dq_other), "join_queries", scalars=1, hbm_out=1, copies=2
     )
-    kept, sent, slope = call(
-        functools.partial(gather_body, (1, 2, 3)),
-        (part, part, slope_part),
-        (done, own, other, slope, near_back, side_back, far_back),
-        "gather_cells",
-    )
-    kv_grad_other = swap(sent, 1)
+    kept, others = [], []
+    for kind in range(2):
+        mine, sent = call(
+            functools.partial(gather_body, kind, (1, 2, 3)),
+            (dq_part, dq_part),
+            (done, own, other, near_back, side_back, far_back),
+            "gather_cells",
+        )
+        kept.append(mine)
+        others.append(swap(sent, 1))
+    slope = call(total_body, slope_part, (slope, far_back), "slope_terms")
+    halves = call(
+        keep_grads_body, (whole, whole), (core, *kept), "keep_grads", scalars=1, hbm_out=2, copies=2
+    )
     dk, dv, slope_grad = call(
         join_pair_body,
         (whole, whole, like(1, heads, dtype=F32)),
-        (core, kept, kv_grad_other, slope, swap(slope, 1)),
+        (core, *halves, *others, slope, swap(slope, 1)),
         "join_kv",
         scalars=1,
+        hbm_in=2,
         hbm_out=3,
-        copies=5,
+        copies=3,
         scratch=(pltpu.VMEM((1, heads), F32),),
+        aliases={1: 0, 2: 1},
     )
     return dq, dk, dv, slope_grad.reshape(heads)
 
@@ -661,7 +678,9 @@
 
 
 def shards(queries, key_rows, value_rows, out_grad, level_slope):
-    few = lax.axis_size("ctx") == 16 and queries.shape[1] % 64 == 0 and level_slope.shape[0] % 16 == 0
+    heads, width = level_slope.shape[0], queries.shape[2]
+    tiles = queries.shape[1] % 64 == 0 and heads % 16 == 0 and width // heads % 128 == 0
+    few = lax.axis_size("ctx") == 16 and tiles
     form = paired if few else by_blocks
     return form(queries, key_rows, value_rows, out_grad, level_slope)
 

time: 57.6 us -> 57.3 us (level)
  waiting for transfers between devices: 19.8 us -> 18.5 us
  Pallas kernels: 9.98 us -> 10.8 us
    ppermute x19 -> x20, waiting for transfers between devices: 17.2 us -> 15.9 us  [swap(): lax.ppermute(value, 'ctx', [(source, source ^ apart) for source in range(...]
    pallas_call x17 -> x20, Pallas kernels: 9.98 us -> 10.8 us  [call(): pl.pallas_call(body, out_shape=out_shape, in_specs=[SMEM] * scalars + [HB...]
    ppermute x19 -> x20, starting transfers between devices: 22.8 us -> 22.9 us  [swap(): lax.ppermute(value, 'ctx', [(source, source ^ apart) for source in range(...]
  transfers between devices with their start and end apart: 21 -> 22, of which waited for: 8 -> 10; matrix products, arithmetic and copies ran while one was open for 0% -> 0% of each run, Pallas kernels for 11% -> 13%
where the time goes in v7:
time: 57.3 us; the launch traced here: 57 us
  starting transfers between devices  24.8 us (43%)
  waiting for transfers between devices  18.5 us (32%)
  Pallas kernels  10.8 us (19%)
  local copies, waits for them, and re-layouts  2.1 us (4%)
  between operations  0.8 us (1%)
    ppermute x20, starting transfers between devices, swap(): lax.ppermute(value, 'ctx', [(source, source ^ apart) for source in range(...  22.9 us
    ppermute x20, waiting for transfers between devices, swap(): lax.ppermute(value, 'ctx', [(source, source ^ apart) for source in range(...  15.9 us
    pallas_call x20, Pallas kernels, call(): pl.pallas_call(body, out_shape=out_shape, in_specs=[SMEM] * scalars + [HB...  10.8 us
    ppermute x2, waiting for transfers between devices, swap(): return lax.ppermute(value, ('dp', 'ctx'), pairs)  2.61 us
    unnamed x10, local copies, waits for them, and re-layouts  2.1 us
    ppermute x2, starting transfers between devices, swap(): return lax.ppermute(value, ('dp', 'ctx'), pairs)  1.97 us
  transfers between devices with their start and end apart: 22, of which 10 were waited for; matrix products, arithmetic and copies ran while one was open for 0% of the time, Pallas kernels for 13%

profile of v7, /device:TPU:0, one launch (start us, length us, event | category | flops | bytes accessed | tf_op | source)
XLA Modules:
  0.0 57.0 jit_solution(4796964450534352311)
XLA Ops:
  0.7 0.5 collective-permute-start.1
  1.2 0.1 collective-permute-start.2
  1.2 1.0 %copy-done.2 = bf16[2,64,2048]{2,1,0:T(8,128)(2,1)S(1)} copy-done((bf16[2,64,2048]{2,1,0:T(8,128)(2,1)S(1)}, bf16[2,64,2048]{2,1,0:T(8,128)(2,1)}, u32[]{:S(2)}) %copy-start.2) | copy-done | bytes 524312
  2.3 1.0 %copy-done.3 = bf16[2,64,2048]{2,1,0:T(8,128)(2,1)S(1)} copy-done((bf16[2,64,2048]{2,1,0:T(8,128)(2,1)S(1)}, bf16[2,64,2048]{2,1,0:T(8,128)(2,1)}, u32[]{:S(2)}) %copy-start.3) | copy-done | bytes 524312
  3.3 0.1 split_qg.1
  3.5 0.5 collective-permute-start
  4.0 0.4 own_summaries.1
  4.4 0.4 summaries.1
  4.8 2.7 %collective-permute-start.3 = (bf16[2,2,64,1024]{3,2,1,0:T(8,128)(2,1)S(1)}, bf16[2,2,64,1024]{3,2,1,0:T(8,128)(2,1)S(1)}, u32[]{:S(2)}, u32[]{:S(2)}) collective-permute-start(bf16[2,2,64,1024]{3,2,1,0:T(8,128)(2,1)S(1)} %get-tuple-element.58), channel_id=1, source_target_pairs={{0,2},{1,3},{2,0},{3,1},{4,6},{5,7},{6,4},{7,5},{8,10},{9,11},{10,... | collective-permute-start | bytes 1572872 | tf_op jit(solution)/shard_map/ppermute | solution.py:21
  7.4 2.6 %collective-permute-start.5 = (bf16[2,2,16,1024]{3,2,1,0:T(8,128)(2,1)S(1)}, bf16[2,2,16,1024]{3,2,1,0:T(8,128)(2,1)S(1)}, u32[]{:S(2)}, u32[]{:S(2)}) collective-permute-start(bf16[2,2,16,1024]{3,2,1,0:T(8,128)(2,1)S(1)} %get-tuple-element.60), channel_id=1, source_target_pairs={{0,8},{1,9},{2,10},{3,11},{4,12},{5,13},{6,14},{7,15},{8,0},{9,1},... | collective-permute-start | bytes 393224 | tf_op jit(solution)/shard_map/ppermute | solution.py:21
  10.0 1.6 %collective-permute-start.4 = (bf16[2,2,32,1024]{3,2,1,0:T(8,128)(2,1)S(1)}, bf16[2,2,32,1024]{3,2,1,0:T(8,128)(2,1)S(1)}, u32[]{:S(2)}, u32[]{:S(2)}) collective-permute-start(bf16[2,2,32,1024]{3,2,1,0:T(8,128)(2,1)S(1)} %get-tuple-element.59), channel_id=1, source_target_pairs={{0,4},{1,5},{2,6},{3,7},{4,0},{5,1},{6,2},{7,3},{8,12},{9,13},{10,... | collective-permute-start | bytes 786440 | tf_op jit(solution)/shard_map/ppermute | solution.py:21
  11.7 0.3 turn.1.turned.refs_6_
  12.0 4.8 %collective-permute-done.5.refs_2_.refs_4_ = bf16[2,2,16,1024]{3,2,1,0:T(8,128)(2,1)S(1)} collective-permute-done((bf16[2,2,16,1024]{3,2,1,0:T(8,128)(2,1)S(1)}, bf16[2,2,16,1024]{3,2,1,0:T(8,128)(2,1)S(1)}, u32[]{:S(2)}, u32[]{:S(2)}) %collective-permute-start.5) | collective-permute-done | bytes 131104 | tf_op jit(solution)/shard_map/ppermute | solution.py:21
  16.8 0.5 collective-permute-start.7
  17.3 0.7 %collective-permute-start.6 = (bf16[2,2,16,1024]{3,2,1,0:T(8,128)(2,1)S(1)}, bf16[2,2,16,1024]{3,2,1,0:T(8,128)(2,1)S(1)}, u32[]{:S(2)}, u32[]{:S(2)}) collective-permute-start(bf16[2,2,16,1024]{3,2,1,0:T(8,128)(2,1)S(1)} %collective-permute-done.5.refs_2_.refs_4_), channel_id=1, source_target_pairs={{0,4},{1,5},{2,6},{3,7},{4,0},{5,1},{6,2},{7,3},{8,12},{9,13},{10,... | collective-permute-start | bytes 393224 | tf_op jit(solution)/shard_map/ppermute | solution.py:21
  18.0 1.0 %scores.2 = (f32[16,128,128]{2,1,0:T(8,128)S(1)}, f32[16,128,128]{2,1,0:T(8,128)S(1)}, f32[16,8,128]{2,1,0:T(8,128)S(1)}) custom-call(s32[1]{0:T(128)} %bitcast.core, f32[16]{0:T(128)S(1)} %copy-done.4, bf16[2,16,128,128]{3,2,1,0:T(8,128)(2,1)S(1)} %turn.1.turned.refs_6_, bf16[2,2,64,1024]{3,2,1,0:T(8,128)(2,1)S(1)} %get-tuple-element.50.refs_0_, ...), custom_call_target="tpu_custom_call" | custom-call | flops 1342177280 | bytes 4259908 | tf_op jit(solution)/shard_map/scores/pallas_call | solution.py:34
  19.0 1.2 %collective-permute-done.3.refs_0_.cells.refs_2_ = bf16[2,2,64,1024]{3,2,1,0:T(8,128)(2,1)S(1)} collective-permute-done((bf16[2,2,64,1024]{3,2,1,0:T(8,128)(2,1)S(1)}, bf16[2,2,64,1024]{3,2,1,0:T(8,128)(2,1)S(1)}, u32[]{:S(2)}, u32[]{:S(2)}) %collective-permute-start.3) | collective-permute-done | bytes 524320 | tf_op jit(solution)/shard_map/ppermute | solution.py:21
  20.2 0.2 coarser.1
  20.4 2.1 %collective-permute-start.8 = (bf16[2,2,32,1024]{3,2,1,0:T(8,128)(2,1)S(1)}, bf16[2,2,32,1024]{3,2,1,0:T(8,128)(2,1)S(1)}, u32[]{:S(2)}, u32[]{:S(2)}) collective-permute-start(bf16[2,2,32,1024]{3,2,1,0:T(8,128)(2,1)S(1)} %coarser.1), channel_id=1, source_target_pairs={{0,4},{1,5},{2,6},{3,7},{4,0},{5,1},{6,2},{7,3},{8,12},{9,13},{10,... | collective-permute-start | bytes 786440 | tf_op jit(solution)/shard_map/ppermute | solution.py:21
  22.5 0.1 collective-permute-done.6.refs_3_.refs_5_
  22.6 1.4 %collective-permute-start.9 = (bf16[2,2,16,1024]{3,2,1,0:T(8,128)(2,1)S(1)}, bf16[2,2,16,1024]{3,2,1,0:T(8,128)(2,1)S(1)}, u32[]{:S(2)}, u32[]{:S(2)}) collective-permute-start(bf16[2,2,16,1024]{3,2,1,0:T(8,128)(2,1)S(1)} %collective-permute-done.6.refs_3_.refs_5_), channel_id=1, source_target_pairs={{0,2},{1,3},{2,0},{3,1},{4,6},{5,7},{6,4},{7,5},{8,10},{9,11},{10,... | collective-permute-start | bytes 393224 | tf_op jit(solution)/shard_map/ppermute | solution.py:21
  24.0 1.3 %scores.3 = (f32[16,144,128]{2,1,0:T(8,128)S(1)}, f32[16,144,128]{2,1,0:T(8,128)S(1)}, f32[16,8,128]{2,1,0:T(8,128)S(1)}) custom-call(s32[1]{0:T(128)} %bitcast.core, f32[16]{0:T(128)S(1)} %copy-done.4, bf16[2,16,128,128]{3,2,1,0:T(8,128)(2,1)S(1)} %turn.1.turned.refs_6_, bf16[2,2,64,1024]{3,2,1,0:T(8,128)(2,1)S(1)} %collective-permute-done.3.refs_0_.cells.refs_2_, ...), custom_call_target="tpu_custom_call" | custom-call | flops 1509949440 | bytes 4653124 | tf_op jit(solution)/shard_map/scores/pallas_call | solution.py:34
  25.4 2.2 %collective-permute-done.9.refs_10_.refs_8_ = bf16[2,2,16,1024]{3,2,1,0:T(8,128)(2,1)S(1)} collective-permute-done((bf16[2,2,16,1024]{3,2,1,0:T(8,128)(2,1)S(1)}, bf16[2,2,16,1024]{3,2,1,0:T(8,128)(2,1)S(1)}, u32[]{:S(2)}, u32[]{:S(2)}) %collective-permute-start.9) | collective-permute-done | bytes 131104 | tf_op jit(solution)/shard_map/ppermute | solution.py:21
  27.6 0.7 %collective-permute-done.8.refs_9_.refs_7_ = bf16[2,2,32,1024]{3,2,1,0:T(8,128)(2,1)S(1)} collective-permute-done((bf16[2,2,32,1024]{3,2,1,0:T(8,128)(2,1)S(1)}, bf16[2,2,32,1024]{3,2,1,0:T(8,128)(2,1)S(1)}, u32[]{:S(2)}, u32[]{:S(2)}) %collective-permute-start.8) | collective-permute-done | bytes 262176 | tf_op jit(solution)/shard_map/ppermute | solution.py:21
  28.3 2.1 %attend.1 = (f32[8,128]{1,0:T(8,128)S(1)}, bf16[2,2,32,1024]{3,2,1,0:T(8,128)(2,1)S(1)}, bf16[1040,128]{1,0:T(8,128)(2,1)S(1)}, bf16[16,320,128]{2,1,0:T(8,128)(2,1)S(1)}, bf16[16,320,128]{2,1,0:T(8,128)(2,1)S(1)}) custom-call(s32[1]{0:T(128)} %bitcast.core, f32[16]{0:T(128)S(1)} %copy-done.4, f32[16,128,128]{2,1,0:T(8,128)S(1)} %get-tuple-element.52.refs_0_, ...), custom_call_target="tpu_custom_call" | custom-call | flops 3355443200 | bytes 10231876 | tf_op jit(solution)/shard_map/attend/pallas_call | solution.py:34
  30.4 1.6 %collective-permute-start.12 = (bf16[1040,128]{1,0:T(8,128)(2,1)S(1)}, bf16[1040,128]{1,0:T(8,128)(2,1)S(1)}, u32[]{:S(2)}, u32[]{:S(2)}) collective-permute-start(bf16[1040,128]{1,0:T(8,128)(2,1)S(1)} %get-tuple-element.75), channel_id=1, source_target_pairs={{0,2},{1,3},{2,0},{3,1},{4,6},{5,7},{6,4},{7,5},{8,10},{9,11},{10,... | collective-permute-start | bytes 798728 | tf_op jit(solution)/shard_map/ppermute | solution.py:21
  32.0 1.6 %collective-permute-start.11 = (bf16[2,2,32,1024]{3,2,1,0:T(8,128)(2,1)S(1)}, bf16[2,2,32,1024]{3,2,1,0:T(8,128)(2,1)S(1)}, u32[]{:S(2)}, u32[]{:S(2)}) collective-permute-start(bf16[2,2,32,1024]{3,2,1,0:T(8,128)(2,1)S(1)} %get-tuple-element.73), channel_id=1, source_target_pairs={{0,4},{1,5},{2,6},{3,7},{4,0},{5,1},{6,2},{7,3},{8,12},{9,13},{10,... | collective-permute-start | bytes 786440 | tf_op jit(solution)/shard_map/ppermute | solution.py:21
  33.5 1.4 %collective-permute-start.14 = (f32[8,128]{1,0:T(8,128)S(1)}, f32[8,128]{1,0:T(8,128)S(1)}, u32[]{:S(2)}, u32[]{:S(2)}) collective-permute-start(f32[8,128]{1,0:T(8,128)S(1)} %get-tuple-element.76.slope), channel_id=1, source_target_pairs={{0,18},{1,19},{2,16},{3,17},{4,22},{5,23},{6,20},{7,21},{8,26},{9,... | collective-permute-start | bytes 12296 | tf_op jit(solution)/shard_map/ppermute | solution.py:24
  35.0 0.5 collective-permute-start.13
  35.5 0.5 cell_grads.1
  36.0 2.1 %collective-permute-done.14.refs_1_ = f32[8,128]{1,0:T(8,128)S(1)} collective-permute-done((f32[8,128]{1,0:T(8,128)S(1)}, f32[8,128]{1,0:T(8,128)S(1)}, u32[]{:S(2)}, u32[]{:S(2)}) %collective-permute-start.14) | collective-permute-done | bytes 4128 | tf_op jit(solution)/shard_map/ppermute | solution.py:24
  38.1 0.5 collective-permute-done.13.refs_0_
  38.7 0.5 collective-permute-start.17
  39.2 0.3 fold.1
  39.5 1.6 %collective-permute-start.15 = (bf16[2,2,64,1024]{3,2,1,0:T(8,128)(2,1)S(1)}, bf16[2,2,64,1024]{3,2,1,0:T(8,128)(2,1)S(1)}, u32[]{:S(2)}, u32[]{:S(2)}) collective-permute-start(bf16[2,2,64,1024]{3,2,1,0:T(8,128)(2,1)S(1)} %fold.1), channel_id=1, source_target_pairs={{0,2},{1,3},{2,0},{3,1},{4,6},{5,7},{6,4},{7,5},{8,10},{9,11},{10,... | collective-permute-start | bytes 1572872 | tf_op jit(solution)/shard_map/ppermute | solution.py:21
  41.0 0.9 %own_grads.1 = (bf16[2,64,1024]{2,1,0:T(8,128)(2,1)S(1)}, bf16[2,64,1024]{2,1,0:T(8,128)(2,1)S(1)}, f32[2,2,64,1024]{3,2,1,0:T(8,128)S(1)}, f32[2,2,64,1024]{3,2,1,0:T(8,128)S(1)}) custom-call(bf16[16,320,128]{2,1,0:T(8,128)(2,1)S(1)} %get-tuple-element.64.dscore, bf16[16,320,128]{2,1,0:T(8,128)(2,1)S(1)} %get-tuple-element.65.probs, ...), custom_call_target="tpu_custom_call" | custom-call | flops 3355443200 | bytes 8912896 | tf_op jit(solution)/shard_map/own_grads/pallas_call | solution.py:34
  42.0 0.1 collective-permute-start.10
  42.0 1.6 %collective-permute-start.16 = (bf16[1024,128]{1,0:T(8,128)(2,1)S(1)}, bf16[1024,128]{1,0:T(8,128)(2,1)S(1)}, u32[]{:S(2)}, u32[]{:S(2)}) collective-permute-start(bf16[1024,128]{1,0:T(8,128)(2,1)S(1)} %get-tuple-element.78), channel_id=1, source_target_pairs={{0,4},{1,5},{2,6},{3,7},{4,0},{5,1},{6,2},{7,3},{8,12},{9,13},{10,... | collective-permute-start | bytes 786440 | tf_op jit(solution)/shard_map/ppermute | solution.py:21
  43.8 2.7 %collective-permute-start.18 = (bf16[528,128]{1,0:T(8,128)(2,1)S(1)}, bf16[528,128]{1,0:T(8,128)(2,1)S(1)}, u32[]{:S(2)}, u32[]{:S(2)}) collective-permute-start(bf16[528,128]{1,0:T(8,128)(2,1)S(1)} %get-tuple-element.81), channel_id=1, source_target_pairs={{0,8},{1,9},{2,10},{3,11},{4,12},{5,13},{6,14},{7,15},{8,0},{9,1},... | collective-permute-start | bytes 405512 | tf_op jit(solution)/shard_map/ppermute | solution.py:21
  46.4 0.8 %join_queries.1 = (bf16[2,64,2048]{2,1,0:T(8,128)(2,1)}, f32[8,128]{1,0:T(8,128)S(1)}) custom-call(s32[1]{0:T(128)} %bitcast.core, bf16[2,64,1024]{2,1,0:T(8,128)(2,1)S(1)} %get-tuple-element.66.own, bf16[2,64,1024]{2,1,0:T(8,128)(2,1)S(1)} %collective-permute-done.10.other), custom_call_target="tpu_custom_call" | custom-call | bytes 1052676 | tf_op jit(solution)/shard_map/join_queries/pallas_call | solution.py:34
  47.2 6.4 %collective-permute-done.16.refs_0_ = bf16[1024,128]{1,0:T(8,128)(2,1)S(1)} collective-permute-done((bf16[1024,128]{1,0:T(8,128)(2,1)S(1)}, bf16[1024,128]{1,0:T(8,128)(2,1)S(1)}, u32[]{:S(2)}, u32[]{:S(2)}) %collective-permute-start.16) | collective-permute-done | bytes 262176 | tf_op jit(solution)/shard_map/ppermute | solution.py:21
  53.7 0.4 gather_cells.3
  54.1 0.3 gather_cells.2
  54.5 0.6 collective-permute-start.19
  55.0 0.1 collective-permute-start.21
  55.1 0.8 %keep_grads.1 = (bf16[2,64,2048]{2,1,0:T(8,128)(2,1)}, bf16[2,64,2048]{2,1,0:T(8,128)(2,1)}) custom-call(s32[1]{0:T(128)} %bitcast.core, bf16[2,64,1024]{2,1,0:T(8,128)(2,1)S(1)} %get-tuple-element.82.first, bf16[2,64,1024]{2,1,0:T(8,128)(2,1)S(1)} %get-tuple-element.83.second), custom_call_target="tpu_custom_call" | custom-call | bytes 1572868 | tf_op jit(solution)/shard_map/keep_grads/pallas_call | solution.py:34
  55.9 0.3 collective-permute-done.21.slope_other
  56.2 0.8 %join_kv.1 = (bf16[2,64,2048]{2,1,0:T(8,128)(2,1)}, bf16[2,64,2048]{2,1,0:T(8,128)(2,1)}, f32[1,16]{1,0:T(1,128)}) custom-call(s32[1]{0:T(128)} %bitcast.core, bf16[2,64,2048]{2,1,0:T(8,128)(2,1)} %get-tuple-element.84.half_done, bf16[2,64,2048]{2,1,0:T(8,128)(2,1)} %get-tuple-element.85.other_half_done, ...), custom_call_target="tpu_custom_call", output_to_operand_aliasing={{0}: (1, {}), {1}: (2, {})} | custom-call | bytes 2629700 | tf_op jit(solution)/shard_map/join_kv/pallas_call | solution.py:34
  (26 shorter events, 0.3 us)
Async XLA Ops:
  0.6 3.3 %copy-start = (bf16[2,64,2048]{2,1,0:T(8,128)(2,1)S(1)}, bf16[2,64,2048]{2,1,0:T(8,128)(2,1)}, u32[]{:S(2)}) copy-start(bf16[2,64,2048]{2,1,0:T(8,128)(2,1)} %k.3) | copy-start | bytes 1572868
  0.6 3.3 %copy-start.1 = (bf16[2,64,2048]{2,1,0:T(8,128)(2,1)S(1)}, bf16[2,64,2048]{2,1,0:T(8,128)(2,1)}, u32[]{:S(2)}) copy-start(bf16[2,64,2048]{2,1,0:T(8,128)(2,1)} %v.3) | copy-start | bytes 1572868
  0.7 3.7 %collective-permute-start.1 = (bf16[2,64,2048]{2,1,0:T(8,128)(2,1)}, bf16[2,64,2048]{2,1,0:T(8,128)(2,1)S(1)}, u32[]{:S(2)}, u32[]{:S(2)}) collective-permute-start(bf16[2,64,2048]{2,1,0:T(8,128)(2,1)} %k.3), channel_id=1, source_target_pairs={{0,1},{1,0},{2,3},{3,2},{4,5},{5,4},{6,7},{7,6},{8,9},{9,8},{10,11... | collective-permute-start | bytes 1572872 | tf_op jit(solution)/shard_map/ppermute | solution.py:21
  1.2 3.2 %collective-permute-start.2 = (bf16[2,64,2048]{2,1,0:T(8,128)(2,1)}, bf16[2,64,2048]{2,1,0:T(8,128)(2,1)S(1)}, u32[]{:S(2)}, u32[]{:S(2)}) collective-permute-start(bf16[2,64,2048]{2,1,0:T(8,128)(2,1)} %v.3), channel_id=1, source_target_pairs={{0,1},{1,0},{2,3},{3,2},{4,5},{5,4},{6,7},{7,6},{8,9},{9,8},{10,11... | collective-permute-start | bytes 1572872 | tf_op jit(solution)/shard_map/ppermute | solution.py:21
  1.2 1.0 %copy-start.2 = (bf16[2,64,2048]{2,1,0:T(8,128)(2,1)S(1)}, bf16[2,64,2048]{2,1,0:T(8,128)(2,1)}, u32[]{:S(2)}) copy-start(bf16[2,64,2048]{2,1,0:T(8,128)(2,1)} %first.1) | copy-start | bytes 1572868
  2.3 1.0 %copy-start.3 = (bf16[2,64,2048]{2,1,0:T(8,128)(2,1)S(1)}, bf16[2,64,2048]{2,1,0:T(8,128)(2,1)}, u32[]{:S(2)}) copy-start(bf16[2,64,2048]{2,1,0:T(8,128)(2,1)} %second.1) | copy-start | bytes 1572868
  3.5 8.2 %collective-permute-start = (bf16[2,2,64,1024]{3,2,1,0:T(8,128)(2,1)S(1)}, bf16[2,2,64,1024]{3,2,1,0:T(8,128)(2,1)S(1)}, u32[]{:S(2)}, u32[]{:S(2)}) collective-permute-start(bf16[2,2,64,1024]{3,2,1,0:T(8,128)(2,1)S(1)} %get-tuple-element.49), channel_id=1, source_target_pairs={{0,1},{1,0},{2,3},{3,2},{4,5},{5,4},{6,7},{7,6},{8,9},{9,8},{10,11... | collective-permute-start | bytes 1572872 | tf_op jit(solution)/shard_map/ppermute | solution.py:21
  4.8 15.4 %collective-permute-start.3 = (bf16[2,2,64,1024]{3,2,1,0:T(8,128)(2,1)S(1)}, bf16[2,2,64,1024]{3,2,1,0:T(8,128)(2,1)S(1)}, u32[]{:S(2)}, u32[]{:S(2)}) collective-permute-start(bf16[2,2,64,1024]{3,2,1,0:T(8,128)(2,1)S(1)} %get-tuple-element.58), channel_id=1, source_target_pairs={{0,2},{1,3},{2,0},{3,1},{4,6},{5,7},{6,4},{7,5},{8,10},{9,11},{10,... | collective-permute-start | bytes 1572872 | tf_op jit(solution)/shard_map/ppermute | solution.py:21
  7.4 9.4 %collective-permute-start.5 = (bf16[2,2,16,1024]{3,2,1,0:T(8,128)(2,1)S(1)}, bf16[2,2,16,1024]{3,2,1,0:T(8,128)(2,1)S(1)}, u32[]{:S(2)}, u32[]{:S(2)}) collective-permute-start(bf16[2,2,16,1024]{3,2,1,0:T(8,128)(2,1)S(1)} %get-tuple-element.60), channel_id=1, source_target_pairs={{0,8},{1,9},{2,10},{3,11},{4,12},{5,13},{6,14},{7,15},{8,0},{9,1},... | collective-permute-start | bytes 393224 | tf_op jit(solution)/shard_map/ppermute | solution.py:21
  10.0 14.0 %collective-permute-start.4 = (bf16[2,2,32,1024]{3,2,1,0:T(8,128)(2,1)S(1)}, bf16[2,2,32,1024]{3,2,1,0:T(8,128)(2,1)S(1)}, u32[]{:S(2)}, u32[]{:S(2)}) collective-permute-start(bf16[2,2,32,1024]{3,2,1,0:T(8,128)(2,1)S(1)} %get-tuple-element.59), channel_id=1, source_target_pairs={{0,4},{1,5},{2,6},{3,7},{4,0},{5,1},{6,2},{7,3},{8,12},{9,13},{10,... | collective-permute-start | bytes 786440 | tf_op jit(solution)/shard_map/ppermute | solution.py:21
  11.7 6.3 %copy-start.4 = (f32[16]{0:T(128)S(1)}, f32[16]{0:T(128)}, u32[]{:S(2)}) copy-start(f32[16]{0:T(128)} %slope.5) | copy-start | bytes 196
  16.8 7.2 %collective-permute-start.7 = (bf16[2,2,16,1024]{3,2,1,0:T(8,128)(2,1)S(1)}, bf16[2,2,16,1024]{3,2,1,0:T(8,128)(2,1)S(1)}, u32[]{:S(2)}, u32[]{:S(2)}) collective-permute-start(bf16[2,2,16,1024]{3,2,1,0:T(8,128)(2,1)S(1)} %collective-permute-done.5.refs_2_.refs_4_), channel_id=1, source_target_pairs={{0,2},{1,3},{2,0},{3,1},{4,6},{5,7},{6,4},{7,5},{8,10},{9,11},{10,... | collective-permute-start | bytes 393224 | tf_op jit(solution)/shard_map/ppermute | solution.py:21
  17.3 5.4 %collective-permute-start.6 = (bf16[2,2,16,1024]{3,2,1,0:T(8,128)(2,1)S(1)}, bf16[2,2,16,1024]{3,2,1,0:T(8,128)(2,1)S(1)}, u32[]{:S(2)}, u32[]{:S(2)}) collective-permute-start(bf16[2,2,16,1024]{3,2,1,0:T(8,128)(2,1)S(1)} %collective-permute-done.5.refs_2_.refs_4_), channel_id=1, source_target_pairs={{0,4},{1,5},{2,6},{3,7},{4,0},{5,1},{6,2},{7,3},{8,12},{9,13},{10,... | collective-permute-start | bytes 393224 | tf_op jit(solution)/shard_map/ppermute | solution.py:21
  20.4 7.9 %collective-permute-start.8 = (bf16[2,2,32,1024]{3,2,1,0:T(8,128)(2,1)S(1)}, bf16[2,2,32,1024]{3,2,1,0:T(8,128)(2,1)S(1)}, u32[]{:S(2)}, u32[]{:S(2)}) collective-permute-start(bf16[2,2,32,1024]{3,2,1,0:T(8,128)(2,1)S(1)} %coarser.1), channel_id=1, source_target_pairs={{0,4},{1,5},{2,6},{3,7},{4,0},{5,1},{6,2},{7,3},{8,12},{9,13},{10,... | collective-permute-start | bytes 786440 | tf_op jit(solution)/shard_map/ppermute | solution.py:21
  22.6 5.0 %collective-permute-start.9 = (bf16[2,2,16,1024]{3,2,1,0:T(8,128)(2,1)S(1)}, bf16[2,2,16,1024]{3,2,1,0:T(8,128)(2,1)S(1)}, u32[]{:S(2)}, u32[]{:S(2)}) collective-permute-start(bf16[2,2,16,1024]{3,2,1,0:T(8,128)(2,1)S(1)} %collective-permute-done.6.refs_3_.refs_5_), channel_id=1, source_target_pairs={{0,2},{1,3},{2,0},{3,1},{4,6},{5,7},{6,4},{7,5},{8,10},{9,11},{10,... | collective-permute-start | bytes 393224 | tf_op jit(solution)/shard_map/ppermute | solution.py:21
  30.4 8.2 %collective-permute-start.12 = (bf16[1040,128]{1,0:T(8,128)(2,1)S(1)}, bf16[1040,128]{1,0:T(8,128)(2,1)S(1)}, u32[]{:S(2)}, u32[]{:S(2)}) collective-permute-start(bf16[1040,128]{1,0:T(8,128)(2,1)S(1)} %get-tuple-element.75), channel_id=1, source_target_pairs={{0,2},{1,3},{2,0},{3,1},{4,6},{5,7},{6,4},{7,5},{8,10},{9,11},{10,... | collective-permute-start | bytes 798728 | tf_op jit(solution)/shard_map/ppermute | solution.py:21
  32.0 7.2 %collective-permute-start.11 = (bf16[2,2,32,1024]{3,2,1,0:T(8,128)(2,1)S(1)}, bf16[2,2,32,1024]{3,2,1,0:T(8,128)(2,1)S(1)}, u32[]{:S(2)}, u32[]{:S(2)}) collective-permute-start(bf16[2,2,32,1024]{3,2,1,0:T(8,128)(2,1)S(1)} %get-tuple-element.73), channel_id=1, source_target_pairs={{0,4},{1,5},{2,6},{3,7},{4,0},{5,1},{6,2},{7,3},{8,12},{9,13},{10,... | collective-permute-start | bytes 786440 | tf_op jit(solution)/shard_map/ppermute | solution.py:21
  33.5 4.5 %collective-permute-start.14 = (f32[8,128]{1,0:T(8,128)S(1)}, f32[8,128]{1,0:T(8,128)S(1)}, u32[]{:S(2)}, u32[]{:S(2)}) collective-permute-start(f32[8,128]{1,0:T(8,128)S(1)} %get-tuple-element.76.slope), channel_id=1, source_target_pairs={{0,18},{1,19},{2,16},{3,17},{4,22},{5,23},{6,20},{7,21},{8,26},{9,... | collective-permute-start | bytes 12296 | tf_op jit(solution)/shard_map/ppermute | solution.py:24
  35.0 3.6 %collective-permute-start.13 = (f32[8,128]{1,0:T(8,128)S(1)}, f32[8,128]{1,0:T(8,128)S(1)}, u32[]{:S(2)}, u32[]{:S(2)}) collective-permute-start(f32[8,128]{1,0:T(8,128)S(1)} %get-tuple-element.76.slope), channel_id=1, source_target_pairs={{0,16},{1,17},{2,18},{3,19},{4,20},{5,21},{6,22},{7,23},{8,24},{9,... | collective-permute-start | bytes 12296 | tf_op jit(solution)/shard_map/ppermute | solution.py:24
  38.7 5.1 %collective-permute-start.17 = (bf16[528,128]{1,0:T(8,128)(2,1)S(1)}, bf16[528,128]{1,0:T(8,128)(2,1)S(1)}, u32[]{:S(2)}, u32[]{:S(2)}) collective-permute-start(bf16[528,128]{1,0:T(8,128)(2,1)S(1)} %get-tuple-element.80), channel_id=1, source_target_pairs={{0,4},{1,5},{2,6},{3,7},{4,0},{5,1},{6,2},{7,3},{8,12},{9,13},{10,... | collective-permute-start | bytes 405512 | tf_op jit(solution)/shard_map/ppermute | solution.py:21
  39.5 14.2 %collective-permute-start.15 = (bf16[2,2,64,1024]{3,2,1,0:T(8,128)(2,1)S(1)}, bf16[2,2,64,1024]{3,2,1,0:T(8,128)(2,1)S(1)}, u32[]{:S(2)}, u32[]{:S(2)}) collective-permute-start(bf16[2,2,64,1024]{3,2,1,0:T(8,128)(2,1)S(1)} %fold.1), channel_id=1, source_target_pairs={{0,2},{1,3},{2,0},{3,1},{4,6},{5,7},{6,4},{7,5},{8,10},{9,11},{10,... | collective-permute-start | bytes 1572872 | tf_op jit(solution)/shard_map/ppermute | solution.py:21
  42.0 4.5 %collective-permute-start.10 = (bf16[2,64,1024]{2,1,0:T(8,128)(2,1)S(1)}, bf16[2,64,1024]{2,1,0:T(8,128)(2,1)S(1)}, u32[]{:S(2)}, u32[]{:S(2)}) collective-permute-start(bf16[2,64,1024]{2,1,0:T(8,128)(2,1)S(1)} %get-tuple-element.67), channel_id=1, source_target_pairs={{0,1},{1,0},{2,3},{3,2},{4,5},{5,4},{6,7},{7,6},{8,9},{9,8},{10,11... | collective-permute-start | bytes 786440 | tf_op jit(solution)/shard_map/ppermute | solution.py:21
  42.0 11.6 %collective-permute-start.16 = (bf16[1024,128]{1,0:T(8,128)(2,1)S(1)}, bf16[1024,128]{1,0:T(8,128)(2,1)S(1)}, u32[]{:S(2)}, u32[]{:S(2)}) collective-permute-start(bf16[1024,128]{1,0:T(8,128)(2,1)S(1)} %get-tuple-element.78), channel_id=1, source_target_pairs={{0,4},{1,5},{2,6},{3,7},{4,0},{5,1},{6,2},{7,3},{8,12},{9,13},{10,... | collective-permute-start | bytes 786440 | tf_op jit(solution)/shard_map/ppermute | solution.py:21
  43.8 9.9 %collective-permute-start.18 = (bf16[528,128]{1,0:T(8,128)(2,1)S(1)}, bf16[528,128]{1,0:T(8,128)(2,1)S(1)}, u32[]{:S(2)}, u32[]{:S(2)}) collective-permute-start(bf16[528,128]{1,0:T(8,128)(2,1)S(1)} %get-tuple-element.81), channel_id=1, source_target_pairs={{0,8},{1,9},{2,10},{3,11},{4,12},{5,13},{6,14},{7,15},{8,0},{9,1},... | collective-permute-start | bytes 405512 | tf_op jit(solution)/shard_map/ppermute | solution.py:21
  54.0 2.2 %collective-permute-start.20 = (bf16[2,64,1024]{2,1,0:T(8,128)(2,1)S(1)}, bf16[2,64,1024]{2,1,0:T(8,128)(2,1)S(1)}, u32[]{:S(2)}, u32[]{:S(2)}) collective-permute-start(bf16[2,64,1024]{2,1,0:T(8,128)(2,1)S(1)} %get-tuple-element.87), channel_id=1, source_target_pairs={{0,1},{1,0},{2,3},{3,2},{4,5},{5,4},{6,7},{7,6},{8,9},{9,8},{10,11... | collective-permute-start | bytes 786440 | tf_op jit(solution)/shard_map/ppermute | solution.py:21
  54.5 1.7 %collective-permute-start.19 = (bf16[2,64,1024]{2,1,0:T(8,128)(2,1)S(1)}, bf16[2,64,1024]{2,1,0:T(8,128)(2,1)S(1)}, u32[]{:S(2)}, u32[]{:S(2)}) collective-permute-start(bf16[2,64,1024]{2,1,0:T(8,128)(2,1)S(1)} %get-tuple-element.86), channel_id=1, source_target_pairs={{0,1},{1,0},{2,3},{3,2},{4,5},{5,4},{6,7},{7,6},{8,9},{9,8},{10,11... | collective-permute-start | bytes 786440 | tf_op jit(solution)/shard_map/ppermute | solution.py:21
  55.0 1.2 %collective-permute-start.21 = (f32[8,128]{1,0:T(8,128)S(1)}, f32[8,128]{1,0:T(8,128)S(1)}, u32[]{:S(2)}, u32[]{:S(2)}) collective-permute-start(f32[8,128]{1,0:T(8,128)S(1)} %slope_terms.1.slope), channel_id=1, source_target_pairs={{0,1},{1,0},{2,3},{3,2},{4,5},{5,4},{6,7},{7,6},{8,9},{9,8},{10,11... | collective-permute-start | bytes 12296 | tf_op jit(solution)/shard_map/ppermute | solution.py:21

commit v8 on v7

--- a/solution.py
+++ b/solution.py
@@ -343,7 +343,7 @@
     message[pl.ds(rows, 2 * slope.shape[0]), :] = two_parts(total)
 
 
-def gather_body(kind, levels_of, done, own, other, near, *refs):
+def gather_body(kind, levels_of, own, other, near, *refs):
     back, (kept, sent) = refs[:-2], refs[-2:]
     _, seqs, block, width = own.shape
     sizes = [2 * block >> level for level in levels_of[1:]]
@@ -365,21 +365,16 @@
     out[...] = slope[...] + one_part(far[pl.ds(far.shape[0] - rows, rows), :])
 
 
-def join_body(core, own, other, out, done, sems):
-    mine, theirs = head_halves(core, own.shape[-1])
-    copy_all([(other, out.at[:, :, theirs]), (own, out.at[:, :, mine])], sems)
-    done[...] = jnp.zeros_like(done)
-
-
-def keep_grads_body(core, first, second, first_out, second_out, sems):
-    mine, _ = head_halves(core, first.shape[-1])
-    copy_all([(first, first_out.at[:, :, mine]), (second, second_out.at[:, :, mine])], sems)
-
-
-def join_pair_body(core, half_done, other_half_done, first, second, slope, slope_other, *refs):
-    first_out, second_out, slope_out, sums, sems = refs
-    _, theirs = head_halves(core, first.shape[-1])
-    moves = [(first, first_out.at[:, :, theirs]), (second, second_out.at[:, :, theirs])]
+def keep_grads_body(core, dq, dk, dv, *refs):
+    *outs, sems = refs
+    mine, _ = head_halves(core, dk.shape[-1])
+    copy_all([(half, out.at[:, :, mine]) for half, out in zip((dq, dk, dv), outs)], sems)
+
+
+def join_grads_body(core, dq_half, dk_half, dv_half, dq, dk, dv, slope, slope_other, *refs):
+    *outs, slope_out, sums, sems = refs
+    _, theirs = head_halves(core, dk.shape[-1])
+    moves = [(half, out.at[:, :, theirs]) for half, out in zip((dq, dk, dv), outs)]
     copies = start_all(moves, sems)
     ours, rest = slope[...], slope_other[...]
     lower = jnp.where(core[0] == 0, ours, rest)
@@ -501,37 +496,34 @@
     far_side_back = swap(far_side, 4)
     near_back = swap(call(fold_body, like(*near.shape), (near, across_back, slope), "fold"), 2)
     side_back = swap(side, 4)
-    slope, far_total = call(meet_body, (slope_part, message), (keep, far_side_back, slope), "meet")
+    slope, far_total = call(meet_body, (slope_part, message), (keep, far_side_back, slope), "meet", flops=int(4e9))
     far_back = swap(far_total, 8)
     whole = like(seqs, block, width)
-    dq, done = call(
-        join_body, (whole, slope_part), (core, dq_own, dq_other), "join_queries", scalars=1, hbm_out=1, copies=2
-    )
     kept, others = [], []
     for kind in range(2):
         mine, sent = call(
             functools.partial(gather_body, kind, (1, 2, 3)),
             (dq_part, dq_part),
-            (done, own, other, near_back, side_back, far_back),
+            (own, other, near_back, side_back, far_back),
             "gather_cells",
         )
         kept.append(mine)
         others.append(swap(sent, 1))
     slope = call(total_body, slope_part, (slope, far_back), "slope_terms")
     halves = call(
-        keep_grads_body, (whole, whole), (core, *kept), "keep_grads", scalars=1, hbm_out=2, copies=2
-    )
-    dk, dv, slope_grad = call(
-        join_pair_body,
-        (whole, whole, like(1, heads, dtype=F32)),
-        (core, *halves, *others, slope, swap(slope, 1)),
-        "join_kv",
+        keep_grads_body, (whole,) * 3, (core, dq_own, *kept), "keep_grads", scalars=1, hbm_out=3, copies=3
+    )
+    dq, dk, dv, slope_grad = call(
+        join_grads_body,
+        (whole, whole, whole, like(1, heads, dtype=F32)),
+        (core, *halves, dq_other, *others, slope, swap(slope, 1)),
+        "join_grads",
         scalars=1,
-        hbm_in=2,
-        hbm_out=3,
-        copies=3,
+        hbm_in=3,
+        hbm_out=4,
+        copies=4,
         scratch=(pltpu.VMEM((1, heads), F32),),
-        aliases={1: 0, 2: 1},
+        aliases={1: 0, 2: 1, 3: 2},
     )
     return dq, dk, dv, slope_grad.reshape(heads)
 

time: 57.3 us -> 56.6 us (0.988)
  Pallas kernels: 10.8 us -> 10.2 us
    pallas_call x20 -> x19, Pallas kernels: 10.8 us -> 10.2 us  [call(): pl.pallas_call(body, out_shape=out_shape, in_specs=[SMEM] * scalars + [HB...]
where the time goes in v8:
time: 56.6 us; the launch traced here: 56.4 us
  starting transfers between devices  24.5 us (43%)
  waiting for transfers between devices  18.8 us (33%)
  Pallas kernels  10.2 us (18%)
  local copies, waits for them, and re-layouts  2.1 us (4%)
  between operations  0.81 us (1%)
    ppermute x20, starting transfers between devices, swap(): lax.ppermute(value, 'ctx', [(source, source ^ apart) for source in range(...  22.6 us
    ppermute x20, waiting for transfers between devices, swap(): lax.ppermute(value, 'ctx', [(source, source ^ apart) for source in range(...  16.2 us
    pallas_call x19, Pallas kernels, call(): pl.pallas_call(body, out_shape=out_shape, in_specs=[SMEM] * scalars + [HB...  10.2 us
    ppermute x2, waiting for transfers between devices, swap(): return lax.ppermute(value, ('dp', 'ctx'), pairs)  2.61 us
    unnamed x10, local copies, waits for them, and re-layouts  2.1 us
    ppermute x2, starting transfers between devices, swap(): return lax.ppermute(value, ('dp', 'ctx'), pairs)  1.97 us
  transfers between devices with their start and end apart: 22, of which 10 were waited for; matrix products, arithmetic and copies ran while one was open for 0% of the time, Pallas kernels for 13%

profile of v8, /device:TPU:0, one launch (start us, length us, event | category | flops | bytes accessed | tf_op | source)
XLA Modules:
  0.0 56.4 jit_solution(8250124149800648557)
XLA Ops:
  0.7 0.5 collective-permute-start.1
  1.2 0.1 collective-permute-start.2
  1.2 1.0 %copy-done.2 = bf16[2,64,2048]{2,1,0:T(8,128)(2,1)S(1)} copy-done((bf16[2,64,2048]{2,1,0:T(8,128)(2,1)S(1)}, bf16[2,64,2048]{2,1,0:T(8,128)(2,1)}, u32[]{:S(2)}) %copy-start.2) | copy-done | bytes 524312
  2.3 1.0 %copy-done.3 = bf16[2,64,2048]{2,1,0:T(8,128)(2,1)S(1)} copy-done((bf16[2,64,2048]{2,1,0:T(8,128)(2,1)S(1)}, bf16[2,64,2048]{2,1,0:T(8,128)(2,1)}, u32[]{:S(2)}) %copy-start.3) | copy-done | bytes 524312
  3.3 0.1 split_qg.1
  3.5 0.5 collective-permute-start
  4.0 0.4 own_summaries.1
  4.4 0.4 summaries.1
  4.8 2.7 %collective-permute-start.3 = (bf16[2,2,64,1024]{3,2,1,0:T(8,128)(2,1)S(1)}, bf16[2,2,64,1024]{3,2,1,0:T(8,128)(2,1)S(1)}, u32[]{:S(2)}, u32[]{:S(2)}) collective-permute-start(bf16[2,2,64,1024]{3,2,1,0:T(8,128)(2,1)S(1)} %get-tuple-element.58), channel_id=1, source_target_pairs={{0,2},{1,3},{2,0},{3,1},{4,6},{5,7},{6,4},{7,5},{8,10},{9,11},{10,... | collective-permute-start | bytes 1572872 | tf_op jit(solution)/shard_map/ppermute | solution.py:21
  7.4 2.6 %collective-permute-start.5 = (bf16[2,2,16,1024]{3,2,1,0:T(8,128)(2,1)S(1)}, bf16[2,2,16,1024]{3,2,1,0:T(8,128)(2,1)S(1)}, u32[]{:S(2)}, u32[]{:S(2)}) collective-permute-start(bf16[2,2,16,1024]{3,2,1,0:T(8,128)(2,1)S(1)} %get-tuple-element.60), channel_id=1, source_target_pairs={{0,8},{1,9},{2,10},{3,11},{4,12},{5,13},{6,14},{7,15},{8,0},{9,1},... | collective-permute-start | bytes 393224 | tf_op jit(solution)/shard_map/ppermute | solution.py:21
  10.0 1.6 %collective-permute-start.4 = (bf16[2,2,32,1024]{3,2,1,0:T(8,128)(2,1)S(1)}, bf16[2,2,32,1024]{3,2,1,0:T(8,128)(2,1)S(1)}, u32[]{:S(2)}, u32[]{:S(2)}) collective-permute-start(bf16[2,2,32,1024]{3,2,1,0:T(8,128)(2,1)S(1)} %get-tuple-element.59), channel_id=1, source_target_pairs={{0,4},{1,5},{2,6},{3,7},{4,0},{5,1},{6,2},{7,3},{8,12},{9,13},{10,... | collective-permute-start | bytes 786440 | tf_op jit(solution)/shard_map/ppermute | solution.py:21
  11.7 0.3 turn.1.turned.refs_6_
  12.0 4.8 %collective-permute-done.5.refs_2_.refs_4_ = bf16[2,2,16,1024]{3,2,1,0:T(8,128)(2,1)S(1)} collective-permute-done((bf16[2,2,16,1024]{3,2,1,0:T(8,128)(2,1)S(1)}, bf16[2,2,16,1024]{3,2,1,0:T(8,128)(2,1)S(1)}, u32[]{:S(2)}, u32[]{:S(2)}) %collective-permute-start.5) | collective-permute-done | bytes 131104 | tf_op jit(solution)/shard_map/ppermute | solution.py:21
  16.8 0.5 collective-permute-start.7
  17.3 0.7 %collective-permute-start.6 = (bf16[2,2,16,1024]{3,2,1,0:T(8,128)(2,1)S(1)}, bf16[2,2,16,1024]{3,2,1,0:T(8,128)(2,1)S(1)}, u32[]{:S(2)}, u32[]{:S(2)}) collective-permute-start(bf16[2,2,16,1024]{3,2,1,0:T(8,128)(2,1)S(1)} %collective-permute-done.5.refs_2_.refs_4_), channel_id=1, source_target_pairs={{0,4},{1,5},{2,6},{3,7},{4,0},{5,1},{6,2},{7,3},{8,12},{9,13},{10,... | collective-permute-start | bytes 393224 | tf_op jit(solution)/shard_map/ppermute | solution.py:21
  18.0 1.0 %scores.2 = (f32[16,128,128]{2,1,0:T(8,128)S(1)}, f32[16,128,128]{2,1,0:T(8,128)S(1)}, f32[16,8,128]{2,1,0:T(8,128)S(1)}) custom-call(s32[1]{0:T(128)} %bitcast.core, f32[16]{0:T(128)S(1)} %copy-done.4, bf16[2,16,128,128]{3,2,1,0:T(8,128)(2,1)S(1)} %turn.1.turned.refs_6_, bf16[2,2,64,1024]{3,2,1,0:T(8,128)(2,1)S(1)} %get-tuple-element.50.refs_0_, ...), custom_call_target="tpu_custom_call" | custom-call | flops 1342177280 | bytes 4259908 | tf_op jit(solution)/shard_map/scores/pallas_call | solution.py:34
  19.0 1.2 %collective-permute-done.3.refs_0_.cells.refs_2_ = bf16[2,2,64,1024]{3,2,1,0:T(8,128)(2,1)S(1)} collective-permute-done((bf16[2,2,64,1024]{3,2,1,0:T(8,128)(2,1)S(1)}, bf16[2,2,64,1024]{3,2,1,0:T(8,128)(2,1)S(1)}, u32[]{:S(2)}, u32[]{:S(2)}) %collective-permute-start.3) | collective-permute-done | bytes 524320 | tf_op jit(solution)/shard_map/ppermute | solution.py:21
  20.2 0.2 coarser.1
  20.4 2.1 %collective-permute-start.8 = (bf16[2,2,32,1024]{3,2,1,0:T(8,128)(2,1)S(1)}, bf16[2,2,32,1024]{3,2,1,0:T(8,128)(2,1)S(1)}, u32[]{:S(2)}, u32[]{:S(2)}) collective-permute-start(bf16[2,2,32,1024]{3,2,1,0:T(8,128)(2,1)S(1)} %coarser.1), channel_id=1, source_target_pairs={{0,4},{1,5},{2,6},{3,7},{4,0},{5,1},{6,2},{7,3},{8,12},{9,13},{10,... | collective-permute-start | bytes 786440 | tf_op jit(solution)/shard_map/ppermute | solution.py:21
  22.5 0.1 collective-permute-done.6.refs_3_.refs_5_
  22.6 1.4 %collective-permute-start.9 = (bf16[2,2,16,1024]{3,2,1,0:T(8,128)(2,1)S(1)}, bf16[2,2,16,1024]{3,2,1,0:T(8,128)(2,1)S(1)}, u32[]{:S(2)}, u32[]{:S(2)}) collective-permute-start(bf16[2,2,16,1024]{3,2,1,0:T(8,128)(2,1)S(1)} %collective-permute-done.6.refs_3_.refs_5_), channel_id=1, source_target_pairs={{0,2},{1,3},{2,0},{3,1},{4,6},{5,7},{6,4},{7,5},{8,10},{9,11},{10,... | collective-permute-start | bytes 393224 | tf_op jit(solution)/shard_map/ppermute | solution.py:21
  24.0 1.3 %scores.3 = (f32[16,144,128]{2,1,0:T(8,128)S(1)}, f32[16,144,128]{2,1,0:T(8,128)S(1)}, f32[16,8,128]{2,1,0:T(8,128)S(1)}) custom-call(s32[1]{0:T(128)} %bitcast.core, f32[16]{0:T(128)S(1)} %copy-done.4, bf16[2,16,128,128]{3,2,1,0:T(8,128)(2,1)S(1)} %turn.1.turned.refs_6_, bf16[2,2,64,1024]{3,2,1,0:T(8,128)(2,1)S(1)} %collective-permute-done.3.refs_0_.cells.refs_2_, ...), custom_call_target="tpu_custom_call" | custom-call | flops 1509949440 | bytes 4653124 | tf_op jit(solution)/shard_map/scores/pallas_call | solution.py:34
  25.4 2.2 %collective-permute-done.9.refs_10_.refs_8_ = bf16[2,2,16,1024]{3,2,1,0:T(8,128)(2,1)S(1)} collective-permute-done((bf16[2,2,16,1024]{3,2,1,0:T(8,128)(2,1)S(1)}, bf16[2,2,16,1024]{3,2,1,0:T(8,128)(2,1)S(1)}, u32[]{:S(2)}, u32[]{:S(2)}) %collective-permute-start.9) | collective-permute-done | bytes 131104 | tf_op jit(solution)/shard_map/ppermute | solution.py:21
  27.6 0.7 %collective-permute-done.8.refs_9_.refs_7_ = bf16[2,2,32,1024]{3,2,1,0:T(8,128)(2,1)S(1)} collective-permute-done((bf16[2,2,32,1024]{3,2,1,0:T(8,128)(2,1)S(1)}, bf16[2,2,32,1024]{3,2,1,0:T(8,128)(2,1)S(1)}, u32[]{:S(2)}, u32[]{:S(2)}) %collective-permute-start.8) | collective-permute-done | bytes 262176 | tf_op jit(solution)/shard_map/ppermute | solution.py:21
  28.3 2.1 %attend.1 = (f32[8,128]{1,0:T(8,128)S(1)}, bf16[2,2,32,1024]{3,2,1,0:T(8,128)(2,1)S(1)}, bf16[1040,128]{1,0:T(8,128)(2,1)S(1)}, bf16[16,320,128]{2,1,0:T(8,128)(2,1)S(1)}, bf16[16,320,128]{2,1,0:T(8,128)(2,1)S(1)}) custom-call(s32[1]{0:T(128)} %bitcast.core, f32[16]{0:T(128)S(1)} %copy-done.4, f32[16,128,128]{2,1,0:T(8,128)S(1)} %get-tuple-element.52.refs_0_, ...), custom_call_target="tpu_custom_call" | custom-call | flops 3355443200 | bytes 10231876 | tf_op jit(solution)/shard_map/attend/pallas_call | solution.py:34
  30.4 1.6 %collective-permute-start.11 = (bf16[1040,128]{1,0:T(8,128)(2,1)S(1)}, bf16[1040,128]{1,0:T(8,128)(2,1)S(1)}, u32[]{:S(2)}, u32[]{:S(2)}) collective-permute-start(bf16[1040,128]{1,0:T(8,128)(2,1)S(1)} %get-tuple-element.72), channel_id=1, source_target_pairs={{0,2},{1,3},{2,0},{3,1},{4,6},{5,7},{6,4},{7,5},{8,10},{9,11},{10,... | collective-permute-start | bytes 798728 | tf_op jit(solution)/shard_map/ppermute | solution.py:21
  32.0 1.6 %collective-permute-start.10 = (bf16[2,2,32,1024]{3,2,1,0:T(8,128)(2,1)S(1)}, bf16[2,2,32,1024]{3,2,1,0:T(8,128)(2,1)S(1)}, u32[]{:S(2)}, u32[]{:S(2)}) collective-permute-start(bf16[2,2,32,1024]{3,2,1,0:T(8,128)(2,1)S(1)} %get-tuple-element.70), channel_id=1, source_target_pairs={{0,4},{1,5},{2,6},{3,7},{4,0},{5,1},{6,2},{7,3},{8,12},{9,13},{10,... | collective-permute-start | bytes 786440 | tf_op jit(solution)/shard_map/ppermute | solution.py:21
  33.5 1.4 %collective-permute-start.13 = (f32[8,128]{1,0:T(8,128)S(1)}, f32[8,128]{1,0:T(8,128)S(1)}, u32[]{:S(2)}, u32[]{:S(2)}) collective-permute-start(f32[8,128]{1,0:T(8,128)S(1)} %get-tuple-element.73.slope), channel_id=1, source_target_pairs={{0,18},{1,19},{2,16},{3,17},{4,22},{5,23},{6,20},{7,21},{8,26},{9,... | collective-permute-start | bytes 12296 | tf_op jit(solution)/shard_map/ppermute | solution.py:24
  35.0 0.5 collective-permute-start.12
  35.5 0.5 cell_grads.1
  36.0 2.1 %collective-permute-done.13.refs_1_ = f32[8,128]{1,0:T(8,128)S(1)} collective-permute-done((f32[8,128]{1,0:T(8,128)S(1)}, f32[8,128]{1,0:T(8,128)S(1)}, u32[]{:S(2)}, u32[]{:S(2)}) %collective-permute-start.13) | collective-permute-done | bytes 4128 | tf_op jit(solution)/shard_map/ppermute | solution.py:24
  38.1 0.5 collective-permute-done.12.refs_0_
  38.7 0.5 collective-permute-start.16
  39.2 1.6 %collective-permute-start.15 = (bf16[1024,128]{1,0:T(8,128)(2,1)S(1)}, bf16[1024,128]{1,0:T(8,128)(2,1)S(1)}, u32[]{:S(2)}, u32[]{:S(2)}) collective-permute-start(bf16[1024,128]{1,0:T(8,128)(2,1)S(1)} %get-tuple-element.75), channel_id=1, source_target_pairs={{0,4},{1,5},{2,6},{3,7},{4,0},{5,1},{6,2},{7,3},{8,12},{9,13},{10,... | collective-permute-start | bytes 786440 | tf_op jit(solution)/shard_map/ppermute | solution.py:21
  40.8 0.3 fold.1
  41.0 1.6 %collective-permute-start.14 = (bf16[2,2,64,1024]{3,2,1,0:T(8,128)(2,1)S(1)}, bf16[2,2,64,1024]{3,2,1,0:T(8,128)(2,1)S(1)}, u32[]{:S(2)}, u32[]{:S(2)}) collective-permute-start(bf16[2,2,64,1024]{3,2,1,0:T(8,128)(2,1)S(1)} %fold.1), channel_id=1, source_target_pairs={{0,2},{1,3},{2,0},{3,1},{4,6},{5,7},{6,4},{7,5},{8,10},{9,11},{10,... | collective-permute-start | bytes 1572872 | tf_op jit(solution)/shard_map/ppermute | solution.py:21
  42.6 2.9 %collective-permute-done.16.back = bf16[528,128]{1,0:T(8,128)(2,1)S(1)} collective-permute-done((bf16[528,128]{1,0:T(8,128)(2,1)S(1)}, bf16[528,128]{1,0:T(8,128)(2,1)S(1)}, u32[]{:S(2)}, u32[]{:S(2)}) %collective-permute-start.16) | collective-permute-done | bytes 135200 | tf_op jit(solution)/shard_map/ppermute | solution.py:21
  45.5 2.4 %collective-permute-start.17 = (bf16[528,128]{1,0:T(8,128)(2,1)S(1)}, bf16[528,128]{1,0:T(8,128)(2,1)S(1)}, u32[]{:S(2)}, u32[]{:S(2)}) collective-permute-start(bf16[528,128]{1,0:T(8,128)(2,1)S(1)} %get-tuple-element.78), channel_id=1, source_target_pairs={{0,8},{1,9},{2,10},{3,11},{4,12},{5,13},{6,14},{7,15},{8,0},{9,1},... | collective-permute-start | bytes 405512 | tf_op jit(solution)/shard_map/ppermute | solution.py:21
  47.9 0.9 %own_grads.1 = (bf16[2,64,1024]{2,1,0:T(8,128)(2,1)S(1)}, bf16[2,64,1024]{2,1,0:T(8,128)(2,1)S(1)}, f32[2,2,64,1024]{3,2,1,0:T(8,128)S(1)}, f32[2,2,64,1024]{3,2,1,0:T(8,128)S(1)}) custom-call(bf16[16,320,128]{2,1,0:T(8,128)(2,1)S(1)} %get-tuple-element.64.dscore, bf16[16,320,128]{2,1,0:T(8,128)(2,1)S(1)} %get-tuple-element.65.probs, ...), custom_call_target="tpu_custom_call" | custom-call | flops 3355443200 | bytes 8912896 | tf_op jit(solution)/shard_map/own_grads/pallas_call | solution.py:34
  48.9 0.1 collective-permute-start.18
  49.0 4.0 %collective-permute-done.17.refs_1_.far = bf16[528,128]{1,0:T(8,128)(2,1)S(1)} collective-permute-done((bf16[528,128]{1,0:T(8,128)(2,1)S(1)}, bf16[528,128]{1,0:T(8,128)(2,1)S(1)}, u32[]{:S(2)}, u32[]{:S(2)}) %collective-permute-start.17) | collective-permute-done | bytes 135200 | tf_op jit(solution)/shard_map/ppermute | solution.py:21
  53.0 0.4 gather_cells.3
  53.4 0.3 gather_cells.2
  53.8 0.6 collective-permute-start.19
  54.3 0.1 collective-permute-start.21
  54.4 0.9 %keep_grads.1 = (bf16[2,64,2048]{2,1,0:T(8,128)(2,1)}, bf16[2,64,2048]{2,1,0:T(8,128)(2,1)}, bf16[2,64,2048]{2,1,0:T(8,128)(2,1)}) custom-call(s32[1]{0:T(128)} %bitcast.core, bf16[2,64,1024]{2,1,0:T(8,128)(2,1)S(1)} %get-tuple-element.66.dq, bf16[2,64,1024]{2,1,0:T(8,128)(2,1)S(1)} %get-tuple-element.79.dk, bf16[2,64,1024]{2,1,0:T(8,128)(2,1)S(1)} %get-tuple-element.80.dv), custom_call_target="tpu_custom_call" | custom-call | bytes 2359300 | tf_op jit(solution)/shard_map/keep_grads/pallas_call | solution.py:34
  55.3 0.2 collective-permute-done.21.slope_other
  55.5 0.9 %join_grads.1 = (bf16[2,64,2048]{2,1,0:T(8,128)(2,1)}, bf16[2,64,2048]{2,1,0:T(8,128)(2,1)}, bf16[2,64,2048]{2,1,0:T(8,128)(2,1)}, f32[1,16]{1,0:T(1,128)}) custom-call(s32[1]{0:T(128)} %bitcast.core, bf16[2,64,2048]{2,1,0:T(8,128)(2,1)} %get-tuple-element.81.dq_half, ...), custom_call_target="tpu_custom_call", output_to_operand_aliasing={{0}: (1, {}), {1}: (2, {}), {2}: (3, {})} | custom-call | bytes 3940420 | tf_op jit(solution)/shard_map/join_grads/pallas_call | solution.py:34
  (25 shorter events, 0.3 us)
Async XLA Ops:
  0.6 3.3 %copy-start = (bf16[2,64,2048]{2,1,0:T(8,128)(2,1)S(1)}, bf16[2,64,2048]{2,1,0:T(8,128)(2,1)}, u32[]{:S(2)}) copy-start(bf16[2,64,2048]{2,1,0:T(8,128)(2,1)} %k.3) | copy-start | bytes 1572868
  0.6 3.3 %copy-start.1 = (bf16[2,64,2048]{2,1,0:T(8,128)(2,1)S(1)}, bf16[2,64,2048]{2,1,0:T(8,128)(2,1)}, u32[]{:S(2)}) copy-start(bf16[2,64,2048]{2,1,0:T(8,128)(2,1)} %v.3) | copy-start | bytes 1572868
  0.7 3.7 %collective-permute-start.1 = (bf16[2,64,2048]{2,1,0:T(8,128)(2,1)}, bf16[2,64,2048]{2,1,0:T(8,128)(2,1)S(1)}, u32[]{:S(2)}, u32[]{:S(2)}) collective-permute-start(bf16[2,64,2048]{2,1,0:T(8,128)(2,1)} %k.3), channel_id=1, source_target_pairs={{0,1},{1,0},{2,3},{3,2},{4,5},{5,4},{6,7},{7,6},{8,9},{9,8},{10,11... | collective-permute-start | bytes 1572872 | tf_op jit(solution)/shard_map/ppermute | solution.py:21
  1.2 3.2 %collective-permute-start.2 = (bf16[2,64,2048]{2,1,0:T(8,128)(2,1)}, bf16[2,64,2048]{2,1,0:T(8,128)(2,1)S(1)}, u32[]{:S(2)}, u32[]{:S(2)}) collective-permute-start(bf16[2,64,2048]{2,1,0:T(8,128)(2,1)} %v.3), channel_id=1, source_target_pairs={{0,1},{1,0},{2,3},{3,2},{4,5},{5,4},{6,7},{7,6},{8,9},{9,8},{10,11... | collective-permute-start | bytes 1572872 | tf_op jit(solution)/shard_map/ppermute | solution.py:21
  1.2 1.0 %copy-start.2 = (bf16[2,64,2048]{2,1,0:T(8,128)(2,1)S(1)}, bf16[2,64,2048]{2,1,0:T(8,128)(2,1)}, u32[]{:S(2)}) copy-start(bf16[2,64,2048]{2,1,0:T(8,128)(2,1)} %first.1) | copy-start | bytes 1572868
  2.3 1.0 %copy-start.3 = (bf16[2,64,2048]{2,1,0:T(8,128)(2,1)S(1)}, bf16[2,64,2048]{2,1,0:T(8,128)(2,1)}, u32[]{:S(2)}) copy-start(bf16[2,64,2048]{2,1,0:T(8,128)(2,1)} %second.1) | copy-start | bytes 1572868
  3.5 8.2 %collective-permute-start = (bf16[2,2,64,1024]{3,2,1,0:T(8,128)(2,1)S(1)}, bf16[2,2,64,1024]{3,2,1,0:T(8,128)(2,1)S(1)}, u32[]{:S(2)}, u32[]{:S(2)}) collective-permute-start(bf16[2,2,64,1024]{3,2,1,0:T(8,128)(2,1)S(1)} %get-tuple-element.49), channel_id=1, source_target_pairs={{0,1},{1,0},{2,3},{3,2},{4,5},{5,4},{6,7},{7,6},{8,9},{9,8},{10,11... | collective-permute-start | bytes 1572872 | tf_op jit(solution)/shard_map/ppermute | solution.py:21
  4.8 15.4 %collective-permute-start.3 = (bf16[2,2,64,1024]{3,2,1,0:T(8,128)(2,1)S(1)}, bf16[2,2,64,1024]{3,2,1,0:T(8,128)(2,1)S(1)}, u32[]{:S(2)}, u32[]{:S(2)}) collective-permute-start(bf16[2,2,64,1024]{3,2,1,0:T(8,128)(2,1)S(1)} %get-tuple-element.58), channel_id=1, source_target_pairs={{0,2},{1,3},{2,0},{3,1},{4,6},{5,7},{6,4},{7,5},{8,10},{9,11},{10,... | collective-permute-start | bytes 1572872 | tf_op jit(solution)/shard_map/ppermute | solution.py:21
  7.4 9.4 %collective-permute-start.5 = (bf16[2,2,16,1024]{3,2,1,0:T(8,128)(2,1)S(1)}, bf16[2,2,16,1024]{3,2,1,0:T(8,128)(2,1)S(1)}, u32[]{:S(2)}, u32[]{:S(2)}) collective-permute-start(bf16[2,2,16,1024]{3,2,1,0:T(8,128)(2,1)S(1)} %get-tuple-element.60), channel_id=1, source_target_pairs={{0,8},{1,9},{2,10},{3,11},{4,12},{5,13},{6,14},{7,15},{8,0},{9,1},... | collective-permute-start | bytes 393224 | tf_op jit(solution)/shard_map/ppermute | solution.py:21
  10.0 14.0 %collective-permute-start.4 = (bf16[2,2,32,1024]{3,2,1,0:T(8,128)(2,1)S(1)}, bf16[2,2,32,1024]{3,2,1,0:T(8,128)(2,1)S(1)}, u32[]{:S(2)}, u32[]{:S(2)}) collective-permute-start(bf16[2,2,32,1024]{3,2,1,0:T(8,128)(2,1)S(1)} %get-tuple-element.59), channel_id=1, source_target_pairs={{0,4},{1,5},{2,6},{3,7},{4,0},{5,1},{6,2},{7,3},{8,12},{9,13},{10,... | collective-permute-start | bytes 786440 | tf_op jit(solution)/shard_map/ppermute | solution.py:21
  11.7 6.3 %copy-start.4 = (f32[16]{0:T(128)S(1)}, f32[16]{0:T(128)}, u32[]{:S(2)}) copy-start(f32[16]{0:T(128)} %slope.5) | copy-start | bytes 196
  16.8 7.2 %collective-permute-start.7 = (bf16[2,2,16,1024]{3,2,1,0:T(8,128)(2,1)S(1)}, bf16[2,2,16,1024]{3,2,1,0:T(8,128)(2,1)S(1)}, u32[]{:S(2)}, u32[]{:S(2)}) collective-permute-start(bf16[2,2,16,1024]{3,2,1,0:T(8,128)(2,1)S(1)} %collective-permute-done.5.refs_2_.refs_4_), channel_id=1, source_target_pairs={{0,2},{1,3},{2,0},{3,1},{4,6},{5,7},{6,4},{7,5},{8,10},{9,11},{10,... | collective-permute-start | bytes 393224 | tf_op jit(solution)/shard_map/ppermute | solution.py:21
  17.3 5.4 %collective-permute-start.6 = (bf16[2,2,16,1024]{3,2,1,0:T(8,128)(2,1)S(1)}, bf16[2,2,16,1024]{3,2,1,0:T(8,128)(2,1)S(1)}, u32[]{:S(2)}, u32[]{:S(2)}) collective-permute-start(bf16[2,2,16,1024]{3,2,1,0:T(8,128)(2,1)S(1)} %collective-permute-done.5.refs_2_.refs_4_), channel_id=1, source_target_pairs={{0,4},{1,5},{2,6},{3,7},{4,0},{5,1},{6,2},{7,3},{8,12},{9,13},{10,... | collective-permute-start | bytes 393224 | tf_op jit(solution)/shard_map/ppermute | solution.py:21
  20.4 7.9 %collective-permute-start.8 = (bf16[2,2,32,1024]{3,2,1,0:T(8,128)(2,1)S(1)}, bf16[2,2,32,1024]{3,2,1,0:T(8,128)(2,1)S(1)}, u32[]{:S(2)}, u32[]{:S(2)}) collective-permute-start(bf16[2,2,32,1024]{3,2,1,0:T(8,128)(2,1)S(1)} %coarser.1), channel_id=1, source_target_pairs={{0,4},{1,5},{2,6},{3,7},{4,0},{5,1},{6,2},{7,3},{8,12},{9,13},{10,... | collective-permute-start | bytes 786440 | tf_op jit(solution)/shard_map/ppermute | solution.py:21
  22.6 5.0 %collective-permute-start.9 = (bf16[2,2,16,1024]{3,2,1,0:T(8,128)(2,1)S(1)}, bf16[2,2,16,1024]{3,2,1,0:T(8,128)(2,1)S(1)}, u32[]{:S(2)}, u32[]{:S(2)}) collective-permute-start(bf16[2,2,16,1024]{3,2,1,0:T(8,128)(2,1)S(1)} %collective-permute-done.6.refs_3_.refs_5_), channel_id=1, source_target_pairs={{0,2},{1,3},{2,0},{3,1},{4,6},{5,7},{6,4},{7,5},{8,10},{9,11},{10,... | collective-permute-start | bytes 393224 | tf_op jit(solution)/shard_map/ppermute | solution.py:21
  30.4 8.2 %collective-permute-start.11 = (bf16[1040,128]{1,0:T(8,128)(2,1)S(1)}, bf16[1040,128]{1,0:T(8,128)(2,1)S(1)}, u32[]{:S(2)}, u32[]{:S(2)}) collective-permute-start(bf16[1040,128]{1,0:T(8,128)(2,1)S(1)} %get-tuple-element.72), channel_id=1, source_target_pairs={{0,2},{1,3},{2,0},{3,1},{4,6},{5,7},{6,4},{7,5},{8,10},{9,11},{10,... | collective-permute-start | bytes 798728 | tf_op jit(solution)/shard_map/ppermute | solution.py:21
  32.0 8.8 %collective-permute-start.10 = (bf16[2,2,32,1024]{3,2,1,0:T(8,128)(2,1)S(1)}, bf16[2,2,32,1024]{3,2,1,0:T(8,128)(2,1)S(1)}, u32[]{:S(2)}, u32[]{:S(2)}) collective-permute-start(bf16[2,2,32,1024]{3,2,1,0:T(8,128)(2,1)S(1)} %get-tuple-element.70), channel_id=1, source_target_pairs={{0,4},{1,5},{2,6},{3,7},{4,0},{5,1},{6,2},{7,3},{8,12},{9,13},{10,... | collective-permute-start | bytes 786440 | tf_op jit(solution)/shard_map/ppermute | solution.py:21
  33.5 4.5 %collective-permute-start.13 = (f32[8,128]{1,0:T(8,128)S(1)}, f32[8,128]{1,0:T(8,128)S(1)}, u32[]{:S(2)}, u32[]{:S(2)}) collective-permute-start(f32[8,128]{1,0:T(8,128)S(1)} %get-tuple-element.73.slope), channel_id=1, source_target_pairs={{0,18},{1,19},{2,16},{3,17},{4,22},{5,23},{6,20},{7,21},{8,26},{9,... | collective-permute-start | bytes 12296 | tf_op jit(solution)/shard_map/ppermute | solution.py:24
  35.0 3.6 %collective-permute-start.12 = (f32[8,128]{1,0:T(8,128)S(1)}, f32[8,128]{1,0:T(8,128)S(1)}, u32[]{:S(2)}, u32[]{:S(2)}) collective-permute-start(f32[8,128]{1,0:T(8,128)S(1)} %get-tuple-element.73.slope), channel_id=1, source_target_pairs={{0,16},{1,17},{2,18},{3,19},{4,20},{5,21},{6,22},{7,23},{8,24},{9,... | collective-permute-start | bytes 12296 | tf_op jit(solution)/shard_map/ppermute | solution.py:24
  38.7 6.8 %collective-permute-start.16 = (bf16[528,128]{1,0:T(8,128)(2,1)S(1)}, bf16[528,128]{1,0:T(8,128)(2,1)S(1)}, u32[]{:S(2)}, u32[]{:S(2)}) collective-permute-start(bf16[528,128]{1,0:T(8,128)(2,1)S(1)} %get-tuple-element.77), channel_id=1, source_target_pairs={{0,4},{1,5},{2,6},{3,7},{4,0},{5,1},{6,2},{7,3},{8,12},{9,13},{10,... | collective-permute-start | bytes 405512 | tf_op jit(solution)/shard_map/ppermute | solution.py:21
  39.2 9.8 %collective-permute-start.15 = (bf16[1024,128]{1,0:T(8,128)(2,1)S(1)}, bf16[1024,128]{1,0:T(8,128)(2,1)S(1)}, u32[]{:S(2)}, u32[]{:S(2)}) collective-permute-start(bf16[1024,128]{1,0:T(8,128)(2,1)S(1)} %get-tuple-element.75), channel_id=1, source_target_pairs={{0,4},{1,5},{2,6},{3,7},{4,0},{5,1},{6,2},{7,3},{8,12},{9,13},{10,... | collective-permute-start | bytes 786440 | tf_op jit(solution)/shard_map/ppermute | solution.py:21
  41.0 11.9 %collective-permute-start.14 = (bf16[2,2,64,1024]{3,2,1,0:T(8,128)(2,1)S(1)}, bf16[2,2,64,1024]{3,2,1,0:T(8,128)(2,1)S(1)}, u32[]{:S(2)}, u32[]{:S(2)}) collective-permute-start(bf16[2,2,64,1024]{3,2,1,0:T(8,128)(2,1)S(1)} %fold.1), channel_id=1, source_target_pairs={{0,2},{1,3},{2,0},{3,1},{4,6},{5,7},{6,4},{7,5},{8,10},{9,11},{10,... | collective-permute-start | bytes 1572872 | tf_op jit(solution)/shard_map/ppermute | solution.py:21
  45.5 7.4 %collective-permute-start.17 = (bf16[528,128]{1,0:T(8,128)(2,1)S(1)}, bf16[528,128]{1,0:T(8,128)(2,1)S(1)}, u32[]{:S(2)}, u32[]{:S(2)}) collective-permute-start(bf16[528,128]{1,0:T(8,128)(2,1)S(1)} %get-tuple-element.78), channel_id=1, source_target_pairs={{0,8},{1,9},{2,10},{3,11},{4,12},{5,13},{6,14},{7,15},{8,0},{9,1},... | collective-permute-start | bytes 405512 | tf_op jit(solution)/shard_map/ppermute | solution.py:21
  48.9 6.5 %collective-permute-start.18 = (bf16[2,64,1024]{2,1,0:T(8,128)(2,1)S(1)}, bf16[2,64,1024]{2,1,0:T(8,128)(2,1)S(1)}, u32[]{:S(2)}, u32[]{:S(2)}) collective-permute-start(bf16[2,64,1024]{2,1,0:T(8,128)(2,1)S(1)} %get-tuple-element.84), channel_id=1, source_target_pairs={{0,1},{1,0},{2,3},{3,2},{4,5},{5,4},{6,7},{7,6},{8,9},{9,8},{10,11... | collective-permute-start | bytes 786440 | tf_op jit(solution)/shard_map/ppermute | solution.py:21
  53.3 2.2 %collective-permute-start.20 = (bf16[2,64,1024]{2,1,0:T(8,128)(2,1)S(1)}, bf16[2,64,1024]{2,1,0:T(8,128)(2,1)S(1)}, u32[]{:S(2)}, u32[]{:S(2)}) collective-permute-start(bf16[2,64,1024]{2,1,0:T(8,128)(2,1)S(1)} %get-tuple-element.86), channel_id=1, source_target_pairs={{0,1},{1,0},{2,3},{3,2},{4,5},{5,4},{6,7},{7,6},{8,9},{9,8},{10,11... | collective-permute-start | bytes 786440 | tf_op jit(solution)/shard_map/ppermute | solution.py:21
  53.8 1.7 %collective-permute-start.19 = (bf16[2,64,1024]{2,1,0:T(8,128)(2,1)S(1)}, bf16[2,64,1024]{2,1,0:T(8,128)(2,1)S(1)}, u32[]{:S(2)}, u32[]{:S(2)}) collective-permute-start(bf16[2,64,1024]{2,1,0:T(8,128)(2,1)S(1)} %get-tuple-element.85), channel_id=1, source_target_pairs={{0,1},{1,0},{2,3},{3,2},{4,5},{5,4},{6,7},{7,6},{8,9},{9,8},{10,11... | collective-permute-start | bytes 786440 | tf_op jit(solution)/shard_map/ppermute | solution.py:21
  54.3 1.2 %collective-permute-start.21 = (f32[8,128]{1,0:T(8,128)S(1)}, f32[8,128]{1,0:T(8,128)S(1)}, u32[]{:S(2)}, u32[]{:S(2)}) collective-permute-start(f32[8,128]{1,0:T(8,128)S(1)} %slope_terms.1.slope), channel_id=1, source_target_pairs={{0,1},{1,0},{2,3},{3,2},{4,5},{5,4},{6,7},{7,6},{8,9},{9,8},{10,11... | collective-permute-start | bytes 12296 | tf_op jit(solution)/shard_map/ppermute | solution.py:21

commit v9 on v8

--- a/solution.py
+++ b/solution.py
@@ -343,7 +343,7 @@
     message[pl.ds(rows, 2 * slope.shape[0]), :] = two_parts(total)
 
 
-def gather_body(kind, levels_of, own, other, near, *refs):
+def gather_body(kind, levels_of, done, own, other, near, *refs):
     back, (kept, sent) = refs[:-2], refs[-2:]
     _, seqs, block, width = own.shape
     sizes = [2 * block >> level for level in levels_of[1:]]
@@ -504,7 +504,7 @@
         mine, sent = call(
             functools.partial(gather_body, kind, (1, 2, 3)),
             (dq_part, dq_part),
-            (own, other, near_back, side_back, far_back),
+            (dq_other, own, other, near_back, side_back, far_back),
             "gather_cells",
         )
         kept.append(mine)

time: 56.6 us -> 57.4 us (1.014)
  transfers between devices with their start and end apart: 22 -> 22, of which waited for: 10 -> 10; matrix products, arithmetic and copies ran while one was open for 0% -> 0% of each run, Pallas kernels for 13% -> 12%
where the time goes in v9:
time: 57.4 us; the launch traced here: 57.1 us
  starting transfers between devices  24.8 us (43%)
  waiting for transfers between devices  19.2 us (33%)
  Pallas kernels  10.2 us (18%)
  local copies, waits for them, and re-layouts  2.1 us (4%)
  between operations  0.8 us (1%)
    ppermute x20, starting transfers between devices, swap(): lax.ppermute(value, 'ctx', [(source, source ^ apart) for source in range(...  22.9 us
    ppermute x20, waiting for transfers between devices, swap(): lax.ppermute(value, 'ctx', [(source, source ^ apart) for source in range(...  16.6 us
    pallas_call x19, Pallas kernels, call(): pl.pallas_call(body, out_shape=out_shape, in_specs=[SMEM] * scalars + [HB...  10.2 us
    ppermute x2, waiting for transfers between devices, swap(): return lax.ppermute(value, ('dp', 'ctx'), pairs)  2.61 us
    unnamed x10, local copies, waits for them, and re-layouts  2.1 us
    ppermute x2, starting transfers between devices, swap(): return lax.ppermute(value, ('dp', 'ctx'), pairs)  1.97 us
  transfers between devices with their start and end apart: 22, of which 10 were waited for; matrix products, arithmetic and copies ran while one was open for 0% of the time, Pallas kernels for 12%

profile of v9, /device:TPU:0, one launch (start us, length us, event | category | flops | bytes accessed | tf_op | source)
XLA Modules:
  0.0 57.1 jit_solution(1626928357445743716)
XLA Ops:
  0.7 0.5 collective-permute-start.1
  1.2 0.1 collective-permute-start.2
  1.2 1.0 %copy-done.2 = bf16[2,64,2048]{2,1,0:T(8,128)(2,1)S(1)} copy-done((bf16[2,64,2048]{2,1,0:T(8,128)(2,1)S(1)}, bf16[2,64,2048]{2,1,0:T(8,128)(2,1)}, u32[]{:S(2)}) %copy-start.2) | copy-done | bytes 524312
  2.3 1.0 %copy-done.3 = bf16[2,64,2048]{2,1,0:T(8,128)(2,1)S(1)} copy-done((bf16[2,64,2048]{2,1,0:T(8,128)(2,1)S(1)}, bf16[2,64,2048]{2,1,0:T(8,128)(2,1)}, u32[]{:S(2)}) %copy-start.3) | copy-done | bytes 524312
  3.3 0.1 split_qg.1
  3.5 0.5 collective-permute-start
  4.0 0.4 own_summaries.1
  4.4 0.4 summaries.1
  4.8 2.7 %collective-permute-start.3 = (bf16[2,2,64,1024]{3,2,1,0:T(8,128)(2,1)S(1)}, bf16[2,2,64,1024]{3,2,1,0:T(8,128)(2,1)S(1)}, u32[]{:S(2)}, u32[]{:S(2)}) collective-permute-start(bf16[2,2,64,1024]{3,2,1,0:T(8,128)(2,1)S(1)} %get-tuple-element.58), channel_id=1, source_target_pairs={{0,2},{1,3},{2,0},{3,1},{4,6},{5,7},{6,4},{7,5},{8,10},{9,11},{10,... | collective-permute-start | bytes 1572872 | tf_op jit(solution)/shard_map/ppermute | solution.py:21
  7.4 2.6 %collective-permute-start.5 = (bf16[2,2,16,1024]{3,2,1,0:T(8,128)(2,1)S(1)}, bf16[2,2,16,1024]{3,2,1,0:T(8,128)(2,1)S(1)}, u32[]{:S(2)}, u32[]{:S(2)}) collective-permute-start(bf16[2,2,16,1024]{3,2,1,0:T(8,128)(2,1)S(1)} %get-tuple-element.60), channel_id=1, source_target_pairs={{0,8},{1,9},{2,10},{3,11},{4,12},{5,13},{6,14},{7,15},{8,0},{9,1},... | collective-permute-start | bytes 393224 | tf_op jit(solution)/shard_map/ppermute | solution.py:21
  10.0 1.6 %collective-permute-start.4 = (bf16[2,2,32,1024]{3,2,1,0:T(8,128)(2,1)S(1)}, bf16[2,2,32,1024]{3,2,1,0:T(8,128)(2,1)S(1)}, u32[]{:S(2)}, u32[]{:S(2)}) collective-permute-start(bf16[2,2,32,1024]{3,2,1,0:T(8,128)(2,1)S(1)} %get-tuple-element.59), channel_id=1, source_target_pairs={{0,4},{1,5},{2,6},{3,7},{4,0},{5,1},{6,2},{7,3},{8,12},{9,13},{10,... | collective-permute-start | bytes 786440 | tf_op jit(solution)/shard_map/ppermute | solution.py:21
  11.7 0.3 turn.1.turned.refs_6_
  12.0 4.8 %collective-permute-done.5.refs_2_.refs_4_ = bf16[2,2,16,1024]{3,2,1,0:T(8,128)(2,1)S(1)} collective-permute-done((bf16[2,2,16,1024]{3,2,1,0:T(8,128)(2,1)S(1)}, bf16[2,2,16,1024]{3,2,1,0:T(8,128)(2,1)S(1)}, u32[]{:S(2)}, u32[]{:S(2)}) %collective-permute-start.5) | collective-permute-done | bytes 131104 | tf_op jit(solution)/shard_map/ppermute | solution.py:21
  16.8 0.5 collective-permute-start.7
  17.3 0.7 %collective-permute-start.6 = (bf16[2,2,16,1024]{3,2,1,0:T(8,128)(2,1)S(1)}, bf16[2,2,16,1024]{3,2,1,0:T(8,128)(2,1)S(1)}, u32[]{:S(2)}, u32[]{:S(2)}) collective-permute-start(bf16[2,2,16,1024]{3,2,1,0:T(8,128)(2,1)S(1)} %collective-permute-done.5.refs_2_.refs_4_), channel_id=1, source_target_pairs={{0,4},{1,5},{2,6},{3,7},{4,0},{5,1},{6,2},{7,3},{8,12},{9,13},{10,... | collective-permute-start | bytes 393224 | tf_op jit(solution)/shard_map/ppermute | solution.py:21
  18.0 1.0 %scores.2 = (f32[16,128,128]{2,1,0:T(8,128)S(1)}, f32[16,128,128]{2,1,0:T(8,128)S(1)}, f32[16,8,128]{2,1,0:T(8,128)S(1)}) custom-call(s32[1]{0:T(128)} %bitcast.core, f32[16]{0:T(128)S(1)} %copy-done.4, bf16[2,16,128,128]{3,2,1,0:T(8,128)(2,1)S(1)} %turn.1.turned.refs_6_, bf16[2,2,64,1024]{3,2,1,0:T(8,128)(2,1)S(1)} %get-tuple-element.50.refs_0_, ...), custom_call_target="tpu_custom_call" | custom-call | flops 1342177280 | bytes 4259908 | tf_op jit(solution)/shard_map/scores/pallas_call | solution.py:34
  19.0 1.2 %collective-permute-done.3.refs_0_.cells.refs_2_ = bf16[2,2,64,1024]{3,2,1,0:T(8,128)(2,1)S(1)} collective-permute-done((bf16[2,2,64,1024]{3,2,1,0:T(8,128)(2,1)S(1)}, bf16[2,2,64,1024]{3,2,1,0:T(8,128)(2,1)S(1)}, u32[]{:S(2)}, u32[]{:S(2)}) %collective-permute-start.3) | collective-permute-done | bytes 524320 | tf_op jit(solution)/shard_map/ppermute | solution.py:21
  20.2 0.2 coarser.1
  20.4 2.1 %collective-permute-start.8 = (bf16[2,2,32,1024]{3,2,1,0:T(8,128)(2,1)S(1)}, bf16[2,2,32,1024]{3,2,1,0:T(8,128)(2,1)S(1)}, u32[]{:S(2)}, u32[]{:S(2)}) collective-permute-start(bf16[2,2,32,1024]{3,2,1,0:T(8,128)(2,1)S(1)} %coarser.1), channel_id=1, source_target_pairs={{0,4},{1,5},{2,6},{3,7},{4,0},{5,1},{6,2},{7,3},{8,12},{9,13},{10,... | collective-permute-start | bytes 786440 | tf_op jit(solution)/shard_map/ppermute | solution.py:21
  22.5 0.1 collective-permute-done.6.refs_3_.refs_5_
  22.6 1.4 %collective-permute-start.9 = (bf16[2,2,16,1024]{3,2,1,0:T(8,128)(2,1)S(1)}, bf16[2,2,16,1024]{3,2,1,0:T(8,128)(2,1)S(1)}, u32[]{:S(2)}, u32[]{:S(2)}) collective-permute-start(bf16[2,2,16,1024]{3,2,1,0:T(8,128)(2,1)S(1)} %collective-permute-done.6.refs_3_.refs_5_), channel_id=1, source_target_pairs={{0,2},{1,3},{2,0},{3,1},{4,6},{5,7},{6,4},{7,5},{8,10},{9,11},{10,... | collective-permute-start | bytes 393224 | tf_op jit(solution)/shard_map/ppermute | solution.py:21
  24.0 1.3 %scores.3 = (f32[16,144,128]{2,1,0:T(8,128)S(1)}, f32[16,144,128]{2,1,0:T(8,128)S(1)}, f32[16,8,128]{2,1,0:T(8,128)S(1)}) custom-call(s32[1]{0:T(128)} %bitcast.core, f32[16]{0:T(128)S(1)} %copy-done.4, bf16[2,16,128,128]{3,2,1,0:T(8,128)(2,1)S(1)} %turn.1.turned.refs_6_, bf16[2,2,64,1024]{3,2,1,0:T(8,128)(2,1)S(1)} %collective-permute-done.3.refs_0_.cells.refs_2_, ...), custom_call_target="tpu_custom_call" | custom-call | flops 1509949440 | bytes 4653124 | tf_op jit(solution)/shard_map/scores/pallas_call | solution.py:34
  25.4 2.2 %collective-permute-done.9.refs_10_.refs_8_ = bf16[2,2,16,1024]{3,2,1,0:T(8,128)(2,1)S(1)} collective-permute-done((bf16[2,2,16,1024]{3,2,1,0:T(8,128)(2,1)S(1)}, bf16[2,2,16,1024]{3,2,1,0:T(8,128)(2,1)S(1)}, u32[]{:S(2)}, u32[]{:S(2)}) %collective-permute-start.9) | collective-permute-done | bytes 131104 | tf_op jit(solution)/shard_map/ppermute | solution.py:21
  27.6 0.7 %collective-permute-done.8.refs_9_.refs_7_ = bf16[2,2,32,1024]{3,2,1,0:T(8,128)(2,1)S(1)} collective-permute-done((bf16[2,2,32,1024]{3,2,1,0:T(8,128)(2,1)S(1)}, bf16[2,2,32,1024]{3,2,1,0:T(8,128)(2,1)S(1)}, u32[]{:S(2)}, u32[]{:S(2)}) %collective-permute-start.8) | collective-permute-done | bytes 262176 | tf_op jit(solution)/shard_map/ppermute | solution.py:21
  28.3 2.1 %attend.1 = (f32[8,128]{1,0:T(8,128)S(1)}, bf16[2,2,32,1024]{3,2,1,0:T(8,128)(2,1)S(1)}, bf16[1040,128]{1,0:T(8,128)(2,1)S(1)}, bf16[16,320,128]{2,1,0:T(8,128)(2,1)S(1)}, bf16[16,320,128]{2,1,0:T(8,128)(2,1)S(1)}) custom-call(s32[1]{0:T(128)} %bitcast.core, f32[16]{0:T(128)S(1)} %copy-done.4, f32[16,128,128]{2,1,0:T(8,128)S(1)} %get-tuple-element.52.refs_0_, ...), custom_call_target="tpu_custom_call" | custom-call | flops 3355443200 | bytes 10231876 | tf_op jit(solution)/shard_map/attend/pallas_call | solution.py:34
  30.4 1.6 %collective-permute-start.12 = (bf16[1040,128]{1,0:T(8,128)(2,1)S(1)}, bf16[1040,128]{1,0:T(8,128)(2,1)S(1)}, u32[]{:S(2)}, u32[]{:S(2)}) collective-permute-start(bf16[1040,128]{1,0:T(8,128)(2,1)S(1)} %get-tuple-element.73), channel_id=1, source_target_pairs={{0,2},{1,3},{2,0},{3,1},{4,6},{5,7},{6,4},{7,5},{8,10},{9,11},{10,... | collective-permute-start | bytes 798728 | tf_op jit(solution)/shard_map/ppermute | solution.py:21
  32.0 1.6 %collective-permute-start.11 = (bf16[2,2,32,1024]{3,2,1,0:T(8,128)(2,1)S(1)}, bf16[2,2,32,1024]{3,2,1,0:T(8,128)(2,1)S(1)}, u32[]{:S(2)}, u32[]{:S(2)}) collective-permute-start(bf16[2,2,32,1024]{3,2,1,0:T(8,128)(2,1)S(1)} %get-tuple-element.71), channel_id=1, source_target_pairs={{0,4},{1,5},{2,6},{3,7},{4,0},{5,1},{6,2},{7,3},{8,12},{9,13},{10,... | collective-permute-start | bytes 786440 | tf_op jit(solution)/shard_map/ppermute | solution.py:21
  33.5 1.4 %collective-permute-start.14 = (f32[8,128]{1,0:T(8,128)S(1)}, f32[8,128]{1,0:T(8,128)S(1)}, u32[]{:S(2)}, u32[]{:S(2)}) collective-permute-start(f32[8,128]{1,0:T(8,128)S(1)} %get-tuple-element.74.slope), channel_id=1, source_target_pairs={{0,18},{1,19},{2,16},{3,17},{4,22},{5,23},{6,20},{7,21},{8,26},{9,... | collective-permute-start | bytes 12296 | tf_op jit(solution)/shard_map/ppermute | solution.py:24
  35.0 0.5 collective-permute-start.13
  35.5 0.5 cell_grads.1
  36.0 2.1 %collective-permute-done.14.refs_1_ = f32[8,128]{1,0:T(8,128)S(1)} collective-permute-done((f32[8,128]{1,0:T(8,128)S(1)}, f32[8,128]{1,0:T(8,128)S(1)}, u32[]{:S(2)}, u32[]{:S(2)}) %collective-permute-start.14) | collective-permute-done | bytes 4128 | tf_op jit(solution)/shard_map/ppermute | solution.py:24
  38.1 0.5 collective-permute-done.13.refs_0_
  38.7 0.5 collective-permute-start.17
  39.2 0.3 fold.1
  39.5 1.6 %collective-permute-start.15 = (bf16[2,2,64,1024]{3,2,1,0:T(8,128)(2,1)S(1)}, bf16[2,2,64,1024]{3,2,1,0:T(8,128)(2,1)S(1)}, u32[]{:S(2)}, u32[]{:S(2)}) collective-permute-start(bf16[2,2,64,1024]{3,2,1,0:T(8,128)(2,1)S(1)} %fold.1), channel_id=1, source_target_pairs={{0,2},{1,3},{2,0},{3,1},{4,6},{5,7},{6,4},{7,5},{8,10},{9,11},{10,... | collective-permute-start | bytes 1572872 | tf_op jit(solution)/shard_map/ppermute | solution.py:21
  41.0 0.9 %own_grads.1 = (bf16[2,64,1024]{2,1,0:T(8,128)(2,1)S(1)}, bf16[2,64,1024]{2,1,0:T(8,128)(2,1)S(1)}, f32[2,2,64,1024]{3,2,1,0:T(8,128)S(1)}, f32[2,2,64,1024]{3,2,1,0:T(8,128)S(1)}) custom-call(bf16[16,320,128]{2,1,0:T(8,128)(2,1)S(1)} %get-tuple-element.64.dscore, bf16[16,320,128]{2,1,0:T(8,128)(2,1)S(1)} %get-tuple-element.65.probs, ...), custom_call_target="tpu_custom_call" | custom-call | flops 3355443200 | bytes 8912896 | tf_op jit(solution)/shard_map/own_grads/pallas_call | solution.py:34
  42.0 0.1 collective-permute-start.10
  42.0 1.6 %collective-permute-start.16 = (bf16[1024,128]{1,0:T(8,128)(2,1)S(1)}, bf16[1024,128]{1,0:T(8,128)(2,1)S(1)}, u32[]{:S(2)}, u32[]{:S(2)}) collective-permute-start(bf16[1024,128]{1,0:T(8,128)(2,1)S(1)} %get-tuple-element.76), channel_id=1, source_target_pairs={{0,4},{1,5},{2,6},{3,7},{4,0},{5,1},{6,2},{7,3},{8,12},{9,13},{10,... | collective-permute-start | bytes 786440 | tf_op jit(solution)/shard_map/ppermute | solution.py:21
  43.8 2.7 %collective-permute-start.18 = (bf16[528,128]{1,0:T(8,128)(2,1)S(1)}, bf16[528,128]{1,0:T(8,128)(2,1)S(1)}, u32[]{:S(2)}, u32[]{:S(2)}) collective-permute-start(bf16[528,128]{1,0:T(8,128)(2,1)S(1)} %get-tuple-element.79), channel_id=1, source_target_pairs={{0,8},{1,9},{2,10},{3,11},{4,12},{5,13},{6,14},{7,15},{8,0},{9,1},... | collective-permute-start | bytes 405512 | tf_op jit(solution)/shard_map/ppermute | solution.py:21
  46.4 7.2 %collective-permute-done.16.refs_0_ = bf16[1024,128]{1,0:T(8,128)(2,1)S(1)} collective-permute-done((bf16[1024,128]{1,0:T(8,128)(2,1)S(1)}, bf16[1024,128]{1,0:T(8,128)(2,1)S(1)}, u32[]{:S(2)}, u32[]{:S(2)}) %collective-permute-start.16) | collective-permute-done | bytes 262176 | tf_op jit(solution)/shard_map/ppermute | solution.py:21
  53.7 0.3 gather_cells.3
  54.0 0.1 collective-permute-start.20
  54.1 0.3 gather_cells.2
  54.5 0.6 collective-permute-start.19
  55.0 0.1 collective-permute-start.21
  55.1 0.9 %keep_grads.1 = (bf16[2,64,2048]{2,1,0:T(8,128)(2,1)}, bf16[2,64,2048]{2,1,0:T(8,128)(2,1)}, bf16[2,64,2048]{2,1,0:T(8,128)(2,1)}) custom-call(s32[1]{0:T(128)} %bitcast.core, bf16[2,64,1024]{2,1,0:T(8,128)(2,1)S(1)} %get-tuple-element.66.dq, bf16[2,64,1024]{2,1,0:T(8,128)(2,1)S(1)} %get-tuple-element.80.dk, bf16[2,64,1024]{2,1,0:T(8,128)(2,1)S(1)} %get-tuple-element.81.dv), custom_call_target="tpu_custom_call" | custom-call | bytes 2359300 | tf_op jit(solution)/shard_map/keep_grads/pallas_call | solution.py:34
  56.0 0.2 collective-permute-done.21.slope_other
  56.2 0.9 %join_grads.1 = (bf16[2,64,2048]{2,1,0:T(8,128)(2,1)}, bf16[2,64,2048]{2,1,0:T(8,128)(2,1)}, bf16[2,64,2048]{2,1,0:T(8,128)(2,1)}, f32[1,16]{1,0:T(1,128)}) custom-call(s32[1]{0:T(128)} %bitcast.core, bf16[2,64,2048]{2,1,0:T(8,128)(2,1)} %get-tuple-element.82.dq_half, ...), custom_call_target="tpu_custom_call", output_to_operand_aliasing={{0}: (1, {}), {1}: (2, {}), {2}: (3, {})} | custom-call | bytes 3940420 | tf_op jit(solution)/shard_map/join_grads/pallas_call | solution.py:34
  (25 shorter events, 0.3 us)
Async XLA Ops:
  0.6 3.3 %copy-start = (bf16[2,64,2048]{2,1,0:T(8,128)(2,1)S(1)}, bf16[2,64,2048]{2,1,0:T(8,128)(2,1)}, u32[]{:S(2)}) copy-start(bf16[2,64,2048]{2,1,0:T(8,128)(2,1)} %k.3) | copy-start | bytes 1572868
  0.6 3.3 %copy-start.1 = (bf16[2,64,2048]{2,1,0:T(8,128)(2,1)S(1)}, bf16[2,64,2048]{2,1,0:T(8,128)(2,1)}, u32[]{:S(2)}) copy-start(bf16[2,64,2048]{2,1,0:T(8,128)(2,1)} %v.3) | copy-start | bytes 1572868
  0.7 3.7 %collective-permute-start.1 = (bf16[2,64,2048]{2,1,0:T(8,128)(2,1)}, bf16[2,64,2048]{2,1,0:T(8,128)(2,1)S(1)}, u32[]{:S(2)}, u32[]{:S(2)}) collective-permute-start(bf16[2,64,2048]{2,1,0:T(8,128)(2,1)} %k.3), channel_id=1, source_target_pairs={{0,1},{1,0},{2,3},{3,2},{4,5},{5,4},{6,7},{7,6},{8,9},{9,8},{10,11... | collective-permute-start | bytes 1572872 | tf_op jit(solution)/shard_map/ppermute | solution.py:21
  1.2 3.2 %collective-permute-start.2 = (bf16[2,64,2048]{2,1,0:T(8,128)(2,1)}, bf16[2,64,2048]{2,1,0:T(8,128)(2,1)S(1)}, u32[]{:S(2)}, u32[]{:S(2)}) collective-permute-start(bf16[2,64,2048]{2,1,0:T(8,128)(2,1)} %v.3), channel_id=1, source_target_pairs={{0,1},{1,0},{2,3},{3,2},{4,5},{5,4},{6,7},{7,6},{8,9},{9,8},{10,11... | collective-permute-start | bytes 1572872 | tf_op jit(solution)/shard_map/ppermute | solution.py:21
  1.2 1.0 %copy-start.2 = (bf16[2,64,2048]{2,1,0:T(8,128)(2,1)S(1)}, bf16[2,64,2048]{2,1,0:T(8,128)(2,1)}, u32[]{:S(2)}) copy-start(bf16[2,64,2048]{2,1,0:T(8,128)(2,1)} %first.1) | copy-start | bytes 1572868
  2.3 1.0 %copy-start.3 = (bf16[2,64,2048]{2,1,0:T(8,128)(2,1)S(1)}, bf16[2,64,2048]{2,1,0:T(8,128)(2,1)}, u32[]{:S(2)}) copy-start(bf16[2,64,2048]{2,1,0:T(8,128)(2,1)} %second.1) | copy-start | bytes 1572868
  3.5 8.2 %collective-permute-start = (bf16[2,2,64,1024]{3,2,1,0:T(8,128)(2,1)S(1)}, bf16[2,2,64,1024]{3,2,1,0:T(8,128)(2,1)S(1)}, u32[]{:S(2)}, u32[]{:S(2)}) collective-permute-start(bf16[2,2,64,1024]{3,2,1,0:T(8,128)(2,1)S(1)} %get-tuple-element.49), channel_id=1, source_target_pairs={{0,1},{1,0},{2,3},{3,2},{4,5},{5,4},{6,7},{7,6},{8,9},{9,8},{10,11... | collective-permute-start | bytes 1572872 | tf_op jit(solution)/shard_map/ppermute | solution.py:21
  4.8 15.4 %collective-permute-start.3 = (bf16[2,2,64,1024]{3,2,1,0:T(8,128)(2,1)S(1)}, bf16[2,2,64,1024]{3,2,1,0:T(8,128)(2,1)S(1)}, u32[]{:S(2)}, u32[]{:S(2)}) collective-permute-start(bf16[2,2,64,1024]{3,2,1,0:T(8,128)(2,1)S(1)} %get-tuple-element.58), channel_id=1, source_target_pairs={{0,2},{1,3},{2,0},{3,1},{4,6},{5,7},{6,4},{7,5},{8,10},{9,11},{10,... | collective-permute-start | bytes 1572872 | tf_op jit(solution)/shard_map/ppermute | solution.py:21
  7.4 9.4 %collective-permute-start.5 = (bf16[2,2,16,1024]{3,2,1,0:T(8,128)(2,1)S(1)}, bf16[2,2,16,1024]{3,2,1,0:T(8,128)(2,1)S(1)}, u32[]{:S(2)}, u32[]{:S(2)}) collective-permute-start(bf16[2,2,16,1024]{3,2,1,0:T(8,128)(2,1)S(1)} %get-tuple-element.60), channel_id=1, source_target_pairs={{0,8},{1,9},{2,10},{3,11},{4,12},{5,13},{6,14},{7,15},{8,0},{9,1},... | collective-permute-start | bytes 393224 | tf_op jit(solution)/shard_map/ppermute | solution.py:21
  10.0 14.0 %collective-permute-start.4 = (bf16[2,2,32,1024]{3,2,1,0:T(8,128)(2,1)S(1)}, bf16[2,2,32,1024]{3,2,1,0:T(8,128)(2,1)S(1)}, u32[]{:S(2)}, u32[]{:S(2)}) collective-permute-start(bf16[2,2,32,1024]{3,2,1,0:T(8,128)(2,1)S(1)} %get-tuple-element.59), channel_id=1, source_target_pairs={{0,4},{1,5},{2,6},{3,7},{4,0},{5,1},{6,2},{7,3},{8,12},{9,13},{10,... | collective-permute-start | bytes 786440 | tf_op jit(solution)/shard_map/ppermute | solution.py:21
  11.7 6.3 %copy-start.4 = (f32[16]{0:T(128)S(1)}, f32[16]{0:T(128)}, u32[]{:S(2)}) copy-start(f32[16]{0:T(128)} %slope.5) | copy-start | bytes 196
  16.8 7.2 %collective-permute-start.7 = (bf16[2,2,16,1024]{3,2,1,0:T(8,128)(2,1)S(1)}, bf16[2,2,16,1024]{3,2,1,0:T(8,128)(2,1)S(1)}, u32[]{:S(2)}, u32[]{:S(2)}) collective-permute-start(bf16[2,2,16,1024]{3,2,1,0:T(8,128)(2,1)S(1)} %collective-permute-done.5.refs_2_.refs_4_), channel_id=1, source_target_pairs={{0,2},{1,3},{2,0},{3,1},{4,6},{5,7},{6,4},{7,5},{8,10},{9,11},{10,... | collective-permute-start | bytes 393224 | tf_op jit(solution)/shard_map/ppermute | solution.py:21
  17.3 5.4 %collective-permute-start.6 = (bf16[2,2,16,1024]{3,2,1,0:T(8,128)(2,1)S(1)}, bf16[2,2,16,1024]{3,2,1,0:T(8,128)(2,1)S(1)}, u32[]{:S(2)}, u32[]{:S(2)}) collective-permute-start(bf16[2,2,16,1024]{3,2,1,0:T(8,128)(2,1)S(1)} %collective-permute-done.5.refs_2_.refs_4_), channel_id=1, source_target_pairs={{0,4},{1,5},{2,6},{3,7},{4,0},{5,1},{6,2},{7,3},{8,12},{9,13},{10,... | collective-permute-start | bytes 393224 | tf_op jit(solution)/shard_map/ppermute | solution.py:21
  20.4 7.9 %collective-permute-start.8 = (bf16[2,2,32,1024]{3,2,1,0:T(8,128)(2,1)S(1)}, bf16[2,2,32,1024]{3,2,1,0:T(8,128)(2,1)S(1)}, u32[]{:S(2)}, u32[]{:S(2)}) collective-permute-start(bf16[2,2,32,1024]{3,2,1,0:T(8,128)(2,1)S(1)} %coarser.1), channel_id=1, source_target_pairs={{0,4},{1,5},{2,6},{3,7},{4,0},{5,1},{6,2},{7,3},{8,12},{9,13},{10,... | collective-permute-start | bytes 786440 | tf_op jit(solution)/shard_map/ppermute | solution.py:21
  22.6 5.0 %collective-permute-start.9 = (bf16[2,2,16,1024]{3,2,1,0:T(8,128)(2,1)S(1)}, bf16[2,2,16,1024]{3,2,1,0:T(8,128)(2,1)S(1)}, u32[]{:S(2)}, u32[]{:S(2)}) collective-permute-start(bf16[2,2,16,1024]{3,2,1,0:T(8,128)(2,1)S(1)} %collective-permute-done.6.refs_3_.refs_5_), channel_id=1, source_target_pairs={{0,2},{1,3},{2,0},{3,1},{4,6},{5,7},{6,4},{7,5},{8,10},{9,11},{10,... | collective-permute-start | bytes 393224 | tf_op jit(solution)/shard_map/ppermute | solution.py:21
  30.4 8.2 %collective-permute-start.12 = (bf16[1040,128]{1,0:T(8,128)(2,1)S(1)}, bf16[1040,128]{1,0:T(8,128)(2,1)S(1)}, u32[]{:S(2)}, u32[]{:S(2)}) collective-permute-start(bf16[1040,128]{1,0:T(8,128)(2,1)S(1)} %get-tuple-element.73), channel_id=1, source_target_pairs={{0,2},{1,3},{2,0},{3,1},{4,6},{5,7},{6,4},{7,5},{8,10},{9,11},{10,... | collective-permute-start | bytes 798728 | tf_op jit(solution)/shard_map/ppermute | solution.py:21
  32.0 7.2 %collective-permute-start.11 = (bf16[2,2,32,1024]{3,2,1,0:T(8,128)(2,1)S(1)}, bf16[2,2,32,1024]{3,2,1,0:T(8,128)(2,1)S(1)}, u32[]{:S(2)}, u32[]{:S(2)}) collective-permute-start(bf16[2,2,32,1024]{3,2,1,0:T(8,128)(2,1)S(1)} %get-tuple-element.71), channel_id=1, source_target_pairs={{0,4},{1,5},{2,6},{3,7},{4,0},{5,1},{6,2},{7,3},{8,12},{9,13},{10,... | collective-permute-start | bytes 786440 | tf_op jit(solution)/shard_map/ppermute | solution.py:21
  33.5 4.5 %collective-permute-start.14 = (f32[8,128]{1,0:T(8,128)S(1)}, f32[8,128]{1,0:T(8,128)S(1)}, u32[]{:S(2)}, u32[]{:S(2)}) collective-permute-start(f32[8,128]{1,0:T(8,128)S(1)} %get-tuple-element.74.slope), channel_id=1, source_target_pairs={{0,18},{1,19},{2,16},{3,17},{4,22},{5,23},{6,20},{7,21},{8,26},{9,... | collective-permute-start | bytes 12296 | tf_op jit(solution)/shard_map/ppermute | solution.py:24
  35.0 3.6 %collective-permute-start.13 = (f32[8,128]{1,0:T(8,128)S(1)}, f32[8,128]{1,0:T(8,128)S(1)}, u32[]{:S(2)}, u32[]{:S(2)}) collective-permute-start(f32[8,128]{1,0:T(8,128)S(1)} %get-tuple-element.74.slope), channel_id=1, source_target_pairs={{0,16},{1,17},{2,18},{3,19},{4,20},{5,21},{6,22},{7,23},{8,24},{9,... | collective-permute-start | bytes 12296 | tf_op jit(solution)/shard_map/ppermute | solution.py:24
  38.7 5.1 %collective-permute-start.17 = (bf16[528,128]{1,0:T(8,128)(2,1)S(1)}, bf16[528,128]{1,0:T(8,128)(2,1)S(1)}, u32[]{:S(2)}, u32[]{:S(2)}) collective-permute-start(bf16[528,128]{1,0:T(8,128)(2,1)S(1)} %get-tuple-element.78), channel_id=1, source_target_pairs={{0,4},{1,5},{2,6},{3,7},{4,0},{5,1},{6,2},{7,3},{8,12},{9,13},{10,... | collective-permute-start | bytes 405512 | tf_op jit(solution)/shard_map/ppermute | solution.py:21
  39.5 14.2 %collective-permute-start.15 = (bf16[2,2,64,1024]{3,2,1,0:T(8,128)(2,1)S(1)}, bf16[2,2,64,1024]{3,2,1,0:T(8,128)(2,1)S(1)}, u32[]{:S(2)}, u32[]{:S(2)}) collective-permute-start(bf16[2,2,64,1024]{3,2,1,0:T(8,128)(2,1)S(1)} %fold.1), channel_id=1, source_target_pairs={{0,2},{1,3},{2,0},{3,1},{4,6},{5,7},{6,4},{7,5},{8,10},{9,11},{10,... | collective-permute-start | bytes 1572872 | tf_op jit(solution)/shard_map/ppermute | solution.py:21
  42.0 4.5 %collective-permute-start.10 = (bf16[2,64,1024]{2,1,0:T(8,128)(2,1)S(1)}, bf16[2,64,1024]{2,1,0:T(8,128)(2,1)S(1)}, u32[]{:S(2)}, u32[]{:S(2)}) collective-permute-start(bf16[2,64,1024]{2,1,0:T(8,128)(2,1)S(1)} %get-tuple-element.67), channel_id=1, source_target_pairs={{0,1},{1,0},{2,3},{3,2},{4,5},{5,4},{6,7},{7,6},{8,9},{9,8},{10,11... | collective-permute-start | bytes 786440 | tf_op jit(solution)/shard_map/ppermute | solution.py:21
  42.0 11.6 %collective-permute-start.16 = (bf16[1024,128]{1,0:T(8,128)(2,1)S(1)}, bf16[1024,128]{1,0:T(8,128)(2,1)S(1)}, u32[]{:S(2)}, u32[]{:S(2)}) collective-permute-start(bf16[1024,128]{1,0:T(8,128)(2,1)S(1)} %get-tuple-element.76), channel_id=1, source_target_pairs={{0,4},{1,5},{2,6},{3,7},{4,0},{5,1},{6,2},{7,3},{8,12},{9,13},{10,... | collective-permute-start | bytes 786440 | tf_op jit(solution)/shard_map/ppermute | solution.py:21
  43.8 9.9 %collective-permute-start.18 = (bf16[528,128]{1,0:T(8,128)(2,1)S(1)}, bf16[528,128]{1,0:T(8,128)(2,1)S(1)}, u32[]{:S(2)}, u32[]{:S(2)}) collective-permute-start(bf16[528,128]{1,0:T(8,128)(2,1)S(1)} %get-tuple-element.79), channel_id=1, source_target_pairs={{0,8},{1,9},{2,10},{3,11},{4,12},{5,13},{6,14},{7,15},{8,0},{9,1},... | collective-permute-start | bytes 405512 | tf_op jit(solution)/shard_map/ppermute | solution.py:21
  54.0 2.2 %collective-permute-start.20 = (bf16[2,64,1024]{2,1,0:T(8,128)(2,1)S(1)}, bf16[2,64,1024]{2,1,0:T(8,128)(2,1)S(1)}, u32[]{:S(2)}, u32[]{:S(2)}) collective-permute-start(bf16[2,64,1024]{2,1,0:T(8,128)(2,1)S(1)} %get-tuple-element.86), channel_id=1, source_target_pairs={{0,1},{1,0},{2,3},{3,2},{4,5},{5,4},{6,7},{7,6},{8,9},{9,8},{10,11... | collective-permute-start | bytes 786440 | tf_op jit(solution)/shard_map/ppermute | solution.py:21
  54.5 1.7 %collective-permute-start.19 = (bf16[2,64,1024]{2,1,0:T(8,128)(2,1)S(1)}, bf16[2,64,1024]{2,1,0:T(8,128)(2,1)S(1)}, u32[]{:S(2)}, u32[]{:S(2)}) collective-permute-start(bf16[2,64,1024]{2,1,0:T(8,128)(2,1)S(1)} %get-tuple-element.85), channel_id=1, source_target_pairs={{0,1},{1,0},{2,3},{3,2},{4,5},{5,4},{6,7},{7,6},{8,9},{9,8},{10,11... | collective-permute-start | bytes 786440 | tf_op jit(solution)/shard_map/ppermute | solution.py:21
  55.0 1.2 %collective-permute-start.21 = (f32[8,128]{1,0:T(8,128)S(1)}, f32[8,128]{1,0:T(8,128)S(1)}, u32[]{:S(2)}, u32[]{:S(2)}) collective-permute-start(f32[8,128]{1,0:T(8,128)S(1)} %slope_terms.1.slope), channel_id=1, source_target_pairs={{0,1},{1,0},{2,3},{3,2},{4,5},{5,4},{6,7},{7,6},{8,9},{9,8},{10,11... | collective-permute-start | bytes 12296 | tf_op jit(solution)/shard_map/ppermute | solution.py:21
